TPU v7x, 256 devices: a whole 4x4x8 slice. The times are simulated.
256 devices in a mesh: row: 32 (over y, x, z_hi), col: 8 (over z_lo, core).
Axes of the slice: x: 4, y: 4, z: 8 (z_hi: 2, z_lo: 4; z = z_hi * 4 + z_lo), core: 2. Of those that a mesh axis runs over, the one named last changes fastest.
Arguments:
- contact_map: bfloat16 [64, 1024, 1024], P(None, 'row', 'col'), may hold values from -6 to 6
- dilations: int32 [3], replicated, may hold values from 1 to 8, as said below
- conv_weight: bfloat16 [3, 9, 32, 64], replicated, may hold values from -0.25 to 0.25
- conv_gain: float32 [3, 32], replicated, may hold values from 0.5 to 2
- conv_shift: float32 [3, 32], replicated, may hold values from -0.5 to 0.5
- out_weight: bfloat16 [3, 64, 32], replicated, may hold values from -1 to 1
Outputs:
- contact_out: bfloat16 [64, 1024, 1024], P(None, 'row', 'col')
Inputs may be any that keep to these rules, and one draw needn't show every extreme that they name: `dilations`: each block's dilation; some block's dilation equals 8.
All inputs are finite; a program needn't handle non-finite values.
Results may differ from a plain program's by a relative error of at most 0.0071.
Values may be sent and summed in bfloat16 or wider, within the bound.
No kernel may reach another device: no remote copies, remote signals or barrier semaphores. Data moves between devices by JAX's collectives and lax.ppermute only.
A program may use at most 64 MiB of HBM per device.

v0:
```python
import jax
import jax.numpy as jnp
from jax import lax
from jax.sharding import PartitionSpec as P

DMAX = 8


def extended(shard, sides, width):
    for axis, dim in sides:
        count, length = (lax.axis_size(axis), shard.shape[dim])
        up = [(i, (i + 1) % count) for i in range(count - 1)]
        down = [(j, i) for i, j in up]
        last = lax.slice_in_dim(shard, length - width, length, axis=dim)
        leading = lax.slice_in_dim(shard, 0, width, axis=dim)
        before = lax.ppermute(last, axis, up)
        after = lax.ppermute(leading, axis, down)
        shard = jnp.concatenate([before, shard, after], axis=dim)
    return shard


def convolve(padded, margin, out_rows, out_cols, spacing, kernel):
    zero_start = jnp.zeros((), jnp.int32)
    accumulated = jnp.zeros((kernel.shape[1], out_rows, out_cols), jnp.float32)
    for offset_row in range(3):
        for offset_col in range(3):
            row_start = margin + (offset_row - 1) * spacing
            col_start = margin + (offset_col - 1) * spacing
            window = lax.dynamic_slice(
                padded, (zero_start, row_start, col_start), (padded.shape[0], out_rows, out_cols)
            )
            accumulated = accumulated + jnp.einsum(
                "oc,cyx->oyx",
                kernel[3 * offset_row + offset_col],
                window,
                preferred_element_type=jnp.float32,
            )
    return accumulated


def residual(
    center, padded, margin, out_rows, out_cols, spacing, kernel, gain_col, shift_col, expand
):
    active = jnp.maximum(padded, jnp.zeros((), padded.dtype))
    accumulated = convolve(active, margin, out_rows, out_cols, spacing, kernel)
    hidden = jnp.maximum(
        gain_col[:, None, None] * accumulated + shift_col[:, None, None], 0.0
    ).astype(jnp.bfloat16)
    updated = center.astype(jnp.float32) + jnp.einsum(
        "oh,hyx->oyx", expand, hidden, preferred_element_type=jnp.float32
    )
    return (updated.astype(jnp.bfloat16), hidden)


def rimmed(feature_map):
    return extended(feature_map, (("row", 1), ("col", 2)), DMAX)


def turn_whole(feature_map):
    channels, tile_rows, tile_cols = feature_map.shape
    col_count = lax.axis_size("col")
    row_count = lax.axis_size("row")
    turned = lax.all_to_all(
        lax.all_to_all(feature_map, "col", split_axis=1, concat_axis=2, tiled=True),
        "row",
        split_axis=2,
        concat_axis=1,
        tiled=True,
    )
    turned = turned.reshape(channels, row_count, 1, tile_rows // col_count, tile_rows)
    settled = lax.all_to_all(turned, "col", split_axis=1, concat_axis=2, tiled=True)
    return jnp.swapaxes(settled.reshape(channels, tile_cols, tile_rows), 1, 2)


def on_device(contact_map, dilations, conv_weight, conv_gain, conv_shift, out_weight):
    channels, tile_rows, tile_cols = contact_map.shape

    def apply_block(layer_index, center, padded, out_rows, out_cols):
        return residual(
            center,
            padded,
            DMAX,
            out_rows,
            out_cols,
            dilations[layer_index],
            conv_weight[layer_index],
            conv_gain[layer_index],
            conv_shift[layer_index],
            out_weight[layer_index],
        )

    first_map, unused_hidden = apply_block(
        0, contact_map, rimmed(contact_map), tile_rows, tile_cols
    )
    second_input = rimmed(first_map)
    second_map, second_hidden = apply_block(1, first_map, second_input, tile_rows, tile_cols)
    mirrored = turn_whole(second_map)
    averaged = (0.5 * (second_map.astype(jnp.float32) + mirrored.astype(jnp.float32))).astype(
        jnp.bfloat16
    )
    layer_index = 2
    averaged, unused_hidden = apply_block(
        layer_index, averaged, rimmed(averaged), tile_rows, tile_cols
    )
    return averaged


def solution(mesh):
    return jax.shard_map(
        on_device,
        mesh=mesh,
        in_specs=(P(None, "row", "col"), P(), P(), P(), P(), P()),
        out_specs=P(None, "row", "col"),
        check_vma=False,
    )
```

profile of v0, /device:TPU:1, one launch (start us, length us, event | category | flops | bytes accessed | tf_op | source)
XLA Modules:
  0.0 231.6 jit_solution(9930131376130635337)
XLA Ops:
  1.1 9.7 %collective-permute-start = (bf16[64,8,128]{2,0,1:T(8,128)(2,1)S(1)}, bf16[64,8,128]{2,0,1:T(8,128)(2,1)S(1)}, u32[]{:S(2)}, u32[]{:S(2)}) collective-permute-start(bf16[64,8,128]{2,0,1:T(8,128)(2,1)S(1)} %copy.49), channel_id=1, source_target_pairs={{0,8},{8,16},{16,24},{24,32},{32,40},{40,48},{48,56},{56,64},{64,7... | collective-permute-start | bytes 393224 | tf_op jit(solution)/shard_map/ppermute | solution.py:16
  13.3 10.0 %collective-permute-done.1 = bf16[64,8,128]{2,0,1:T(8,128)(2,1)S(1)} collective-permute-done((bf16[64,8,128]{2,0,1:T(8,128)(2,1)S(1)}, bf16[64,8,128]{2,0,1:T(8,128)(2,1)S(1)}, u32[]{:S(2)}, u32[]{:S(2)}) %collective-permute-start.1) | collective-permute-done | bytes 131104 | tf_op jit(solution)/shard_map/ppermute | solution.py:17
  24.0 5.1 %collective-permute-start.2 = (bf16[64,48,8]{0,2,1:T(8,128)(2,1)S(1)}, bf16[64,48,8]{0,2,1:T(8,128)(2,1)S(1)}, u32[]{:S(2)}, u32[]{:S(2)}) collective-permute-start(bf16[64,48,8]{0,2,1:T(8,128)(2,1)S(1)} %copy.26), channel_id=1, source_target_pairs={{0,1},{1,2},{2,3},{3,4},{4,5},{5,6},{6,7},{8,9},{9,10},{10,11},{11... | collective-permute-start | bytes 147464 | tf_op jit(solution)/shard_map/ppermute | solution.py:16
  29.4 1.9 collective-permute-start.3
  36.9 2.4 %maximum_maximum_fusion = bf16[64,48,144]{2,0,1:T(8,128)(2,1)S(1)} fusion(bf16[64,48,8]{2,0,1:T(8,128)(2,1)} %copy.29, bf16[64,48,128]{2,0,1:T(8,128)(2,1)S(1)} %constant_dynamic-update-slice_fusion, bf16[64,48,8]{2,0,1:T(8,128)(2,1)} %copy.28), kind=kLoop, calls=%fused_computation.1 | loop fusion | flops 3538944 | bytes 1769472 | tf_op jit(solution)/shard_map/max | solution.py:44
  53.3 2.7 %fusion.5 = bf16[64,32,128]{2,0,1:T(8,128)(2,1)S(1)} fusion(f32[32,128,32]{1,2,0:T(8,128)} %fusion.82, f32[32,128,32]{1,2,0:T(8,128)} %fusion.84, f32[32,128,32]{1,2,0:T(8,128)S(1)} %fusion.86, f32[32,128,32]{1,2,0:T(8,128)} %fusion.88, f32[32,128,32]{1,2,0:T(8,128)} %fusion.48, f32[32,128,32]{1,2,0:T(8,128)} %fusion.90, f32[32,128,32]{1,2,0:T(8,128)} %fusion.92, ...), kind=kOutput, calls=%fused_computation.12 | convolution fusion | flops 35913728 | bytes 5784584 | tf_op jit(solution)/shard_map/oh,hyx->oyx/dot_general | solution.py:49
  56.0 5.9 %collective-permute-start.4 = (bf16[64,8,128]{2,0,1:T(8,128)(2,1)S(1)}, bf16[64,8,128]{2,0,1:T(8,128)(2,1)S(1)}, u32[]{:S(2)}, u32[]{:S(2)}) collective-permute-start(bf16[64,8,128]{2,0,1:T(8,128)(2,1)S(1)} %get-tuple-element.13), channel_id=1, source_target_pairs={{0,8},{8,16},{16,24},{24,32},{32,40},{40,48},{48,56},{56,64},{64,7... | collective-permute-start | bytes 393224 | tf_op jit(solution)/shard_map/ppermute | solution.py:16
  63.2 3.1 %collective-permute-done.4 = bf16[64,8,128]{2,0,1:T(8,128)(2,1)S(1)} collective-permute-done((bf16[64,8,128]{2,0,1:T(8,128)(2,1)S(1)}, bf16[64,8,128]{2,0,1:T(8,128)(2,1)S(1)}, u32[]{:S(2)}, u32[]{:S(2)}) %collective-permute-start.4) | collective-permute-done | bytes 131104 | tf_op jit(solution)/shard_map/ppermute | solution.py:16
  66.3 7.1 %collective-permute-done.5 = bf16[64,8,128]{2,0,1:T(8,128)(2,1)S(1)} collective-permute-done((bf16[64,8,128]{2,0,1:T(8,128)(2,1)S(1)}, bf16[64,8,128]{2,0,1:T(8,128)(2,1)S(1)}, u32[]{:S(2)}, u32[]{:S(2)}) %collective-permute-start.5) | collective-permute-done | bytes 131104 | tf_op jit(solution)/shard_map/ppermute | solution.py:17
  74.8 4.2 %collective-permute-start.6 = (bf16[64,48,8]{0,2,1:T(8,128)(2,1)S(1)}, bf16[64,48,8]{0,2,1:T(8,128)(2,1)S(1)}, u32[]{:S(2)}, u32[]{:S(2)}) collective-permute-start(bf16[64,48,8]{0,2,1:T(8,128)(2,1)S(1)} %copy.30), channel_id=1, source_target_pairs={{0,1},{1,2},{2,3},{3,4},{4,5},{5,6},{6,7},{8,9},{9,10},{10,11},{11... | collective-permute-start | bytes 147464 | tf_op jit(solution)/shard_map/ppermute | solution.py:16
  79.3 1.9 collective-permute-start.7
  86.4 2.1 maximum_maximum_fusion.1
  102.5 2.7 %fusion.4 = bf16[64,32,128]{2,0,1:T(8,128)(2,1)S(1)} fusion(f32[32,128,32]{1,2,0:T(8,128)} %fusion.66, f32[32,128,32]{1,2,0:T(8,128)} %fusion.68, f32[32,128,32]{1,2,0:T(8,128)S(1)} %fusion.70, f32[32,128,32]{1,2,0:T(8,128)} %fusion.72, f32[32,128,32]{1,2,0:T(8,128)} %fusion.46, f32[32,128,32]{1,2,0:T(8,128)} %fusion.74, f32[32,128,32]{1,2,0:T(8,128)} %fusion.76, ...), kind=kOutput, calls=%fused_computation.11 | convolution fusion | flops 35913728 | bytes 5784584 | tf_op jit(solution)/shard_map/oh,hyx->oyx/dot_general | solution.py:49
  105.2 17.7 %all_to_all.42 = bf16[64,32,128]{2,0,1:T(8,128)(2,1)S(1)} all-to-all(bf16[64,32,128]{2,0,1:T(8,128)(2,1)S(1)} %fusion.4), channel_id=1, replica_groups=mesh['row'=32,'col'=8] {'col'}, dimensions={1} | all-to-all | bytes 1048576 | tf_op jit(solution)/shard_map/all_to_all | solution.py:64
  124.3 29.6 %all_to_all.43 = bf16[32,2,4096]{2,1,0:T(2,128)(2,1)S(1)} all-to-all(bf16[32,2,4096]{2,1,0:T(2,128)(2,1)S(1)} %reshape.145), channel_id=1, replica_groups=mesh['row'=32,'col'=8] {'row'}, dimensions={0} | all-to-all | bytes 1048576 | tf_op jit(solution)/shard_map/all_to_all | solution.py:63
  155.6 19.9 %all_to_all.44 = bf16[8,2,16384]{2,1,0:T(2,128)(2,1)S(1)} all-to-all(bf16[8,2,16384]{2,1,0:T(2,128)(2,1)S(1)} %reshape.147), channel_id=1, replica_groups=mesh['row'=32,'col'=8] {'col'}, dimensions={0} | all-to-all | bytes 1048576 | tf_op jit(solution)/shard_map/all_to_all | solution.py:71
  176.7 2.3 copy.39
  180.4 4.0 %collective-permute-start.8 = (bf16[64,8,128]{2,0,1:T(8,128)(2,1)S(1)}, bf16[64,8,128]{2,0,1:T(8,128)(2,1)S(1)}, u32[]{:S(2)}, u32[]{:S(2)}) collective-permute-start(bf16[64,8,128]{2,0,1:T(8,128)(2,1)S(1)} %get-tuple-element.11), channel_id=1, source_target_pairs={{0,8},{8,16},{16,24},{24,32},{32,40},{40,48},{48,56},{56,64},{64,7... | collective-permute-start | bytes 393224 | tf_op jit(solution)/shard_map/ppermute | solution.py:16
  185.7 4.9 %collective-permute-done.8 = bf16[64,8,128]{2,0,1:T(8,128)(2,1)S(1)} collective-permute-done((bf16[64,8,128]{2,0,1:T(8,128)(2,1)S(1)}, bf16[64,8,128]{2,0,1:T(8,128)(2,1)S(1)}, u32[]{:S(2)}, u32[]{:S(2)}) %collective-permute-start.8) | collective-permute-done | bytes 131104 | tf_op jit(solution)/shard_map/ppermute | solution.py:16
  190.6 4.8 %collective-permute-done.9 = bf16[64,8,128]{2,0,1:T(8,128)(2,1)S(1)} collective-permute-done((bf16[64,8,128]{2,0,1:T(8,128)(2,1)S(1)}, bf16[64,8,128]{2,0,1:T(8,128)(2,1)S(1)}, u32[]{:S(2)}, u32[]{:S(2)}) %collective-permute-start.9) | collective-permute-done | bytes 131104 | tf_op jit(solution)/shard_map/ppermute | solution.py:17
  196.2 7.3 %collective-permute-start.10 = (bf16[64,48,8]{0,2,1:T(8,128)(2,1)S(1)}, bf16[64,48,8]{0,2,1:T(8,128)(2,1)S(1)}, u32[]{:S(2)}, u32[]{:S(2)}) collective-permute-start(bf16[64,48,8]{0,2,1:T(8,128)(2,1)S(1)} %copy.40), channel_id=1, source_target_pairs={{0,1},{1,2},{2,3},{3,4},{4,5},{5,6},{6,7},{8,9},{9,10},{10,11},{11... | collective-permute-start | bytes 147464 | tf_op jit(solution)/shard_map/ppermute | solution.py:16
  210.8 2.1 maximum_maximum_fusion.2
  226.1 3.3 %fusion.3 = bf16[64,32,128]{2,0,1:T(8,128)(2,1)} fusion(f32[32,128,32]{1,2,0:T(8,128)} %fusion.50, f32[32,128,32]{1,2,0:T(8,128)} %fusion.52, f32[32,128,32]{1,2,0:T(8,128)S(1)} %fusion.54, f32[32,128,32]{1,2,0:T(8,128)} %fusion.56, f32[32,128,32]{1,2,0:T(8,128)} %fusion.44, f32[32,128,32]{1,2,0:T(8,128)} %fusion.58, f32[32,128,32]{1,2,0:T(8,128)S(1)} %fusion.60, ...), kind=kOutput, calls=%fused_computation.10 | convolution fusion | flops 35913728 | bytes 5784584 | tf_op jit(solution)/shard_map/oh,hyx->oyx/dot_general | solution.py:49
  229.4 2.2 copy.44
  (80 shorter events, 67.3 us)
Async XLA Ops:
  0.0 13.1 %copy-start = (bf16[64,32,128]{2,1,0:T(8,128)(2,1)S(1)}, bf16[64,32,128]{2,1,0:T(8,128)(2,1)}, u32[]{:S(2)}) copy-start(bf16[64,32,128]{2,1,0:T(8,128)(2,1)} %param.6) | copy-start | bytes 1572868
  1.1 12.0 %collective-permute-start = (bf16[64,8,128]{2,0,1:T(8,128)(2,1)S(1)}, bf16[64,8,128]{2,0,1:T(8,128)(2,1)S(1)}, u32[]{:S(2)}, u32[]{:S(2)}) collective-permute-start(bf16[64,8,128]{2,0,1:T(8,128)(2,1)S(1)} %copy.49), channel_id=1, source_target_pairs={{0,8},{8,16},{16,24},{24,32},{32,40},{40,48},{48,56},{56,64},{64,7... | collective-permute-start | bytes 393224 | tf_op jit(solution)/shard_map/ppermute | solution.py:16
  10.8 12.6 %collective-permute-start.1 = (bf16[64,8,128]{2,0,1:T(8,128)(2,1)S(1)}, bf16[64,8,128]{2,0,1:T(8,128)(2,1)S(1)}, u32[]{:S(2)}, u32[]{:S(2)}) collective-permute-start(bf16[64,8,128]{2,0,1:T(8,128)(2,1)S(1)} %copy.50), channel_id=1, source_target_pairs={{8,0},{16,8},{24,16},{32,24},{40,32},{48,40},{56,48},{64,56},{72,6... | collective-permute-start | bytes 393224 | tf_op jit(solution)/shard_map/ppermute | solution.py:17
  23.7 7.6 %copy-start.3 = (s32[3]{0:T(128)S(1)}, s32[3]{0:T(128)}, u32[]{:S(2)}) copy-start(s32[3]{0:T(128)} %param.7) | copy-start | bytes 40
  24.0 10.5 %collective-permute-start.2 = (bf16[64,48,8]{0,2,1:T(8,128)(2,1)S(1)}, bf16[64,48,8]{0,2,1:T(8,128)(2,1)S(1)}, u32[]{:S(2)}, u32[]{:S(2)}) collective-permute-start(bf16[64,48,8]{0,2,1:T(8,128)(2,1)S(1)} %copy.26), channel_id=1, source_target_pairs={{0,1},{1,2},{2,3},{3,4},{4,5},{5,6},{6,7},{8,9},{9,10},{10,11},{11... | collective-permute-start | bytes 147464 | tf_op jit(solution)/shard_map/ppermute | solution.py:16
  29.4 6.3 %collective-permute-start.3 = (bf16[64,48,8]{0,2,1:T(8,128)(2,1)S(1)}, bf16[64,48,8]{0,2,1:T(8,128)(2,1)S(1)}, u32[]{:S(2)}, u32[]{:S(2)}) collective-permute-start(bf16[64,48,8]{0,2,1:T(8,128)(2,1)S(1)} %copy.27), channel_id=1, source_target_pairs={{1,0},{2,1},{3,2},{4,3},{5,4},{6,5},{7,6},{9,8},{10,9},{11,10},{12... | collective-permute-start | bytes 147464 | tf_op jit(solution)/shard_map/ppermute | solution.py:17
  56.0 10.3 %collective-permute-start.4 = (bf16[64,8,128]{2,0,1:T(8,128)(2,1)S(1)}, bf16[64,8,128]{2,0,1:T(8,128)(2,1)S(1)}, u32[]{:S(2)}, u32[]{:S(2)}) collective-permute-start(bf16[64,8,128]{2,0,1:T(8,128)(2,1)S(1)} %get-tuple-element.13), channel_id=1, source_target_pairs={{0,8},{8,16},{16,24},{24,32},{32,40},{40,48},{48,56},{56,64},{64,7... | collective-permute-start | bytes 393224 | tf_op jit(solution)/shard_map/ppermute | solution.py:16
  61.9 11.5 %collective-permute-start.5 = (bf16[64,8,128]{2,0,1:T(8,128)(2,1)S(1)}, bf16[64,8,128]{2,0,1:T(8,128)(2,1)S(1)}, u32[]{:S(2)}, u32[]{:S(2)}) collective-permute-start(bf16[64,8,128]{2,0,1:T(8,128)(2,1)S(1)} %get-tuple-element.14), channel_id=1, source_target_pairs={{8,0},{16,8},{24,16},{32,24},{40,32},{48,40},{56,48},{64,56},{72,6... | collective-permute-start | bytes 393224 | tf_op jit(solution)/shard_map/ppermute | solution.py:17
  73.4 0.7 copy-start.1
  74.8 8.7 %collective-permute-start.6 = (bf16[64,48,8]{0,2,1:T(8,128)(2,1)S(1)}, bf16[64,48,8]{0,2,1:T(8,128)(2,1)S(1)}, u32[]{:S(2)}, u32[]{:S(2)}) collective-permute-start(bf16[64,48,8]{0,2,1:T(8,128)(2,1)S(1)} %copy.30), channel_id=1, source_target_pairs={{0,1},{1,2},{2,3},{3,4},{4,5},{5,6},{6,7},{8,9},{9,10},{10,11},{11... | collective-permute-start | bytes 147464 | tf_op jit(solution)/shard_map/ppermute | solution.py:16
  79.3 5.9 %collective-permute-start.7 = (bf16[64,48,8]{0,2,1:T(8,128)(2,1)S(1)}, bf16[64,48,8]{0,2,1:T(8,128)(2,1)S(1)}, u32[]{:S(2)}, u32[]{:S(2)}) collective-permute-start(bf16[64,48,8]{0,2,1:T(8,128)(2,1)S(1)} %copy.31), channel_id=1, source_target_pairs={{1,0},{2,1},{3,2},{4,3},{5,4},{6,5},{7,6},{9,8},{10,9},{11,10},{12... | collective-permute-start | bytes 147464 | tf_op jit(solution)/shard_map/ppermute | solution.py:17
  97.0 5.5 %copy-start.2 = (bf16[3,64,32]{1,2,0:T(8,128)(2,1)S(1)}, bf16[3,64,32]{1,2,0:T(8,128)(2,1)}, u32[]{:S(2)}) copy-start(bf16[3,64,32]{1,2,0:T(8,128)(2,1)} %param.11) | copy-start | bytes 36868
  180.4 10.1 %collective-permute-start.8 = (bf16[64,8,128]{2,0,1:T(8,128)(2,1)S(1)}, bf16[64,8,128]{2,0,1:T(8,128)(2,1)S(1)}, u32[]{:S(2)}, u32[]{:S(2)}) collective-permute-start(bf16[64,8,128]{2,0,1:T(8,128)(2,1)S(1)} %get-tuple-element.11), channel_id=1, source_target_pairs={{0,8},{8,16},{16,24},{24,32},{32,40},{40,48},{48,56},{56,64},{64,7... | collective-permute-start | bytes 393224 | tf_op jit(solution)/shard_map/ppermute | solution.py:16
  184.4 11.0 %collective-permute-start.9 = (bf16[64,8,128]{2,0,1:T(8,128)(2,1)S(1)}, bf16[64,8,128]{2,0,1:T(8,128)(2,1)S(1)}, u32[]{:S(2)}, u32[]{:S(2)}) collective-permute-start(bf16[64,8,128]{2,0,1:T(8,128)(2,1)S(1)} %get-tuple-element.12), channel_id=1, source_target_pairs={{8,0},{16,8},{24,16},{32,24},{40,32},{48,40},{56,48},{64,56},{72,6... | collective-permute-start | bytes 393224 | tf_op jit(solution)/shard_map/ppermute | solution.py:17
  196.2 11.8 %collective-permute-start.10 = (bf16[64,48,8]{0,2,1:T(8,128)(2,1)S(1)}, bf16[64,48,8]{0,2,1:T(8,128)(2,1)S(1)}, u32[]{:S(2)}, u32[]{:S(2)}) collective-permute-start(bf16[64,48,8]{0,2,1:T(8,128)(2,1)S(1)} %copy.40), channel_id=1, source_target_pairs={{0,1},{1,2},{2,3},{3,4},{4,5},{5,6},{6,7},{8,9},{9,10},{10,11},{11... | collective-permute-start | bytes 147464 | tf_op jit(solution)/shard_map/ppermute | solution.py:16
  203.7 5.9 %collective-permute-start.11 = (bf16[64,48,8]{0,2,1:T(8,128)(2,1)S(1)}, bf16[64,48,8]{0,2,1:T(8,128)(2,1)S(1)}, u32[]{:S(2)}, u32[]{:S(2)}) collective-permute-start(bf16[64,48,8]{0,2,1:T(8,128)(2,1)S(1)} %copy.41), channel_id=1, source_target_pairs={{1,0},{2,1},{3,2},{4,3},{5,4},{6,5},{7,6},{9,8},{10,9},{11,10},{12... | collective-permute-start | bytes 147464 | tf_op jit(solution)/shard_map/ppermute | solution.py:17
where the time goes:
time: 234 us; the launch traced here: 232 us
  blocking collectives  67.2 us (29%)
  matrix products  49.8 us (21%)
  starting transfers between devices  45.7 us (20%)
  waiting for transfers between devices  32.8 us (14%)
  local copies, waits for them, and re-layouts  20.1 us (9%)
  other arithmetic  8.48 us (4%)
  between operations  7.52 us (3%)
    dot_general x24, matrix products, convolve(): jnp.einsum('oc,cyx->oyx', kernel[3 * offset_row + offset_col], window, pr...  41.1 us
    ppermute x6, starting transfers between devices, extended(): before = lax.ppermute(last, axis, up)  36.1 us
    all_to_all x1, blocking collectives, turn_whole(): lax.all_to_all(lax.all_to_all(feature_map, 'col', split_axis=1, concat_ax...  29.6 us
    ppermute x6, waiting for transfers between devices, extended(): after = lax.ppermute(leading, axis, down)  24.7 us
    all_to_all x1, blocking collectives, turn_whole(): lax.all_to_all(turned, 'col', split_axis=1, concat_axis=2, tiled=True)  19.9 us
    all_to_all x1, blocking collectives, turn_whole(): lax.all_to_all(feature_map, 'col', split_axis=1, concat_axis=2, tiled=True)  17.7 us
    ppermute x6, starting transfers between devices, extended(): after = lax.ppermute(leading, axis, down)  9.63 us
    dot_general x3, matrix products, residual(): jnp.einsum('oh,hyx->oyx', expand, hidden, preferred_element_type=jnp.floa...  8.67 us
  transfers between devices with their start and end apart: 12, of which 8 were waited for; matrix products, arithmetic and copies ran while one was open for 2% of the time, Pallas kernels for 0%

commit v1 on v0

v1 whole, which is shorter than its diff:
```python
import functools

import jax
import jax.numpy as jnp
from jax import lax
from jax.experimental import pallas as pl
from jax.experimental.pallas import tpu as pltpu
from jax.sharding import PartitionSpec as P

D = 8
BOTH = ("row", "col")
BF = jnp.bfloat16
F32 = jnp.float32
VMEM = pl.BlockSpec(memory_space=pltpu.VMEM)
SMEM = pl.BlockSpec(memory_space=pltpu.SMEM)
LIMIT = 40 * 1024 * 1024


def call(body, outs, args, n_smem, scratch, flops, moved):
    return pl.pallas_call(
        body,
        out_shape=outs,
        in_specs=[SMEM] * n_smem + [VMEM] * (len(args) - n_smem),
        out_specs=jax.tree.map(lambda _: VMEM, outs),
        scratch_shapes=scratch,
        compiler_params=pltpu.CompilerParams(vmem_limit_bytes=LIMIT),
        cost_estimate=pl.CostEstimate(flops=flops, bytes_accessed=moved, transcendentals=0),
    )(*args)


def lanes(rows):
    return lax.broadcasted_iota(jnp.int32, (rows, 128), 1)


def pack_strips(pieces, start, width, count):
    lane = lanes(64)
    total = None
    for place, piece in enumerate(pieces):
        moved = pltpu.roll(piece.astype(F32), (place * width - start) % 128, 1)
        total = moved if total is None else jnp.where(lane >= place * width, moved, total)
    return total.astype(BF)


def side_lanes(from_right, from_left, place, width):
    lane = lanes(64)
    right = pltpu.roll(from_right.astype(F32), (-place * width) % 128, 1)
    left = pltpu.roll(from_left.astype(F32), (128 - width - place * width) % 128, 1)
    side = jnp.where(lane < width, right, jnp.where(lane >= 128 - width, left, 0.0))
    return side.astype(BF)


def block_row(source, at, spacing, kernel, gain, shift, expand):
    stacked = jnp.concatenate(
        [source[at - spacing], source[at], source[at + spacing]], axis=0
    )
    taps = jnp.dot(kernel, jnp.maximum(stacked, 0), preferred_element_type=F32)
    conv = (
        taps[32:64]
        + pltpu.roll(taps[:32], spacing, 1)
        + pltpu.roll(taps[64:], 256 - spacing, 1)
    )
    hidden = jnp.maximum(gain * conv + shift, 0.0).astype(BF)
    return source[at].astype(F32) + jnp.dot(expand, hidden, preferred_element_type=F32)


def pack_first(up_ref, own_ref, down_ref, left_ref, right_ref):
    def step(g, _):
        pieces = [up_ref[g], own_ref[g], own_ref[g + 16], down_ref[g]]
        left_ref[g] = pack_strips(pieces, 0, 32, 4)
        right_ref[g] = pack_strips(pieces, 96, 32, 4)
        return _

    lax.fori_loop(0, 16, step, 0)


def first_blocks(
    spacing_ref, place_ref, up_ref, own_ref, down_ref, from_left, from_right,
    kernel_ref, gain_ref, shift_ref, expand_ref,
    center_ref, message_ref, wide, middle, turned, pair,
):
    row, col = place_ref[0], place_ref[1]
    members = place_ref[2]

    def fill(g, _):
        for q, ref in enumerate((up_ref, own_ref, own_ref, down_ref)):
            wide[q * 16 + g, :, :128] = ref[g + (16 if q == 2 else 0)]
            wide[q * 16 + g, :, 128:] = side_lanes(from_right[g], from_left[g], q, 32)
        return _

    lax.fori_loop(0, 16, fill, 0)
    lane = lax.broadcasted_iota(jnp.int32, (64, 256), 1)
    inside = (lane < 128) | ((lane < 192) & (col < 7)) | ((lane >= 192) & (col > 0))

    def one(r, _):
        out = block_row(
            wide, r + 8, spacing_ref[0], kernel_ref[0], gain_ref[0], shift_ref[0], expand_ref[0]
        )
        number = 32 * row - 8 + r
        alive = inside & (number >= 0) & (number < 1024)
        middle[r] = jnp.where(alive, out, 0.0).astype(BF)
        return _

    lax.fori_loop(0, 48, one, 0, unroll=4)

    def two(i, _):
        for half in range(2):
            r = i + 16 * half
            out = block_row(
                middle, r + 8, spacing_ref[1], kernel_ref[1], gain_ref[1], shift_ref[1],
                expand_ref[1],
            )
            out = jnp.where(inside, out, 0.0).astype(BF)
            center_ref[r] = out[:, :128]
            pair[64 * half : 64 * half + 64] = pltpu.roll(out.astype(F32), 8, 1)
        across = jnp.transpose(pair[...])
        turned[pl.ds(i, 144, stride=16), :] = across[:144]
        return _

    lax.fori_loop(0, 16, two, 0, unroll=2)
    for m in range(4):
        message_ref[lax.rem(m - members + 4, 4)] = turned[
            512 * m : 512 * m + 768
        ].astype(BF)


def average(
    place_ref, center_ref, up_ref, down_ref, m0, m1, m2, m3,
    mean_ref, left_ref, right_ref, gathered,
):
    members = place_ref[2]
    for t, ref in enumerate((m0, m1, m2, m3)):
        gathered[lax.rem(members - t + 4, 4)] = ref[...]

    def step(j, mine):
        blocks = []
        start = pl.multiple_of(j * 16, 16)
        for k in range(4):
            part = gathered[k, pl.ds(start, 16), :].astype(F32)
            blocks += [part, pltpu.roll(part, 64, 1)]
        mirrored = jnp.transpose(jnp.concatenate(blocks, axis=0))[:64]
        mean_ref[j] = (0.5 * (mine.astype(F32) + mirrored)).astype(BF)

    def above(j, _):
        step(j, up_ref[j])
        return _

    def inner(j, _):
        step(j + 8, center_ref[j])
        return _

    def below(j, _):
        step(j + 40, down_ref[j])
        return _

    lax.fori_loop(0, 8, above, 0, unroll=2)
    lax.fori_loop(0, 32, inner, 0, unroll=2)
    lax.fori_loop(0, 8, below, 0, unroll=2)

    def strips(g, _):
        pieces = [mean_ref[8 * g + q] for q in range(8)]
        left_ref[g] = pack_strips(pieces, 0, 16, 8)
        right_ref[g] = pack_strips(pieces, 112, 16, 8)
        return _

    lax.fori_loop(0, 6, strips, 0)


def last_block(
    spacing_ref, mean_ref, from_left, from_right, kernel_ref, gain_ref, shift_ref, expand_ref,
    out_ref, wide,
):
    def fill(g, _):
        for q in range(8):
            wide[8 * g + q, :, :128] = mean_ref[8 * g + q]
            wide[8 * g + q, :, 128:] = side_lanes(from_right[g], from_left[g], q, 16)
        return _

    lax.fori_loop(0, 6, fill, 0)

    def one(r, _):
        out = block_row(
            wide, r + 8, spacing_ref[2], kernel_ref[2], gain_ref[2], shift_ref[2], expand_ref[2]
        )
        out_ref[r] = out[:, :128].astype(BF)
        return _

    lax.fori_loop(0, 32, one, 0, unroll=4)


def on_device(contact_map, dilations, conv_weight, conv_gain, conv_shift, out_weight):
    rows, cols = lax.axis_size("row"), lax.axis_size("col")
    row, col = lax.axis_index("row"), lax.axis_index("col")
    place = jnp.stack([row, col, lax.rem(row, 4)]).astype(jnp.int32)
    down_way = [(r, r + 1) for r in range(rows - 1)]
    up_way = [(r + 1, r) for r in range(rows - 1)]
    right_way = [(c, c + 1) for c in range(cols - 1)]
    left_way = [(c + 1, c) for c in range(cols - 1)]

    own = jnp.transpose(contact_map, (1, 0, 2))
    above = lax.ppermute(own[16:], "row", down_way)
    below = lax.ppermute(own[:16], "row", up_way)
    kernel = jnp.transpose(conv_weight.reshape(3, 3, 3, 32, 64), (0, 2, 3, 1, 4)).reshape(3, 96, 192)
    gain = jnp.broadcast_to(conv_gain[:, :, None], (3, 32, 256))
    shift = jnp.broadcast_to(conv_shift[:, :, None], (3, 32, 256))
    weights = (kernel, gain, shift, out_weight)

    strip = jax.ShapeDtypeStruct((16, 64, 128), BF)
    to_left, to_right = call(
        pack_first, (strip, strip), (above, own, below), 0, [], 0, 2 << 20
    )
    from_left = lax.ppermute(to_right, "col", right_way)
    from_right = lax.ppermute(to_left, "col", left_way)

    center, messages = call(
        first_blocks,
        (jax.ShapeDtypeStruct((32, 64, 128), BF), jax.ShapeDtypeStruct((4, 768, 128), BF)),
        (dilations, place, above, own, below, from_left, from_right, *weights),
        2,
        [
            pltpu.VMEM((64, 64, 256), BF),
            pltpu.VMEM((48, 64, 256), BF),
            pltpu.VMEM((144 * 16, 128), F32),
            pltpu.VMEM((128, 256), F32),
        ],
        80 * 256 * 64 * 32 * 20,
        4 << 20,
    )
    above = lax.ppermute(center[24:], "row", down_way)
    below = lax.ppermute(center[:8], "row", up_way)
    received = []
    for t in range(4):
        pairs = []
        for a in range(rows // 4):
            for k in range(4):
                for b in range(cols):
                    pairs.append(((4 * a + k) * cols + b, (4 * b + (k + t) % 4) * cols + a))
        received.append(lax.ppermute(messages[t], BOTH, pairs))

    strip = jax.ShapeDtypeStruct((6, 64, 128), BF)
    mean, to_left, to_right = call(
        average,
        (jax.ShapeDtypeStruct((48, 64, 128), BF), strip, strip),
        (place, center, above, below, *received),
        1,
        [pltpu.VMEM((4, 768, 128), BF)],
        0,
        3 << 20,
    )
    from_left = lax.ppermute(to_right, "col", right_way)
    from_right = lax.ppermute(to_left, "col", left_way)
    out = call(
        last_block,
        jax.ShapeDtypeStruct((32, 64, 128), BF),
        (dilations, mean, from_left, from_right, *weights),
        1,
        [pltpu.VMEM((48, 64, 256), BF)],
        32 * 256 * 64 * 32 * 20,
        2 << 20,
    )
    return jnp.transpose(out, (1, 0, 2))


def solution(mesh):
    return jax.shard_map(
        on_device,
        mesh=mesh,
        in_specs=(P(None, "row", "col"), P(), P(), P(), P(), P()),
        out_specs=P(None, "row", "col"),
        check_vma=False,
    )
```

time: 234 us -> 149 us (0.64)
  the two profiles are of different devices: /device:TPU:1 before, /device:TPU:43 now
where the time goes in v1:
time: 149 us
  starting transfers between devices  66.8 us (45%)
  waiting for transfers between devices  47.7 us (32%)
  Pallas kernels  30.4 us (20%)
  local copies, waits for them, and re-layouts  3.69 us (2%)
    ppermute x2, starting transfers between devices, on_device(): from_left = lax.ppermute(to_right, 'col', right_way)  32.2 us
    pallas_call x4, Pallas kernels, call(): pl.pallas_call(body, out_shape=outs, in_specs=[SMEM] * n_smem + [VMEM] *...  30.4 us
    ppermute x2, waiting for transfers between devices, on_device(): from_right = lax.ppermute(to_left, 'col', left_way)  12 us
    ppermute x1, waiting for transfers between devices, on_device(): above = lax.ppermute(center[24:], 'row', down_way)  11.6 us
    ppermute x4, starting transfers between devices, on_device(): received.append(lax.ppermute(messages[t], BOTH, pairs))  11.5 us
    ppermute x1, waiting for transfers between devices, on_device(): above = lax.ppermute(own[16:], 'row', down_way)  10.5 us
    ppermute x1, waiting for transfers between devices, on_device(): below = lax.ppermute(own[:16], 'row', up_way)  10.4 us
    ppermute x1, starting transfers between devices, on_device(): below = lax.ppermute(own[:16], 'row', up_way)  7.89 us
  transfers between devices with their start and end apart: 12, of which 7 were waited for; matrix products, arithmetic and copies ran while one was open for 0% of the time, Pallas kernels for 0%

profile of v1, /device:TPU:43, one launch (start us, length us, event | category | flops | bytes accessed | tf_op | source)
XLA Modules:
  0.0 148.9 jit_solution(17671443601857028315)
XLA Ops:
  0.0 1.2 copy.19
  1.3 7.9 %collective-permute-start.1 = (bf16[16,64,128]{2,1,0:T(8,128)(2,1)S(1)}, bf16[16,64,128]{2,1,0:T(8,128)(2,1)S(1)}, u32[]{:S(2)}, u32[]{:S(2)}) collective-permute-start(bf16[16,64,128]{2,1,0:T(8,128)(2,1)S(1)} %get-tuple-element.25), channel_id=1, source_target_pairs={{8,0},{16,8},{24,16},{32,24},{40,32},{48,40},{56,48},{64,56},{72,6... | collective-permute-start | bytes 786440 | tf_op jit(solution)/shard_map/ppermute | solution.py:201
  9.2 1.9 %collective-permute-start = (bf16[16,64,128]{2,1,0:T(8,128)(2,1)S(1)}, bf16[16,64,128]{2,1,0:T(8,128)(2,1)S(1)}, u32[]{:S(2)}, u32[]{:S(2)}) collective-permute-start(bf16[16,64,128]{2,1,0:T(8,128)(2,1)S(1)} %get-tuple-element.26), channel_id=1, source_target_pairs={{0,8},{8,16},{16,24},{24,32},{32,40},{40,48},{48,56},{56,64},{64,7... | collective-permute-start | bytes 786440 | tf_op jit(solution)/shard_map/ppermute | solution.py:200
  11.1 10.4 %collective-permute-done.1.down_ref = bf16[16,64,128]{2,1,0:T(8,128)(2,1)S(1)} collective-permute-done((bf16[16,64,128]{2,1,0:T(8,128)(2,1)S(1)}, bf16[16,64,128]{2,1,0:T(8,128)(2,1)S(1)}, u32[]{:S(2)}, u32[]{:S(2)}) %collective-permute-start.1) | collective-permute-done | bytes 262176 | tf_op jit(solution)/shard_map/ppermute | solution.py:201
  21.5 10.5 %collective-permute-done.up_ref = bf16[16,64,128]{2,1,0:T(8,128)(2,1)S(1)} collective-permute-done((bf16[16,64,128]{2,1,0:T(8,128)(2,1)S(1)}, bf16[16,64,128]{2,1,0:T(8,128)(2,1)S(1)}, u32[]{:S(2)}, u32[]{:S(2)}) %collective-permute-start) | collective-permute-done | bytes 262176 | tf_op jit(solution)/shard_map/ppermute | solution.py:200
  32.1 1.5 %shard_map.64 = (bf16[16,64,128]{2,1,0:T(8,128)(2,1)S(1)}, bf16[16,64,128]{2,1,0:T(8,128)(2,1)S(1)}) custom-call(bf16[16,64,128]{2,1,0:T(8,128)(2,1)S(1)} %collective-permute-done.up_ref, bf16[32,64,128]{2,1,0:T(8,128)(2,1)S(1)} %bitcast.20, bf16[16,64,128]{2,1,0:T(8,128)(2,1)S(1)} %collective-permute-done.1.down_ref), custom_call_target="tpu_custom_call" | custom-call | bytes 2097152 | tf_op jit(solution)/shard_map/pallas_call | solution.py:20
  33.6 4.2 %collective-permute-start.2 = (bf16[16,64,128]{2,1,0:T(8,128)(2,1)S(1)}, bf16[16,64,128]{2,1,0:T(8,128)(2,1)S(1)}, u32[]{:S(2)}, u32[]{:S(2)}) collective-permute-start(bf16[16,64,128]{2,1,0:T(8,128)(2,1)S(1)} %get-tuple-element.12), channel_id=1, source_target_pairs={{0,1},{1,2},{2,3},{3,4},{4,5},{5,6},{6,7},{8,9},{9,10},{10,11},{11... | collective-permute-start | bytes 786440 | tf_op jit(solution)/shard_map/ppermute | solution.py:211
  37.8 1.9 %collective-permute-start.3 = (bf16[16,64,128]{2,1,0:T(8,128)(2,1)S(1)}, bf16[16,64,128]{2,1,0:T(8,128)(2,1)S(1)}, u32[]{:S(2)}, u32[]{:S(2)}) collective-permute-start(bf16[16,64,128]{2,1,0:T(8,128)(2,1)S(1)} %get-tuple-element.13), channel_id=1, source_target_pairs={{1,0},{2,1},{3,2},{4,3},{5,4},{6,5},{7,6},{9,8},{10,9},{11,10},{12... | collective-permute-start | bytes 786440 | tf_op jit(solution)/shard_map/ppermute | solution.py:212
  40.4 0.8 collective-permute-done.2.from_left
  41.1 4.4 %collective-permute-done.3.from_right = bf16[16,64,128]{2,1,0:T(8,128)(2,1)S(1)} collective-permute-done((bf16[16,64,128]{2,1,0:T(8,128)(2,1)S(1)}, bf16[16,64,128]{2,1,0:T(8,128)(2,1)S(1)}, u32[]{:S(2)}, u32[]{:S(2)}) %collective-permute-start.3) | collective-permute-done | bytes 262176 | tf_op jit(solution)/shard_map/ppermute | solution.py:212
  46.3 17.0 %shard_map.65 = (bf16[32,64,128]{2,1,0:T(8,128)(2,1)S(1)}, bf16[4,768,128]{2,1,0:T(8,128)(2,1)S(1)}) custom-call(s32[3]{0:T(128)S(1)} %copy-done, s32[3]{0:T(128)S(1)} %pad_add_fusion.place_ref, bf16[16,64,128]{2,1,0:T(8,128)(2,1)S(1)} %collective-permute-done.up_ref, bf16[32,64,128]{2,1,0:T(8,128)(2,1)S(1)} %bitcast.21, ...), custom_call_target="tpu_custom_call" | custom-call | flops 838860800 | bytes 4194304 | tf_op jit(solution)/shard_map/pallas_call | solution.py:20
  63.3 6.9 %collective-permute-start.5 = (bf16[8,64,128]{2,1,0:T(8,128)(2,1)S(1)}, bf16[8,64,128]{2,1,0:T(8,128)(2,1)S(1)}, u32[]{:S(2)}, u32[]{:S(2)}) collective-permute-start(bf16[8,64,128]{2,1,0:T(8,128)(2,1)S(1)} %get-tuple-element.23), channel_id=1, source_target_pairs={{8,0},{16,8},{24,16},{32,24},{40,32},{48,40},{56,48},{64,56},{72,6... | collective-permute-start | bytes 393224 | tf_op jit(solution)/shard_map/ppermute | solution.py:229
  70.7 1.5 collective-permute-start.8
  72.2 7.3 %collective-permute-start.7 = (bf16[768,128]{1,0:T(8,128)(2,1)S(1)}, bf16[768,128]{1,0:T(8,128)(2,1)S(1)}, u32[]{:S(2)}, u32[]{:S(2)}) collective-permute-start(bf16[768,128]{1,0:T(8,128)(2,1)S(1)} %get-tuple-element.21), channel_id=1, source_target_pairs={{0,8},{1,40},{2,72},{3,104},{4,136},{5,168},{6,200},{7,232},{8,16}... | collective-permute-start | bytes 589832 | tf_op jit(solution)/shard_map/ppermute | solution.py:237
  79.5 2.2 %collective-permute-start.6 = (bf16[768,128]{1,0:T(8,128)(2,1)S(1)}, bf16[768,128]{1,0:T(8,128)(2,1)S(1)}, u32[]{:S(2)}, u32[]{:S(2)}) collective-permute-start(bf16[768,128]{1,0:T(8,128)(2,1)S(1)} %get-tuple-element.22), channel_id=1, source_target_pairs={{0,0},{1,32},{2,64},{3,96},{4,128},{5,160},{6,192},{7,224},{8,8},{... | collective-permute-start | bytes 589832 | tf_op jit(solution)/shard_map/ppermute | solution.py:237
  81.7 2.5 %collective-permute-start.4 = (bf16[8,64,128]{2,1,0:T(8,128)(2,1)S(1)}, bf16[8,64,128]{2,1,0:T(8,128)(2,1)S(1)}, u32[]{:S(2)}, u32[]{:S(2)}) collective-permute-start(bf16[8,64,128]{2,1,0:T(8,128)(2,1)S(1)} %get-tuple-element.24), channel_id=1, source_target_pairs={{0,8},{8,16},{16,24},{24,32},{32,40},{40,48},{48,56},{56,64},{64,7... | collective-permute-start | bytes 393224 | tf_op jit(solution)/shard_map/ppermute | solution.py:228
  84.3 11.6 %collective-permute-done.4.up_ref = bf16[8,64,128]{2,1,0:T(8,128)(2,1)S(1)} collective-permute-done((bf16[8,64,128]{2,1,0:T(8,128)(2,1)S(1)}, bf16[8,64,128]{2,1,0:T(8,128)(2,1)S(1)}, u32[]{:S(2)}, u32[]{:S(2)}) %collective-permute-start.4) | collective-permute-done | bytes 131104 | tf_op jit(solution)/shard_map/ppermute | solution.py:228
  95.9 2.4 %collective-permute-done.6.m0 = bf16[768,128]{1,0:T(8,128)(2,1)S(1)} collective-permute-done((bf16[768,128]{1,0:T(8,128)(2,1)S(1)}, bf16[768,128]{1,0:T(8,128)(2,1)S(1)}, u32[]{:S(2)}, u32[]{:S(2)}) %collective-permute-start.6) | collective-permute-done | bytes 196640 | tf_op jit(solution)/shard_map/ppermute | solution.py:237
  98.3 5.1 %shard_map.66 = (bf16[48,64,128]{2,1,0:T(8,128)(2,1)S(1)}, bf16[6,64,128]{2,1,0:T(8,128)(2,1)S(1)}, bf16[6,64,128]{2,1,0:T(8,128)(2,1)S(1)}) custom-call(s32[3]{0:T(128)S(1)} %pad_add_fusion.place_ref, bf16[32,64,128]{2,1,0:T(8,128)(2,1)S(1)} %get-tuple-element.14.center_ref, bf16[8,64,128]{2,1,0:T(8,128)(2,1)S(1)} %collective-permute-done.4.up_ref, ...), custom_call_target="tpu_custom_call" | custom-call | bytes 3145728 | tf_op jit(solution)/shard_map/pallas_call | solution.py:20
  103.3 28.0 %collective-permute-start.10 = (bf16[6,64,128]{2,1,0:T(8,128)(2,1)S(1)}, bf16[6,64,128]{2,1,0:T(8,128)(2,1)S(1)}, u32[]{:S(2)}, u32[]{:S(2)}) collective-permute-start(bf16[6,64,128]{2,1,0:T(8,128)(2,1)S(1)} %get-tuple-element.17), channel_id=1, source_target_pairs={{0,1},{1,2},{2,3},{3,4},{4,5},{5,6},{6,7},{8,9},{9,10},{10,11},{11... | collective-permute-start | bytes 294920 | tf_op jit(solution)/shard_map/ppermute | solution.py:249
  131.4 1.9 %collective-permute-start.11 = (bf16[6,64,128]{2,1,0:T(8,128)(2,1)S(1)}, bf16[6,64,128]{2,1,0:T(8,128)(2,1)S(1)}, u32[]{:S(2)}, u32[]{:S(2)}) collective-permute-start(bf16[6,64,128]{2,1,0:T(8,128)(2,1)S(1)} %get-tuple-element.18), channel_id=1, source_target_pairs={{1,0},{2,1},{3,2},{4,3},{5,4},{6,5},{7,6},{9,8},{10,9},{11,10},{12... | collective-permute-start | bytes 294920 | tf_op jit(solution)/shard_map/ppermute | solution.py:250
  133.3 7.6 %collective-permute-done.11.from_right = bf16[6,64,128]{2,1,0:T(8,128)(2,1)S(1)} collective-permute-done((bf16[6,64,128]{2,1,0:T(8,128)(2,1)S(1)}, bf16[6,64,128]{2,1,0:T(8,128)(2,1)S(1)}, u32[]{:S(2)}, u32[]{:S(2)}) %collective-permute-start.11) | collective-permute-done | bytes 98336 | tf_op jit(solution)/shard_map/ppermute | solution.py:250
  140.9 6.8 %shard_map.67 = bf16[32,64,128]{2,1,0:T(8,128)(2,1)S(1)} custom-call(s32[3]{0:T(128)S(1)} %copy-done, bf16[48,64,128]{2,1,0:T(8,128)(2,1)S(1)} %get-tuple-element.16.mean_ref, bf16[6,64,128]{2,1,0:T(8,128)(2,1)S(1)} %collective-permute-done.10.from_left, bf16[6,64,128]{2,1,0:T(8,128)(2,1)S(1)} %collective-permute-done.11.from_right, ...), custom_call_target="tpu_custom_call" | custom-call | flops 335544320 | bytes 2097152 | tf_op jit(solution)/shard_map/pallas_call | solution.py:20
  147.7 1.1 copy.16
  (25 shorter events, 1.9 us)
Async XLA Ops:
  1.3 20.2 %collective-permute-start.1 = (bf16[16,64,128]{2,1,0:T(8,128)(2,1)S(1)}, bf16[16,64,128]{2,1,0:T(8,128)(2,1)S(1)}, u32[]{:S(2)}, u32[]{:S(2)}) collective-permute-start(bf16[16,64,128]{2,1,0:T(8,128)(2,1)S(1)} %get-tuple-element.25), channel_id=1, source_target_pairs={{8,0},{16,8},{24,16},{32,24},{40,32},{48,40},{56,48},{64,56},{72,6... | collective-permute-start | bytes 786440 | tf_op jit(solution)/shard_map/ppermute | solution.py:201
  9.2 22.9 %collective-permute-start = (bf16[16,64,128]{2,1,0:T(8,128)(2,1)S(1)}, bf16[16,64,128]{2,1,0:T(8,128)(2,1)S(1)}, u32[]{:S(2)}, u32[]{:S(2)}) collective-permute-start(bf16[16,64,128]{2,1,0:T(8,128)(2,1)S(1)} %get-tuple-element.26), channel_id=1, source_target_pairs={{0,8},{8,16},{16,24},{24,32},{32,40},{40,48},{48,56},{56,64},{64,7... | collective-permute-start | bytes 786440 | tf_op jit(solution)/shard_map/ppermute | solution.py:200
  32.1 7.8 %copy-start.1 = (bf16[3,9,32,64]{3,2,1,0:T(8,128)(2,1)S(1)}, bf16[3,9,32,64]{3,2,1,0:T(8,128)(2,1)}, u32[]{:S(2)}) copy-start(bf16[3,9,32,64]{3,2,1,0:T(8,128)(2,1)} %param.8) | copy-start | bytes 331780
  33.6 6.2 %copy-start.2 = (bf16[3,64,32]{1,2,0:T(8,128)(2,1)S(1)}, bf16[3,64,32]{1,2,0:T(8,128)(2,1)}, u32[]{:S(2)}) copy-start(bf16[3,64,32]{1,2,0:T(8,128)(2,1)} %param.11) | copy-start | bytes 36868
  33.6 7.5 %collective-permute-start.2 = (bf16[16,64,128]{2,1,0:T(8,128)(2,1)S(1)}, bf16[16,64,128]{2,1,0:T(8,128)(2,1)S(1)}, u32[]{:S(2)}, u32[]{:S(2)}) collective-permute-start(bf16[16,64,128]{2,1,0:T(8,128)(2,1)S(1)} %get-tuple-element.12), channel_id=1, source_target_pairs={{0,1},{1,2},{2,3},{3,4},{4,5},{5,6},{6,7},{8,9},{9,10},{10,11},{11... | collective-permute-start | bytes 786440 | tf_op jit(solution)/shard_map/ppermute | solution.py:211
  37.8 7.7 %collective-permute-start.3 = (bf16[16,64,128]{2,1,0:T(8,128)(2,1)S(1)}, bf16[16,64,128]{2,1,0:T(8,128)(2,1)S(1)}, u32[]{:S(2)}, u32[]{:S(2)}) collective-permute-start(bf16[16,64,128]{2,1,0:T(8,128)(2,1)S(1)} %get-tuple-element.13), channel_id=1, source_target_pairs={{1,0},{2,1},{3,2},{4,3},{5,4},{6,5},{7,6},{9,8},{10,9},{11,10},{12... | collective-permute-start | bytes 786440 | tf_op jit(solution)/shard_map/ppermute | solution.py:212
  40.3 5.3 %copy-start.3 = (f32[3,32]{1,0:T(4,128)S(1)}, f32[3,32]{1,0:T(4,128)}, u32[]{:S(2)}) copy-start(f32[3,32]{1,0:T(4,128)} %param.9) | copy-start | bytes 1156
  40.4 5.3 %copy-start.4 = (f32[3,32]{1,0:T(4,128)S(1)}, f32[3,32]{1,0:T(4,128)}, u32[]{:S(2)}) copy-start(f32[3,32]{1,0:T(4,128)} %param.10) | copy-start | bytes 1156
  45.6 0.7 copy-start
  63.3 18.4 %collective-permute-start.5 = (bf16[8,64,128]{2,1,0:T(8,128)(2,1)S(1)}, bf16[8,64,128]{2,1,0:T(8,128)(2,1)S(1)}, u32[]{:S(2)}, u32[]{:S(2)}) collective-permute-start(bf16[8,64,128]{2,1,0:T(8,128)(2,1)S(1)} %get-tuple-element.23), channel_id=1, source_target_pairs={{8,0},{16,8},{24,16},{32,24},{40,32},{48,40},{56,48},{64,56},{72,6... | collective-permute-start | bytes 393224 | tf_op jit(solution)/shard_map/ppermute | solution.py:229
  70.2 25.6 %collective-permute-start.9 = (bf16[768,128]{1,0:T(8,128)(2,1)S(1)}, bf16[768,128]{1,0:T(8,128)(2,1)S(1)}, u32[]{:S(2)}, u32[]{:S(2)}) collective-permute-start(bf16[768,128]{1,0:T(8,128)(2,1)S(1)} %get-tuple-element.19), channel_id=1, source_target_pairs={{0,24},{1,56},{2,88},{3,120},{4,152},{5,184},{6,216},{7,248},{8,0}... | collective-permute-start | bytes 589832 | tf_op jit(solution)/shard_map/ppermute | solution.py:237
  70.7 25.1 %collective-permute-start.8 = (bf16[768,128]{1,0:T(8,128)(2,1)S(1)}, bf16[768,128]{1,0:T(8,128)(2,1)S(1)}, u32[]{:S(2)}, u32[]{:S(2)}) collective-permute-start(bf16[768,128]{1,0:T(8,128)(2,1)S(1)} %get-tuple-element.20), channel_id=1, source_target_pairs={{0,16},{1,48},{2,80},{3,112},{4,144},{5,176},{6,208},{7,240},{8,24... | collective-permute-start | bytes 589832 | tf_op jit(solution)/shard_map/ppermute | solution.py:237
  72.2 23.7 %collective-permute-start.7 = (bf16[768,128]{1,0:T(8,128)(2,1)S(1)}, bf16[768,128]{1,0:T(8,128)(2,1)S(1)}, u32[]{:S(2)}, u32[]{:S(2)}) collective-permute-start(bf16[768,128]{1,0:T(8,128)(2,1)S(1)} %get-tuple-element.21), channel_id=1, source_target_pairs={{0,8},{1,40},{2,72},{3,104},{4,136},{5,168},{6,200},{7,232},{8,16}... | collective-permute-start | bytes 589832 | tf_op jit(solution)/shard_map/ppermute | solution.py:237
  79.5 18.8 %collective-permute-start.6 = (bf16[768,128]{1,0:T(8,128)(2,1)S(1)}, bf16[768,128]{1,0:T(8,128)(2,1)S(1)}, u32[]{:S(2)}, u32[]{:S(2)}) collective-permute-start(bf16[768,128]{1,0:T(8,128)(2,1)S(1)} %get-tuple-element.22), channel_id=1, source_target_pairs={{0,0},{1,32},{2,64},{3,96},{4,128},{5,160},{6,192},{7,224},{8,8},{... | collective-permute-start | bytes 589832 | tf_op jit(solution)/shard_map/ppermute | solution.py:237
  81.7 14.1 %collective-permute-start.4 = (bf16[8,64,128]{2,1,0:T(8,128)(2,1)S(1)}, bf16[8,64,128]{2,1,0:T(8,128)(2,1)S(1)}, u32[]{:S(2)}, u32[]{:S(2)}) collective-permute-start(bf16[8,64,128]{2,1,0:T(8,128)(2,1)S(1)} %get-tuple-element.24), channel_id=1, source_target_pairs={{0,8},{8,16},{16,24},{24,32},{32,40},{40,48},{48,56},{56,64},{64,7... | collective-permute-start | bytes 393224 | tf_op jit(solution)/shard_map/ppermute | solution.py:228
  103.3 30.0 %collective-permute-start.10 = (bf16[6,64,128]{2,1,0:T(8,128)(2,1)S(1)}, bf16[6,64,128]{2,1,0:T(8,128)(2,1)S(1)}, u32[]{:S(2)}, u32[]{:S(2)}) collective-permute-start(bf16[6,64,128]{2,1,0:T(8,128)(2,1)S(1)} %get-tuple-element.17), channel_id=1, source_target_pairs={{0,1},{1,2},{2,3},{3,4},{4,5},{5,6},{6,7},{8,9},{9,10},{10,11},{11... | collective-permute-start | bytes 294920 | tf_op jit(solution)/shard_map/ppermute | solution.py:249
  131.4 9.5 %collective-permute-start.11 = (bf16[6,64,128]{2,1,0:T(8,128)(2,1)S(1)}, bf16[6,64,128]{2,1,0:T(8,128)(2,1)S(1)}, u32[]{:S(2)}, u32[]{:S(2)}) collective-permute-start(bf16[6,64,128]{2,1,0:T(8,128)(2,1)S(1)} %get-tuple-element.18), channel_id=1, source_target_pairs={{1,0},{2,1},{3,2},{4,3},{5,4},{6,5},{7,6},{9,8},{10,9},{11,10},{12... | collective-permute-start | bytes 294920 | tf_op jit(solution)/shard_map/ppermute | solution.py:250

commit v2 on v1

v2 whole, which is shorter than its diff:
```python
import functools

import jax
import jax.numpy as jnp
from jax import lax
from jax.experimental import pallas as pl
from jax.experimental.pallas import tpu as pltpu
from jax.sharding import PartitionSpec as P

D = 8
BOTH = ("row", "col")
BF = jnp.bfloat16
F32 = jnp.float32
VMEM = pl.BlockSpec(memory_space=pltpu.VMEM)
SMEM = pl.BlockSpec(memory_space=pltpu.SMEM)
LIMIT = 40 * 1024 * 1024


def call(body, outs, args, n_smem, scratch, flops, moved):
    return pl.pallas_call(
        body,
        out_shape=outs,
        in_specs=[SMEM] * n_smem + [VMEM] * (len(args) - n_smem),
        out_specs=jax.tree.map(lambda _: VMEM, outs),
        scratch_shapes=scratch,
        compiler_params=pltpu.CompilerParams(vmem_limit_bytes=LIMIT),
        cost_estimate=pl.CostEstimate(flops=flops, bytes_accessed=moved, transcendentals=0),
    )(*args)


def lanes(rows):
    return lax.broadcasted_iota(jnp.int32, (rows, 128), 1)


def pack_strips(pieces, start, width):
    lane = lanes(64)
    total = None
    for place, piece in enumerate(pieces):
        moved = pltpu.roll(piece.astype(F32), (place * width - start) % 128, 1)
        total = moved if total is None else jnp.where(lane >= place * width, moved, total)
    return total.astype(BF)


def side_lanes(from_right, from_left, place, width):
    lane = lanes(64)
    right = pltpu.roll(from_right.astype(F32), (-place * width) % 128, 1)
    left = pltpu.roll(from_left.astype(F32), (128 - width - place * width) % 128, 1)
    side = jnp.where(lane < width, right, jnp.where(lane >= 128 - width, left, 0.0))
    return side.astype(BF)


def block_rows(source, rows, spacing, kernel, gain, shift, expand, narrow=False):
    taps = []
    for at in rows:
        stacked = jnp.concatenate(
            [source[at - spacing], source[at], source[at + spacing]], axis=0
        )
        taps.append(jnp.dot(kernel, jnp.maximum(stacked, 0), preferred_element_type=F32))
    lane = lanes(32)
    before, after = lane >= spacing, lane < 128 - spacing
    hidden = []
    for tap in taps:
        left = [pltpu.roll(tap[:32, h : h + 128], spacing, 1) for h in (0, 128)]
        right = [pltpu.roll(tap[64:, h : h + 128], 128 - spacing, 1) for h in (0, 128)]
        convs = []
        for h in range(1 if narrow else 2):
            convs.append(
                tap[32:64, 128 * h : 128 * h + 128]
                + jnp.where(before, left[h], left[1 - h])
                + jnp.where(after, right[h], right[1 - h])
            )
        hidden.append(
            [jnp.maximum(gain * conv + shift, 0.0).astype(BF) for conv in convs]
        )
    if narrow:
        hidden = [[h[0] for h in hidden[i : i + 2]] for i in range(0, len(rows), 2)]
    grown = [
        jnp.dot(expand, jnp.concatenate(h, axis=1), preferred_element_type=F32) for h in hidden
    ]
    if narrow:
        halves = [g[:, h : h + 128] for g in grown for h in (0, 128)]
        return [source[at, :, :128].astype(F32) + half for at, half in zip(rows, halves)]
    return [source[at].astype(F32) + g for at, g in zip(rows, grown)]


def block_of(layer, spacing_ref, kernel_ref, gain_ref, shift_ref, expand_ref):
    return (
        spacing_ref[layer], kernel_ref[layer], gain_ref[layer], shift_ref[layer], expand_ref[layer]
    )


def pack_first(up_ref, own_ref, down_ref, left_ref, right_ref):
    for ref, groups, first in ((up_ref, 6, 0), (own_ref, 8, 6), (down_ref, 6, 14)):

        def step(g, _):
            pieces = [ref[4 * g + q] for q in range(4)]
            left_ref[first + g] = pack_strips(pieces, 0, 32)
            right_ref[first + g] = pack_strips(pieces, 96, 32)
            return _

        lax.fori_loop(0, groups, step, 0, unroll=groups)


def first_blocks(
    spacing_ref, place_ref, up_ref, own_ref, down_ref, from_left, from_right,
    kernel_ref, gain_ref, shift_ref, expand_ref,
    center_ref, message_ref, wide, middle, turned,
):
    row, col = place_ref[0], place_ref[1]
    members = place_ref[2]
    weights = (spacing_ref, kernel_ref, gain_ref, shift_ref, expand_ref)

    for ref, groups, first in ((up_ref, 6, 0), (own_ref, 8, 6), (down_ref, 6, 14)):

        def fill(g, _):
            for q in range(4):
                at = 4 * (g + first) + q
                wide[at, :, :128] = ref[4 * g + q]
                wide[at, :, 128:] = side_lanes(
                    from_right[first + g], from_left[first + g], q, 32
                )
            return _

        lax.fori_loop(0, groups, fill, 0, unroll=2)
    lane = lax.broadcasted_iota(jnp.int32, (64, 256), 1)
    inside = (lane < 128) | ((lane < 192) & (col < 7)) | ((lane >= 192) & (col > 0))

    def kept(out, number):
        alive = inside & (number >= 0) & (number < 1024)
        return jnp.where(alive, out, 0.0)

    def one(i, _):
        start = i * 32
        outs = block_rows(wide, [start + b + 8 for b in range(32)], *block_of(0, *weights))
        for b, out in enumerate(outs):
            middle[start + b] = kept(out, 32 * row - 16 + start + b).astype(BF)
        return _

    lax.fori_loop(0, 2, one, 0)

    def two(i, _):
        start = i * 8
        rows = [40 * i + b for b in range(8)]
        for b in range(8):
            rows += [8 + start + b, 24 + start + b]
        outs = block_rows(middle, [r + 8 for r in rows], *block_of(1, *weights))
        outs = [kept(out, 32 * row - 8 + r) for r, out in zip(rows, outs)]
        for r, out in zip(rows, outs):
            center_ref[r] = out[:, :128].astype(BF)
        for b in range(8):
            pair = jnp.concatenate(outs[8 + 2 * b : 10 + 2 * b], axis=0).astype(BF)
            across = jnp.transpose(pltpu.roll(pair.astype(F32), 8, 1))
            turned[pl.ds(start + b, 144, stride=16), :] = across[:144]
        return _

    lax.fori_loop(0, 2, two, 0)
    for m in range(4):
        message_ref[lax.rem(m - members + 4, 4)] = turned[512 * m : 512 * m + 768].astype(BF)


def average(
    place_ref, center_ref, m0, m1, m2, m3, mean_ref, left_ref, right_ref, gathered
):
    members = place_ref[2]
    for t, ref in enumerate((m0, m1, m2, m3)):
        gathered[lax.rem(members - t + 4, 4)] = ref[...]

    def step(j, _):
        blocks = []
        start = pl.multiple_of(j * 16, 16)
        for k in range(4):
            part = gathered[k, pl.ds(start, 16), :].astype(F32)
            blocks += [part, pltpu.roll(part, 64, 1)]
        mirrored = jnp.transpose(jnp.concatenate(blocks, axis=0))[:64]
        mean_ref[j] = (0.5 * (center_ref[j].astype(F32) + mirrored)).astype(BF)
        return _

    lax.fori_loop(0, 48, step, 0, unroll=8)
    for g in range(6):
        pieces = [mean_ref[8 * g + q] for q in range(8)]
        left_ref[g] = pack_strips(pieces, 0, 16)
        right_ref[g] = pack_strips(pieces, 112, 16)


def last_block(
    spacing_ref, mean_ref, from_left, from_right, kernel_ref, gain_ref, shift_ref, expand_ref,
    out_ref, wide,
):
    weights = (spacing_ref, kernel_ref, gain_ref, shift_ref, expand_ref)
    for g in range(6):
        for q in range(8):
            wide[8 * g + q, :, :128] = mean_ref[8 * g + q]
            wide[8 * g + q, :, 128:] = side_lanes(from_right[g], from_left[g], q, 16)
    outs = block_rows(wide, [r + 8 for r in range(32)], *block_of(2, *weights), narrow=True)
    for r, out in enumerate(outs):
        out_ref[r] = out.astype(BF)


def on_device(contact_map, dilations, conv_weight, conv_gain, conv_shift, out_weight):
    rows, cols = lax.axis_size("row"), lax.axis_size("col")
    row, col = lax.axis_index("row"), lax.axis_index("col")
    place = jnp.stack([row, col, lax.rem(row, 4)]).astype(jnp.int32)
    down_way = [(r, r + 1) for r in range(rows - 1)]
    up_way = [(r + 1, r) for r in range(rows - 1)]
    right_way = [(c, c + 1) for c in range(cols - 1)]
    left_way = [(c + 1, c) for c in range(cols - 1)]

    own = jnp.transpose(contact_map, (1, 0, 2))
    above = lax.ppermute(own[8:], "row", down_way)
    below = lax.ppermute(own[:24], "row", up_way)
    kernel = jnp.transpose(conv_weight.reshape(3, 3, 3, 32, 64), (0, 2, 3, 1, 4)).reshape(3, 96, 192)
    gain = jnp.broadcast_to(conv_gain[:, :, None], (3, 32, 128))
    shift = jnp.broadcast_to(conv_shift[:, :, None], (3, 32, 128))
    weights = (kernel, gain, shift, out_weight)

    strip = jax.ShapeDtypeStruct((20, 64, 128), BF)
    to_left, to_right = call(
        pack_first, (strip, strip), (above, own, below), 0, [], 0, 2 << 20
    )
    from_left = lax.ppermute(to_right, "col", right_way)
    from_right = lax.ppermute(to_left, "col", left_way)

    center, messages = call(
        first_blocks,
        (jax.ShapeDtypeStruct((48, 64, 128), BF), jax.ShapeDtypeStruct((4, 768, 128), BF)),
        (dilations, place, above, own, below, from_left, from_right, *weights),
        2,
        [
            pltpu.VMEM((80, 64, 256), BF),
            pltpu.VMEM((64, 64, 256), BF),
            pltpu.VMEM((144 * 16, 128), F32),
        ],
        112 * 256 * 64 * 32 * 20,
        4 << 20,
    )
    received = []
    for t in range(4):
        pairs = []
        for a in range(rows // 4):
            for k in range(4):
                for b in range(cols):
                    pairs.append(((4 * a + k) * cols + b, (4 * b + (k + t) % 4) * cols + a))
        received.append(lax.ppermute(messages[t], BOTH, pairs))

    strip = jax.ShapeDtypeStruct((6, 64, 128), BF)
    mean, to_left, to_right = call(
        average,
        (jax.ShapeDtypeStruct((48, 64, 128), BF), strip, strip),
        (place, center, *received),
        1,
        [pltpu.VMEM((4, 768, 128), BF)],
        0,
        3 << 20,
    )
    from_left = lax.ppermute(to_right, "col", right_way)
    from_right = lax.ppermute(to_left, "col", left_way)
    out = call(
        last_block,
        jax.ShapeDtypeStruct((32, 64, 128), BF),
        (dilations, mean, from_left, from_right, *weights),
        1,
        [pltpu.VMEM((48, 64, 256), BF)],
        32 * 256 * 64 * 32 * 20,
        2 << 20,
    )
    return jnp.transpose(out, (1, 0, 2))


def solution(mesh):
    return jax.shard_map(
        on_device,
        mesh=mesh,
        in_specs=(P(None, "row", "col"), P(), P(), P(), P(), P()),
        out_specs=P(None, "row", "col"),
        check_vma=False,
    )
```

time: 149 us -> 132 us (0.89)
  the two profiles are of different devices: /device:TPU:43 before, /device:TPU:41 now
where the time goes in v2:
time: 132 us
  waiting for transfers between devices  59 us (45%)
  starting transfers between devices  56.3 us (43%)
  Pallas kernels  12.2 us (9%)
  local copies, waits for them, and re-layouts  3.79 us (3%)
    ppermute x2, starting transfers between devices, on_device(): from_left = lax.ppermute(to_right, 'col', right_way)  28.8 us
    ppermute x1, waiting for transfers between devices, on_device(): below = lax.ppermute(own[:24], 'row', up_way)  21.7 us
    ppermute x4, waiting for transfers between devices, on_device(): received.append(lax.ppermute(messages[t], BOTH, pairs))  16.9 us
    pallas_call x4, Pallas kernels, call(): pl.pallas_call(body, out_shape=outs, in_specs=[SMEM] * n_smem + [VMEM] *...  12.2 us
    ppermute x4, starting transfers between devices, on_device(): received.append(lax.ppermute(messages[t], BOTH, pairs))  11.8 us
    ppermute x1, waiting for transfers between devices, on_device(): above = lax.ppermute(own[8:], 'row', down_way)  10.5 us
    ppermute x1, starting transfers between devices, on_device(): below = lax.ppermute(own[:24], 'row', up_way)  10 us
    ppermute x2, waiting for transfers between devices, on_device(): from_right = lax.ppermute(to_left, 'col', left_way)  8.39 us
  transfers between devices with their start and end apart: 10, of which 8 were waited for; matrix products, arithmetic and copies ran while one was open for 0% of the time, Pallas kernels for 0%

profile of v2, /device:TPU:41, one launch (start us, length us, event | category | flops | bytes accessed | tf_op | source)
XLA Modules:
  0.0 131.6 jit_solution(13663510276354374537)
XLA Ops:
  0.0 1.2 copy.19
  1.4 10.0 %collective-permute-start.1 = (bf16[24,64,128]{2,1,0:T(8,128)(2,1)S(1)}, bf16[24,64,128]{2,1,0:T(8,128)(2,1)S(1)}, u32[]{:S(2)}, u32[]{:S(2)}) collective-permute-start(bf16[24,64,128]{2,1,0:T(8,128)(2,1)S(1)} %get-tuple-element.23), channel_id=1, source_target_pairs={{8,0},{16,8},{24,16},{32,24},{40,32},{48,40},{56,48},{64,56},{72,6... | collective-permute-start | bytes 1179656 | tf_op jit(solution)/shard_map/ppermute | solution.py:210
  11.4 1.9 %collective-permute-start = (bf16[24,64,128]{2,1,0:T(8,128)(2,1)S(1)}, bf16[24,64,128]{2,1,0:T(8,128)(2,1)S(1)}, u32[]{:S(2)}, u32[]{:S(2)}) collective-permute-start(bf16[24,64,128]{2,1,0:T(8,128)(2,1)S(1)} %get-tuple-element.24), channel_id=1, source_target_pairs={{0,8},{8,16},{16,24},{24,32},{32,40},{40,48},{48,56},{56,64},{64,7... | collective-permute-start | bytes 1179656 | tf_op jit(solution)/shard_map/ppermute | solution.py:209
  13.3 21.7 %collective-permute-done.1.down_ref = bf16[24,64,128]{2,1,0:T(8,128)(2,1)S(1)} collective-permute-done((bf16[24,64,128]{2,1,0:T(8,128)(2,1)S(1)}, bf16[24,64,128]{2,1,0:T(8,128)(2,1)S(1)}, u32[]{:S(2)}, u32[]{:S(2)}) %collective-permute-start.1) | collective-permute-done | bytes 393248 | tf_op jit(solution)/shard_map/ppermute | solution.py:210
  35.0 10.5 %collective-permute-done.up_ref = bf16[24,64,128]{2,1,0:T(8,128)(2,1)S(1)} collective-permute-done((bf16[24,64,128]{2,1,0:T(8,128)(2,1)S(1)}, bf16[24,64,128]{2,1,0:T(8,128)(2,1)S(1)}, u32[]{:S(2)}, u32[]{:S(2)}) %collective-permute-start) | collective-permute-done | bytes 393248 | tf_op jit(solution)/shard_map/ppermute | solution.py:209
  46.1 4.2 %collective-permute-start.2 = (bf16[20,64,128]{2,1,0:T(8,128)(2,1)S(1)}, bf16[20,64,128]{2,1,0:T(8,128)(2,1)S(1)}, u32[]{:S(2)}, u32[]{:S(2)}) collective-permute-start(bf16[20,64,128]{2,1,0:T(8,128)(2,1)S(1)} %get-tuple-element.12), channel_id=1, source_target_pairs={{0,1},{1,2},{2,3},{3,4},{4,5},{5,6},{6,7},{8,9},{9,10},{10,11},{11... | collective-permute-start | bytes 983048 | tf_op jit(solution)/shard_map/ppermute | solution.py:220
  50.3 1.9 %collective-permute-start.3 = (bf16[20,64,128]{2,1,0:T(8,128)(2,1)S(1)}, bf16[20,64,128]{2,1,0:T(8,128)(2,1)S(1)}, u32[]{:S(2)}, u32[]{:S(2)}) collective-permute-start(bf16[20,64,128]{2,1,0:T(8,128)(2,1)S(1)} %get-tuple-element.13), channel_id=1, source_target_pairs={{1,0},{2,1},{3,2},{4,3},{5,4},{6,5},{7,6},{9,8},{10,9},{11,10},{12... | collective-permute-start | bytes 983048 | tf_op jit(solution)/shard_map/ppermute | solution.py:221
  52.8 1.5 %collective-permute-done.2.from_left = bf16[20,64,128]{2,1,0:T(8,128)(2,1)S(1)} collective-permute-done((bf16[20,64,128]{2,1,0:T(8,128)(2,1)S(1)}, bf16[20,64,128]{2,1,0:T(8,128)(2,1)S(1)}, u32[]{:S(2)}, u32[]{:S(2)}) %collective-permute-start.2) | collective-permute-done | bytes 327712 | tf_op jit(solution)/shard_map/ppermute | solution.py:220
  54.3 4.4 %collective-permute-done.3.from_right = bf16[20,64,128]{2,1,0:T(8,128)(2,1)S(1)} collective-permute-done((bf16[20,64,128]{2,1,0:T(8,128)(2,1)S(1)}, bf16[20,64,128]{2,1,0:T(8,128)(2,1)S(1)}, u32[]{:S(2)}, u32[]{:S(2)}) %collective-permute-start.3) | collective-permute-done | bytes 327712 | tf_op jit(solution)/shard_map/ppermute | solution.py:221
  58.8 0.6 copy-done
  59.4 6.7 %shard_map.65 = (bf16[48,64,128]{2,1,0:T(8,128)(2,1)S(1)}, bf16[4,768,128]{2,1,0:T(8,128)(2,1)S(1)}) custom-call(s32[3]{0:T(128)S(1)} %copy-done, s32[3]{0:T(128)S(1)} %pad_add_fusion.place_ref, bf16[24,64,128]{2,1,0:T(8,128)(2,1)S(1)} %collective-permute-done.up_ref, bf16[32,64,128]{2,1,0:T(8,128)(2,1)S(1)} %bitcast.21, ...), custom_call_target="tpu_custom_call" | custom-call | flops 1174405120 | bytes 4194304 | tf_op jit(solution)/shard_map/pallas_call | solution.py:20
  66.2 4.5 %collective-permute-start.7 = (bf16[768,128]{1,0:T(8,128)(2,1)S(1)}, bf16[768,128]{1,0:T(8,128)(2,1)S(1)}, u32[]{:S(2)}, u32[]{:S(2)}) collective-permute-start(bf16[768,128]{1,0:T(8,128)(2,1)S(1)} %get-tuple-element.19), channel_id=1, source_target_pairs={{0,24},{1,56},{2,88},{3,120},{4,152},{5,184},{6,216},{7,248},{8,0}... | collective-permute-start | bytes 589832 | tf_op jit(solution)/shard_map/ppermute | solution.py:243
  70.7 0.9 collective-permute-start.6
  71.6 2.7 %collective-permute-start.5 = (bf16[768,128]{1,0:T(8,128)(2,1)S(1)}, bf16[768,128]{1,0:T(8,128)(2,1)S(1)}, u32[]{:S(2)}, u32[]{:S(2)}) collective-permute-start(bf16[768,128]{1,0:T(8,128)(2,1)S(1)} %get-tuple-element.21), channel_id=1, source_target_pairs={{0,8},{1,40},{2,72},{3,104},{4,136},{5,168},{6,200},{7,232},{8,16}... | collective-permute-start | bytes 589832 | tf_op jit(solution)/shard_map/ppermute | solution.py:243
  74.3 3.7 %collective-permute-start.4 = (bf16[768,128]{1,0:T(8,128)(2,1)S(1)}, bf16[768,128]{1,0:T(8,128)(2,1)S(1)}, u32[]{:S(2)}, u32[]{:S(2)}) collective-permute-start(bf16[768,128]{1,0:T(8,128)(2,1)S(1)} %get-tuple-element.22), channel_id=1, source_target_pairs={{0,0},{1,32},{2,64},{3,96},{4,128},{5,160},{6,192},{7,224},{8,8},{... | collective-permute-start | bytes 589832 | tf_op jit(solution)/shard_map/ppermute | solution.py:243
  78.0 2.1 %collective-permute-done.7.m3 = bf16[768,128]{1,0:T(8,128)(2,1)S(1)} collective-permute-done((bf16[768,128]{1,0:T(8,128)(2,1)S(1)}, bf16[768,128]{1,0:T(8,128)(2,1)S(1)}, u32[]{:S(2)}, u32[]{:S(2)}) %collective-permute-start.7) | collective-permute-done | bytes 196640 | tf_op jit(solution)/shard_map/ppermute | solution.py:243
  80.1 10.6 %collective-permute-done.6.m2 = bf16[768,128]{1,0:T(8,128)(2,1)S(1)} collective-permute-done((bf16[768,128]{1,0:T(8,128)(2,1)S(1)}, bf16[768,128]{1,0:T(8,128)(2,1)S(1)}, u32[]{:S(2)}, u32[]{:S(2)}) %collective-permute-start.6) | collective-permute-done | bytes 196640 | tf_op jit(solution)/shard_map/ppermute | solution.py:243
  90.7 4.2 %collective-permute-done.4.m0 = bf16[768,128]{1,0:T(8,128)(2,1)S(1)} collective-permute-done((bf16[768,128]{1,0:T(8,128)(2,1)S(1)}, bf16[768,128]{1,0:T(8,128)(2,1)S(1)}, u32[]{:S(2)}, u32[]{:S(2)}) %collective-permute-start.4) | collective-permute-done | bytes 196640 | tf_op jit(solution)/shard_map/ppermute | solution.py:243
  94.9 3.0 %shard_map.66 = (bf16[48,64,128]{2,1,0:T(8,128)(2,1)S(1)}, bf16[6,64,128]{2,1,0:T(8,128)(2,1)S(1)}, bf16[6,64,128]{2,1,0:T(8,128)(2,1)S(1)}) custom-call(s32[3]{0:T(128)S(1)} %pad_add_fusion.place_ref, bf16[48,64,128]{2,1,0:T(8,128)(2,1)S(1)} %get-tuple-element.14.center_ref, bf16[768,128]{1,0:T(8,128)(2,1)S(1)} %collective-permute-done.4.m0, ...), custom_call_target="tpu_custom_call" | custom-call | bytes 3145728 | tf_op jit(solution)/shard_map/pallas_call | solution.py:20
  97.9 24.6 %collective-permute-start.8 = (bf16[6,64,128]{2,1,0:T(8,128)(2,1)S(1)}, bf16[6,64,128]{2,1,0:T(8,128)(2,1)S(1)}, u32[]{:S(2)}, u32[]{:S(2)}) collective-permute-start(bf16[6,64,128]{2,1,0:T(8,128)(2,1)S(1)} %get-tuple-element.17), channel_id=1, source_target_pairs={{0,1},{1,2},{2,3},{3,4},{4,5},{5,6},{6,7},{8,9},{9,10},{10,11},{11... | collective-permute-start | bytes 294920 | tf_op jit(solution)/shard_map/ppermute | solution.py:255
  122.5 1.9 %collective-permute-start.9 = (bf16[6,64,128]{2,1,0:T(8,128)(2,1)S(1)}, bf16[6,64,128]{2,1,0:T(8,128)(2,1)S(1)}, u32[]{:S(2)}, u32[]{:S(2)}) collective-permute-start(bf16[6,64,128]{2,1,0:T(8,128)(2,1)S(1)} %get-tuple-element.18), channel_id=1, source_target_pairs={{1,0},{2,1},{3,2},{4,3},{5,4},{6,5},{7,6},{9,8},{10,9},{11,10},{12... | collective-permute-start | bytes 294920 | tf_op jit(solution)/shard_map/ppermute | solution.py:256
  124.5 4.0 %collective-permute-done.9.from_right = bf16[6,64,128]{2,1,0:T(8,128)(2,1)S(1)} collective-permute-done((bf16[6,64,128]{2,1,0:T(8,128)(2,1)S(1)}, bf16[6,64,128]{2,1,0:T(8,128)(2,1)S(1)}, u32[]{:S(2)}, u32[]{:S(2)}) %collective-permute-start.9) | collective-permute-done | bytes 98336 | tf_op jit(solution)/shard_map/ppermute | solution.py:256
  128.5 2.0 %shard_map.67 = bf16[32,64,128]{2,1,0:T(8,128)(2,1)S(1)} custom-call(s32[3]{0:T(128)S(1)} %copy-done, bf16[48,64,128]{2,1,0:T(8,128)(2,1)S(1)} %get-tuple-element.16.mean_ref, bf16[6,64,128]{2,1,0:T(8,128)(2,1)S(1)} %collective-permute-done.8.from_left, bf16[6,64,128]{2,1,0:T(8,128)(2,1)S(1)} %collective-permute-done.9.from_right, ...), custom_call_target="tpu_custom_call" | custom-call | flops 335544320 | bytes 2097152 | tf_op jit(solution)/shard_map/pallas_call | solution.py:20
  130.4 1.1 copy.16
  (20 shorter events, 1.5 us)
Async XLA Ops:
  1.4 33.6 %collective-permute-start.1 = (bf16[24,64,128]{2,1,0:T(8,128)(2,1)S(1)}, bf16[24,64,128]{2,1,0:T(8,128)(2,1)S(1)}, u32[]{:S(2)}, u32[]{:S(2)}) collective-permute-start(bf16[24,64,128]{2,1,0:T(8,128)(2,1)S(1)} %get-tuple-element.23), channel_id=1, source_target_pairs={{8,0},{16,8},{24,16},{32,24},{40,32},{48,40},{56,48},{64,56},{72,6... | collective-permute-start | bytes 1179656 | tf_op jit(solution)/shard_map/ppermute | solution.py:210
  11.4 34.1 %collective-permute-start = (bf16[24,64,128]{2,1,0:T(8,128)(2,1)S(1)}, bf16[24,64,128]{2,1,0:T(8,128)(2,1)S(1)}, u32[]{:S(2)}, u32[]{:S(2)}) collective-permute-start(bf16[24,64,128]{2,1,0:T(8,128)(2,1)S(1)} %get-tuple-element.24), channel_id=1, source_target_pairs={{0,8},{8,16},{16,24},{24,32},{32,40},{40,48},{48,56},{56,64},{64,7... | collective-permute-start | bytes 1179656 | tf_op jit(solution)/shard_map/ppermute | solution.py:209
  45.5 6.8 %copy-start.1 = (bf16[3,9,32,64]{3,2,1,0:T(8,128)(2,1)S(1)}, bf16[3,9,32,64]{3,2,1,0:T(8,128)(2,1)}, u32[]{:S(2)}) copy-start(bf16[3,9,32,64]{3,2,1,0:T(8,128)(2,1)} %param.8) | copy-start | bytes 331780
  46.1 6.1 %copy-start.2 = (bf16[3,64,32]{1,2,0:T(8,128)(2,1)S(1)}, bf16[3,64,32]{1,2,0:T(8,128)(2,1)}, u32[]{:S(2)}) copy-start(bf16[3,64,32]{1,2,0:T(8,128)(2,1)} %param.11) | copy-start | bytes 36868
  46.1 8.2 %collective-permute-start.2 = (bf16[20,64,128]{2,1,0:T(8,128)(2,1)S(1)}, bf16[20,64,128]{2,1,0:T(8,128)(2,1)S(1)}, u32[]{:S(2)}, u32[]{:S(2)}) collective-permute-start(bf16[20,64,128]{2,1,0:T(8,128)(2,1)S(1)} %get-tuple-element.12), channel_id=1, source_target_pairs={{0,1},{1,2},{2,3},{3,4},{4,5},{5,6},{6,7},{8,9},{9,10},{10,11},{11... | collective-permute-start | bytes 983048 | tf_op jit(solution)/shard_map/ppermute | solution.py:220
  50.3 8.4 %collective-permute-start.3 = (bf16[20,64,128]{2,1,0:T(8,128)(2,1)S(1)}, bf16[20,64,128]{2,1,0:T(8,128)(2,1)S(1)}, u32[]{:S(2)}, u32[]{:S(2)}) collective-permute-start(bf16[20,64,128]{2,1,0:T(8,128)(2,1)S(1)} %get-tuple-element.13), channel_id=1, source_target_pairs={{1,0},{2,1},{3,2},{4,3},{5,4},{6,5},{7,6},{9,8},{10,9},{11,10},{12... | collective-permute-start | bytes 983048 | tf_op jit(solution)/shard_map/ppermute | solution.py:221
  52.7 6.0 %copy-start.3 = (f32[3,32]{1,0:T(4,128)S(1)}, f32[3,32]{1,0:T(4,128)}, u32[]{:S(2)}) copy-start(f32[3,32]{1,0:T(4,128)} %param.9) | copy-start | bytes 1156
  52.8 6.0 %copy-start.4 = (f32[3,32]{1,0:T(4,128)S(1)}, f32[3,32]{1,0:T(4,128)}, u32[]{:S(2)}) copy-start(f32[3,32]{1,0:T(4,128)} %param.10) | copy-start | bytes 1156
  58.8 0.7 copy-start
  66.2 13.9 %collective-permute-start.7 = (bf16[768,128]{1,0:T(8,128)(2,1)S(1)}, bf16[768,128]{1,0:T(8,128)(2,1)S(1)}, u32[]{:S(2)}, u32[]{:S(2)}) collective-permute-start(bf16[768,128]{1,0:T(8,128)(2,1)S(1)} %get-tuple-element.19), channel_id=1, source_target_pairs={{0,24},{1,56},{2,88},{3,120},{4,152},{5,184},{6,216},{7,248},{8,0}... | collective-permute-start | bytes 589832 | tf_op jit(solution)/shard_map/ppermute | solution.py:243
  70.7 20.0 %collective-permute-start.6 = (bf16[768,128]{1,0:T(8,128)(2,1)S(1)}, bf16[768,128]{1,0:T(8,128)(2,1)S(1)}, u32[]{:S(2)}, u32[]{:S(2)}) collective-permute-start(bf16[768,128]{1,0:T(8,128)(2,1)S(1)} %get-tuple-element.20), channel_id=1, source_target_pairs={{0,16},{1,48},{2,80},{3,112},{4,144},{5,176},{6,208},{7,240},{8,24... | collective-permute-start | bytes 589832 | tf_op jit(solution)/shard_map/ppermute | solution.py:243
  71.6 19.1 %collective-permute-start.5 = (bf16[768,128]{1,0:T(8,128)(2,1)S(1)}, bf16[768,128]{1,0:T(8,128)(2,1)S(1)}, u32[]{:S(2)}, u32[]{:S(2)}) collective-permute-start(bf16[768,128]{1,0:T(8,128)(2,1)S(1)} %get-tuple-element.21), channel_id=1, source_target_pairs={{0,8},{1,40},{2,72},{3,104},{4,136},{5,168},{6,200},{7,232},{8,16}... | collective-permute-start | bytes 589832 | tf_op jit(solution)/shard_map/ppermute | solution.py:243
  74.3 20.6 %collective-permute-start.4 = (bf16[768,128]{1,0:T(8,128)(2,1)S(1)}, bf16[768,128]{1,0:T(8,128)(2,1)S(1)}, u32[]{:S(2)}, u32[]{:S(2)}) collective-permute-start(bf16[768,128]{1,0:T(8,128)(2,1)S(1)} %get-tuple-element.22), channel_id=1, source_target_pairs={{0,0},{1,32},{2,64},{3,96},{4,128},{5,160},{6,192},{7,224},{8,8},{... | collective-permute-start | bytes 589832 | tf_op jit(solution)/shard_map/ppermute | solution.py:243
  97.9 26.5 %collective-permute-start.8 = (bf16[6,64,128]{2,1,0:T(8,128)(2,1)S(1)}, bf16[6,64,128]{2,1,0:T(8,128)(2,1)S(1)}, u32[]{:S(2)}, u32[]{:S(2)}) collective-permute-start(bf16[6,64,128]{2,1,0:T(8,128)(2,1)S(1)} %get-tuple-element.17), channel_id=1, source_target_pairs={{0,1},{1,2},{2,3},{3,4},{4,5},{5,6},{6,7},{8,9},{9,10},{10,11},{11... | collective-permute-start | bytes 294920 | tf_op jit(solution)/shard_map/ppermute | solution.py:255
  122.5 5.9 %collective-permute-start.9 = (bf16[6,64,128]{2,1,0:T(8,128)(2,1)S(1)}, bf16[6,64,128]{2,1,0:T(8,128)(2,1)S(1)}, u32[]{:S(2)}, u32[]{:S(2)}) collective-permute-start(bf16[6,64,128]{2,1,0:T(8,128)(2,1)S(1)} %get-tuple-element.18), channel_id=1, source_target_pairs={{1,0},{2,1},{3,2},{4,3},{5,4},{6,5},{7,6},{9,8},{10,9},{11,10},{12... | collective-permute-start | bytes 294920 | tf_op jit(solution)/shard_map/ppermute | solution.py:256

commit v3 on v2

v3 whole, which is shorter than its diff:
```python
import functools

import jax
import jax.numpy as jnp
from jax import lax
from jax.experimental import pallas as pl
from jax.experimental.pallas import tpu as pltpu
from jax.sharding import PartitionSpec as P

D = 8
BOTH = ("row", "col")
BF = jnp.bfloat16
F32 = jnp.float32
VMEM = pl.BlockSpec(memory_space=pltpu.VMEM)
SMEM = pl.BlockSpec(memory_space=pltpu.SMEM)
LIMIT = 40 * 1024 * 1024


def call(body, outs, args, n_smem, scratch, flops, moved):
    return pl.pallas_call(
        body,
        out_shape=outs,
        in_specs=[SMEM] * n_smem + [VMEM] * (len(args) - n_smem),
        out_specs=jax.tree.map(lambda _: VMEM, outs),
        scratch_shapes=scratch,
        compiler_params=pltpu.CompilerParams(vmem_limit_bytes=LIMIT),
        cost_estimate=pl.CostEstimate(flops=flops, bytes_accessed=moved, transcendentals=0),
    )(*args)


def lanes(rows):
    return lax.broadcasted_iota(jnp.int32, (rows, 128), 1)


def pack_strips(pieces, start, width):
    lane = lanes(64)
    total = None
    for place, piece in enumerate(pieces):
        moved = pltpu.roll(piece.astype(F32), (place * width - start) % 128, 1)
        total = moved if total is None else jnp.where(lane >= place * width, moved, total)
    return total.astype(BF)


def side_lanes(from_right, from_left, place, width):
    lane = lanes(64)
    right = pltpu.roll(from_right.astype(F32), (-place * width) % 128, 1)
    left = pltpu.roll(from_left.astype(F32), (128 - width - place * width) % 128, 1)
    side = jnp.where(lane < width, right, jnp.where(lane >= 128 - width, left, 0.0))
    return side.astype(BF)


def block_rows(source, rows, spacing, kernel, gain, shift, expand, narrow=False):
    taps = []
    for at in rows:
        stacked = jnp.concatenate(
            [source[at - spacing], source[at], source[at + spacing]], axis=0
        )
        taps.append(jnp.dot(kernel, jnp.maximum(stacked, 0), preferred_element_type=F32))
    lane = lanes(32)
    before, after = lane >= spacing, lane < 128 - spacing
    hidden = []
    for tap in taps:
        left = [pltpu.roll(tap[:32, h : h + 128], spacing, 1) for h in (0, 128)]
        right = [pltpu.roll(tap[64:, h : h + 128], 128 - spacing, 1) for h in (0, 128)]
        convs = []
        for h in range(1 if narrow else 2):
            convs.append(
                tap[32:64, 128 * h : 128 * h + 128]
                + jnp.where(before, left[h], left[1 - h])
                + jnp.where(after, right[h], right[1 - h])
            )
        hidden.append(
            [jnp.maximum(gain * conv + shift, 0.0).astype(BF) for conv in convs]
        )
    if narrow:
        hidden = [[h[0] for h in hidden[i : i + 2]] for i in range(0, len(rows), 2)]
    grown = [
        jnp.dot(expand, jnp.concatenate(h, axis=1), preferred_element_type=F32) for h in hidden
    ]
    if narrow:
        halves = [g[:, h : h + 128] for g in grown for h in (0, 128)]
        return [source[at, :, :128].astype(F32) + half for at, half in zip(rows, halves)]
    return [source[at].astype(F32) + g for at, g in zip(rows, grown)]


def block_of(layer, spacing_ref, kernel_ref, gain_ref, shift_ref, expand_ref):
    return (
        spacing_ref[layer], kernel_ref[layer], gain_ref[layer], shift_ref[layer], expand_ref[layer]
    )


def pack_sides(up_ref, own_ref, down_ref, left_ref, right_ref):
    first = 0
    for ref in (up_ref, own_ref, down_ref):
        for g in range(ref.shape[0] // 8):
            pieces = [ref[8 * g + q] for q in range(8)]
            left_ref[first + g] = pack_strips(pieces, 0, 16)
            right_ref[first + g] = pack_strips(pieces, 112, 16)
        first += ref.shape[0] // 8


def fill_wide(wide, up_ref, own_ref, down_ref, from_left, from_right):
    first = 0
    for ref in (up_ref, own_ref, down_ref):
        for r in range(ref.shape[0]):
            at = first + r
            wide[at, :, :128] = ref[r]
            wide[at, :, 128:] = side_lanes(from_right[at // 8], from_left[at // 8], at % 8, 16)
        first += ref.shape[0]


def first_blocks(
    spacing_ref, place_ref, up_ref, own_ref, down_ref, from_left, from_right,
    kernel_ref, gain_ref, shift_ref, expand_ref,
    second_ref, message_ref, wide, middle, turned,
):
    row, col = place_ref[0], place_ref[1]
    members = place_ref[2]
    weights = (spacing_ref, kernel_ref, gain_ref, shift_ref, expand_ref)
    fill_wide(wide, up_ref, own_ref, down_ref, from_left, from_right)
    lane = lax.broadcasted_iota(jnp.int32, (64, 256), 1)
    inside = (lane < 128) | ((lane < 192) & (col < 7)) | ((lane >= 192) & (col > 0))

    def one(i, _):
        start = i * 24
        outs = block_rows(wide, [start + b + 8 for b in range(24)], *block_of(0, *weights))
        for b, out in enumerate(outs):
            number = 32 * row - 8 + start + b
            alive = inside & (number >= 0) & (number < 1024)
            middle[start + b] = jnp.where(alive, out, 0.0).astype(BF)
        return _

    lax.fori_loop(0, 2, one, 0)
    rows = [r for b in range(16) for r in (b, b + 16)]
    outs = block_rows(middle, [r + 8 for r in rows], *block_of(1, *weights), narrow=True)
    for r, out in zip(rows, outs):
        second_ref[r] = out.astype(BF)
    for b in range(16):
        pair = jnp.concatenate(outs[2 * b : 2 * b + 2], axis=0).astype(BF)
        turned[pl.ds(b, 128, stride=16), :] = jnp.transpose(pair.astype(F32))
    for m in range(4):
        message_ref[lax.rem(m - members + 4, 4)] = turned[512 * m : 512 * m + 512].astype(BF)


def average(place_ref, second_ref, m0, m1, m2, m3, mean_ref, gathered):
    members = place_ref[2]
    for t, ref in enumerate((m0, m1, m2, m3)):
        gathered[lax.rem(members - t + 4, 4)] = ref[...]
    for j in range(32):
        blocks = []
        for k in range(4):
            part = gathered[k, 16 * j : 16 * j + 16, :].astype(F32)
            blocks += [part, pltpu.roll(part, 64, 1)]
        mirrored = jnp.transpose(jnp.concatenate(blocks, axis=0))[:64]
        mean_ref[j] = (0.5 * (second_ref[j].astype(F32) + mirrored)).astype(BF)


def last_block(
    spacing_ref, up_ref, own_ref, down_ref, from_left, from_right,
    kernel_ref, gain_ref, shift_ref, expand_ref, out_ref, wide,
):
    weights = (spacing_ref, kernel_ref, gain_ref, shift_ref, expand_ref)
    fill_wide(wide, up_ref, own_ref, down_ref, from_left, from_right)
    outs = block_rows(wide, [r + 8 for r in range(32)], *block_of(2, *weights), narrow=True)
    for r, out in enumerate(outs):
        out_ref[r] = out.astype(BF)


def on_device(contact_map, dilations, conv_weight, conv_gain, conv_shift, out_weight):
    rows, cols = lax.axis_size("row"), lax.axis_size("col")
    row, col = lax.axis_index("row"), lax.axis_index("col")
    place = jnp.stack([row, col, lax.rem(row, 4)]).astype(jnp.int32)
    down_way = [(r, r + 1) for r in range(rows - 1)]
    up_way = [(r + 1, r) for r in range(rows - 1)]
    right_way = [(c, c + 1) for c in range(cols - 1)]
    left_way = [(c + 1, c) for c in range(cols - 1)]

    def rims(own, depth):
        above = lax.ppermute(own[32 - depth :], "row", down_way)
        below = lax.ppermute(own[:depth], "row", up_way)
        strip = jax.ShapeDtypeStruct(((32 + 2 * depth) // 8, 64, 128), BF)
        to_left, to_right = call(
            pack_sides, (strip, strip), (above, own, below), 0, [], 0, 1 << 20
        )
        from_left = lax.ppermute(to_right, "col", right_way)
        from_right = lax.ppermute(to_left, "col", left_way)
        return above, own, below, from_left, from_right

    own = jnp.transpose(contact_map, (1, 0, 2))
    kernel = jnp.transpose(conv_weight.reshape(3, 3, 3, 32, 64), (0, 2, 3, 1, 4)).reshape(3, 96, 192)
    gain = jnp.broadcast_to(conv_gain[:, :, None], (3, 32, 128))
    shift = jnp.broadcast_to(conv_shift[:, :, None], (3, 32, 128))
    weights = (kernel, gain, shift, out_weight)

    tile = jax.ShapeDtypeStruct((32, 64, 128), BF)
    second, messages = call(
        first_blocks,
        (tile, jax.ShapeDtypeStruct((4, 512, 128), BF)),
        (dilations, place, *rims(own, 16), *weights),
        2,
        [
            pltpu.VMEM((64, 64, 256), BF),
            pltpu.VMEM((48, 64, 256), BF),
            pltpu.VMEM((128 * 16, 128), F32),
        ],
        80 * 256 * 64 * 32 * 20,
        4 << 20,
    )
    received = []
    for t in range(4):
        pairs = []
        for a in range(rows // 4):
            for k in range(4):
                for b in range(cols):
                    pairs.append(((4 * a + k) * cols + b, (4 * b + (k + t) % 4) * cols + a))
        received.append(lax.ppermute(messages[t], BOTH, pairs))
    mean = call(
        average,
        tile,
        (place, second, *received),
        1,
        [pltpu.VMEM((4, 512, 128), BF)],
        0,
        2 << 20,
    )
    out = call(
        last_block,
        tile,
        (dilations, *rims(mean, 8), *weights),
        1,
        [pltpu.VMEM((48, 64, 256), BF)],
        32 * 256 * 64 * 32 * 20,
        2 << 20,
    )
    return jnp.transpose(out, (1, 0, 2))


def solution(mesh):
    return jax.shard_map(
        on_device,
        mesh=mesh,
        in_specs=(P(None, "row", "col"), P(), P(), P(), P(), P()),
        out_specs=P(None, "row", "col"),
        check_vma=False,
    )
```

time: 132 us -> 121 us (0.917)
  the two profiles are of different devices: /device:TPU:41 before, /device:TPU:25 now
where the time goes in v3:
time: 121 us
  waiting for transfers between devices  54.2 us (45%)
  starting transfers between devices  54.1 us (45%)
  Pallas kernels  8.5 us (7%)
  local copies, waits for them, and re-layouts  3.68 us (3%)
    ppermute x2, waiting for transfers between devices, rims(): above = lax.ppermute(own[32 - depth:], 'row', down_way)  26.6 us
    ppermute x2, starting transfers between devices, rims(): below = lax.ppermute(own[:depth], 'row', up_way)  16.5 us
    ppermute x4, starting transfers between devices, on_device(): received.append(lax.ppermute(messages[t], BOTH, pairs))  14.8 us
    ppermute x4, waiting for transfers between devices, on_device(): received.append(lax.ppermute(messages[t], BOTH, pairs))  14.7 us
    ppermute x2, starting transfers between devices, rims(): from_left = lax.ppermute(to_right, 'col', right_way)  12 us
    pallas_call x5, Pallas kernels, call(): pl.pallas_call(body, out_shape=outs, in_specs=[SMEM] * n_smem + [VMEM] *...  8.5 us
    ppermute x2, waiting for transfers between devices, rims(): from_right = lax.ppermute(to_left, 'col', left_way)  6.93 us
    ppermute x2, starting transfers between devices, rims(): above = lax.ppermute(own[32 - depth:], 'row', down_way)  6.18 us
  transfers between devices with their start and end apart: 12, of which 8 were waited for; matrix products, arithmetic and copies ran while one was open for 0% of the time, Pallas kernels for 0%

profile of v3, /device:TPU:25, one launch (start us, length us, event | category | flops | bytes accessed | tf_op | source)
XLA Modules:
  0.0 120.8 jit_solution(9781330785101177643)
XLA Ops:
  0.0 1.2 %copy.19 = bf16[64,32,128]{2,0,1:T(8,128)(2,1)S(1)} copy(bf16[64,32,128]{2,1,0:T(8,128)(2,1)} %param.6) | data formatting | bytes 1048576 | tf_op args[0]
  1.3 11.2 %collective-permute-start.1 = (bf16[16,64,128]{2,1,0:T(8,128)(2,1)S(1)}, bf16[16,64,128]{2,1,0:T(8,128)(2,1)S(1)}, u32[]{:S(2)}, u32[]{:S(2)}) collective-permute-start(bf16[16,64,128]{2,1,0:T(8,128)(2,1)S(1)} %get-tuple-element.23), channel_id=1, source_target_pairs={{8,0},{16,8},{24,16},{32,24},{40,32},{48,40},{56,48},{64,56},{72,6... | collective-permute-start | bytes 786440 | tf_op jit(solution)/shard_map/ppermute | solution.py:180
  12.5 1.9 %collective-permute-start = (bf16[16,64,128]{2,1,0:T(8,128)(2,1)S(1)}, bf16[16,64,128]{2,1,0:T(8,128)(2,1)S(1)}, u32[]{:S(2)}, u32[]{:S(2)}) collective-permute-start(bf16[16,64,128]{2,1,0:T(8,128)(2,1)S(1)} %get-tuple-element.24), channel_id=1, source_target_pairs={{0,8},{8,16},{16,24},{24,32},{32,40},{40,48},{48,56},{56,64},{64,7... | collective-permute-start | bytes 786440 | tf_op jit(solution)/shard_map/ppermute | solution.py:179
  14.4 5.6 %collective-permute-done.1.down_ref = bf16[16,64,128]{2,1,0:T(8,128)(2,1)S(1)} collective-permute-done((bf16[16,64,128]{2,1,0:T(8,128)(2,1)S(1)}, bf16[16,64,128]{2,1,0:T(8,128)(2,1)S(1)}, u32[]{:S(2)}, u32[]{:S(2)}) %collective-permute-start.1) | collective-permute-done | bytes 262176 | tf_op jit(solution)/shard_map/ppermute | solution.py:180
  20.0 18.3 %collective-permute-done.up_ref = bf16[16,64,128]{2,1,0:T(8,128)(2,1)S(1)} collective-permute-done((bf16[16,64,128]{2,1,0:T(8,128)(2,1)S(1)}, bf16[16,64,128]{2,1,0:T(8,128)(2,1)S(1)}, u32[]{:S(2)}, u32[]{:S(2)}) %collective-permute-start) | collective-permute-done | bytes 262176 | tf_op jit(solution)/shard_map/ppermute | solution.py:179
  38.8 1.9 %collective-permute-start.2 = (bf16[8,64,128]{2,1,0:T(8,128)(2,1)S(1)}, bf16[8,64,128]{2,1,0:T(8,128)(2,1)S(1)}, u32[]{:S(2)}, u32[]{:S(2)}) collective-permute-start(bf16[8,64,128]{2,1,0:T(8,128)(2,1)S(1)} %get-tuple-element.11), channel_id=1, source_target_pairs={{0,1},{1,2},{2,3},{3,4},{4,5},{5,6},{6,7},{8,9},{9,10},{10,11},{11... | collective-permute-start | bytes 393224 | tf_op jit(solution)/shard_map/ppermute | solution.py:185
  40.8 2.8 %collective-permute-start.3 = (bf16[8,64,128]{2,1,0:T(8,128)(2,1)S(1)}, bf16[8,64,128]{2,1,0:T(8,128)(2,1)S(1)}, u32[]{:S(2)}, u32[]{:S(2)}) collective-permute-start(bf16[8,64,128]{2,1,0:T(8,128)(2,1)S(1)} %get-tuple-element.12), channel_id=1, source_target_pairs={{1,0},{2,1},{3,2},{4,3},{5,4},{6,5},{7,6},{9,8},{10,9},{11,10},{12... | collective-permute-start | bytes 393224 | tf_op jit(solution)/shard_map/ppermute | solution.py:186
  44.1 2.9 %collective-permute-done.3.from_right = bf16[8,64,128]{2,1,0:T(8,128)(2,1)S(1)} collective-permute-done((bf16[8,64,128]{2,1,0:T(8,128)(2,1)S(1)}, bf16[8,64,128]{2,1,0:T(8,128)(2,1)S(1)}, u32[]{:S(2)}, u32[]{:S(2)}) %collective-permute-start.3) | collective-permute-done | bytes 131104 | tf_op jit(solution)/shard_map/ppermute | solution.py:186
  47.2 0.6 copy-done
  47.8 4.1 %shard_map.65 = (bf16[32,64,128]{2,1,0:T(8,128)(2,1)S(1)}, bf16[4,512,128]{2,1,0:T(8,128)(2,1)S(1)}) custom-call(s32[3]{0:T(128)S(1)} %copy-done, s32[3]{0:T(128)S(1)} %pad_add_fusion.place_ref, bf16[16,64,128]{2,1,0:T(8,128)(2,1)S(1)} %collective-permute-done.up_ref, bf16[32,64,128]{2,1,0:T(8,128)(2,1)S(1)} %bitcast.21, ...), custom_call_target="tpu_custom_call" | custom-call | flops 838860800 | bytes 4194304 | tf_op jit(solution)/shard_map/pallas_call | solution.py:20
  52.0 0.7 collective-permute-start.7
  52.7 8.4 %collective-permute-start.6 = (bf16[512,128]{1,0:T(8,128)(2,1)S(1)}, bf16[512,128]{1,0:T(8,128)(2,1)S(1)}, u32[]{:S(2)}, u32[]{:S(2)}) collective-permute-start(bf16[512,128]{1,0:T(8,128)(2,1)S(1)} %get-tuple-element.20), channel_id=1, source_target_pairs={{0,16},{1,48},{2,80},{3,112},{4,144},{5,176},{6,208},{7,240},{8,24... | collective-permute-start | bytes 393224 | tf_op jit(solution)/shard_map/ppermute | solution.py:216
  61.2 5.6 %collective-permute-start.4 = (bf16[512,128]{1,0:T(8,128)(2,1)S(1)}, bf16[512,128]{1,0:T(8,128)(2,1)S(1)}, u32[]{:S(2)}, u32[]{:S(2)}) collective-permute-start(bf16[512,128]{1,0:T(8,128)(2,1)S(1)} %get-tuple-element.22), channel_id=1, source_target_pairs={{0,0},{1,32},{2,64},{3,96},{4,128},{5,160},{6,192},{7,224},{8,8},{... | collective-permute-start | bytes 393224 | tf_op jit(solution)/shard_map/ppermute | solution.py:216
  66.8 13.3 %collective-permute-done.7.m3 = bf16[512,128]{1,0:T(8,128)(2,1)S(1)} collective-permute-done((bf16[512,128]{1,0:T(8,128)(2,1)S(1)}, bf16[512,128]{1,0:T(8,128)(2,1)S(1)}, u32[]{:S(2)}, u32[]{:S(2)}) %collective-permute-start.7) | collective-permute-done | bytes 131104 | tf_op jit(solution)/shard_map/ppermute | solution.py:216
  80.1 1.4 %collective-permute-done.5.m1 = bf16[512,128]{1,0:T(8,128)(2,1)S(1)} collective-permute-done((bf16[512,128]{1,0:T(8,128)(2,1)S(1)}, bf16[512,128]{1,0:T(8,128)(2,1)S(1)}, u32[]{:S(2)}, u32[]{:S(2)}) %collective-permute-start.5) | collective-permute-done | bytes 131104 | tf_op jit(solution)/shard_map/ppermute | solution.py:216
  81.5 1.4 %shard_map.66.own_ref = bf16[32,64,128]{2,1,0:T(8,128)(2,1)S(1)} custom-call(s32[3]{0:T(128)S(1)} %pad_add_fusion.place_ref, bf16[32,64,128]{2,1,0:T(8,128)(2,1)S(1)} %get-tuple-element.13.second_ref, bf16[512,128]{1,0:T(8,128)(2,1)S(1)} %collective-permute-done.4.m0, bf16[512,128]{1,0:T(8,128)(2,1)S(1)} %collective-permute-done.5.m1, ...), custom_call_target="tpu_custom_call" | custom-call | bytes 2097152 | tf_op jit(solution)/shard_map/pallas_call | solution.py:20
  82.9 5.3 %collective-permute-start.9 = (bf16[8,64,128]{2,1,0:T(8,128)(2,1)S(1)}, bf16[8,64,128]{2,1,0:T(8,128)(2,1)S(1)}, u32[]{:S(2)}, u32[]{:S(2)}) collective-permute-start(bf16[8,64,128]{2,1,0:T(8,128)(2,1)S(1)} %get-tuple-element.17), channel_id=1, source_target_pairs={{8,0},{16,8},{24,16},{32,24},{40,32},{48,40},{56,48},{64,56},{72,6... | collective-permute-start | bytes 393224 | tf_op jit(solution)/shard_map/ppermute | solution.py:180
  88.2 4.3 %collective-permute-start.8 = (bf16[8,64,128]{2,1,0:T(8,128)(2,1)S(1)}, bf16[8,64,128]{2,1,0:T(8,128)(2,1)S(1)}, u32[]{:S(2)}, u32[]{:S(2)}) collective-permute-start(bf16[8,64,128]{2,1,0:T(8,128)(2,1)S(1)} %get-tuple-element.18), channel_id=1, source_target_pairs={{0,8},{8,16},{16,24},{24,32},{32,40},{40,48},{48,56},{56,64},{64,7... | collective-permute-start | bytes 393224 | tf_op jit(solution)/shard_map/ppermute | solution.py:179
  92.9 8.3 %collective-permute-done.8.up_ref = bf16[8,64,128]{2,1,0:T(8,128)(2,1)S(1)} collective-permute-done((bf16[8,64,128]{2,1,0:T(8,128)(2,1)S(1)}, bf16[8,64,128]{2,1,0:T(8,128)(2,1)S(1)}, u32[]{:S(2)}, u32[]{:S(2)}) %collective-permute-start.8) | collective-permute-done | bytes 131104 | tf_op jit(solution)/shard_map/ppermute | solution.py:179
  101.6 10.1 %collective-permute-start.10 = (bf16[6,64,128]{2,1,0:T(8,128)(2,1)S(1)}, bf16[6,64,128]{2,1,0:T(8,128)(2,1)S(1)}, u32[]{:S(2)}, u32[]{:S(2)}) collective-permute-start(bf16[6,64,128]{2,1,0:T(8,128)(2,1)S(1)} %get-tuple-element.15), channel_id=1, source_target_pairs={{0,1},{1,2},{2,3},{3,4},{4,5},{5,6},{6,7},{8,9},{9,10},{10,11},{11... | collective-permute-start | bytes 294920 | tf_op jit(solution)/shard_map/ppermute | solution.py:185
  111.7 1.9 %collective-permute-start.11 = (bf16[6,64,128]{2,1,0:T(8,128)(2,1)S(1)}, bf16[6,64,128]{2,1,0:T(8,128)(2,1)S(1)}, u32[]{:S(2)}, u32[]{:S(2)}) collective-permute-start(bf16[6,64,128]{2,1,0:T(8,128)(2,1)S(1)} %get-tuple-element.16), channel_id=1, source_target_pairs={{1,0},{2,1},{3,2},{4,3},{5,4},{6,5},{7,6},{9,8},{10,9},{11,10},{12... | collective-permute-start | bytes 294920 | tf_op jit(solution)/shard_map/ppermute | solution.py:186
  113.7 4.0 %collective-permute-done.11.from_right = bf16[6,64,128]{2,1,0:T(8,128)(2,1)S(1)} collective-permute-done((bf16[6,64,128]{2,1,0:T(8,128)(2,1)S(1)}, bf16[6,64,128]{2,1,0:T(8,128)(2,1)S(1)}, u32[]{:S(2)}, u32[]{:S(2)}) %collective-permute-start.11) | collective-permute-done | bytes 98336 | tf_op jit(solution)/shard_map/ppermute | solution.py:186
  117.7 2.0 %shard_map.68 = bf16[32,64,128]{2,1,0:T(8,128)(2,1)S(1)} custom-call(s32[3]{0:T(128)S(1)} %copy-done, bf16[8,64,128]{2,1,0:T(8,128)(2,1)S(1)} %collective-permute-done.8.up_ref, bf16[32,64,128]{2,1,0:T(8,128)(2,1)S(1)} %shard_map.66.own_ref, bf16[8,64,128]{2,1,0:T(8,128)(2,1)S(1)} %collective-permute-done.9.down_ref, ...), custom_call_target="tpu_custom_call" | custom-call | flops 335544320 | bytes 2097152 | tf_op jit(solution)/shard_map/pallas_call | solution.py:20
  119.7 1.1 copy.16
  (26 shorter events, 2.2 us)
Async XLA Ops:
  1.3 18.7 %collective-permute-start.1 = (bf16[16,64,128]{2,1,0:T(8,128)(2,1)S(1)}, bf16[16,64,128]{2,1,0:T(8,128)(2,1)S(1)}, u32[]{:S(2)}, u32[]{:S(2)}) collective-permute-start(bf16[16,64,128]{2,1,0:T(8,128)(2,1)S(1)} %get-tuple-element.23), channel_id=1, source_target_pairs={{8,0},{16,8},{24,16},{32,24},{40,32},{48,40},{56,48},{64,56},{72,6... | collective-permute-start | bytes 786440 | tf_op jit(solution)/shard_map/ppermute | solution.py:180
  12.5 25.8 %collective-permute-start = (bf16[16,64,128]{2,1,0:T(8,128)(2,1)S(1)}, bf16[16,64,128]{2,1,0:T(8,128)(2,1)S(1)}, u32[]{:S(2)}, u32[]{:S(2)}) collective-permute-start(bf16[16,64,128]{2,1,0:T(8,128)(2,1)S(1)} %get-tuple-element.24), channel_id=1, source_target_pairs={{0,8},{8,16},{16,24},{24,32},{32,40},{40,48},{48,56},{56,64},{64,7... | collective-permute-start | bytes 786440 | tf_op jit(solution)/shard_map/ppermute | solution.py:179
  38.3 5.4 %copy-start.1 = (bf16[3,9,32,64]{3,2,1,0:T(8,128)(2,1)S(1)}, bf16[3,9,32,64]{3,2,1,0:T(8,128)(2,1)}, u32[]{:S(2)}) copy-start(bf16[3,9,32,64]{3,2,1,0:T(8,128)(2,1)} %param.8) | copy-start | bytes 331780
  38.8 4.7 %copy-start.2 = (bf16[3,64,32]{1,2,0:T(8,128)(2,1)S(1)}, bf16[3,64,32]{1,2,0:T(8,128)(2,1)}, u32[]{:S(2)}) copy-start(bf16[3,64,32]{1,2,0:T(8,128)(2,1)} %param.11) | copy-start | bytes 36868
  38.8 5.3 %collective-permute-start.2 = (bf16[8,64,128]{2,1,0:T(8,128)(2,1)S(1)}, bf16[8,64,128]{2,1,0:T(8,128)(2,1)S(1)}, u32[]{:S(2)}, u32[]{:S(2)}) collective-permute-start(bf16[8,64,128]{2,1,0:T(8,128)(2,1)S(1)} %get-tuple-element.11), channel_id=1, source_target_pairs={{0,1},{1,2},{2,3},{3,4},{4,5},{5,6},{6,7},{8,9},{9,10},{10,11},{11... | collective-permute-start | bytes 393224 | tf_op jit(solution)/shard_map/ppermute | solution.py:185
  40.8 6.3 %collective-permute-start.3 = (bf16[8,64,128]{2,1,0:T(8,128)(2,1)S(1)}, bf16[8,64,128]{2,1,0:T(8,128)(2,1)S(1)}, u32[]{:S(2)}, u32[]{:S(2)}) collective-permute-start(bf16[8,64,128]{2,1,0:T(8,128)(2,1)S(1)} %get-tuple-element.12), channel_id=1, source_target_pairs={{1,0},{2,1},{3,2},{4,3},{5,4},{6,5},{7,6},{9,8},{10,9},{11,10},{12... | collective-permute-start | bytes 393224 | tf_op jit(solution)/shard_map/ppermute | solution.py:186
  44.0 3.0 %copy-start.3 = (f32[3,32]{1,0:T(4,128)S(1)}, f32[3,32]{1,0:T(4,128)}, u32[]{:S(2)}) copy-start(f32[3,32]{1,0:T(4,128)} %param.9) | copy-start | bytes 1156
  44.1 3.0 %copy-start.4 = (f32[3,32]{1,0:T(4,128)S(1)}, f32[3,32]{1,0:T(4,128)}, u32[]{:S(2)}) copy-start(f32[3,32]{1,0:T(4,128)} %param.10) | copy-start | bytes 1156
  47.1 0.7 copy-start
  52.0 28.1 %collective-permute-start.7 = (bf16[512,128]{1,0:T(8,128)(2,1)S(1)}, bf16[512,128]{1,0:T(8,128)(2,1)S(1)}, u32[]{:S(2)}, u32[]{:S(2)}) collective-permute-start(bf16[512,128]{1,0:T(8,128)(2,1)S(1)} %get-tuple-element.19), channel_id=1, source_target_pairs={{0,24},{1,56},{2,88},{3,120},{4,152},{5,184},{6,216},{7,248},{8,0}... | collective-permute-start | bytes 393224 | tf_op jit(solution)/shard_map/ppermute | solution.py:216
  52.7 27.4 %collective-permute-start.6 = (bf16[512,128]{1,0:T(8,128)(2,1)S(1)}, bf16[512,128]{1,0:T(8,128)(2,1)S(1)}, u32[]{:S(2)}, u32[]{:S(2)}) collective-permute-start(bf16[512,128]{1,0:T(8,128)(2,1)S(1)} %get-tuple-element.20), channel_id=1, source_target_pairs={{0,16},{1,48},{2,80},{3,112},{4,144},{5,176},{6,208},{7,240},{8,24... | collective-permute-start | bytes 393224 | tf_op jit(solution)/shard_map/ppermute | solution.py:216
  61.2 20.3 %collective-permute-start.5 = (bf16[512,128]{1,0:T(8,128)(2,1)S(1)}, bf16[512,128]{1,0:T(8,128)(2,1)S(1)}, u32[]{:S(2)}, u32[]{:S(2)}) collective-permute-start(bf16[512,128]{1,0:T(8,128)(2,1)S(1)} %get-tuple-element.21), channel_id=1, source_target_pairs={{0,8},{1,40},{2,72},{3,104},{4,136},{5,168},{6,200},{7,232},{8,16}... | collective-permute-start | bytes 393224 | tf_op jit(solution)/shard_map/ppermute | solution.py:216
  61.2 20.3 %collective-permute-start.4 = (bf16[512,128]{1,0:T(8,128)(2,1)S(1)}, bf16[512,128]{1,0:T(8,128)(2,1)S(1)}, u32[]{:S(2)}, u32[]{:S(2)}) collective-permute-start(bf16[512,128]{1,0:T(8,128)(2,1)S(1)} %get-tuple-element.22), channel_id=1, source_target_pairs={{0,0},{1,32},{2,64},{3,96},{4,128},{5,160},{6,192},{7,224},{8,8},{... | collective-permute-start | bytes 393224 | tf_op jit(solution)/shard_map/ppermute | solution.py:216
  82.9 10.0 %collective-permute-start.9 = (bf16[8,64,128]{2,1,0:T(8,128)(2,1)S(1)}, bf16[8,64,128]{2,1,0:T(8,128)(2,1)S(1)}, u32[]{:S(2)}, u32[]{:S(2)}) collective-permute-start(bf16[8,64,128]{2,1,0:T(8,128)(2,1)S(1)} %get-tuple-element.17), channel_id=1, source_target_pairs={{8,0},{16,8},{24,16},{32,24},{40,32},{48,40},{56,48},{64,56},{72,6... | collective-permute-start | bytes 393224 | tf_op jit(solution)/shard_map/ppermute | solution.py:180
  88.2 13.0 %collective-permute-start.8 = (bf16[8,64,128]{2,1,0:T(8,128)(2,1)S(1)}, bf16[8,64,128]{2,1,0:T(8,128)(2,1)S(1)}, u32[]{:S(2)}, u32[]{:S(2)}) collective-permute-start(bf16[8,64,128]{2,1,0:T(8,128)(2,1)S(1)} %get-tuple-element.18), channel_id=1, source_target_pairs={{0,8},{8,16},{16,24},{24,32},{32,40},{40,48},{48,56},{56,64},{64,7... | collective-permute-start | bytes 393224 | tf_op jit(solution)/shard_map/ppermute | solution.py:179
  101.6 12.0 %collective-permute-start.10 = (bf16[6,64,128]{2,1,0:T(8,128)(2,1)S(1)}, bf16[6,64,128]{2,1,0:T(8,128)(2,1)S(1)}, u32[]{:S(2)}, u32[]{:S(2)}) collective-permute-start(bf16[6,64,128]{2,1,0:T(8,128)(2,1)S(1)} %get-tuple-element.15), channel_id=1, source_target_pairs={{0,1},{1,2},{2,3},{3,4},{4,5},{5,6},{6,7},{8,9},{9,10},{10,11},{11... | collective-permute-start | bytes 294920 | tf_op jit(solution)/shard_map/ppermute | solution.py:185
  111.7 5.9 %collective-permute-start.11 = (bf16[6,64,128]{2,1,0:T(8,128)(2,1)S(1)}, bf16[6,64,128]{2,1,0:T(8,128)(2,1)S(1)}, u32[]{:S(2)}, u32[]{:S(2)}) collective-permute-start(bf16[6,64,128]{2,1,0:T(8,128)(2,1)S(1)} %get-tuple-element.16), channel_id=1, source_target_pairs={{1,0},{2,1},{3,2},{4,3},{5,4},{6,5},{7,6},{9,8},{10,9},{11,10},{12... | collective-permute-start | bytes 294920 | tf_op jit(solution)/shard_map/ppermute | solution.py:186

commit v4 on v3

--- a/solution.py
+++ b/solution.py
@@ -139,13 +139,13 @@
         pair = jnp.concatenate(outs[2 * b : 2 * b + 2], axis=0).astype(BF)
         turned[pl.ds(b, 128, stride=16), :] = jnp.transpose(pair.astype(F32))
     for m in range(4):
-        message_ref[lax.rem(m - members + 4, 4)] = turned[512 * m : 512 * m + 512].astype(BF)
+        message_ref[lax.bitwise_xor(members, m)] = turned[512 * m : 512 * m + 512].astype(BF)
 
 
 def average(place_ref, second_ref, m0, m1, m2, m3, mean_ref, gathered):
     members = place_ref[2]
     for t, ref in enumerate((m0, m1, m2, m3)):
-        gathered[lax.rem(members - t + 4, 4)] = ref[...]
+        gathered[lax.bitwise_xor(members, t)] = ref[...]
     for j in range(32):
         blocks = []
         for k in range(4):
@@ -169,7 +169,8 @@
 def on_device(contact_map, dilations, conv_weight, conv_gain, conv_shift, out_weight):
     rows, cols = lax.axis_size("row"), lax.axis_size("col")
     row, col = lax.axis_index("row"), lax.axis_index("col")
-    place = jnp.stack([row, col, lax.rem(row, 4)]).astype(jnp.int32)
+    mixed = lax.bitwise_xor(lax.rem(row, 4), lax.rem(lax.div(row, 4) + col, 4))
+    place = jnp.stack([row, col, mixed]).astype(jnp.int32)
     down_way = [(r, r + 1) for r in range(rows - 1)]
     up_way = [(r + 1, r) for r in range(rows - 1)]
     right_way = [(c, c + 1) for c in range(cols - 1)]
@@ -212,7 +213,7 @@
         for a in range(rows // 4):
             for k in range(4):
                 for b in range(cols):
-                    pairs.append(((4 * a + k) * cols + b, (4 * b + (k + t) % 4) * cols + a))
+                    pairs.append(((4 * a + k) * cols + b, (4 * b + (k ^ t ^ (a + b) % 4)) * cols + a))
         received.append(lax.ppermute(messages[t], BOTH, pairs))
     mean = call(
         average,

time: 121 us -> 118 us (0.975)
  starting transfers between devices: 54.1 us -> 50.5 us
    ppermute x2, starting transfers between devices: 12 us -> 3.84 us  [rims(): from_left = lax.ppermute(to_right, 'col', right_way)]
    ppermute x4, starting transfers between devices: 14.8 us -> 19.2 us  [on_device(): received.append(lax.ppermute(messages[t], BOTH, pairs))]
    ppermute x2, waiting for transfers between devices: 6 us -> 8.27 us  [rims(): below = lax.ppermute(own[:depth], 'row', up_way)]
    ppermute x4, waiting for transfers between devices: 14.7 us -> 12.5 us  [on_device(): received.append(lax.ppermute(messages[t], BOTH, pairs))]
  transfers between devices with their start and end apart: 12 -> 12, of which waited for: 8 -> 7; matrix products, arithmetic and copies ran while one was open for 0% -> 0% of each run, Pallas kernels for 0% -> 0%
where the time goes in v4:
time: 118 us
  waiting for transfers between devices  54.6 us (46%)
  starting transfers between devices  50.5 us (43%)
  Pallas kernels  8.48 us (7%)
  local copies, waits for them, and re-layouts  3.69 us (3%)
    ppermute x2, waiting for transfers between devices, rims(): above = lax.ppermute(own[32 - depth:], 'row', down_way)  27.4 us
    ppermute x4, starting transfers between devices, on_device(): received.append(lax.ppermute(messages[t], BOTH, pairs))  19.2 us
    ppermute x2, starting transfers between devices, rims(): below = lax.ppermute(own[:depth], 'row', up_way)  16 us
    ppermute x4, waiting for transfers between devices, on_device(): received.append(lax.ppermute(messages[t], BOTH, pairs))  12.5 us
    pallas_call x5, Pallas kernels, call(): pl.pallas_call(body, out_shape=outs, in_specs=[SMEM] * n_smem + [VMEM] *...  8.48 us
    ppermute x2, waiting for transfers between devices, rims(): below = lax.ppermute(own[:depth], 'row', up_way)  8.27 us
    ppermute x2, waiting for transfers between devices, rims(): from_right = lax.ppermute(to_left, 'col', left_way)  6.44 us
    ppermute x2, starting transfers between devices, rims(): above = lax.ppermute(own[32 - depth:], 'row', down_way)  6.31 us
  transfers between devices with their start and end apart: 12, of which 7 were waited for; matrix products, arithmetic and copies ran while one was open for 0% of the time, Pallas kernels for 0%

profile of v4, /device:TPU:25, one launch (start us, length us, event | category | flops | bytes accessed | tf_op | source)
XLA Modules:
  0.0 117.6 jit_solution(11377233851782246855)
XLA Ops:
  0.0 1.2 %copy.19 = bf16[64,32,128]{2,0,1:T(8,128)(2,1)S(1)} copy(bf16[64,32,128]{2,1,0:T(8,128)(2,1)} %param.6) | data formatting | bytes 1048576 | tf_op args[0]
  1.3 11.2 %collective-permute-start.1 = (bf16[16,64,128]{2,1,0:T(8,128)(2,1)S(1)}, bf16[16,64,128]{2,1,0:T(8,128)(2,1)S(1)}, u32[]{:S(2)}, u32[]{:S(2)}) collective-permute-start(bf16[16,64,128]{2,1,0:T(8,128)(2,1)S(1)} %get-tuple-element.23), channel_id=1, source_target_pairs={{8,0},{16,8},{24,16},{32,24},{40,32},{48,40},{56,48},{64,56},{72,6... | collective-permute-start | bytes 786440 | tf_op jit(solution)/shard_map/ppermute | solution.py:181
  12.5 1.9 %collective-permute-start = (bf16[16,64,128]{2,1,0:T(8,128)(2,1)S(1)}, bf16[16,64,128]{2,1,0:T(8,128)(2,1)S(1)}, u32[]{:S(2)}, u32[]{:S(2)}) collective-permute-start(bf16[16,64,128]{2,1,0:T(8,128)(2,1)S(1)} %get-tuple-element.24), channel_id=1, source_target_pairs={{0,8},{8,16},{16,24},{24,32},{32,40},{40,48},{48,56},{56,64},{64,7... | collective-permute-start | bytes 786440 | tf_op jit(solution)/shard_map/ppermute | solution.py:180
  14.4 5.6 %collective-permute-done.1.down_ref = bf16[16,64,128]{2,1,0:T(8,128)(2,1)S(1)} collective-permute-done((bf16[16,64,128]{2,1,0:T(8,128)(2,1)S(1)}, bf16[16,64,128]{2,1,0:T(8,128)(2,1)S(1)}, u32[]{:S(2)}, u32[]{:S(2)}) %collective-permute-start.1) | collective-permute-done | bytes 262176 | tf_op jit(solution)/shard_map/ppermute | solution.py:181
  20.0 18.3 %collective-permute-done.up_ref = bf16[16,64,128]{2,1,0:T(8,128)(2,1)S(1)} collective-permute-done((bf16[16,64,128]{2,1,0:T(8,128)(2,1)S(1)}, bf16[16,64,128]{2,1,0:T(8,128)(2,1)S(1)}, u32[]{:S(2)}, u32[]{:S(2)}) %collective-permute-start) | collective-permute-done | bytes 262176 | tf_op jit(solution)/shard_map/ppermute | solution.py:180
  38.3 0.5 shard_map.64
  38.8 1.9 %collective-permute-start.2 = (bf16[8,64,128]{2,1,0:T(8,128)(2,1)S(1)}, bf16[8,64,128]{2,1,0:T(8,128)(2,1)S(1)}, u32[]{:S(2)}, u32[]{:S(2)}) collective-permute-start(bf16[8,64,128]{2,1,0:T(8,128)(2,1)S(1)} %get-tuple-element.11), channel_id=1, source_target_pairs={{0,1},{1,2},{2,3},{3,4},{4,5},{5,6},{6,7},{8,9},{9,10},{10,11},{11... | collective-permute-start | bytes 393224 | tf_op jit(solution)/shard_map/ppermute | solution.py:186
  40.8 2.8 %collective-permute-start.3 = (bf16[8,64,128]{2,1,0:T(8,128)(2,1)S(1)}, bf16[8,64,128]{2,1,0:T(8,128)(2,1)S(1)}, u32[]{:S(2)}, u32[]{:S(2)}) collective-permute-start(bf16[8,64,128]{2,1,0:T(8,128)(2,1)S(1)} %get-tuple-element.12), channel_id=1, source_target_pairs={{1,0},{2,1},{3,2},{4,3},{5,4},{6,5},{7,6},{9,8},{10,9},{11,10},{12... | collective-permute-start | bytes 393224 | tf_op jit(solution)/shard_map/ppermute | solution.py:187
  44.1 2.9 %collective-permute-done.3.from_right = bf16[8,64,128]{2,1,0:T(8,128)(2,1)S(1)} collective-permute-done((bf16[8,64,128]{2,1,0:T(8,128)(2,1)S(1)}, bf16[8,64,128]{2,1,0:T(8,128)(2,1)S(1)}, u32[]{:S(2)}, u32[]{:S(2)}) %collective-permute-start.3) | collective-permute-done | bytes 131104 | tf_op jit(solution)/shard_map/ppermute | solution.py:187
  47.2 0.6 copy-done
  47.8 4.1 %shard_map.65 = (bf16[32,64,128]{2,1,0:T(8,128)(2,1)S(1)}, bf16[4,512,128]{2,1,0:T(8,128)(2,1)S(1)}) custom-call(s32[3]{0:T(128)S(1)} %copy-done, s32[3]{0:T(128)S(1)} %pad_add_fusion.place_ref, bf16[16,64,128]{2,1,0:T(8,128)(2,1)S(1)} %collective-permute-done.up_ref, bf16[32,64,128]{2,1,0:T(8,128)(2,1)S(1)} %bitcast.21, ...), custom_call_target="tpu_custom_call" | custom-call | flops 838860800 | bytes 4194304 | tf_op jit(solution)/shard_map/pallas_call | solution.py:20
  52.1 11.3 %collective-permute-start.6 = (bf16[512,128]{1,0:T(8,128)(2,1)S(1)}, bf16[512,128]{1,0:T(8,128)(2,1)S(1)}, u32[]{:S(2)}, u32[]{:S(2)}) collective-permute-start(bf16[512,128]{1,0:T(8,128)(2,1)S(1)} %get-tuple-element.20), channel_id=1, source_target_pairs={{0,16},{1,56},{2,64},{3,104},{4,144},{5,184},{6,192},{7,232},{8,24... | collective-permute-start | bytes 393224 | tf_op jit(solution)/shard_map/ppermute | solution.py:217
  63.5 7.7 %collective-permute-start.4 = (bf16[512,128]{1,0:T(8,128)(2,1)S(1)}, bf16[512,128]{1,0:T(8,128)(2,1)S(1)}, u32[]{:S(2)}, u32[]{:S(2)}) collective-permute-start(bf16[512,128]{1,0:T(8,128)(2,1)S(1)} %get-tuple-element.22), channel_id=1, source_target_pairs={{0,0},{1,40},{2,80},{3,120},{4,128},{5,168},{6,208},{7,248},{8,8},... | collective-permute-start | bytes 393224 | tf_op jit(solution)/shard_map/ppermute | solution.py:217
  71.2 12.5 %collective-permute-done.6.m2 = bf16[512,128]{1,0:T(8,128)(2,1)S(1)} collective-permute-done((bf16[512,128]{1,0:T(8,128)(2,1)S(1)}, bf16[512,128]{1,0:T(8,128)(2,1)S(1)}, u32[]{:S(2)}, u32[]{:S(2)}) %collective-permute-start.6) | collective-permute-done | bytes 131104 | tf_op jit(solution)/shard_map/ppermute | solution.py:217
  83.8 1.4 %shard_map.66.own_ref = bf16[32,64,128]{2,1,0:T(8,128)(2,1)S(1)} custom-call(s32[3]{0:T(128)S(1)} %pad_add_fusion.place_ref, bf16[32,64,128]{2,1,0:T(8,128)(2,1)S(1)} %get-tuple-element.13.second_ref, bf16[512,128]{1,0:T(8,128)(2,1)S(1)} %collective-permute-done.4.m0, bf16[512,128]{1,0:T(8,128)(2,1)S(1)} %collective-permute-done.5.m1, ...), custom_call_target="tpu_custom_call" | custom-call | bytes 2097152 | tf_op jit(solution)/shard_map/pallas_call | solution.py:20
  85.2 4.8 %collective-permute-start.9 = (bf16[8,64,128]{2,1,0:T(8,128)(2,1)S(1)}, bf16[8,64,128]{2,1,0:T(8,128)(2,1)S(1)}, u32[]{:S(2)}, u32[]{:S(2)}) collective-permute-start(bf16[8,64,128]{2,1,0:T(8,128)(2,1)S(1)} %get-tuple-element.17), channel_id=1, source_target_pairs={{8,0},{16,8},{24,16},{32,24},{40,32},{48,40},{56,48},{64,56},{72,6... | collective-permute-start | bytes 393224 | tf_op jit(solution)/shard_map/ppermute | solution.py:181
  90.0 4.4 %collective-permute-start.8 = (bf16[8,64,128]{2,1,0:T(8,128)(2,1)S(1)}, bf16[8,64,128]{2,1,0:T(8,128)(2,1)S(1)}, u32[]{:S(2)}, u32[]{:S(2)}) collective-permute-start(bf16[8,64,128]{2,1,0:T(8,128)(2,1)S(1)} %get-tuple-element.18), channel_id=1, source_target_pairs={{0,8},{8,16},{16,24},{24,32},{32,40},{40,48},{48,56},{56,64},{64,7... | collective-permute-start | bytes 393224 | tf_op jit(solution)/shard_map/ppermute | solution.py:180
  94.4 2.7 %collective-permute-done.9.down_ref = bf16[8,64,128]{2,1,0:T(8,128)(2,1)S(1)} collective-permute-done((bf16[8,64,128]{2,1,0:T(8,128)(2,1)S(1)}, bf16[8,64,128]{2,1,0:T(8,128)(2,1)S(1)}, u32[]{:S(2)}, u32[]{:S(2)}) %collective-permute-start.9) | collective-permute-done | bytes 131104 | tf_op jit(solution)/shard_map/ppermute | solution.py:181
  97.1 9.1 %collective-permute-done.8.up_ref = bf16[8,64,128]{2,1,0:T(8,128)(2,1)S(1)} collective-permute-done((bf16[8,64,128]{2,1,0:T(8,128)(2,1)S(1)}, bf16[8,64,128]{2,1,0:T(8,128)(2,1)S(1)}, u32[]{:S(2)}, u32[]{:S(2)}) %collective-permute-start.8) | collective-permute-done | bytes 131104 | tf_op jit(solution)/shard_map/ppermute | solution.py:180
  106.6 1.9 %collective-permute-start.10 = (bf16[6,64,128]{2,1,0:T(8,128)(2,1)S(1)}, bf16[6,64,128]{2,1,0:T(8,128)(2,1)S(1)}, u32[]{:S(2)}, u32[]{:S(2)}) collective-permute-start(bf16[6,64,128]{2,1,0:T(8,128)(2,1)S(1)} %get-tuple-element.15), channel_id=1, source_target_pairs={{0,1},{1,2},{2,3},{3,4},{4,5},{5,6},{6,7},{8,9},{9,10},{10,11},{11... | collective-permute-start | bytes 294920 | tf_op jit(solution)/shard_map/ppermute | solution.py:186
  108.5 2.4 %collective-permute-start.11 = (bf16[6,64,128]{2,1,0:T(8,128)(2,1)S(1)}, bf16[6,64,128]{2,1,0:T(8,128)(2,1)S(1)}, u32[]{:S(2)}, u32[]{:S(2)}) collective-permute-start(bf16[6,64,128]{2,1,0:T(8,128)(2,1)S(1)} %get-tuple-element.16), channel_id=1, source_target_pairs={{1,0},{2,1},{3,2},{4,3},{5,4},{6,5},{7,6},{9,8},{10,9},{11,10},{12... | collective-permute-start | bytes 294920 | tf_op jit(solution)/shard_map/ppermute | solution.py:187
  110.9 3.5 %collective-permute-done.11.from_right = bf16[6,64,128]{2,1,0:T(8,128)(2,1)S(1)} collective-permute-done((bf16[6,64,128]{2,1,0:T(8,128)(2,1)S(1)}, bf16[6,64,128]{2,1,0:T(8,128)(2,1)S(1)}, u32[]{:S(2)}, u32[]{:S(2)}) %collective-permute-start.11) | collective-permute-done | bytes 98336 | tf_op jit(solution)/shard_map/ppermute | solution.py:187
  114.5 2.0 %shard_map.68 = bf16[32,64,128]{2,1,0:T(8,128)(2,1)S(1)} custom-call(s32[3]{0:T(128)S(1)} %copy-done, bf16[8,64,128]{2,1,0:T(8,128)(2,1)S(1)} %collective-permute-done.8.up_ref, bf16[32,64,128]{2,1,0:T(8,128)(2,1)S(1)} %shard_map.66.own_ref, bf16[8,64,128]{2,1,0:T(8,128)(2,1)S(1)} %collective-permute-done.9.down_ref, ...), custom_call_target="tpu_custom_call" | custom-call | flops 335544320 | bytes 2097152 | tf_op jit(solution)/shard_map/pallas_call | solution.py:20
  116.4 1.1 copy.16
  (26 shorter events, 1.4 us)
Async XLA Ops:
  1.3 18.7 %collective-permute-start.1 = (bf16[16,64,128]{2,1,0:T(8,128)(2,1)S(1)}, bf16[16,64,128]{2,1,0:T(8,128)(2,1)S(1)}, u32[]{:S(2)}, u32[]{:S(2)}) collective-permute-start(bf16[16,64,128]{2,1,0:T(8,128)(2,1)S(1)} %get-tuple-element.23), channel_id=1, source_target_pairs={{8,0},{16,8},{24,16},{32,24},{40,32},{48,40},{56,48},{64,56},{72,6... | collective-permute-start | bytes 786440 | tf_op jit(solution)/shard_map/ppermute | solution.py:181
  12.5 25.8 %collective-permute-start = (bf16[16,64,128]{2,1,0:T(8,128)(2,1)S(1)}, bf16[16,64,128]{2,1,0:T(8,128)(2,1)S(1)}, u32[]{:S(2)}, u32[]{:S(2)}) collective-permute-start(bf16[16,64,128]{2,1,0:T(8,128)(2,1)S(1)} %get-tuple-element.24), channel_id=1, source_target_pairs={{0,8},{8,16},{16,24},{24,32},{32,40},{40,48},{48,56},{56,64},{64,7... | collective-permute-start | bytes 786440 | tf_op jit(solution)/shard_map/ppermute | solution.py:180
  38.3 5.4 %copy-start.1 = (bf16[3,9,32,64]{3,2,1,0:T(8,128)(2,1)S(1)}, bf16[3,9,32,64]{3,2,1,0:T(8,128)(2,1)}, u32[]{:S(2)}) copy-start(bf16[3,9,32,64]{3,2,1,0:T(8,128)(2,1)} %param.8) | copy-start | bytes 331780
  38.8 4.7 %copy-start.2 = (bf16[3,64,32]{1,2,0:T(8,128)(2,1)S(1)}, bf16[3,64,32]{1,2,0:T(8,128)(2,1)}, u32[]{:S(2)}) copy-start(bf16[3,64,32]{1,2,0:T(8,128)(2,1)} %param.11) | copy-start | bytes 36868
  38.8 5.3 %collective-permute-start.2 = (bf16[8,64,128]{2,1,0:T(8,128)(2,1)S(1)}, bf16[8,64,128]{2,1,0:T(8,128)(2,1)S(1)}, u32[]{:S(2)}, u32[]{:S(2)}) collective-permute-start(bf16[8,64,128]{2,1,0:T(8,128)(2,1)S(1)} %get-tuple-element.11), channel_id=1, source_target_pairs={{0,1},{1,2},{2,3},{3,4},{4,5},{5,6},{6,7},{8,9},{9,10},{10,11},{11... | collective-permute-start | bytes 393224 | tf_op jit(solution)/shard_map/ppermute | solution.py:186
  40.8 6.3 %collective-permute-start.3 = (bf16[8,64,128]{2,1,0:T(8,128)(2,1)S(1)}, bf16[8,64,128]{2,1,0:T(8,128)(2,1)S(1)}, u32[]{:S(2)}, u32[]{:S(2)}) collective-permute-start(bf16[8,64,128]{2,1,0:T(8,128)(2,1)S(1)} %get-tuple-element.12), channel_id=1, source_target_pairs={{1,0},{2,1},{3,2},{4,3},{5,4},{6,5},{7,6},{9,8},{10,9},{11,10},{12... | collective-permute-start | bytes 393224 | tf_op jit(solution)/shard_map/ppermute | solution.py:187
  44.0 3.0 %copy-start.3 = (f32[3,32]{1,0:T(4,128)S(1)}, f32[3,32]{1,0:T(4,128)}, u32[]{:S(2)}) copy-start(f32[3,32]{1,0:T(4,128)} %param.9) | copy-start | bytes 1156
  44.1 3.0 %copy-start.4 = (f32[3,32]{1,0:T(4,128)S(1)}, f32[3,32]{1,0:T(4,128)}, u32[]{:S(2)}) copy-start(f32[3,32]{1,0:T(4,128)} %param.10) | copy-start | bytes 1156
  47.1 0.7 copy-start
  52.0 19.2 %collective-permute-start.7 = (bf16[512,128]{1,0:T(8,128)(2,1)S(1)}, bf16[512,128]{1,0:T(8,128)(2,1)S(1)}, u32[]{:S(2)}, u32[]{:S(2)}) collective-permute-start(bf16[512,128]{1,0:T(8,128)(2,1)S(1)} %get-tuple-element.19), channel_id=1, source_target_pairs={{0,24},{1,48},{2,72},{3,96},{4,152},{5,176},{6,200},{7,224},{8,16}... | collective-permute-start | bytes 393224 | tf_op jit(solution)/shard_map/ppermute | solution.py:217
  52.1 31.7 %collective-permute-start.6 = (bf16[512,128]{1,0:T(8,128)(2,1)S(1)}, bf16[512,128]{1,0:T(8,128)(2,1)S(1)}, u32[]{:S(2)}, u32[]{:S(2)}) collective-permute-start(bf16[512,128]{1,0:T(8,128)(2,1)S(1)} %get-tuple-element.20), channel_id=1, source_target_pairs={{0,16},{1,56},{2,64},{3,104},{4,144},{5,184},{6,192},{7,232},{8,24... | collective-permute-start | bytes 393224 | tf_op jit(solution)/shard_map/ppermute | solution.py:217
  63.4 20.4 %collective-permute-start.5 = (bf16[512,128]{1,0:T(8,128)(2,1)S(1)}, bf16[512,128]{1,0:T(8,128)(2,1)S(1)}, u32[]{:S(2)}, u32[]{:S(2)}) collective-permute-start(bf16[512,128]{1,0:T(8,128)(2,1)S(1)} %get-tuple-element.21), channel_id=1, source_target_pairs={{0,8},{1,32},{2,88},{3,112},{4,136},{5,160},{6,216},{7,240},{8,0},... | collective-permute-start | bytes 393224 | tf_op jit(solution)/shard_map/ppermute | solution.py:217
  63.5 20.3 %collective-permute-start.4 = (bf16[512,128]{1,0:T(8,128)(2,1)S(1)}, bf16[512,128]{1,0:T(8,128)(2,1)S(1)}, u32[]{:S(2)}, u32[]{:S(2)}) collective-permute-start(bf16[512,128]{1,0:T(8,128)(2,1)S(1)} %get-tuple-element.22), channel_id=1, source_target_pairs={{0,0},{1,40},{2,80},{3,120},{4,128},{5,168},{6,208},{7,248},{8,8},... | collective-permute-start | bytes 393224 | tf_op jit(solution)/shard_map/ppermute | solution.py:217
  85.2 11.9 %collective-permute-start.9 = (bf16[8,64,128]{2,1,0:T(8,128)(2,1)S(1)}, bf16[8,64,128]{2,1,0:T(8,128)(2,1)S(1)}, u32[]{:S(2)}, u32[]{:S(2)}) collective-permute-start(bf16[8,64,128]{2,1,0:T(8,128)(2,1)S(1)} %get-tuple-element.17), channel_id=1, source_target_pairs={{8,0},{16,8},{24,16},{32,24},{40,32},{48,40},{56,48},{64,56},{72,6... | collective-permute-start | bytes 393224 | tf_op jit(solution)/shard_map/ppermute | solution.py:181
  90.0 16.2 %collective-permute-start.8 = (bf16[8,64,128]{2,1,0:T(8,128)(2,1)S(1)}, bf16[8,64,128]{2,1,0:T(8,128)(2,1)S(1)}, u32[]{:S(2)}, u32[]{:S(2)}) collective-permute-start(bf16[8,64,128]{2,1,0:T(8,128)(2,1)S(1)} %get-tuple-element.18), channel_id=1, source_target_pairs={{0,8},{8,16},{16,24},{24,32},{32,40},{40,48},{48,56},{56,64},{64,7... | collective-permute-start | bytes 393224 | tf_op jit(solution)/shard_map/ppermute | solution.py:180
  106.6 4.3 %collective-permute-start.10 = (bf16[6,64,128]{2,1,0:T(8,128)(2,1)S(1)}, bf16[6,64,128]{2,1,0:T(8,128)(2,1)S(1)}, u32[]{:S(2)}, u32[]{:S(2)}) collective-permute-start(bf16[6,64,128]{2,1,0:T(8,128)(2,1)S(1)} %get-tuple-element.15), channel_id=1, source_target_pairs={{0,1},{1,2},{2,3},{3,4},{4,5},{5,6},{6,7},{8,9},{9,10},{10,11},{11... | collective-permute-start | bytes 294920 | tf_op jit(solution)/shard_map/ppermute | solution.py:186
  108.5 5.9 %collective-permute-start.11 = (bf16[6,64,128]{2,1,0:T(8,128)(2,1)S(1)}, bf16[6,64,128]{2,1,0:T(8,128)(2,1)S(1)}, u32[]{:S(2)}, u32[]{:S(2)}) collective-permute-start(bf16[6,64,128]{2,1,0:T(8,128)(2,1)S(1)} %get-tuple-element.16), channel_id=1, source_target_pairs={{1,0},{2,1},{3,2},{4,3},{5,4},{6,5},{7,6},{9,8},{10,9},{11,10},{12... | collective-permute-start | bytes 294920 | tf_op jit(solution)/shard_map/ppermute | solution.py:187

commit v5 on v4

--- a/solution.py
+++ b/solution.py
@@ -49,38 +49,54 @@
     return side.astype(BF)
 
 
-def block_rows(source, rows, spacing, kernel, gain, shift, expand, narrow=False):
+def tap_sums(taps, spacing, narrow):
+    lane = lanes(32)
+    before, after = lane >= spacing, lane < 128 - spacing
+    sums = []
+    for tap in taps:
+        left = [pltpu.roll(tap[:32, h : h + 128], spacing, 1) for h in (0, 128)]
+        right = [pltpu.roll(tap[64:, h : h + 128], 128 - spacing, 1) for h in (0, 128)]
+        sums.append(
+            [
+                tap[32:64, 128 * h : 128 * h + 128]
+                + jnp.where(before, left[h], left[1 - h])
+                + jnp.where(after, right[h], right[1 - h])
+                for h in range(1 if narrow else 2)
+            ]
+        )
+    return sums
+
+
+def conv_rows(source, rows, spacing, kernel, narrow):
     taps = []
     for at in rows:
         stacked = jnp.concatenate(
             [source[at - spacing], source[at], source[at + spacing]], axis=0
         )
         taps.append(jnp.dot(kernel, jnp.maximum(stacked, 0), preferred_element_type=F32))
-    lane = lanes(32)
-    before, after = lane >= spacing, lane < 128 - spacing
-    hidden = []
-    for tap in taps:
-        left = [pltpu.roll(tap[:32, h : h + 128], spacing, 1) for h in (0, 128)]
-        right = [pltpu.roll(tap[64:, h : h + 128], 128 - spacing, 1) for h in (0, 128)]
-        convs = []
-        for h in range(1 if narrow else 2):
-            convs.append(
-                tap[32:64, 128 * h : 128 * h + 128]
-                + jnp.where(before, left[h], left[1 - h])
-                + jnp.where(after, right[h], right[1 - h])
-            )
-        hidden.append(
-            [jnp.maximum(gain * conv + shift, 0.0).astype(BF) for conv in convs]
+    return tap_sums(taps, spacing, narrow)
+
+
+def grow(sums, gain, shift, expand):
+    hidden = [jnp.maximum(gain * conv + shift, 0.0).astype(BF) for conv in sums]
+    grown = []
+    for i in range(0, len(hidden), 2):
+        both = jnp.dot(
+            expand, jnp.concatenate(hidden[i : i + 2], axis=1), preferred_element_type=F32
         )
+        grown += [both[:, :128], both[:, 128:]]
+    return grown
+
+
+def block_rows(source, rows, spacing, kernel, gain, shift, expand, narrow=False):
+    sums = conv_rows(source, rows, spacing, kernel, narrow)
+    grown = grow([conv for row in sums for conv in row], gain, shift, expand)
     if narrow:
-        hidden = [[h[0] for h in hidden[i : i + 2]] for i in range(0, len(rows), 2)]
-    grown = [
-        jnp.dot(expand, jnp.concatenate(h, axis=1), preferred_element_type=F32) for h in hidden
+        return [source[at, :, :128].astype(F32) + g for at, g in zip(rows, grown)]
+    return [
+        source[at].astype(F32) + jnp.concatenate(grown[2 * i : 2 * i + 2], axis=1)
+        for i, at in enumerate(rows)
     ]
-    if narrow:
-        halves = [g[:, h : h + 128] for g in grown for h in (0, 128)]
-        return [source[at, :, :128].astype(F32) + half for at, half in zip(rows, halves)]
-    return [source[at].astype(F32) + g for at, g in zip(rows, grown)]
 
 
 def block_of(layer, spacing_ref, kernel_ref, gain_ref, shift_ref, expand_ref):
@@ -89,9 +105,9 @@
     )
 
 
-def pack_sides(up_ref, own_ref, down_ref, left_ref, right_ref):
+def pack_rows(refs, left_ref, right_ref):
     first = 0
-    for ref in (up_ref, own_ref, down_ref):
+    for ref in refs:
         for g in range(ref.shape[0] // 8):
             pieces = [ref[8 * g + q] for q in range(8)]
             left_ref[first + g] = pack_strips(pieces, 0, 16)
@@ -99,14 +115,19 @@
         first += ref.shape[0] // 8
 
 
-def fill_wide(wide, up_ref, own_ref, down_ref, from_left, from_right):
-    first = 0
-    for ref in (up_ref, own_ref, down_ref):
+def pack_sides(up_ref, own_ref, down_ref, left_ref, right_ref):
+    pack_rows((up_ref, own_ref, down_ref), left_ref, right_ref)
+
+
+def fill_wide(wide, refs, from_left, from_right, first=0):
+    at = 0
+    for ref in refs:
         for r in range(ref.shape[0]):
-            at = first + r
-            wide[at, :, :128] = ref[r]
-            wide[at, :, 128:] = side_lanes(from_right[at // 8], from_left[at // 8], at % 8, 16)
-        first += ref.shape[0]
+            wide[first + at, :, :128] = ref[r]
+            wide[first + at, :, 128:] = side_lanes(
+                from_right[at // 8], from_left[at // 8], at % 8, 16
+            )
+            at += 1
 
 
 def first_blocks(
@@ -117,7 +138,7 @@
     row, col = place_ref[0], place_ref[1]
     members = place_ref[2]
     weights = (spacing_ref, kernel_ref, gain_ref, shift_ref, expand_ref)
-    fill_wide(wide, up_ref, own_ref, down_ref, from_left, from_right)
+    fill_wide(wide, (up_ref, own_ref, down_ref), from_left, from_right)
     lane = lax.broadcasted_iota(jnp.int32, (64, 256), 1)
     inside = (lane < 128) | ((lane < 192) & (col < 7)) | ((lane >= 192) & (col > 0))
 
@@ -142,7 +163,7 @@
         message_ref[lax.bitwise_xor(members, m)] = turned[512 * m : 512 * m + 512].astype(BF)
 
 
-def average(place_ref, second_ref, m0, m1, m2, m3, mean_ref, gathered):
+def average(place_ref, second_ref, m0, m1, m2, m3, mean_ref, left_ref, right_ref, gathered):
     members = place_ref[2]
     for t, ref in enumerate((m0, m1, m2, m3)):
         gathered[lax.bitwise_xor(members, t)] = ref[...]
@@ -153,17 +174,58 @@
             blocks += [part, pltpu.roll(part, 64, 1)]
         mirrored = jnp.transpose(jnp.concatenate(blocks, axis=0))[:64]
         mean_ref[j] = (0.5 * (second_ref[j].astype(F32) + mirrored)).astype(BF)
-
-
-def last_block(
-    spacing_ref, up_ref, own_ref, down_ref, from_left, from_right,
-    kernel_ref, gain_ref, shift_ref, expand_ref, out_ref, wide,
+    pack_rows((mean_ref,), left_ref, right_ref)
+
+
+def fill_last(wide, mean_ref, from_left, from_right):
+    for at in range(8):
+        wide[at] = jnp.zeros((64, 256), BF)
+        wide[40 + at] = jnp.zeros((64, 256), BF)
+    fill_wide(wide, (mean_ref,), from_left, from_right, 8)
+
+
+def last_edges(
+    spacing_ref, mean_ref, from_left, from_right, kernel_ref, to_up_ref, to_down_ref, wide
 ):
-    weights = (spacing_ref, kernel_ref, gain_ref, shift_ref, expand_ref)
-    fill_wide(wide, up_ref, own_ref, down_ref, from_left, from_right)
-    outs = block_rows(wide, [r + 8 for r in range(32)], *block_of(2, *weights), narrow=True)
-    for r, out in enumerate(outs):
-        out_ref[r] = out.astype(BF)
+    spacing, kernel = spacing_ref[2], kernel_ref[2]
+    fill_last(wide, mean_ref, from_left, from_right)
+    taps = []
+    for i in range(8):
+        up = jnp.maximum(wide[i + spacing], 0)
+        taps.append(jnp.dot(kernel[:, 128:], up, preferred_element_type=F32))
+        down = jnp.maximum(wide[40 + i - spacing], 0)
+        taps.append(jnp.dot(kernel[:, :64], down, preferred_element_type=F32))
+    sums = tap_sums(taps, spacing, True)
+    for i in range(8):
+        to_up_ref[i] = sums[2 * i][0].astype(BF)
+        to_down_ref[i] = sums[2 * i + 1][0].astype(BF)
+
+
+def last_inner(
+    spacing_ref, mean_ref, from_left, from_right, kernel_ref, gain_ref, shift_ref, expand_ref,
+    out_ref, conv_ref, wide,
+):
+    fill_last(wide, mean_ref, from_left, from_right)
+    sums = conv_rows(wide, [r + 8 for r in range(32)], spacing_ref[2], kernel_ref[2], True)
+    sums = [row[0] for row in sums]
+    for i in range(8):
+        conv_ref[i] = sums[i]
+        conv_ref[8 + i] = sums[24 + i]
+    grown = grow(sums[8:24], gain_ref[2], shift_ref[2], expand_ref[2])
+    for i in range(16):
+        out_ref[8 + i] = (mean_ref[8 + i].astype(F32) + grown[i]).astype(BF)
+
+
+def last_outer(
+    inner_ref, mean_ref, conv_ref, up_ref, down_ref, gain_ref, shift_ref, expand_ref, out_ref
+):
+    sums = [conv_ref[i] + up_ref[i].astype(F32) for i in range(8)]
+    sums += [conv_ref[8 + i] + down_ref[i].astype(F32) for i in range(8)]
+    grown = grow(sums, gain_ref[2], shift_ref[2], expand_ref[2])
+    out_ref[8:24] = inner_ref[8:24]
+    for i in range(16):
+        at = i if i < 8 else 16 + i
+        out_ref[at] = (mean_ref[at].astype(F32) + grown[i]).astype(BF)
 
 
 def on_device(contact_map, dilations, conv_weight, conv_gain, conv_shift, out_weight):
@@ -176,18 +238,15 @@
     right_way = [(c, c + 1) for c in range(cols - 1)]
     left_way = [(c + 1, c) for c in range(cols - 1)]
 
-    def rims(own, depth):
-        above = lax.ppermute(own[32 - depth :], "row", down_way)
-        below = lax.ppermute(own[:depth], "row", up_way)
-        strip = jax.ShapeDtypeStruct(((32 + 2 * depth) // 8, 64, 128), BF)
-        to_left, to_right = call(
-            pack_sides, (strip, strip), (above, own, below), 0, [], 0, 1 << 20
-        )
-        from_left = lax.ppermute(to_right, "col", right_way)
-        from_right = lax.ppermute(to_left, "col", left_way)
-        return above, own, below, from_left, from_right
-
     own = jnp.transpose(contact_map, (1, 0, 2))
+    above = lax.ppermute(own[16:], "row", down_way)
+    below = lax.ppermute(own[:16], "row", up_way)
+    strip = jax.ShapeDtypeStruct((8, 64, 128), BF)
+    to_left, to_right = call(
+        pack_sides, (strip, strip), (above, own, below), 0, [], 0, 1 << 20
+    )
+    from_left = lax.ppermute(to_right, "col", right_way)
+    from_right = lax.ppermute(to_left, "col", left_way)
     kernel = jnp.transpose(conv_weight.reshape(3, 3, 3, 32, 64), (0, 2, 3, 1, 4)).reshape(3, 96, 192)
     gain = jnp.broadcast_to(conv_gain[:, :, None], (3, 32, 128))
     shift = jnp.broadcast_to(conv_shift[:, :, None], (3, 32, 128))
@@ -197,7 +256,7 @@
     second, messages = call(
         first_blocks,
         (tile, jax.ShapeDtypeStruct((4, 512, 128), BF)),
-        (dilations, place, *rims(own, 16), *weights),
+        (dilations, place, above, own, below, from_left, from_right, *weights),
         2,
         [
             pltpu.VMEM((64, 64, 256), BF),
@@ -215,22 +274,47 @@
                 for b in range(cols):
                     pairs.append(((4 * a + k) * cols + b, (4 * b + (k ^ t ^ (a + b) % 4)) * cols + a))
         received.append(lax.ppermute(messages[t], BOTH, pairs))
-    mean = call(
+    strip = jax.ShapeDtypeStruct((4, 64, 128), BF)
+    mean, to_left, to_right = call(
         average,
-        tile,
+        (tile, strip, strip),
         (place, second, *received),
         1,
         [pltpu.VMEM((4, 512, 128), BF)],
         0,
         2 << 20,
     )
+    from_left = lax.ppermute(to_right, "col", right_way)
+    from_right = lax.ppermute(to_left, "col", left_way)
+    wide = [pltpu.VMEM((48, 64, 256), BF)]
+    edge = jax.ShapeDtypeStruct((8, 32, 128), BF)
+    to_up, to_down = call(
+        last_edges,
+        (edge, edge),
+        (dilations, mean, from_left, from_right, kernel),
+        1,
+        wide,
+        16 * 256 * 64 * 96 * 2,
+        1 << 20,
+    )
+    above = lax.ppermute(to_down, "row", down_way)
+    below = lax.ppermute(to_up, "row", up_way)
+    inner, conv = call(
+        last_inner,
+        (tile, jax.ShapeDtypeStruct((16, 32, 128), F32)),
+        (dilations, mean, from_left, from_right, *weights),
+        1,
+        wide,
+        32 * 256 * 64 * 32 * 20,
+        2 << 20,
+    )
     out = call(
-        last_block,
+        last_outer,
         tile,
-        (dilations, *rims(mean, 8), *weights),
-        1,
-        [pltpu.VMEM((48, 64, 256), BF)],
-        32 * 256 * 64 * 32 * 20,
+        (inner, mean, conv, above, below, gain, shift, out_weight),
+        0,
+        [],
+        16 * 256 * 64 * 32 * 2,
         2 << 20,
     )
     return jnp.transpose(out, (1, 0, 2))

time: 118 us -> 110 us (0.932)
  waiting for transfers between devices: 54.6 us -> 42.2 us
  starting transfers between devices: 50.5 us -> 53.5 us
  Pallas kernels: 8.48 us -> 9.69 us
    ppermute x8, waiting for transfers between devices: 42.1 us -> 29.9 us  [the longest x1 18.3 us: on_device(): above = lax.ppermute(own[16:], 'row', down_way)]
    ppermute x8, starting transfers between devices: 31.3 us -> 34.3 us  [the longest x1 11.2 us: on_device(): below = lax.ppermute(own[:16], 'row', up_way)]
    pallas_call x5 -> x6, Pallas kernels: 8.48 us -> 9.69 us  [call(): pl.pallas_call(body, out_shape=outs, in_specs=[SMEM] * n_smem + [VMEM] *...]
  transfers between devices with their start and end apart: 12 -> 12, of which waited for: 7 -> 5; matrix products, arithmetic and copies ran while one was open for 0% -> 0% of each run, Pallas kernels for 0% -> 2%
where the time goes in v5:
time: 110 us; the launch traced here: 109 us
  starting transfers between devices  53.5 us (49%)
  waiting for transfers between devices  42.2 us (38%)
  Pallas kernels  9.69 us (9%)
  local copies, waits for them, and re-layouts  3.66 us (3%)
    ppermute x4, starting transfers between devices, on_device(): received.append(lax.ppermute(messages[t], BOTH, pairs))  19.2 us
    ppermute x1, waiting for transfers between devices, on_device(): above = lax.ppermute(own[16:], 'row', down_way)  18.3 us
    ppermute x4, waiting for transfers between devices, on_device(): received.append(lax.ppermute(messages[t], BOTH, pairs))  12.2 us
    ppermute x1, starting transfers between devices, on_device(): below = lax.ppermute(own[:16], 'row', up_way)  11.2 us
    pallas_call x6, Pallas kernels, call(): pl.pallas_call(body, out_shape=outs, in_specs=[SMEM] * n_smem + [VMEM] *...  9.69 us
    ppermute x1, starting transfers between devices, on_device(): below = lax.ppermute(to_up, 'row', up_way)  8.62 us
    ppermute x2, waiting for transfers between devices, on_device(): from_right = lax.ppermute(to_left, 'col', left_way)  6.09 us
    ppermute x1, waiting for transfers between devices, on_device(): below = lax.ppermute(own[:16], 'row', up_way)  5.58 us
  transfers between devices with their start and end apart: 12, of which 5 were waited for; matrix products, arithmetic and copies ran while one was open for 0% of the time, Pallas kernels for 2%

profile of v5, /device:TPU:25, one launch (start us, length us, event | category | flops | bytes accessed | tf_op | source)
XLA Modules:
  0.0 109.3 jit_solution(9088206169948067211)
XLA Ops:
  0.0 1.2 %copy.21 = bf16[64,32,128]{2,0,1:T(8,128)(2,1)S(1)} copy(bf16[64,32,128]{2,1,0:T(8,128)(2,1)} %param.6) | data formatting | bytes 1048576 | tf_op args[0]
  1.3 11.2 %collective-permute-start.1 = (bf16[16,64,128]{2,1,0:T(8,128)(2,1)S(1)}, bf16[16,64,128]{2,1,0:T(8,128)(2,1)S(1)}, u32[]{:S(2)}, u32[]{:S(2)}) collective-permute-start(bf16[16,64,128]{2,1,0:T(8,128)(2,1)S(1)} %get-tuple-element.31), channel_id=1, source_target_pairs={{8,0},{16,8},{24,16},{32,24},{40,32},{48,40},{56,48},{64,56},{72,6... | collective-permute-start | bytes 786440 | tf_op jit(solution)/shard_map/ppermute | solution.py:243
  12.5 1.9 %collective-permute-start = (bf16[16,64,128]{2,1,0:T(8,128)(2,1)S(1)}, bf16[16,64,128]{2,1,0:T(8,128)(2,1)S(1)}, u32[]{:S(2)}, u32[]{:S(2)}) collective-permute-start(bf16[16,64,128]{2,1,0:T(8,128)(2,1)S(1)} %get-tuple-element.32), channel_id=1, source_target_pairs={{0,8},{8,16},{16,24},{24,32},{32,40},{40,48},{48,56},{56,64},{64,7... | collective-permute-start | bytes 786440 | tf_op jit(solution)/shard_map/ppermute | solution.py:242
  14.4 5.6 %collective-permute-done.1.down_ref = bf16[16,64,128]{2,1,0:T(8,128)(2,1)S(1)} collective-permute-done((bf16[16,64,128]{2,1,0:T(8,128)(2,1)S(1)}, bf16[16,64,128]{2,1,0:T(8,128)(2,1)S(1)}, u32[]{:S(2)}, u32[]{:S(2)}) %collective-permute-start.1) | collective-permute-done | bytes 262176 | tf_op jit(solution)/shard_map/ppermute | solution.py:243
  20.0 18.3 %collective-permute-done.up_ref = bf16[16,64,128]{2,1,0:T(8,128)(2,1)S(1)} collective-permute-done((bf16[16,64,128]{2,1,0:T(8,128)(2,1)S(1)}, bf16[16,64,128]{2,1,0:T(8,128)(2,1)S(1)}, u32[]{:S(2)}, u32[]{:S(2)}) %collective-permute-start) | collective-permute-done | bytes 262176 | tf_op jit(solution)/shard_map/ppermute | solution.py:242
  38.3 0.5 shard_map.64
  38.8 1.9 %collective-permute-start.2 = (bf16[8,64,128]{2,1,0:T(8,128)(2,1)S(1)}, bf16[8,64,128]{2,1,0:T(8,128)(2,1)S(1)}, u32[]{:S(2)}, u32[]{:S(2)}) collective-permute-start(bf16[8,64,128]{2,1,0:T(8,128)(2,1)S(1)} %get-tuple-element.16), channel_id=1, source_target_pairs={{0,1},{1,2},{2,3},{3,4},{4,5},{5,6},{6,7},{8,9},{9,10},{10,11},{11... | collective-permute-start | bytes 393224 | tf_op jit(solution)/shard_map/ppermute | solution.py:248
  40.8 2.8 %collective-permute-start.3 = (bf16[8,64,128]{2,1,0:T(8,128)(2,1)S(1)}, bf16[8,64,128]{2,1,0:T(8,128)(2,1)S(1)}, u32[]{:S(2)}, u32[]{:S(2)}) collective-permute-start(bf16[8,64,128]{2,1,0:T(8,128)(2,1)S(1)} %get-tuple-element.17), channel_id=1, source_target_pairs={{1,0},{2,1},{3,2},{4,3},{5,4},{6,5},{7,6},{9,8},{10,9},{11,10},{12... | collective-permute-start | bytes 393224 | tf_op jit(solution)/shard_map/ppermute | solution.py:249
  44.1 2.9 %collective-permute-done.3.from_right = bf16[8,64,128]{2,1,0:T(8,128)(2,1)S(1)} collective-permute-done((bf16[8,64,128]{2,1,0:T(8,128)(2,1)S(1)}, bf16[8,64,128]{2,1,0:T(8,128)(2,1)S(1)}, u32[]{:S(2)}, u32[]{:S(2)}) %collective-permute-start.3) | collective-permute-done | bytes 131104 | tf_op jit(solution)/shard_map/ppermute | solution.py:249
  47.2 0.6 copy-done
  47.8 4.1 %shard_map.65 = (bf16[32,64,128]{2,1,0:T(8,128)(2,1)S(1)}, bf16[4,512,128]{2,1,0:T(8,128)(2,1)S(1)}) custom-call(s32[3]{0:T(128)S(1)} %copy-done, s32[3]{0:T(128)S(1)} %pad_add_fusion.place_ref, bf16[16,64,128]{2,1,0:T(8,128)(2,1)S(1)} %collective-permute-done.up_ref, bf16[32,64,128]{2,1,0:T(8,128)(2,1)S(1)} %bitcast.21, ...), custom_call_target="tpu_custom_call" | custom-call | flops 838860800 | bytes 4194304 | tf_op jit(solution)/shard_map/pallas_call | solution.py:20
  52.1 11.3 %collective-permute-start.6 = (bf16[512,128]{1,0:T(8,128)(2,1)S(1)}, bf16[512,128]{1,0:T(8,128)(2,1)S(1)}, u32[]{:S(2)}, u32[]{:S(2)}) collective-permute-start(bf16[512,128]{1,0:T(8,128)(2,1)S(1)} %get-tuple-element.28), channel_id=1, source_target_pairs={{0,16},{1,56},{2,64},{3,104},{4,144},{5,184},{6,192},{7,232},{8,24... | collective-permute-start | bytes 393224 | tf_op jit(solution)/shard_map/ppermute | solution.py:276
  63.5 7.7 %collective-permute-start.4 = (bf16[512,128]{1,0:T(8,128)(2,1)S(1)}, bf16[512,128]{1,0:T(8,128)(2,1)S(1)}, u32[]{:S(2)}, u32[]{:S(2)}) collective-permute-start(bf16[512,128]{1,0:T(8,128)(2,1)S(1)} %get-tuple-element.30), channel_id=1, source_target_pairs={{0,0},{1,40},{2,80},{3,120},{4,128},{5,168},{6,208},{7,248},{8,8},... | collective-permute-start | bytes 393224 | tf_op jit(solution)/shard_map/ppermute | solution.py:276
  71.2 12.2 %collective-permute-done.6.m2 = bf16[512,128]{1,0:T(8,128)(2,1)S(1)} collective-permute-done((bf16[512,128]{1,0:T(8,128)(2,1)S(1)}, bf16[512,128]{1,0:T(8,128)(2,1)S(1)}, u32[]{:S(2)}, u32[]{:S(2)}) %collective-permute-start.6) | collective-permute-done | bytes 131104 | tf_op jit(solution)/shard_map/ppermute | solution.py:276
  83.4 1.7 %shard_map.66 = (bf16[32,64,128]{2,1,0:T(8,128)(2,1)S(1)}, bf16[4,64,128]{2,1,0:T(8,128)(2,1)S(1)}, bf16[4,64,128]{2,1,0:T(8,128)(2,1)S(1)}) custom-call(s32[3]{0:T(128)S(1)} %pad_add_fusion.place_ref, bf16[32,64,128]{2,1,0:T(8,128)(2,1)S(1)} %get-tuple-element.18.second_ref, bf16[512,128]{1,0:T(8,128)(2,1)S(1)} %collective-permute-done.4.m0, ...), custom_call_target="tpu_custom_call" | custom-call | bytes 2097152 | tf_op jit(solution)/shard_map/pallas_call | solution.py:20
  85.1 1.9 %collective-permute-start.8 = (bf16[4,64,128]{2,1,0:T(8,128)(2,1)S(1)}, bf16[4,64,128]{2,1,0:T(8,128)(2,1)S(1)}, u32[]{:S(2)}, u32[]{:S(2)}) collective-permute-start(bf16[4,64,128]{2,1,0:T(8,128)(2,1)S(1)} %get-tuple-element.21), channel_id=1, source_target_pairs={{0,1},{1,2},{2,3},{3,4},{4,5},{5,6},{6,7},{8,9},{9,10},{10,11},{11... | collective-permute-start | bytes 196616 | tf_op jit(solution)/shard_map/ppermute | solution.py:287
  87.0 2.4 %collective-permute-start.9 = (bf16[4,64,128]{2,1,0:T(8,128)(2,1)S(1)}, bf16[4,64,128]{2,1,0:T(8,128)(2,1)S(1)}, u32[]{:S(2)}, u32[]{:S(2)}) collective-permute-start(bf16[4,64,128]{2,1,0:T(8,128)(2,1)S(1)} %get-tuple-element.22), channel_id=1, source_target_pairs={{1,0},{2,1},{3,2},{4,3},{5,4},{6,5},{7,6},{9,8},{10,9},{11,10},{12... | collective-permute-start | bytes 196616 | tf_op jit(solution)/shard_map/ppermute | solution.py:288
  89.5 3.2 %collective-permute-done.9.from_right = bf16[4,64,128]{2,1,0:T(8,128)(2,1)S(1)} collective-permute-done((bf16[4,64,128]{2,1,0:T(8,128)(2,1)S(1)}, bf16[4,64,128]{2,1,0:T(8,128)(2,1)S(1)}, u32[]{:S(2)}, u32[]{:S(2)}) %collective-permute-start.9) | collective-permute-done | bytes 65568 | tf_op jit(solution)/shard_map/ppermute | solution.py:288
  92.6 1.4 %shard_map.68 = (bf16[8,32,128]{2,1,0:T(8,128)(2,1)S(1)}, bf16[8,32,128]{2,1,0:T(8,128)(2,1)S(1)}) custom-call(s32[3]{0:T(128)S(1)} %copy-done, bf16[32,64,128]{2,1,0:T(8,128)(2,1)S(1)} %get-tuple-element.20.mean_ref, bf16[4,64,128]{2,1,0:T(8,128)(2,1)S(1)} %collective-permute-done.8.from_left, bf16[4,64,128]{2,1,0:T(8,128)(2,1)S(1)} %collective-permute-done.9.from_right, ...), custom_call_target="tpu_custom_call" | custom-call | flops 50331648 | bytes 1048576 | tf_op jit(solution)/shard_map/pallas_call | solution.py:20
  94.0 3.6 %collective-permute-start.10 = (bf16[8,32,128]{2,1,0:T(8,128)(2,1)S(1)}, bf16[8,32,128]{2,1,0:T(8,128)(2,1)S(1)}, u32[]{:S(2)}, u32[]{:S(2)}) collective-permute-start(bf16[8,32,128]{2,1,0:T(8,128)(2,1)S(1)} %get-tuple-element.25), channel_id=1, source_target_pairs={{0,8},{8,16},{16,24},{24,32},{32,40},{40,48},{48,56},{56,64},{64,7... | collective-permute-start | bytes 196616 | tf_op jit(solution)/shard_map/ppermute | solution.py:300
  97.6 8.6 %collective-permute-start.11 = (bf16[8,32,128]{2,1,0:T(8,128)(2,1)S(1)}, bf16[8,32,128]{2,1,0:T(8,128)(2,1)S(1)}, u32[]{:S(2)}, u32[]{:S(2)}) collective-permute-start(bf16[8,32,128]{2,1,0:T(8,128)(2,1)S(1)} %get-tuple-element.26), channel_id=1, source_target_pairs={{8,0},{16,8},{24,16},{32,24},{40,32},{48,40},{56,48},{64,56},{72,6... | collective-permute-start | bytes 196616 | tf_op jit(solution)/shard_map/ppermute | solution.py:301
  106.2 1.7 %shard_map.67 = (bf16[32,64,128]{2,1,0:T(8,128)(2,1)S(1)}, f32[16,32,128]{2,1,0:T(8,128)S(1)}) custom-call(s32[3]{0:T(128)S(1)} %copy-done, bf16[32,64,128]{2,1,0:T(8,128)(2,1)S(1)} %get-tuple-element.20.mean_ref, bf16[4,64,128]{2,1,0:T(8,128)(2,1)S(1)} %collective-permute-done.8.from_left, bf16[4,64,128]{2,1,0:T(8,128)(2,1)S(1)} %collective-permute-done.9.from_right, ...), custom_call_target="tpu_custom_call" | custom-call | flops 335544320 | bytes 2097152 | tf_op jit(solution)/shard_map/pallas_call | solution.py:20
  108.0 0.2 shard_map.69
  108.2 1.1 %copy.18 = bf16[64,32,128]{2,1,0:T(8,128)(2,1)} copy(bf16[64,32,128]{2,0,1:T(8,128)(2,1)S(1)} %bitcast.22) | data formatting | bytes 1048576 | tf_op jit(solution)/shard_map/transpose | solution.py:320
  (26 shorter events, 1.0 us)
Async XLA Ops:
  1.3 18.7 %collective-permute-start.1 = (bf16[16,64,128]{2,1,0:T(8,128)(2,1)S(1)}, bf16[16,64,128]{2,1,0:T(8,128)(2,1)S(1)}, u32[]{:S(2)}, u32[]{:S(2)}) collective-permute-start(bf16[16,64,128]{2,1,0:T(8,128)(2,1)S(1)} %get-tuple-element.31), channel_id=1, source_target_pairs={{8,0},{16,8},{24,16},{32,24},{40,32},{48,40},{56,48},{64,56},{72,6... | collective-permute-start | bytes 786440 | tf_op jit(solution)/shard_map/ppermute | solution.py:243
  12.5 25.8 %collective-permute-start = (bf16[16,64,128]{2,1,0:T(8,128)(2,1)S(1)}, bf16[16,64,128]{2,1,0:T(8,128)(2,1)S(1)}, u32[]{:S(2)}, u32[]{:S(2)}) collective-permute-start(bf16[16,64,128]{2,1,0:T(8,128)(2,1)S(1)} %get-tuple-element.32), channel_id=1, source_target_pairs={{0,8},{8,16},{16,24},{24,32},{32,40},{40,48},{48,56},{56,64},{64,7... | collective-permute-start | bytes 786440 | tf_op jit(solution)/shard_map/ppermute | solution.py:242
  38.3 5.4 %copy-start.1 = (bf16[3,9,32,64]{3,2,1,0:T(8,128)(2,1)S(1)}, bf16[3,9,32,64]{3,2,1,0:T(8,128)(2,1)}, u32[]{:S(2)}) copy-start(bf16[3,9,32,64]{3,2,1,0:T(8,128)(2,1)} %param.8) | copy-start | bytes 331780
  38.8 4.7 %copy-start.2 = (bf16[3,64,32]{1,2,0:T(8,128)(2,1)S(1)}, bf16[3,64,32]{1,2,0:T(8,128)(2,1)}, u32[]{:S(2)}) copy-start(bf16[3,64,32]{1,2,0:T(8,128)(2,1)} %param.11) | copy-start | bytes 36868
  38.8 5.3 %collective-permute-start.2 = (bf16[8,64,128]{2,1,0:T(8,128)(2,1)S(1)}, bf16[8,64,128]{2,1,0:T(8,128)(2,1)S(1)}, u32[]{:S(2)}, u32[]{:S(2)}) collective-permute-start(bf16[8,64,128]{2,1,0:T(8,128)(2,1)S(1)} %get-tuple-element.16), channel_id=1, source_target_pairs={{0,1},{1,2},{2,3},{3,4},{4,5},{5,6},{6,7},{8,9},{9,10},{10,11},{11... | collective-permute-start | bytes 393224 | tf_op jit(solution)/shard_map/ppermute | solution.py:248
  40.8 6.3 %collective-permute-start.3 = (bf16[8,64,128]{2,1,0:T(8,128)(2,1)S(1)}, bf16[8,64,128]{2,1,0:T(8,128)(2,1)S(1)}, u32[]{:S(2)}, u32[]{:S(2)}) collective-permute-start(bf16[8,64,128]{2,1,0:T(8,128)(2,1)S(1)} %get-tuple-element.17), channel_id=1, source_target_pairs={{1,0},{2,1},{3,2},{4,3},{5,4},{6,5},{7,6},{9,8},{10,9},{11,10},{12... | collective-permute-start | bytes 393224 | tf_op jit(solution)/shard_map/ppermute | solution.py:249
  44.0 3.0 %copy-start.3 = (f32[3,32]{1,0:T(4,128)S(1)}, f32[3,32]{1,0:T(4,128)}, u32[]{:S(2)}) copy-start(f32[3,32]{1,0:T(4,128)} %param.9) | copy-start | bytes 1156
  44.1 3.0 %copy-start.4 = (f32[3,32]{1,0:T(4,128)S(1)}, f32[3,32]{1,0:T(4,128)}, u32[]{:S(2)}) copy-start(f32[3,32]{1,0:T(4,128)} %param.10) | copy-start | bytes 1156
  47.1 0.7 copy-start
  52.0 19.2 %collective-permute-start.7 = (bf16[512,128]{1,0:T(8,128)(2,1)S(1)}, bf16[512,128]{1,0:T(8,128)(2,1)S(1)}, u32[]{:S(2)}, u32[]{:S(2)}) collective-permute-start(bf16[512,128]{1,0:T(8,128)(2,1)S(1)} %get-tuple-element.27), channel_id=1, source_target_pairs={{0,24},{1,48},{2,72},{3,96},{4,152},{5,176},{6,200},{7,224},{8,16}... | collective-permute-start | bytes 393224 | tf_op jit(solution)/shard_map/ppermute | solution.py:276
  52.1 31.3 %collective-permute-start.6 = (bf16[512,128]{1,0:T(8,128)(2,1)S(1)}, bf16[512,128]{1,0:T(8,128)(2,1)S(1)}, u32[]{:S(2)}, u32[]{:S(2)}) collective-permute-start(bf16[512,128]{1,0:T(8,128)(2,1)S(1)} %get-tuple-element.28), channel_id=1, source_target_pairs={{0,16},{1,56},{2,64},{3,104},{4,144},{5,184},{6,192},{7,232},{8,24... | collective-permute-start | bytes 393224 | tf_op jit(solution)/shard_map/ppermute | solution.py:276
  63.4 20.1 %collective-permute-start.5 = (bf16[512,128]{1,0:T(8,128)(2,1)S(1)}, bf16[512,128]{1,0:T(8,128)(2,1)S(1)}, u32[]{:S(2)}, u32[]{:S(2)}) collective-permute-start(bf16[512,128]{1,0:T(8,128)(2,1)S(1)} %get-tuple-element.29), channel_id=1, source_target_pairs={{0,8},{1,32},{2,88},{3,112},{4,136},{5,160},{6,216},{7,240},{8,0},... | collective-permute-start | bytes 393224 | tf_op jit(solution)/shard_map/ppermute | solution.py:276
  63.5 20.0 %collective-permute-start.4 = (bf16[512,128]{1,0:T(8,128)(2,1)S(1)}, bf16[512,128]{1,0:T(8,128)(2,1)S(1)}, u32[]{:S(2)}, u32[]{:S(2)}) collective-permute-start(bf16[512,128]{1,0:T(8,128)(2,1)S(1)} %get-tuple-element.30), channel_id=1, source_target_pairs={{0,0},{1,40},{2,80},{3,120},{4,128},{5,168},{6,208},{7,248},{8,8},... | collective-permute-start | bytes 393224 | tf_op jit(solution)/shard_map/ppermute | solution.py:276
  85.1 4.3 %collective-permute-start.8 = (bf16[4,64,128]{2,1,0:T(8,128)(2,1)S(1)}, bf16[4,64,128]{2,1,0:T(8,128)(2,1)S(1)}, u32[]{:S(2)}, u32[]{:S(2)}) collective-permute-start(bf16[4,64,128]{2,1,0:T(8,128)(2,1)S(1)} %get-tuple-element.21), channel_id=1, source_target_pairs={{0,1},{1,2},{2,3},{3,4},{4,5},{5,6},{6,7},{8,9},{9,10},{10,11},{11... | collective-permute-start | bytes 196616 | tf_op jit(solution)/shard_map/ppermute | solution.py:287
  87.0 5.6 %collective-permute-start.9 = (bf16[4,64,128]{2,1,0:T(8,128)(2,1)S(1)}, bf16[4,64,128]{2,1,0:T(8,128)(2,1)S(1)}, u32[]{:S(2)}, u32[]{:S(2)}) collective-permute-start(bf16[4,64,128]{2,1,0:T(8,128)(2,1)S(1)} %get-tuple-element.22), channel_id=1, source_target_pairs={{1,0},{2,1},{3,2},{4,3},{5,4},{6,5},{7,6},{9,8},{10,9},{11,10},{12... | collective-permute-start | bytes 196616 | tf_op jit(solution)/shard_map/ppermute | solution.py:288
  94.0 13.9 %collective-permute-start.10 = (bf16[8,32,128]{2,1,0:T(8,128)(2,1)S(1)}, bf16[8,32,128]{2,1,0:T(8,128)(2,1)S(1)}, u32[]{:S(2)}, u32[]{:S(2)}) collective-permute-start(bf16[8,32,128]{2,1,0:T(8,128)(2,1)S(1)} %get-tuple-element.25), channel_id=1, source_target_pairs={{0,8},{8,16},{16,24},{24,32},{32,40},{40,48},{48,56},{56,64},{64,7... | collective-permute-start | bytes 196616 | tf_op jit(solution)/shard_map/ppermute | solution.py:300
  97.6 10.3 %collective-permute-start.11 = (bf16[8,32,128]{2,1,0:T(8,128)(2,1)S(1)}, bf16[8,32,128]{2,1,0:T(8,128)(2,1)S(1)}, u32[]{:S(2)}, u32[]{:S(2)}) collective-permute-start(bf16[8,32,128]{2,1,0:T(8,128)(2,1)S(1)} %get-tuple-element.26), channel_id=1, source_target_pairs={{8,0},{16,8},{24,16},{32,24},{40,32},{48,40},{56,48},{64,56},{72,6... | collective-permute-start | bytes 196616 | tf_op jit(solution)/shard_map/ppermute | solution.py:301

commit v6 on v5

--- a/solution.py
+++ b/solution.py
@@ -105,40 +105,43 @@
     )
 
 
-def pack_rows(refs, left_ref, right_ref):
+def pack_rows(refs, place_ref, sides_ref):
+    odd = lax.rem(place_ref[1], 2)
     first = 0
     for ref in refs:
         for g in range(ref.shape[0] // 8):
             pieces = [ref[8 * g + q] for q in range(8)]
-            left_ref[first + g] = pack_strips(pieces, 0, 16)
-            right_ref[first + g] = pack_strips(pieces, 112, 16)
+            sides_ref[1 - odd, first + g] = pack_strips(pieces, 0, 16)
+            sides_ref[odd, first + g] = pack_strips(pieces, 112, 16)
         first += ref.shape[0] // 8
 
 
-def pack_sides(up_ref, own_ref, down_ref, left_ref, right_ref):
-    pack_rows((up_ref, own_ref, down_ref), left_ref, right_ref)
-
-
-def fill_wide(wide, refs, from_left, from_right, first=0):
+def pack_sides(place_ref, up_ref, own_ref, down_ref, sides_ref):
+    pack_rows((up_ref, own_ref, down_ref), place_ref, sides_ref)
+
+
+def fill_wide(wide, refs, place_ref, near_ref, far_ref, first=0):
+    odd = lax.rem(place_ref[1], 2) == 1
     at = 0
     for ref in refs:
         for r in range(ref.shape[0]):
+            if at % 8 == 0:
+                near, far = near_ref[at // 8], far_ref[at // 8]
+                from_left, from_right = jnp.where(odd, near, far), jnp.where(odd, far, near)
             wide[first + at, :, :128] = ref[r]
-            wide[first + at, :, 128:] = side_lanes(
-                from_right[at // 8], from_left[at // 8], at % 8, 16
-            )
+            wide[first + at, :, 128:] = side_lanes(from_right, from_left, at % 8, 16)
             at += 1
 
 
 def first_blocks(
-    spacing_ref, place_ref, up_ref, own_ref, down_ref, from_left, from_right,
+    spacing_ref, place_ref, up_ref, own_ref, down_ref, near_ref, far_ref,
     kernel_ref, gain_ref, shift_ref, expand_ref,
     second_ref, message_ref, wide, middle, turned,
 ):
     row, col = place_ref[0], place_ref[1]
     members = place_ref[2]
     weights = (spacing_ref, kernel_ref, gain_ref, shift_ref, expand_ref)
-    fill_wide(wide, (up_ref, own_ref, down_ref), from_left, from_right)
+    fill_wide(wide, (up_ref, own_ref, down_ref), place_ref, near_ref, far_ref)
     lane = lax.broadcasted_iota(jnp.int32, (64, 256), 1)
     inside = (lane < 128) | ((lane < 192) & (col < 7)) | ((lane >= 192) & (col > 0))
 
@@ -163,7 +166,7 @@
         message_ref[lax.bitwise_xor(members, m)] = turned[512 * m : 512 * m + 512].astype(BF)
 
 
-def average(place_ref, second_ref, m0, m1, m2, m3, mean_ref, left_ref, right_ref, gathered):
+def average(place_ref, second_ref, m0, m1, m2, m3, mean_ref, sides_ref, gathered):
     members = place_ref[2]
     for t, ref in enumerate((m0, m1, m2, m3)):
         gathered[lax.bitwise_xor(members, t)] = ref[...]
@@ -174,21 +177,21 @@
             blocks += [part, pltpu.roll(part, 64, 1)]
         mirrored = jnp.transpose(jnp.concatenate(blocks, axis=0))[:64]
         mean_ref[j] = (0.5 * (second_ref[j].astype(F32) + mirrored)).astype(BF)
-    pack_rows((mean_ref,), left_ref, right_ref)
-
-
-def fill_last(wide, mean_ref, from_left, from_right):
+    pack_rows((mean_ref,), place_ref, sides_ref)
+
+
+def fill_last(wide, place_ref, mean_ref, near_ref, far_ref):
     for at in range(8):
         wide[at] = jnp.zeros((64, 256), BF)
         wide[40 + at] = jnp.zeros((64, 256), BF)
-    fill_wide(wide, (mean_ref,), from_left, from_right, 8)
+    fill_wide(wide, (mean_ref,), place_ref, near_ref, far_ref, 8)
 
 
 def last_edges(
-    spacing_ref, mean_ref, from_left, from_right, kernel_ref, to_up_ref, to_down_ref, wide
+    spacing_ref, place_ref, mean_ref, near_ref, far_ref, kernel_ref, to_up_ref, to_down_ref, wide
 ):
     spacing, kernel = spacing_ref[2], kernel_ref[2]
-    fill_last(wide, mean_ref, from_left, from_right)
+    fill_last(wide, place_ref, mean_ref, near_ref, far_ref)
     taps = []
     for i in range(8):
         up = jnp.maximum(wide[i + spacing], 0)
@@ -202,10 +205,10 @@
 
 
 def last_inner(
-    spacing_ref, mean_ref, from_left, from_right, kernel_ref, gain_ref, shift_ref, expand_ref,
+    spacing_ref, place_ref, mean_ref, near_ref, far_ref, kernel_ref, gain_ref, shift_ref, expand_ref,
     out_ref, conv_ref, wide,
 ):
-    fill_last(wide, mean_ref, from_left, from_right)
+    fill_last(wide, place_ref, mean_ref, near_ref, far_ref)
     sums = conv_rows(wide, [r + 8 for r in range(32)], spacing_ref[2], kernel_ref[2], True)
     sums = [row[0] for row in sums]
     for i in range(8):
@@ -235,18 +238,24 @@
     place = jnp.stack([row, col, mixed]).astype(jnp.int32)
     down_way = [(r, r + 1) for r in range(rows - 1)]
     up_way = [(r + 1, r) for r in range(rows - 1)]
-    right_way = [(c, c + 1) for c in range(cols - 1)]
-    left_way = [(c + 1, c) for c in range(cols - 1)]
+    near_pairs = [(c, c ^ 1) for c in range(cols)]
+    far_pairs = [(c, c + 1) for c in range(1, cols - 1, 2)]
+    far_pairs += [(d, c) for c, d in far_pairs]
 
     own = jnp.transpose(contact_map, (1, 0, 2))
     above = lax.ppermute(own[16:], "row", down_way)
     below = lax.ppermute(own[:16], "row", up_way)
-    strip = jax.ShapeDtypeStruct((8, 64, 128), BF)
-    to_left, to_right = call(
-        pack_sides, (strip, strip), (above, own, below), 0, [], 0, 1 << 20
-    )
-    from_left = lax.ppermute(to_right, "col", right_way)
-    from_right = lax.ppermute(to_left, "col", left_way)
+    sides = call(
+        pack_sides,
+        jax.ShapeDtypeStruct((2, 8, 64, 128), BF),
+        (place, above, own, below),
+        1,
+        [],
+        0,
+        1 << 20,
+    )
+    far = lax.ppermute(sides[1], "col", far_pairs)
+    near = lax.ppermute(sides[0], "col", near_pairs)
     kernel = jnp.transpose(conv_weight.reshape(3, 3, 3, 32, 64), (0, 2, 3, 1, 4)).reshape(3, 96, 192)
     gain = jnp.broadcast_to(conv_gain[:, :, None], (3, 32, 128))
     shift = jnp.broadcast_to(conv_shift[:, :, None], (3, 32, 128))
@@ -256,7 +265,7 @@
     second, messages = call(
         first_blocks,
         (tile, jax.ShapeDtypeStruct((4, 512, 128), BF)),
-        (dilations, place, above, own, below, from_left, from_right, *weights),
+        (dilations, place, above, own, below, near, far, *weights),
         2,
         [
             pltpu.VMEM((64, 64, 256), BF),
@@ -274,25 +283,24 @@
                 for b in range(cols):
                     pairs.append(((4 * a + k) * cols + b, (4 * b + (k ^ t ^ (a + b) % 4)) * cols + a))
         received.append(lax.ppermute(messages[t], BOTH, pairs))
-    strip = jax.ShapeDtypeStruct((4, 64, 128), BF)
-    mean, to_left, to_right = call(
+    mean, sides = call(
         average,
-        (tile, strip, strip),
+        (tile, jax.ShapeDtypeStruct((2, 4, 64, 128), BF)),
         (place, second, *received),
         1,
         [pltpu.VMEM((4, 512, 128), BF)],
         0,
         2 << 20,
     )
-    from_left = lax.ppermute(to_right, "col", right_way)
-    from_right = lax.ppermute(to_left, "col", left_way)
+    far = lax.ppermute(sides[1], "col", far_pairs)
+    near = lax.ppermute(sides[0], "col", near_pairs)
     wide = [pltpu.VMEM((48, 64, 256), BF)]
     edge = jax.ShapeDtypeStruct((8, 32, 128), BF)
     to_up, to_down = call(
         last_edges,
         (edge, edge),
-        (dilations, mean, from_left, from_right, kernel),
-        1,
+        (dilations, place, mean, near, far, kernel),
+        2,
         wide,
         16 * 256 * 64 * 96 * 2,
         1 << 20,
@@ -302,8 +310,8 @@
     inner, conv = call(
         last_inner,
         (tile, jax.ShapeDtypeStruct((16, 32, 128), F32)),
-        (dilations, mean, from_left, from_right, *weights),
-        1,
+        (dilations, place, mean, near, far, *weights),
+        2,
         wide,
         32 * 256 * 64 * 32 * 20,
         2 << 20,

time: 110 us -> 106 us (0.964)
  starting transfers between devices: 53.5 us -> 48.9 us
    ppermute x4, starting transfers between devices: 9 us -> 4.37 us  [the longest x2 3.97 us: on_device(): far = lax.ppermute(sides[1], 'col', far_pairs)]
    ppermute x4, waiting for transfers between devices: 12.2 us -> 10.8 us  [on_device(): received.append(lax.ppermute(messages[t], BOTH, pairs))]
    ppermute x1, starting transfers between devices: 3.58 us -> 4.74 us  [on_device(): above = lax.ppermute(to_down, 'row', down_way)]
    ppermute x1, starting transfers between devices: 8.62 us -> 7.45 us  [on_device(): below = lax.ppermute(to_up, 'row', up_way)]
    ppermute x1, waiting for transfers between devices: 0.01 us -> 1.16 us  [on_device(): below = lax.ppermute(to_up, 'row', up_way)]
  transfers between devices with their start and end apart: 12 -> 12, of which waited for: 5 -> 6; matrix products, arithmetic and copies ran while one was open for 0% -> 1% of each run, Pallas kernels for 2% -> 2%
where the time goes in v6:
time: 106 us
  starting transfers between devices  48.9 us (46%)
  waiting for transfers between devices  42.8 us (40%)
  Pallas kernels  10.3 us (10%)
  local copies, waits for them, and re-layouts  3.7 us (3%)
    ppermute x4, starting transfers between devices, on_device(): received.append(lax.ppermute(messages[t], BOTH, pairs))  19.2 us
    ppermute x1, waiting for transfers between devices, on_device(): above = lax.ppermute(own[16:], 'row', down_way)  18.3 us
    ppermute x1, starting transfers between devices, on_device(): below = lax.ppermute(own[:16], 'row', up_way)  11.2 us
    ppermute x4, waiting for transfers between devices, on_device(): received.append(lax.ppermute(messages[t], BOTH, pairs))  10.8 us
    pallas_call x6, Pallas kernels, call(): pl.pallas_call(body, out_shape=outs, in_specs=[SMEM] * n_smem + [VMEM] *...  10.3 us
    ppermute x1, starting transfers between devices, on_device(): below = lax.ppermute(to_up, 'row', up_way)  7.45 us
    ppermute x2, waiting for transfers between devices, on_device(): far = lax.ppermute(sides[1], 'col', far_pairs)  7.11 us
    ppermute x1, waiting for transfers between devices, on_device(): below = lax.ppermute(own[:16], 'row', up_way)  5.49 us
  transfers between devices with their start and end apart: 12, of which 6 were waited for; matrix products, arithmetic and copies ran while one was open for 1% of the time, Pallas kernels for 2%

profile of v6, /device:TPU:25, one launch (start us, length us, event | category | flops | bytes accessed | tf_op | source)
XLA Modules:
  0.0 106.0 jit_solution(173314757598023194)
XLA Ops:
  0.0 1.2 %copy.21 = bf16[64,32,128]{2,0,1:T(8,128)(2,1)S(1)} copy(bf16[64,32,128]{2,1,0:T(8,128)(2,1)} %param.6) | data formatting | bytes 1048576 | tf_op args[0]
  1.3 11.2 %collective-permute-start.1 = (bf16[16,64,128]{2,1,0:T(8,128)(2,1)S(1)}, bf16[16,64,128]{2,1,0:T(8,128)(2,1)S(1)}, u32[]{:S(2)}, u32[]{:S(2)}) collective-permute-start(bf16[16,64,128]{2,1,0:T(8,128)(2,1)S(1)} %get-tuple-element.25), channel_id=1, source_target_pairs={{8,0},{16,8},{24,16},{32,24},{40,32},{48,40},{56,48},{64,56},{72,6... | collective-permute-start | bytes 786440 | tf_op jit(solution)/shard_map/ppermute | solution.py:247
  12.5 1.9 %collective-permute-start = (bf16[16,64,128]{2,1,0:T(8,128)(2,1)S(1)}, bf16[16,64,128]{2,1,0:T(8,128)(2,1)S(1)}, u32[]{:S(2)}, u32[]{:S(2)}) collective-permute-start(bf16[16,64,128]{2,1,0:T(8,128)(2,1)S(1)} %get-tuple-element.26), channel_id=1, source_target_pairs={{0,8},{8,16},{16,24},{24,32},{32,40},{40,48},{48,56},{56,64},{64,7... | collective-permute-start | bytes 786440 | tf_op jit(solution)/shard_map/ppermute | solution.py:246
  14.5 5.5 %collective-permute-done.1.down_ref = bf16[16,64,128]{2,1,0:T(8,128)(2,1)S(1)} collective-permute-done((bf16[16,64,128]{2,1,0:T(8,128)(2,1)S(1)}, bf16[16,64,128]{2,1,0:T(8,128)(2,1)S(1)}, u32[]{:S(2)}, u32[]{:S(2)}) %collective-permute-start.1) | collective-permute-done | bytes 262176 | tf_op jit(solution)/shard_map/ppermute | solution.py:247
  20.0 18.3 %collective-permute-done.up_ref = bf16[16,64,128]{2,1,0:T(8,128)(2,1)S(1)} collective-permute-done((bf16[16,64,128]{2,1,0:T(8,128)(2,1)S(1)}, bf16[16,64,128]{2,1,0:T(8,128)(2,1)S(1)}, u32[]{:S(2)}, u32[]{:S(2)}) %collective-permute-start) | collective-permute-done | bytes 262176 | tf_op jit(solution)/shard_map/ppermute | solution.py:246
  38.3 1.1 %shard_map.64 = bf16[2,8,64,128]{3,2,1,0:T(8,128)(2,1)S(1)} custom-call(s32[3]{0:T(128)S(1)} %pad_add_fusion.place_ref, bf16[16,64,128]{2,1,0:T(8,128)(2,1)S(1)} %collective-permute-done.up_ref, bf16[32,64,128]{2,1,0:T(8,128)(2,1)S(1)} %bitcast.28, bf16[16,64,128]{2,1,0:T(8,128)(2,1)S(1)} %collective-permute-done.1.down_ref), custom_call_target="tpu_custom_call" | custom-call | bytes 1048576 | tf_op jit(solution)/shard_map/pallas_call | solution.py:20
  39.4 2.1 %collective-permute-start.3 = (bf16[8,64,128]{2,1,0:T(8,128)(2,1)S(1)}, bf16[8,64,128]{2,1,0:T(8,128)(2,1)S(1)}, u32[]{:S(2)}, u32[]{:S(2)}) collective-permute-start(bf16[8,64,128]{2,1,0:T(8,128)(2,1)S(1)} %get-tuple-element.27), channel_id=1, source_target_pairs={{1,2},{3,4},{5,6},{2,1},{4,3},{6,5},{9,10},{11,12},{13,14},{10,9},... | collective-permute-start | bytes 393224 | tf_op jit(solution)/shard_map/ppermute | solution.py:257
  41.5 0.3 collective-permute-start.2
  42.3 3.6 %collective-permute-done.3.far_ref = bf16[8,64,128]{2,1,0:T(8,128)(2,1)S(1)} collective-permute-done((bf16[8,64,128]{2,1,0:T(8,128)(2,1)S(1)}, bf16[8,64,128]{2,1,0:T(8,128)(2,1)S(1)}, u32[]{:S(2)}, u32[]{:S(2)}) %collective-permute-start.3) | collective-permute-done | bytes 131104 | tf_op jit(solution)/shard_map/ppermute | solution.py:257
  46.0 0.6 copy-done
  46.6 4.2 %shard_map.65 = (bf16[32,64,128]{2,1,0:T(8,128)(2,1)S(1)}, bf16[4,512,128]{2,1,0:T(8,128)(2,1)S(1)}) custom-call(s32[3]{0:T(128)S(1)} %copy-done, s32[3]{0:T(128)S(1)} %pad_add_fusion.place_ref, bf16[16,64,128]{2,1,0:T(8,128)(2,1)S(1)} %collective-permute-done.up_ref, bf16[32,64,128]{2,1,0:T(8,128)(2,1)S(1)} %bitcast.29, ...), custom_call_target="tpu_custom_call" | custom-call | flops 838860800 | bytes 4194304 | tf_op jit(solution)/shard_map/pallas_call | solution.py:20
  50.9 9.5 %collective-permute-start.6 = (bf16[512,128]{1,0:T(8,128)(2,1)S(1)}, bf16[512,128]{1,0:T(8,128)(2,1)S(1)}, u32[]{:S(2)}, u32[]{:S(2)}) collective-permute-start(bf16[512,128]{1,0:T(8,128)(2,1)S(1)} %get-tuple-element.22), channel_id=1, source_target_pairs={{0,16},{1,56},{2,64},{3,104},{4,144},{5,184},{6,192},{7,232},{8,24... | collective-permute-start | bytes 393224 | tf_op jit(solution)/shard_map/ppermute | solution.py:285
  60.4 1.3 %collective-permute-start.5 = (bf16[512,128]{1,0:T(8,128)(2,1)S(1)}, bf16[512,128]{1,0:T(8,128)(2,1)S(1)}, u32[]{:S(2)}, u32[]{:S(2)}) collective-permute-start(bf16[512,128]{1,0:T(8,128)(2,1)S(1)} %get-tuple-element.23), channel_id=1, source_target_pairs={{0,8},{1,32},{2,88},{3,112},{4,136},{5,160},{6,216},{7,240},{8,0},... | collective-permute-start | bytes 393224 | tf_op jit(solution)/shard_map/ppermute | solution.py:285
  61.7 8.3 %collective-permute-start.4 = (bf16[512,128]{1,0:T(8,128)(2,1)S(1)}, bf16[512,128]{1,0:T(8,128)(2,1)S(1)}, u32[]{:S(2)}, u32[]{:S(2)}) collective-permute-start(bf16[512,128]{1,0:T(8,128)(2,1)S(1)} %get-tuple-element.24), channel_id=1, source_target_pairs={{0,0},{1,40},{2,80},{3,120},{4,128},{5,168},{6,208},{7,248},{8,8},... | collective-permute-start | bytes 393224 | tf_op jit(solution)/shard_map/ppermute | solution.py:285
  70.0 10.8 %collective-permute-done.6.m2 = bf16[512,128]{1,0:T(8,128)(2,1)S(1)} collective-permute-done((bf16[512,128]{1,0:T(8,128)(2,1)S(1)}, bf16[512,128]{1,0:T(8,128)(2,1)S(1)}, u32[]{:S(2)}, u32[]{:S(2)}) %collective-permute-start.6) | collective-permute-done | bytes 131104 | tf_op jit(solution)/shard_map/ppermute | solution.py:285
  80.8 1.7 %shard_map.66 = (bf16[32,64,128]{2,1,0:T(8,128)(2,1)S(1)}, bf16[2,4,64,128]{3,2,1,0:T(8,128)(2,1)S(1)}) custom-call(s32[3]{0:T(128)S(1)} %pad_add_fusion.place_ref, bf16[32,64,128]{2,1,0:T(8,128)(2,1)S(1)} %get-tuple-element.13.second_ref, bf16[512,128]{1,0:T(8,128)(2,1)S(1)} %collective-permute-done.4.m0, bf16[512,128]{1,0:T(8,128)(2,1)S(1)} %collective-permute-done.5.m1, ...), custom_call_target="tpu_custom_call" | custom-call | bytes 2097152 | tf_op jit(solution)/shard_map/pallas_call | solution.py:20
  82.5 1.9 %collective-permute-start.9 = (bf16[4,64,128]{2,1,0:T(8,128)(2,1)S(1)}, bf16[4,64,128]{2,1,0:T(8,128)(2,1)S(1)}, u32[]{:S(2)}, u32[]{:S(2)}) collective-permute-start(bf16[4,64,128]{2,1,0:T(8,128)(2,1)S(1)} %get-tuple-element.29), channel_id=1, source_target_pairs={{1,2},{3,4},{5,6},{2,1},{4,3},{6,5},{9,10},{11,12},{13,14},{10,9},... | collective-permute-start | bytes 196616 | tf_op jit(solution)/shard_map/ppermute | solution.py:295
  84.5 3.6 %collective-permute-done.9.far_ref = bf16[4,64,128]{2,1,0:T(8,128)(2,1)S(1)} collective-permute-done((bf16[4,64,128]{2,1,0:T(8,128)(2,1)S(1)}, bf16[4,64,128]{2,1,0:T(8,128)(2,1)S(1)}, u32[]{:S(2)}, u32[]{:S(2)}) %collective-permute-start.9) | collective-permute-done | bytes 65568 | tf_op jit(solution)/shard_map/ppermute | solution.py:295
  88.1 1.4 %shard_map.68 = (bf16[8,32,128]{2,1,0:T(8,128)(2,1)S(1)}, bf16[8,32,128]{2,1,0:T(8,128)(2,1)S(1)}) custom-call(s32[3]{0:T(128)S(1)} %copy-done, s32[3]{0:T(128)S(1)} %pad_add_fusion.place_ref, bf16[32,64,128]{2,1,0:T(8,128)(2,1)S(1)} %get-tuple-element.15.mean_ref, bf16[4,64,128]{2,1,0:T(8,128)(2,1)S(1)} %collective-permute-done.8.near_ref, ...), custom_call_target="tpu_custom_call" | custom-call | flops 50331648 | bytes 1048576 | tf_op jit(solution)/shard_map/pallas_call | solution.py:20
  89.5 4.7 %collective-permute-start.10 = (bf16[8,32,128]{2,1,0:T(8,128)(2,1)S(1)}, bf16[8,32,128]{2,1,0:T(8,128)(2,1)S(1)}, u32[]{:S(2)}, u32[]{:S(2)}) collective-permute-start(bf16[8,32,128]{2,1,0:T(8,128)(2,1)S(1)} %get-tuple-element.19), channel_id=1, source_target_pairs={{0,8},{8,16},{16,24},{24,32},{32,40},{40,48},{48,56},{56,64},{64,7... | collective-permute-start | bytes 196616 | tf_op jit(solution)/shard_map/ppermute | solution.py:308
  94.3 7.5 %collective-permute-start.11 = (bf16[8,32,128]{2,1,0:T(8,128)(2,1)S(1)}, bf16[8,32,128]{2,1,0:T(8,128)(2,1)S(1)}, u32[]{:S(2)}, u32[]{:S(2)}) collective-permute-start(bf16[8,32,128]{2,1,0:T(8,128)(2,1)S(1)} %get-tuple-element.20), channel_id=1, source_target_pairs={{8,0},{16,8},{24,16},{32,24},{40,32},{48,40},{56,48},{64,56},{72,6... | collective-permute-start | bytes 196616 | tf_op jit(solution)/shard_map/ppermute | solution.py:309
  101.7 1.7 %shard_map.67 = (bf16[32,64,128]{2,1,0:T(8,128)(2,1)S(1)}, f32[16,32,128]{2,1,0:T(8,128)S(1)}) custom-call(s32[3]{0:T(128)S(1)} %copy-done, s32[3]{0:T(128)S(1)} %pad_add_fusion.place_ref, bf16[32,64,128]{2,1,0:T(8,128)(2,1)S(1)} %get-tuple-element.15.mean_ref, bf16[4,64,128]{2,1,0:T(8,128)(2,1)S(1)} %collective-permute-done.8.near_ref, ...), custom_call_target="tpu_custom_call" | custom-call | flops 335544320 | bytes 2097152 | tf_op jit(solution)/shard_map/pallas_call | solution.py:20
  103.4 1.2 %collective-permute-done.11.down_ref = bf16[8,32,128]{2,1,0:T(8,128)(2,1)S(1)} collective-permute-done((bf16[8,32,128]{2,1,0:T(8,128)(2,1)S(1)}, bf16[8,32,128]{2,1,0:T(8,128)(2,1)S(1)}, u32[]{:S(2)}, u32[]{:S(2)}) %collective-permute-start.11) | collective-permute-done | bytes 65568 | tf_op jit(solution)/shard_map/ppermute | solution.py:309
  104.8 1.1 %copy.18 = bf16[64,32,128]{2,1,0:T(8,128)(2,1)} copy(bf16[64,32,128]{2,0,1:T(8,128)(2,1)S(1)} %bitcast.30) | data formatting | bytes 1048576 | tf_op jit(solution)/shard_map/transpose | solution.py:328
  (28 shorter events, 1.2 us)
Async XLA Ops:
  1.3 18.7 %collective-permute-start.1 = (bf16[16,64,128]{2,1,0:T(8,128)(2,1)S(1)}, bf16[16,64,128]{2,1,0:T(8,128)(2,1)S(1)}, u32[]{:S(2)}, u32[]{:S(2)}) collective-permute-start(bf16[16,64,128]{2,1,0:T(8,128)(2,1)S(1)} %get-tuple-element.25), channel_id=1, source_target_pairs={{8,0},{16,8},{24,16},{32,24},{40,32},{48,40},{56,48},{64,56},{72,6... | collective-permute-start | bytes 786440 | tf_op jit(solution)/shard_map/ppermute | solution.py:247
  12.5 25.8 %collective-permute-start = (bf16[16,64,128]{2,1,0:T(8,128)(2,1)S(1)}, bf16[16,64,128]{2,1,0:T(8,128)(2,1)S(1)}, u32[]{:S(2)}, u32[]{:S(2)}) collective-permute-start(bf16[16,64,128]{2,1,0:T(8,128)(2,1)S(1)} %get-tuple-element.26), channel_id=1, source_target_pairs={{0,8},{8,16},{16,24},{24,32},{32,40},{40,48},{48,56},{56,64},{64,7... | collective-permute-start | bytes 786440 | tf_op jit(solution)/shard_map/ppermute | solution.py:246
  39.4 2.4 %copy-start.2 = (bf16[3,64,32]{1,2,0:T(8,128)(2,1)S(1)}, bf16[3,64,32]{1,2,0:T(8,128)(2,1)}, u32[]{:S(2)}) copy-start(bf16[3,64,32]{1,2,0:T(8,128)(2,1)} %param.11) | copy-start | bytes 36868
  39.4 2.5 %copy-start.1 = (bf16[3,9,32,64]{3,2,1,0:T(8,128)(2,1)S(1)}, bf16[3,9,32,64]{3,2,1,0:T(8,128)(2,1)}, u32[]{:S(2)}) copy-start(bf16[3,9,32,64]{3,2,1,0:T(8,128)(2,1)} %param.8) | copy-start | bytes 331780
  39.4 6.4 %collective-permute-start.3 = (bf16[8,64,128]{2,1,0:T(8,128)(2,1)S(1)}, bf16[8,64,128]{2,1,0:T(8,128)(2,1)S(1)}, u32[]{:S(2)}, u32[]{:S(2)}) collective-permute-start(bf16[8,64,128]{2,1,0:T(8,128)(2,1)S(1)} %get-tuple-element.27), channel_id=1, source_target_pairs={{1,2},{3,4},{5,6},{2,1},{4,3},{6,5},{9,10},{11,12},{13,14},{10,9},... | collective-permute-start | bytes 393224 | tf_op jit(solution)/shard_map/ppermute | solution.py:257
  41.5 4.4 %collective-permute-start.2 = (bf16[8,64,128]{2,1,0:T(8,128)(2,1)S(1)}, bf16[8,64,128]{2,1,0:T(8,128)(2,1)S(1)}, u32[]{:S(2)}, u32[]{:S(2)}) collective-permute-start(bf16[8,64,128]{2,1,0:T(8,128)(2,1)S(1)} %get-tuple-element.28), channel_id=1, source_target_pairs={{0,1},{1,0},{2,3},{3,2},{4,5},{5,4},{6,7},{7,6},{8,9},{9,8},{10,11... | collective-permute-start | bytes 393224 | tf_op jit(solution)/shard_map/ppermute | solution.py:258
  42.1 3.8 %copy-start.3 = (f32[3,32]{1,0:T(4,128)S(1)}, f32[3,32]{1,0:T(4,128)}, u32[]{:S(2)}) copy-start(f32[3,32]{1,0:T(4,128)} %param.9) | copy-start | bytes 1156
  42.3 3.6 %copy-start.4 = (f32[3,32]{1,0:T(4,128)S(1)}, f32[3,32]{1,0:T(4,128)}, u32[]{:S(2)}) copy-start(f32[3,32]{1,0:T(4,128)} %param.10) | copy-start | bytes 1156
  45.9 0.7 copy-start
  50.8 19.2 %collective-permute-start.7 = (bf16[512,128]{1,0:T(8,128)(2,1)S(1)}, bf16[512,128]{1,0:T(8,128)(2,1)S(1)}, u32[]{:S(2)}, u32[]{:S(2)}) collective-permute-start(bf16[512,128]{1,0:T(8,128)(2,1)S(1)} %get-tuple-element.21), channel_id=1, source_target_pairs={{0,24},{1,48},{2,72},{3,96},{4,152},{5,176},{6,200},{7,224},{8,16}... | collective-permute-start | bytes 393224 | tf_op jit(solution)/shard_map/ppermute | solution.py:285
  50.9 29.9 %collective-permute-start.6 = (bf16[512,128]{1,0:T(8,128)(2,1)S(1)}, bf16[512,128]{1,0:T(8,128)(2,1)S(1)}, u32[]{:S(2)}, u32[]{:S(2)}) collective-permute-start(bf16[512,128]{1,0:T(8,128)(2,1)S(1)} %get-tuple-element.22), channel_id=1, source_target_pairs={{0,16},{1,56},{2,64},{3,104},{4,144},{5,184},{6,192},{7,232},{8,24... | collective-permute-start | bytes 393224 | tf_op jit(solution)/shard_map/ppermute | solution.py:285
  60.4 20.4 %collective-permute-start.5 = (bf16[512,128]{1,0:T(8,128)(2,1)S(1)}, bf16[512,128]{1,0:T(8,128)(2,1)S(1)}, u32[]{:S(2)}, u32[]{:S(2)}) collective-permute-start(bf16[512,128]{1,0:T(8,128)(2,1)S(1)} %get-tuple-element.23), channel_id=1, source_target_pairs={{0,8},{1,32},{2,88},{3,112},{4,136},{5,160},{6,216},{7,240},{8,0},... | collective-permute-start | bytes 393224 | tf_op jit(solution)/shard_map/ppermute | solution.py:285
  61.7 19.1 %collective-permute-start.4 = (bf16[512,128]{1,0:T(8,128)(2,1)S(1)}, bf16[512,128]{1,0:T(8,128)(2,1)S(1)}, u32[]{:S(2)}, u32[]{:S(2)}) collective-permute-start(bf16[512,128]{1,0:T(8,128)(2,1)S(1)} %get-tuple-element.24), channel_id=1, source_target_pairs={{0,0},{1,40},{2,80},{3,120},{4,128},{5,168},{6,208},{7,248},{8,8},... | collective-permute-start | bytes 393224 | tf_op jit(solution)/shard_map/ppermute | solution.py:285
  82.5 5.6 %collective-permute-start.9 = (bf16[4,64,128]{2,1,0:T(8,128)(2,1)S(1)}, bf16[4,64,128]{2,1,0:T(8,128)(2,1)S(1)}, u32[]{:S(2)}, u32[]{:S(2)}) collective-permute-start(bf16[4,64,128]{2,1,0:T(8,128)(2,1)S(1)} %get-tuple-element.29), channel_id=1, source_target_pairs={{1,2},{3,4},{5,6},{2,1},{4,3},{6,5},{9,10},{11,12},{13,14},{10,9},... | collective-permute-start | bytes 196616 | tf_op jit(solution)/shard_map/ppermute | solution.py:295
  84.4 3.7 %collective-permute-start.8 = (bf16[4,64,128]{2,1,0:T(8,128)(2,1)S(1)}, bf16[4,64,128]{2,1,0:T(8,128)(2,1)S(1)}, u32[]{:S(2)}, u32[]{:S(2)}) collective-permute-start(bf16[4,64,128]{2,1,0:T(8,128)(2,1)S(1)} %get-tuple-element.30), channel_id=1, source_target_pairs={{0,1},{1,0},{2,3},{3,2},{4,5},{5,4},{6,7},{7,6},{8,9},{9,8},{10,11... | collective-permute-start | bytes 196616 | tf_op jit(solution)/shard_map/ppermute | solution.py:296
  89.5 13.9 %collective-permute-start.10 = (bf16[8,32,128]{2,1,0:T(8,128)(2,1)S(1)}, bf16[8,32,128]{2,1,0:T(8,128)(2,1)S(1)}, u32[]{:S(2)}, u32[]{:S(2)}) collective-permute-start(bf16[8,32,128]{2,1,0:T(8,128)(2,1)S(1)} %get-tuple-element.19), channel_id=1, source_target_pairs={{0,8},{8,16},{16,24},{24,32},{32,40},{40,48},{48,56},{56,64},{64,7... | collective-permute-start | bytes 196616 | tf_op jit(solution)/shard_map/ppermute | solution.py:308
  94.3 10.3 %collective-permute-start.11 = (bf16[8,32,128]{2,1,0:T(8,128)(2,1)S(1)}, bf16[8,32,128]{2,1,0:T(8,128)(2,1)S(1)}, u32[]{:S(2)}, u32[]{:S(2)}) collective-permute-start(bf16[8,32,128]{2,1,0:T(8,128)(2,1)S(1)} %get-tuple-element.20), channel_id=1, source_target_pairs={{8,0},{16,8},{24,16},{32,24},{40,32},{48,40},{56,48},{64,56},{72,6... | collective-permute-start | bytes 196616 | tf_op jit(solution)/shard_map/ppermute | solution.py:309

commit v7 on v6

--- a/solution.py
+++ b/solution.py
@@ -106,17 +106,22 @@
 
 
 def pack_rows(refs, place_ref, sides_ref):
-    odd = lax.rem(place_ref[1], 2)
+    odd = lax.rem(place_ref[1], 2) == 1
     first = 0
     for ref in refs:
         for g in range(ref.shape[0] // 8):
             pieces = [ref[8 * g + q] for q in range(8)]
-            sides_ref[1 - odd, first + g] = pack_strips(pieces, 0, 16)
-            sides_ref[odd, first + g] = pack_strips(pieces, 112, 16)
+            left, right = pack_strips(pieces, 0, 16), pack_strips(pieces, 112, 16)
+            sides_ref[0, first + g] = jnp.where(odd, left, right)
+            sides_ref[1, first + g] = jnp.where(odd, right, left)
         first += ref.shape[0] // 8
 
 
-def pack_sides(place_ref, up_ref, own_ref, down_ref, sides_ref):
+def pack_sides(place_ref, near_row, far_row, own_ref, up_ref, down_ref, sides_ref):
+    odd = lax.rem(place_ref[0], 2) == 1
+    for r in range(16):
+        near, far = near_row[r], far_row[r]
+        up_ref[r], down_ref[r] = jnp.where(odd, near, far), jnp.where(odd, far, near)
     pack_rows((up_ref, own_ref, down_ref), place_ref, sides_ref)
 
 
@@ -188,9 +193,10 @@
 
 
 def last_edges(
-    spacing_ref, place_ref, mean_ref, near_ref, far_ref, kernel_ref, to_up_ref, to_down_ref, wide
+    spacing_ref, place_ref, mean_ref, near_ref, far_ref, kernel_ref, near_row, far_row, wide
 ):
     spacing, kernel = spacing_ref[2], kernel_ref[2]
+    odd = lax.rem(place_ref[0], 2) == 1
     fill_last(wide, place_ref, mean_ref, near_ref, far_ref)
     taps = []
     for i in range(8):
@@ -200,8 +206,9 @@
         taps.append(jnp.dot(kernel[:, :64], down, preferred_element_type=F32))
     sums = tap_sums(taps, spacing, True)
     for i in range(8):
-        to_up_ref[i] = sums[2 * i][0].astype(BF)
-        to_down_ref[i] = sums[2 * i + 1][0].astype(BF)
+        up, down = sums[2 * i][0], sums[2 * i + 1][0]
+        near_row[i] = jnp.where(odd, up, down).astype(BF)
+        far_row[i] = jnp.where(odd, down, up).astype(BF)
 
 
 def last_inner(
@@ -220,10 +227,14 @@
 
 
 def last_outer(
-    inner_ref, mean_ref, conv_ref, up_ref, down_ref, gain_ref, shift_ref, expand_ref, out_ref
+    place_ref, inner_ref, mean_ref, conv_ref, near_row, far_row, gain_ref, shift_ref, expand_ref,
+    out_ref,
 ):
-    sums = [conv_ref[i] + up_ref[i].astype(F32) for i in range(8)]
-    sums += [conv_ref[8 + i] + down_ref[i].astype(F32) for i in range(8)]
+    odd = lax.rem(place_ref[0], 2) == 1
+    near = [near_row[i].astype(F32) for i in range(8)]
+    far = [far_row[i].astype(F32) for i in range(8)]
+    sums = [conv_ref[i] + jnp.where(odd, near[i], far[i]) for i in range(8)]
+    sums += [conv_ref[8 + i] + jnp.where(odd, far[i], near[i]) for i in range(8)]
     grown = grow(sums, gain_ref[2], shift_ref[2], expand_ref[2])
     out_ref[8:24] = inner_ref[8:24]
     for i in range(16):
@@ -236,19 +247,26 @@
     row, col = lax.axis_index("row"), lax.axis_index("col")
     mixed = lax.bitwise_xor(lax.rem(row, 4), lax.rem(lax.div(row, 4) + col, 4))
     place = jnp.stack([row, col, mixed]).astype(jnp.int32)
-    down_way = [(r, r + 1) for r in range(rows - 1)]
-    up_way = [(r + 1, r) for r in range(rows - 1)]
+    near_rows = [(r, r ^ 1) for r in range(rows)]
+    far_rows = [(r, r + 1) for r in range(1, rows - 1, 2)]
+    far_rows += [(d, r) for r, d in far_rows]
     near_pairs = [(c, c ^ 1) for c in range(cols)]
     far_pairs = [(c, c + 1) for c in range(1, cols - 1, 2)]
     far_pairs += [(d, c) for c, d in far_pairs]
 
     own = jnp.transpose(contact_map, (1, 0, 2))
-    above = lax.ppermute(own[16:], "row", down_way)
-    below = lax.ppermute(own[:16], "row", up_way)
-    sides = call(
+    odd_row = lax.rem(row, 2)
+    far_row = lax.ppermute(
+        lax.dynamic_slice_in_dim(own, 16 * odd_row, 16, 0), "row", far_rows
+    )
+    near_row = lax.ppermute(
+        lax.dynamic_slice_in_dim(own, 16 - 16 * odd_row, 16, 0), "row", near_rows
+    )
+    rim = jax.ShapeDtypeStruct((16, 64, 128), BF)
+    above, below, sides = call(
         pack_sides,
-        jax.ShapeDtypeStruct((2, 8, 64, 128), BF),
-        (place, above, own, below),
+        (rim, rim, jax.ShapeDtypeStruct((2, 8, 64, 128), BF)),
+        (place, near_row, far_row, own),
         1,
         [],
         0,
@@ -296,7 +314,7 @@
     near = lax.ppermute(sides[0], "col", near_pairs)
     wide = [pltpu.VMEM((48, 64, 256), BF)]
     edge = jax.ShapeDtypeStruct((8, 32, 128), BF)
-    to_up, to_down = call(
+    to_near, to_far = call(
         last_edges,
         (edge, edge),
         (dilations, place, mean, near, far, kernel),
@@ -305,8 +323,8 @@
         16 * 256 * 64 * 96 * 2,
         1 << 20,
     )
-    above = lax.ppermute(to_down, "row", down_way)
-    below = lax.ppermute(to_up, "row", up_way)
+    far_row = lax.ppermute(to_far, "row", far_rows)
+    near_row = lax.ppermute(to_near, "row", near_rows)
     inner, conv = call(
         last_inner,
         (tile, jax.ShapeDtypeStruct((16, 32, 128), F32)),
@@ -319,8 +337,8 @@
     out = call(
         last_outer,
         tile,
-        (inner, mean, conv, above, below, gain, shift, out_weight),
-        0,
+        (place, inner, mean, conv, near_row, far_row, gain, shift, out_weight),
+        1,
         [],
         16 * 256 * 64 * 32 * 2,
         2 << 20,

time: 106 us -> 108 us (1.019)
  waiting for transfers between devices: 42.8 us -> 48.9 us
  starting transfers between devices: 48.9 us -> 43.4 us
    ppermute x4, starting transfers between devices: 25.3 us -> 17.9 us  [the longest x1 11.2 us: on_device(): lax.ppermute(lax.dynamic_slice_in_dim(own, 16 * odd_row, 16, 0), 'row', f...]
    ppermute x4, waiting for transfers between devices: 24.9 us -> 29.5 us  [the longest x1 14.6 us: on_device(): lax.ppermute(lax.dynamic_slice_in_dim(own, 16 - 16 * odd_row, 16, 0), 'ro...]
    ppermute x4, waiting for transfers between devices: 10.8 us -> 13.8 us  [on_device(): received.append(lax.ppermute(messages[t], BOTH, pairs))]
    ppermute x2, starting transfers between devices: 3.97 us -> 6.15 us  [on_device(): far = lax.ppermute(sides[1], 'col', far_pairs)]
    ppermute x2, waiting for transfers between devices: 7.11 us -> 5.58 us  [on_device(): far = lax.ppermute(sides[1], 'col', far_pairs)]
where the time goes in v7:
time: 108 us; the launch traced here: 107 us
  waiting for transfers between devices  48.9 us (45%)
  starting transfers between devices  43.4 us (40%)
  Pallas kernels  10.9 us (10%)
  local copies, waits for them, and re-layouts  3.79 us (4%)
    ppermute x4, starting transfers between devices, on_device(): received.append(lax.ppermute(messages[t], BOTH, pairs))  19.2 us
    ppermute x1, waiting for transfers between devices, on_device(): lax.ppermute(lax.dynamic_slice_in_dim(own, 16 - 16 * odd_row, 16, 0), 'ro...  14.6 us
    ppermute x4, waiting for transfers between devices, on_device(): received.append(lax.ppermute(messages[t], BOTH, pairs))  13.8 us
    ppermute x1, starting transfers between devices, on_device(): lax.ppermute(lax.dynamic_slice_in_dim(own, 16 * odd_row, 16, 0), 'row', f...  11.2 us
    pallas_call x6, Pallas kernels, call(): pl.pallas_call(body, out_shape=outs, in_specs=[SMEM] * n_smem + [VMEM] *...  10.9 us
    ppermute x1, waiting for transfers between devices, on_device(): far_row = lax.ppermute(to_far, 'row', far_rows)  7.96 us
    ppermute x1, waiting for transfers between devices, on_device(): lax.ppermute(lax.dynamic_slice_in_dim(own, 16 * odd_row, 16, 0), 'row', f...  6.99 us
    ppermute x2, starting transfers between devices, on_device(): far = lax.ppermute(sides[1], 'col', far_pairs)  6.15 us
  transfers between devices with their start and end apart: 12, of which 6 were waited for; matrix products, arithmetic and copies ran while one was open for 1% of the time, Pallas kernels for 2%

profile of v7, /device:TPU:25, one launch (start us, length us, event | category | flops | bytes accessed | tf_op | source)
XLA Modules:
  0.0 107.4 jit_solution(7631486683244867792)
XLA Ops:
  0.0 1.2 %copy.27 = bf16[64,32,128]{2,0,1:T(8,128)(2,1)S(1)} copy(bf16[64,32,128]{2,1,0:T(8,128)(2,1)} %param.6) | data formatting | bytes 1048576 | tf_op args[0]
  1.3 11.2 %collective-permute-start.1 = (bf16[16,64,128]{2,1,0:T(8,128)(2,1)S(1)}, bf16[16,64,128]{2,1,0:T(8,128)(2,1)S(1)}, u32[]{:S(2)}, u32[]{:S(2)}) collective-permute-start(bf16[16,64,128]{2,1,0:T(8,128)(2,1)S(1)} %get-tuple-element.33), channel_id=1, source_target_pairs={{8,16},{24,32},{40,48},{56,64},{72,80},{88,96},{104,112},{120,128}... | collective-permute-start | bytes 786440 | tf_op jit(solution)/shard_map/ppermute | solution.py:259
  12.7 7.0 %collective-permute-done.1.far_row = bf16[16,64,128]{2,1,0:T(8,128)(2,1)S(1)} collective-permute-done((bf16[16,64,128]{2,1,0:T(8,128)(2,1)S(1)}, bf16[16,64,128]{2,1,0:T(8,128)(2,1)S(1)}, u32[]{:S(2)}, u32[]{:S(2)}) %collective-permute-start.1) | collective-permute-done | bytes 262176 | tf_op jit(solution)/shard_map/ppermute | solution.py:259
  19.7 14.6 %collective-permute-done.near_row = bf16[16,64,128]{2,1,0:T(8,128)(2,1)S(1)} collective-permute-done((bf16[16,64,128]{2,1,0:T(8,128)(2,1)S(1)}, bf16[16,64,128]{2,1,0:T(8,128)(2,1)S(1)}, u32[]{:S(2)}, u32[]{:S(2)}) %collective-permute-start) | collective-permute-done | bytes 262176 | tf_op jit(solution)/shard_map/ppermute | solution.py:262
  34.3 1.1 %shard_map.64 = (bf16[16,64,128]{2,1,0:T(8,128)(2,1)S(1)}, bf16[16,64,128]{2,1,0:T(8,128)(2,1)S(1)}, bf16[2,8,64,128]{3,2,1,0:T(8,128)(2,1)S(1)}) custom-call(s32[3]{0:T(128)S(1)} %pad_add_fusion.place_ref, bf16[16,64,128]{2,1,0:T(8,128)(2,1)S(1)} %collective-permute-done.near_row, bf16[16,64,128]{2,1,0:T(8,128)(2,1)S(1)} %collective-permute-done.1.far_row, ...), custom_call_target="tpu_custom_call" | custom-call | bytes 1048576 | tf_op jit(solution)/shard_map/pallas_call | solution.py:20
  35.5 4.2 %collective-permute-start.3 = (bf16[8,64,128]{2,1,0:T(8,128)(2,1)S(1)}, bf16[8,64,128]{2,1,0:T(8,128)(2,1)S(1)}, u32[]{:S(2)}, u32[]{:S(2)}) collective-permute-start(bf16[8,64,128]{2,1,0:T(8,128)(2,1)S(1)} %get-tuple-element.35), channel_id=1, source_target_pairs={{1,2},{3,4},{5,6},{2,1},{4,3},{6,5},{9,10},{11,12},{13,14},{10,9},... | collective-permute-start | bytes 393224 | tf_op jit(solution)/shard_map/ppermute | solution.py:275
  40.3 2.0 %collective-permute-done.3.far_ref = bf16[8,64,128]{2,1,0:T(8,128)(2,1)S(1)} collective-permute-done((bf16[8,64,128]{2,1,0:T(8,128)(2,1)S(1)}, bf16[8,64,128]{2,1,0:T(8,128)(2,1)S(1)}, u32[]{:S(2)}, u32[]{:S(2)}) %collective-permute-start.3) | collective-permute-done | bytes 131104 | tf_op jit(solution)/shard_map/ppermute | solution.py:275
  42.5 0.7 copy-done
  43.2 4.2 %shard_map.65 = (bf16[32,64,128]{2,1,0:T(8,128)(2,1)S(1)}, bf16[4,512,128]{2,1,0:T(8,128)(2,1)S(1)}) custom-call(s32[3]{0:T(128)S(1)} %copy-done, s32[3]{0:T(128)S(1)} %pad_add_fusion.place_ref, bf16[16,64,128]{2,1,0:T(8,128)(2,1)S(1)} %get-tuple-element.16.up_ref, bf16[32,64,128]{2,1,0:T(8,128)(2,1)S(1)} %bitcast.32, ...), custom_call_target="tpu_custom_call" | custom-call | flops 838860800 | bytes 4194304 | tf_op jit(solution)/shard_map/pallas_call | solution.py:20
  47.4 4.9 %collective-permute-start.7 = (bf16[512,128]{1,0:T(8,128)(2,1)S(1)}, bf16[512,128]{1,0:T(8,128)(2,1)S(1)}, u32[]{:S(2)}, u32[]{:S(2)}) collective-permute-start(bf16[512,128]{1,0:T(8,128)(2,1)S(1)} %get-tuple-element.27), channel_id=1, source_target_pairs={{0,24},{1,48},{2,72},{3,96},{4,152},{5,176},{6,200},{7,224},{8,16}... | collective-permute-start | bytes 393224 | tf_op jit(solution)/shard_map/ppermute | solution.py:303
  52.3 8.3 %collective-permute-start.6 = (bf16[512,128]{1,0:T(8,128)(2,1)S(1)}, bf16[512,128]{1,0:T(8,128)(2,1)S(1)}, u32[]{:S(2)}, u32[]{:S(2)}) collective-permute-start(bf16[512,128]{1,0:T(8,128)(2,1)S(1)} %get-tuple-element.28), channel_id=1, source_target_pairs={{0,16},{1,56},{2,64},{3,104},{4,144},{5,184},{6,192},{7,232},{8,24... | collective-permute-start | bytes 393224 | tf_op jit(solution)/shard_map/ppermute | solution.py:303
  60.6 1.5 %collective-permute-start.5 = (bf16[512,128]{1,0:T(8,128)(2,1)S(1)}, bf16[512,128]{1,0:T(8,128)(2,1)S(1)}, u32[]{:S(2)}, u32[]{:S(2)}) collective-permute-start(bf16[512,128]{1,0:T(8,128)(2,1)S(1)} %get-tuple-element.29), channel_id=1, source_target_pairs={{0,8},{1,32},{2,88},{3,112},{4,136},{5,160},{6,216},{7,240},{8,0},... | collective-permute-start | bytes 393224 | tf_op jit(solution)/shard_map/ppermute | solution.py:303
  62.1 4.5 %collective-permute-start.4 = (bf16[512,128]{1,0:T(8,128)(2,1)S(1)}, bf16[512,128]{1,0:T(8,128)(2,1)S(1)}, u32[]{:S(2)}, u32[]{:S(2)}) collective-permute-start(bf16[512,128]{1,0:T(8,128)(2,1)S(1)} %get-tuple-element.30), channel_id=1, source_target_pairs={{0,0},{1,40},{2,80},{3,120},{4,128},{5,168},{6,208},{7,248},{8,8},... | collective-permute-start | bytes 393224 | tf_op jit(solution)/shard_map/ppermute | solution.py:303
  66.7 13.8 %collective-permute-done.6.m2 = bf16[512,128]{1,0:T(8,128)(2,1)S(1)} collective-permute-done((bf16[512,128]{1,0:T(8,128)(2,1)S(1)}, bf16[512,128]{1,0:T(8,128)(2,1)S(1)}, u32[]{:S(2)}, u32[]{:S(2)}) %collective-permute-start.6) | collective-permute-done | bytes 131104 | tf_op jit(solution)/shard_map/ppermute | solution.py:303
  80.4 1.7 %shard_map.66 = (bf16[32,64,128]{2,1,0:T(8,128)(2,1)S(1)}, bf16[2,4,64,128]{3,2,1,0:T(8,128)(2,1)S(1)}) custom-call(s32[3]{0:T(128)S(1)} %pad_add_fusion.place_ref, bf16[32,64,128]{2,1,0:T(8,128)(2,1)S(1)} %get-tuple-element.19.second_ref, bf16[512,128]{1,0:T(8,128)(2,1)S(1)} %collective-permute-done.4.m0, bf16[512,128]{1,0:T(8,128)(2,1)S(1)} %collective-permute-done.5.m1, ...), custom_call_target="tpu_custom_call" | custom-call | bytes 2097152 | tf_op jit(solution)/shard_map/pallas_call | solution.py:20
  82.1 1.9 %collective-permute-start.9 = (bf16[4,64,128]{2,1,0:T(8,128)(2,1)S(1)}, bf16[4,64,128]{2,1,0:T(8,128)(2,1)S(1)}, u32[]{:S(2)}, u32[]{:S(2)}) collective-permute-start(bf16[4,64,128]{2,1,0:T(8,128)(2,1)S(1)} %get-tuple-element.37), channel_id=1, source_target_pairs={{1,2},{3,4},{5,6},{2,1},{4,3},{6,5},{9,10},{11,12},{13,14},{10,9},... | collective-permute-start | bytes 196616 | tf_op jit(solution)/shard_map/ppermute | solution.py:313
  84.2 3.6 %collective-permute-done.9.far_ref = bf16[4,64,128]{2,1,0:T(8,128)(2,1)S(1)} collective-permute-done((bf16[4,64,128]{2,1,0:T(8,128)(2,1)S(1)}, bf16[4,64,128]{2,1,0:T(8,128)(2,1)S(1)}, u32[]{:S(2)}, u32[]{:S(2)}) %collective-permute-start.9) | collective-permute-done | bytes 65568 | tf_op jit(solution)/shard_map/ppermute | solution.py:313
  87.7 1.4 %shard_map.68 = (bf16[8,32,128]{2,1,0:T(8,128)(2,1)S(1)}, bf16[8,32,128]{2,1,0:T(8,128)(2,1)S(1)}) custom-call(s32[3]{0:T(128)S(1)} %copy-done, s32[3]{0:T(128)S(1)} %pad_add_fusion.place_ref, bf16[32,64,128]{2,1,0:T(8,128)(2,1)S(1)} %get-tuple-element.21.mean_ref, bf16[4,64,128]{2,1,0:T(8,128)(2,1)S(1)} %collective-permute-done.8.near_ref, ...), custom_call_target="tpu_custom_call" | custom-call | flops 50331648 | bytes 1048576 | tf_op jit(solution)/shard_map/pallas_call | solution.py:20
  89.2 3.6 %collective-permute-start.10 = (bf16[8,32,128]{2,1,0:T(8,128)(2,1)S(1)}, bf16[8,32,128]{2,1,0:T(8,128)(2,1)S(1)}, u32[]{:S(2)}, u32[]{:S(2)}) collective-permute-start(bf16[8,32,128]{2,1,0:T(8,128)(2,1)S(1)} %get-tuple-element.25), channel_id=1, source_target_pairs={{0,8},{8,0},{16,24},{24,16},{32,40},{40,32},{48,56},{56,48},{64,72... | collective-permute-start | bytes 196616 | tf_op jit(solution)/shard_map/ppermute | solution.py:327
  92.7 3.0 %collective-permute-start.11 = (bf16[8,32,128]{2,1,0:T(8,128)(2,1)S(1)}, bf16[8,32,128]{2,1,0:T(8,128)(2,1)S(1)}, u32[]{:S(2)}, u32[]{:S(2)}) collective-permute-start(bf16[8,32,128]{2,1,0:T(8,128)(2,1)S(1)} %get-tuple-element.26), channel_id=1, source_target_pairs={{8,16},{24,32},{40,48},{56,64},{72,80},{88,96},{104,112},{120,128}... | collective-permute-start | bytes 196616 | tf_op jit(solution)/shard_map/ppermute | solution.py:326
  95.8 1.7 %shard_map.67 = (bf16[32,64,128]{2,1,0:T(8,128)(2,1)S(1)}, f32[16,32,128]{2,1,0:T(8,128)S(1)}) custom-call(s32[3]{0:T(128)S(1)} %copy-done, s32[3]{0:T(128)S(1)} %pad_add_fusion.place_ref, bf16[32,64,128]{2,1,0:T(8,128)(2,1)S(1)} %get-tuple-element.21.mean_ref, bf16[4,64,128]{2,1,0:T(8,128)(2,1)S(1)} %collective-permute-done.8.near_ref, ...), custom_call_target="tpu_custom_call" | custom-call | flops 335544320 | bytes 2097152 | tf_op jit(solution)/shard_map/pallas_call | solution.py:20
  97.5 8.0 %collective-permute-done.11.far_row = bf16[8,32,128]{2,1,0:T(8,128)(2,1)S(1)} collective-permute-done((bf16[8,32,128]{2,1,0:T(8,128)(2,1)S(1)}, bf16[8,32,128]{2,1,0:T(8,128)(2,1)S(1)}, u32[]{:S(2)}, u32[]{:S(2)}) %collective-permute-start.11) | collective-permute-done | bytes 65568 | tf_op jit(solution)/shard_map/ppermute | solution.py:326
  105.5 0.8 shard_map.69
  106.2 1.1 %copy.22 = bf16[64,32,128]{2,1,0:T(8,128)(2,1)} copy(bf16[64,32,128]{2,0,1:T(8,128)(2,1)S(1)} %bitcast.33) | data formatting | bytes 1048576 | tf_op jit(solution)/shard_map/transpose | solution.py:346
  (28 shorter events, 1.1 us)
Async XLA Ops:
  1.3 18.4 %collective-permute-start.1 = (bf16[16,64,128]{2,1,0:T(8,128)(2,1)S(1)}, bf16[16,64,128]{2,1,0:T(8,128)(2,1)S(1)}, u32[]{:S(2)}, u32[]{:S(2)}) collective-permute-start(bf16[16,64,128]{2,1,0:T(8,128)(2,1)S(1)} %get-tuple-element.33), channel_id=1, source_target_pairs={{8,16},{24,32},{40,48},{56,64},{72,80},{88,96},{104,112},{120,128}... | collective-permute-start | bytes 786440 | tf_op jit(solution)/shard_map/ppermute | solution.py:259
  12.5 21.8 %collective-permute-start = (bf16[16,64,128]{2,1,0:T(8,128)(2,1)S(1)}, bf16[16,64,128]{2,1,0:T(8,128)(2,1)S(1)}, u32[]{:S(2)}, u32[]{:S(2)}) collective-permute-start(bf16[16,64,128]{2,1,0:T(8,128)(2,1)S(1)} %get-tuple-element.34), channel_id=1, source_target_pairs={{0,8},{8,0},{16,24},{24,16},{32,40},{40,32},{48,56},{56,48},{64,72... | collective-permute-start | bytes 786440 | tf_op jit(solution)/shard_map/ppermute | solution.py:262
  35.4 4.4 %copy-start.2 = (bf16[3,64,32]{1,2,0:T(8,128)(2,1)S(1)}, bf16[3,64,32]{1,2,0:T(8,128)(2,1)}, u32[]{:S(2)}) copy-start(bf16[3,64,32]{1,2,0:T(8,128)(2,1)} %param.11) | copy-start | bytes 36868
  35.4 4.5 %copy-start.1 = (bf16[3,9,32,64]{3,2,1,0:T(8,128)(2,1)S(1)}, bf16[3,9,32,64]{3,2,1,0:T(8,128)(2,1)}, u32[]{:S(2)}) copy-start(bf16[3,9,32,64]{3,2,1,0:T(8,128)(2,1)} %param.8) | copy-start | bytes 331780
  35.5 6.9 %collective-permute-start.3 = (bf16[8,64,128]{2,1,0:T(8,128)(2,1)S(1)}, bf16[8,64,128]{2,1,0:T(8,128)(2,1)S(1)}, u32[]{:S(2)}, u32[]{:S(2)}) collective-permute-start(bf16[8,64,128]{2,1,0:T(8,128)(2,1)S(1)} %get-tuple-element.35), channel_id=1, source_target_pairs={{1,2},{3,4},{5,6},{2,1},{4,3},{6,5},{9,10},{11,12},{13,14},{10,9},... | collective-permute-start | bytes 393224 | tf_op jit(solution)/shard_map/ppermute | solution.py:275
  39.7 2.6 %collective-permute-start.2 = (bf16[8,64,128]{2,1,0:T(8,128)(2,1)S(1)}, bf16[8,64,128]{2,1,0:T(8,128)(2,1)S(1)}, u32[]{:S(2)}, u32[]{:S(2)}) collective-permute-start(bf16[8,64,128]{2,1,0:T(8,128)(2,1)S(1)} %get-tuple-element.36), channel_id=1, source_target_pairs={{0,1},{1,0},{2,3},{3,2},{4,5},{5,4},{6,7},{7,6},{8,9},{9,8},{10,11... | collective-permute-start | bytes 393224 | tf_op jit(solution)/shard_map/ppermute | solution.py:276
  40.1 2.3 %copy-start.3 = (f32[3,32]{1,0:T(4,128)S(1)}, f32[3,32]{1,0:T(4,128)}, u32[]{:S(2)}) copy-start(f32[3,32]{1,0:T(4,128)} %param.9) | copy-start | bytes 1156
  40.3 2.1 %copy-start.4 = (f32[3,32]{1,0:T(4,128)S(1)}, f32[3,32]{1,0:T(4,128)}, u32[]{:S(2)}) copy-start(f32[3,32]{1,0:T(4,128)} %param.10) | copy-start | bytes 1156
  42.5 0.7 copy-start
  47.4 19.2 %collective-permute-start.7 = (bf16[512,128]{1,0:T(8,128)(2,1)S(1)}, bf16[512,128]{1,0:T(8,128)(2,1)S(1)}, u32[]{:S(2)}, u32[]{:S(2)}) collective-permute-start(bf16[512,128]{1,0:T(8,128)(2,1)S(1)} %get-tuple-element.27), channel_id=1, source_target_pairs={{0,24},{1,48},{2,72},{3,96},{4,152},{5,176},{6,200},{7,224},{8,16}... | collective-permute-start | bytes 393224 | tf_op jit(solution)/shard_map/ppermute | solution.py:303
  52.3 28.1 %collective-permute-start.6 = (bf16[512,128]{1,0:T(8,128)(2,1)S(1)}, bf16[512,128]{1,0:T(8,128)(2,1)S(1)}, u32[]{:S(2)}, u32[]{:S(2)}) collective-permute-start(bf16[512,128]{1,0:T(8,128)(2,1)S(1)} %get-tuple-element.28), channel_id=1, source_target_pairs={{0,16},{1,56},{2,64},{3,104},{4,144},{5,184},{6,192},{7,232},{8,24... | collective-permute-start | bytes 393224 | tf_op jit(solution)/shard_map/ppermute | solution.py:303
  60.6 19.8 %collective-permute-start.5 = (bf16[512,128]{1,0:T(8,128)(2,1)S(1)}, bf16[512,128]{1,0:T(8,128)(2,1)S(1)}, u32[]{:S(2)}, u32[]{:S(2)}) collective-permute-start(bf16[512,128]{1,0:T(8,128)(2,1)S(1)} %get-tuple-element.29), channel_id=1, source_target_pairs={{0,8},{1,32},{2,88},{3,112},{4,136},{5,160},{6,216},{7,240},{8,0},... | collective-permute-start | bytes 393224 | tf_op jit(solution)/shard_map/ppermute | solution.py:303
  62.1 18.3 %collective-permute-start.4 = (bf16[512,128]{1,0:T(8,128)(2,1)S(1)}, bf16[512,128]{1,0:T(8,128)(2,1)S(1)}, u32[]{:S(2)}, u32[]{:S(2)}) collective-permute-start(bf16[512,128]{1,0:T(8,128)(2,1)S(1)} %get-tuple-element.30), channel_id=1, source_target_pairs={{0,0},{1,40},{2,80},{3,120},{4,128},{5,168},{6,208},{7,248},{8,8},... | collective-permute-start | bytes 393224 | tf_op jit(solution)/shard_map/ppermute | solution.py:303
  82.1 5.6 %collective-permute-start.9 = (bf16[4,64,128]{2,1,0:T(8,128)(2,1)S(1)}, bf16[4,64,128]{2,1,0:T(8,128)(2,1)S(1)}, u32[]{:S(2)}, u32[]{:S(2)}) collective-permute-start(bf16[4,64,128]{2,1,0:T(8,128)(2,1)S(1)} %get-tuple-element.37), channel_id=1, source_target_pairs={{1,2},{3,4},{5,6},{2,1},{4,3},{6,5},{9,10},{11,12},{13,14},{10,9},... | collective-permute-start | bytes 196616 | tf_op jit(solution)/shard_map/ppermute | solution.py:313
  84.1 3.7 %collective-permute-start.8 = (bf16[4,64,128]{2,1,0:T(8,128)(2,1)S(1)}, bf16[4,64,128]{2,1,0:T(8,128)(2,1)S(1)}, u32[]{:S(2)}, u32[]{:S(2)}) collective-permute-start(bf16[4,64,128]{2,1,0:T(8,128)(2,1)S(1)} %get-tuple-element.38), channel_id=1, source_target_pairs={{0,1},{1,0},{2,3},{3,2},{4,5},{5,4},{6,7},{7,6},{8,9},{9,8},{10,11... | collective-permute-start | bytes 196616 | tf_op jit(solution)/shard_map/ppermute | solution.py:314
  89.2 8.4 %collective-permute-start.10 = (bf16[8,32,128]{2,1,0:T(8,128)(2,1)S(1)}, bf16[8,32,128]{2,1,0:T(8,128)(2,1)S(1)}, u32[]{:S(2)}, u32[]{:S(2)}) collective-permute-start(bf16[8,32,128]{2,1,0:T(8,128)(2,1)S(1)} %get-tuple-element.25), channel_id=1, source_target_pairs={{0,8},{8,0},{16,24},{24,16},{32,40},{40,32},{48,56},{56,48},{64,72... | collective-permute-start | bytes 196616 | tf_op jit(solution)/shard_map/ppermute | solution.py:327
  92.7 12.7 %collective-permute-start.11 = (bf16[8,32,128]{2,1,0:T(8,128)(2,1)S(1)}, bf16[8,32,128]{2,1,0:T(8,128)(2,1)S(1)}, u32[]{:S(2)}, u32[]{:S(2)}) collective-permute-start(bf16[8,32,128]{2,1,0:T(8,128)(2,1)S(1)} %get-tuple-element.26), channel_id=1, source_target_pairs={{8,16},{24,32},{40,48},{56,64},{72,80},{88,96},{104,112},{120,128}... | collective-permute-start | bytes 196616 | tf_op jit(solution)/shard_map/ppermute | solution.py:326

commit v8 on v7

--- a/solution.py
+++ b/solution.py
@@ -38,7 +38,7 @@
     for place, piece in enumerate(pieces):
         moved = pltpu.roll(piece.astype(F32), (place * width - start) % 128, 1)
         total = moved if total is None else jnp.where(lane >= place * width, moved, total)
-    return total.astype(BF)
+    return total
 
 
 def side_lanes(from_right, from_left, place, width):
@@ -105,24 +105,24 @@
     )
 
 
-def pack_rows(refs, place_ref, sides_ref):
+def pack_rows(rows, place_ref, sides_ref):
     odd = lax.rem(place_ref[1], 2) == 1
-    first = 0
-    for ref in refs:
-        for g in range(ref.shape[0] // 8):
-            pieces = [ref[8 * g + q] for q in range(8)]
-            left, right = pack_strips(pieces, 0, 16), pack_strips(pieces, 112, 16)
-            sides_ref[0, first + g] = jnp.where(odd, left, right)
-            sides_ref[1, first + g] = jnp.where(odd, right, left)
-        first += ref.shape[0] // 8
+    for g in range(len(rows) // 8):
+        pieces = rows[8 * g : 8 * g + 8]
+        left, right = pack_strips(pieces, 0, 16), pack_strips(pieces, 112, 16)
+        sides_ref[0, g] = jnp.where(odd, left, right).astype(BF)
+        sides_ref[1, g] = jnp.where(odd, right, left).astype(BF)
 
 
 def pack_sides(place_ref, near_row, far_row, own_ref, up_ref, down_ref, sides_ref):
     odd = lax.rem(place_ref[0], 2) == 1
+    up, down = [], []
     for r in range(16):
         near, far = near_row[r], far_row[r]
-        up_ref[r], down_ref[r] = jnp.where(odd, near, far), jnp.where(odd, far, near)
-    pack_rows((up_ref, own_ref, down_ref), place_ref, sides_ref)
+        up.append(jnp.where(odd, near, far))
+        down.append(jnp.where(odd, far, near))
+        up_ref[r], down_ref[r] = up[r], down[r]
+    pack_rows(up + [own_ref[r] for r in range(32)] + down, place_ref, sides_ref)
 
 
 def fill_wide(wide, refs, place_ref, near_ref, far_ref, first=0):
@@ -175,14 +175,16 @@
     members = place_ref[2]
     for t, ref in enumerate((m0, m1, m2, m3)):
         gathered[lax.bitwise_xor(members, t)] = ref[...]
+    mean = []
     for j in range(32):
         blocks = []
         for k in range(4):
             part = gathered[k, 16 * j : 16 * j + 16, :].astype(F32)
             blocks += [part, pltpu.roll(part, 64, 1)]
         mirrored = jnp.transpose(jnp.concatenate(blocks, axis=0))[:64]
-        mean_ref[j] = (0.5 * (second_ref[j].astype(F32) + mirrored)).astype(BF)
-    pack_rows((mean_ref,), place_ref, sides_ref)
+        mean.append((0.5 * (second_ref[j].astype(F32) + mirrored)).astype(BF))
+        mean_ref[j] = mean[j]
+    pack_rows(mean, place_ref, sides_ref)
 
 
 def fill_last(wide, place_ref, mean_ref, near_ref, far_ref):
@@ -256,11 +258,24 @@
 
     own = jnp.transpose(contact_map, (1, 0, 2))
     odd_row = lax.rem(row, 2)
-    far_row = lax.ppermute(
-        lax.dynamic_slice_in_dim(own, 16 * odd_row, 16, 0), "row", far_rows
-    )
-    near_row = lax.ppermute(
-        lax.dynamic_slice_in_dim(own, 16 - 16 * odd_row, 16, 0), "row", near_rows
+
+    def row_rims(depth):
+        def exchange(own, odd):
+            first, last = (32 - depth) * odd, (32 - depth) * (1 - odd)
+            far = lax.ppermute(lax.dynamic_slice_in_dim(own, first, depth, 0), "row", far_rows)
+            near = lax.ppermute(lax.dynamic_slice_in_dim(own, last, depth, 0), "row", near_rows)
+            empty = jnp.zeros((16, 64, 128), BF)
+            spare = 16 - depth
+            return (
+                lax.dynamic_update_slice_in_dim(empty, far, spare * (1 - odd), 0),
+                lax.dynamic_update_slice_in_dim(empty, near, spare * odd, 0),
+            )
+
+        return exchange
+
+    reach = dilations[0] + dilations[1]
+    far_row, near_row = lax.switch(
+        lax.div(reach - 1, 2), [row_rims(depth) for depth in range(2, 17, 2)], own, odd_row
     )
     rim = jax.ShapeDtypeStruct((16, 64, 128), BF)
     above, below, sides = call(

time: 108 us -> 108 us (level); the launches traced: 107 us -> 106 us
  waiting for transfers between devices: 48.9 us -> 41.3 us
  local copies, waits for them, and re-layouts: 3.79 us -> 7.32 us
  between operations: 0.25 us -> 1.54 us
  starting transfers between devices: 43.4 us -> 44.6 us
    ppermute x2, waiting for transfers between devices: 21.6 us -> 14.7 us  [the longest x1 7.58 us: exchange(): lax.ppermute(lax.dynamic_slice_in_dim(own, last, depth, 0), 'row', near_r...]
    another operation x0 -> x2, local copies, waits for them, and re-layouts: none -> 1.52 us
    ppermute x1, starting transfers between devices: 3.04 us -> 4.45 us  [on_device(): far_row = lax.ppermute(to_far, 'row', far_rows)]
    dynamic_update_slice x0 -> x2, local copies, waits for them, and re-layouts: none -> 1.38 us  [the longest x1 0.69 us: exchange(): lax.dynamic_update_slice_in_dim(empty, far, spare * (1 - odd), 0)]
  transfers between devices with their start and end apart: 12 -> 12, of which waited for: 6 -> 7; matrix products, arithmetic and copies ran while one was open for 1% -> 2% of each run, Pallas kernels for 2% -> 2%
where the time goes in v8:
time: 108 us; the launch traced here: 106 us
  starting transfers between devices  44.6 us (41%)
  waiting for transfers between devices  41.3 us (38%)
  Pallas kernels  11.3 us (10%)
  local copies, waits for them, and re-layouts  7.32 us (7%)
  between operations  1.54 us (1%)
    ppermute x4, starting transfers between devices, on_device(): received.append(lax.ppermute(messages[t], BOTH, pairs))  19.4 us
    ppermute x4, waiting for transfers between devices, on_device(): received.append(lax.ppermute(messages[t], BOTH, pairs))  13.1 us
    pallas_call x6, Pallas kernels, call(): pl.pallas_call(body, out_shape=outs, in_specs=[SMEM] * n_smem + [VMEM] *...  11.3 us
    ppermute x1, starting transfers between devices, exchange(): lax.ppermute(lax.dynamic_slice_in_dim(own, first, depth, 0), 'row', far_r...  11.2 us
    ppermute x1, waiting for transfers between devices, on_device(): far_row = lax.ppermute(to_far, 'row', far_rows)  7.93 us
    ppermute x1, waiting for transfers between devices, exchange(): lax.ppermute(lax.dynamic_slice_in_dim(own, last, depth, 0), 'row', near_r...  7.58 us
    ppermute x1, waiting for transfers between devices, exchange(): lax.ppermute(lax.dynamic_slice_in_dim(own, first, depth, 0), 'row', far_r...  7.07 us
    ppermute x2, starting transfers between devices, on_device(): far = lax.ppermute(sides[1], 'col', far_pairs)  6.11 us
  transfers between devices with their start and end apart: 12, of which 7 were waited for; matrix products, arithmetic and copies ran while one was open for 2% of the time, Pallas kernels for 2%

profile of v8, /device:TPU:25, one launch (start us, length us, event | category | flops | bytes accessed | tf_op | source)
XLA Modules:
  0.0 106.3 jit_solution(1990246524562731639)
XLA Ops:
  2.6 1.2 %copy.21 = bf16[64,32,128]{2,0,1:T(8,128)(2,1)S(1)} copy(bf16[64,32,128]{2,1,0:T(8,128)(2,1)} %param.14) | data formatting | bytes 1048576 | tf_op args[0]
  3.9 29.0 %conditional.1 = (bf16[16,64,128]{2,1,0:T(8,128)(2,1)}, bf16[16,64,128]{2,1,0:T(8,128)(2,1)}) conditional(s32[]{:T(128)} %clamp.3, (s32[]{:T(128)}, bf16[32,64,128]{2,1,0:T(8,128)(2,1)S(1)}) %tuple.60, (s32[]{:T(128)}, bf16[32,64,128]{2,1,0:T(8,128)(2,1)S(1)}) %tuple.61, (s32[]{:T(128)}, ...), branch_computations={%region_0.0_spmd, %region_1.0_spmd, %region_2.0_spmd, %region_3.0_... | conditional | flops 17 | bytes 4194616 | solution.py:277
  4.0 11.2 %collective-permute-start.10 = (bf16[12,64,128]{2,1,0:T(8,128)(2,1)S(1)}, bf16[12,64,128]{2,1,0:T(8,128)(2,1)S(1)}, u32[]{:S(2)}, u32[]{:S(2)}) collective-permute-start(bf16[12,64,128]{2,1,0:T(8,128)(2,1)S(1)} %get-tuple-element.90), channel_id=1, source_target_pairs={{8,16},{24,32},{40,48},{56,64},{72,80},{88,96},{104,112},{120,128}... | collective-permute-start | bytes 589832 | tf_op jit(solution)/shard_map/cond/branch_5_fun/ppermute | solution.py:265
  15.3 7.1 %collective-permute-done.10 = bf16[12,64,128]{2,1,0:T(8,128)(2,1)S(1)} collective-permute-done((bf16[12,64,128]{2,1,0:T(8,128)(2,1)S(1)}, bf16[12,64,128]{2,1,0:T(8,128)(2,1)S(1)}, u32[]{:S(2)}, u32[]{:S(2)}) %collective-permute-start.10) | collective-permute-done | bytes 196640 | tf_op jit(solution)/shard_map/cond/branch_5_fun/ppermute | solution.py:265
  23.8 7.6 %collective-permute-done.11 = bf16[12,64,128]{2,1,0:T(8,128)(2,1)S(1)} collective-permute-done((bf16[12,64,128]{2,1,0:T(8,128)(2,1)S(1)}, bf16[12,64,128]{2,1,0:T(8,128)(2,1)S(1)}, u32[]{:S(2)}, u32[]{:S(2)}) %collective-permute-start.11) | collective-permute-done | bytes 196640 | tf_op jit(solution)/shard_map/cond/branch_5_fun/ppermute | solution.py:266
  32.9 1.6 %shard_map.64 = (bf16[16,64,128]{2,1,0:T(8,128)(2,1)S(1)}, bf16[16,64,128]{2,1,0:T(8,128)(2,1)S(1)}, bf16[2,8,64,128]{3,2,1,0:T(8,128)(2,1)S(1)}) custom-call(s32[3]{0:T(128)S(1)} %pad_add_fusion.place_ref, bf16[16,64,128]{2,1,0:T(8,128)(2,1)} %get-tuple-element.66.near_row, bf16[16,64,128]{2,1,0:T(8,128)(2,1)} %get-tuple-element.67.far_row, ...), custom_call_target="tpu_custom_call" | custom-call | bytes 1048576 | tf_op jit(solution)/shard_map/pallas_call | solution.py:20
  34.6 4.2 %collective-permute-start.17 = (bf16[8,64,128]{2,1,0:T(8,128)(2,1)S(1)}, bf16[8,64,128]{2,1,0:T(8,128)(2,1)S(1)}, u32[]{:S(2)}, u32[]{:S(2)}) collective-permute-start(bf16[8,64,128]{2,1,0:T(8,128)(2,1)S(1)} %get-tuple-element.99), channel_id=1, source_target_pairs={{1,2},{3,4},{5,6},{2,1},{4,3},{6,5},{9,10},{11,12},{13,14},{10,9},... | collective-permute-start | bytes 393224 | tf_op jit(solution)/shard_map/ppermute | solution.py:290
  39.4 2.0 %collective-permute-done.17.far_ref = bf16[8,64,128]{2,1,0:T(8,128)(2,1)S(1)} collective-permute-done((bf16[8,64,128]{2,1,0:T(8,128)(2,1)S(1)}, bf16[8,64,128]{2,1,0:T(8,128)(2,1)S(1)}, u32[]{:S(2)}, u32[]{:S(2)}) %collective-permute-start.17) | collective-permute-done | bytes 131104 | tf_op jit(solution)/shard_map/ppermute | solution.py:290
  41.6 4.2 %shard_map.65 = (bf16[32,64,128]{2,1,0:T(8,128)(2,1)S(1)}, bf16[4,512,128]{2,1,0:T(8,128)(2,1)S(1)}) custom-call(s32[3]{0:T(128)S(1)} %copy-done, s32[3]{0:T(128)S(1)} %pad_add_fusion.place_ref, bf16[16,64,128]{2,1,0:T(8,128)(2,1)S(1)} %get-tuple-element.68.up_ref, bf16[32,64,128]{2,1,0:T(8,128)(2,1)S(1)} %bitcast.38, ...), custom_call_target="tpu_custom_call" | custom-call | flops 838860800 | bytes 4194304 | tf_op jit(solution)/shard_map/pallas_call | solution.py:20
  45.8 4.8 %collective-permute-start.21 = (bf16[512,128]{1,0:T(8,128)(2,1)S(1)}, bf16[512,128]{1,0:T(8,128)(2,1)S(1)}, u32[]{:S(2)}, u32[]{:S(2)}) collective-permute-start(bf16[512,128]{1,0:T(8,128)(2,1)S(1)} %get-tuple-element.95), channel_id=1, source_target_pairs={{0,24},{1,48},{2,72},{3,96},{4,152},{5,176},{6,200},{7,224},{8,16}... | collective-permute-start | bytes 393224 | tf_op jit(solution)/shard_map/ppermute | solution.py:318
  50.6 8.4 %collective-permute-start.20 = (bf16[512,128]{1,0:T(8,128)(2,1)S(1)}, bf16[512,128]{1,0:T(8,128)(2,1)S(1)}, u32[]{:S(2)}, u32[]{:S(2)}) collective-permute-start(bf16[512,128]{1,0:T(8,128)(2,1)S(1)} %get-tuple-element.96), channel_id=1, source_target_pairs={{0,16},{1,56},{2,64},{3,104},{4,144},{5,184},{6,192},{7,232},{8,24... | collective-permute-start | bytes 393224 | tf_op jit(solution)/shard_map/ppermute | solution.py:318
  59.0 1.7 %collective-permute-start.19 = (bf16[512,128]{1,0:T(8,128)(2,1)S(1)}, bf16[512,128]{1,0:T(8,128)(2,1)S(1)}, u32[]{:S(2)}, u32[]{:S(2)}) collective-permute-start(bf16[512,128]{1,0:T(8,128)(2,1)S(1)} %get-tuple-element.97), channel_id=1, source_target_pairs={{0,8},{1,32},{2,88},{3,112},{4,136},{5,160},{6,216},{7,240},{8,0},... | collective-permute-start | bytes 393224 | tf_op jit(solution)/shard_map/ppermute | solution.py:318
  60.7 4.5 %collective-permute-start.18 = (bf16[512,128]{1,0:T(8,128)(2,1)S(1)}, bf16[512,128]{1,0:T(8,128)(2,1)S(1)}, u32[]{:S(2)}, u32[]{:S(2)}) collective-permute-start(bf16[512,128]{1,0:T(8,128)(2,1)S(1)} %get-tuple-element.98), channel_id=1, source_target_pairs={{0,0},{1,40},{2,80},{3,120},{4,128},{5,168},{6,208},{7,248},{8,8},... | collective-permute-start | bytes 393224 | tf_op jit(solution)/shard_map/ppermute | solution.py:318
  65.2 11.9 %collective-permute-done.20.m2 = bf16[512,128]{1,0:T(8,128)(2,1)S(1)} collective-permute-done((bf16[512,128]{1,0:T(8,128)(2,1)S(1)}, bf16[512,128]{1,0:T(8,128)(2,1)S(1)}, u32[]{:S(2)}, u32[]{:S(2)}) %collective-permute-start.20) | collective-permute-done | bytes 131104 | tf_op jit(solution)/shard_map/ppermute | solution.py:318
  77.1 1.3 %collective-permute-done.18.m0 = bf16[512,128]{1,0:T(8,128)(2,1)S(1)} collective-permute-done((bf16[512,128]{1,0:T(8,128)(2,1)S(1)}, bf16[512,128]{1,0:T(8,128)(2,1)S(1)}, u32[]{:S(2)}, u32[]{:S(2)}) %collective-permute-start.18) | collective-permute-done | bytes 131104 | tf_op jit(solution)/shard_map/ppermute | solution.py:318
  78.4 1.6 %shard_map.66 = (bf16[32,64,128]{2,1,0:T(8,128)(2,1)S(1)}, bf16[2,4,64,128]{3,2,1,0:T(8,128)(2,1)S(1)}) custom-call(s32[3]{0:T(128)S(1)} %pad_add_fusion.place_ref, bf16[32,64,128]{2,1,0:T(8,128)(2,1)S(1)} %get-tuple-element.71.second_ref, bf16[512,128]{1,0:T(8,128)(2,1)S(1)} %collective-permute-done.18.m0, bf16[512,128]{1,0:T(8,128)(2,1)S(1)} %collective-permute-done.19.m1, ...), custom_call_target="tpu_custom_call" | custom-call | bytes 2097152 | tf_op jit(solution)/shard_map/pallas_call | solution.py:20
  80.0 1.9 %collective-permute-start.23 = (bf16[4,64,128]{2,1,0:T(8,128)(2,1)S(1)}, bf16[4,64,128]{2,1,0:T(8,128)(2,1)S(1)}, u32[]{:S(2)}, u32[]{:S(2)}) collective-permute-start(bf16[4,64,128]{2,1,0:T(8,128)(2,1)S(1)} %get-tuple-element.101), channel_id=1, source_target_pairs={{1,2},{3,4},{5,6},{2,1},{4,3},{6,5},{9,10},{11,12},{13,14},{10,9},... | collective-permute-start | bytes 196616 | tf_op jit(solution)/shard_map/ppermute | solution.py:328
  82.0 3.6 %collective-permute-done.23.far_ref = bf16[4,64,128]{2,1,0:T(8,128)(2,1)S(1)} collective-permute-done((bf16[4,64,128]{2,1,0:T(8,128)(2,1)S(1)}, bf16[4,64,128]{2,1,0:T(8,128)(2,1)S(1)}, u32[]{:S(2)}, u32[]{:S(2)}) %collective-permute-start.23) | collective-permute-done | bytes 65568 | tf_op jit(solution)/shard_map/ppermute | solution.py:328
  85.6 1.4 %shard_map.68 = (bf16[8,32,128]{2,1,0:T(8,128)(2,1)S(1)}, bf16[8,32,128]{2,1,0:T(8,128)(2,1)S(1)}) custom-call(s32[3]{0:T(128)S(1)} %copy-done, s32[3]{0:T(128)S(1)} %pad_add_fusion.place_ref, bf16[32,64,128]{2,1,0:T(8,128)(2,1)S(1)} %get-tuple-element.73.mean_ref, bf16[4,64,128]{2,1,0:T(8,128)(2,1)S(1)} %collective-permute-done.22.near_ref, ...), custom_call_target="tpu_custom_call" | custom-call | flops 50331648 | bytes 1048576 | tf_op jit(solution)/shard_map/pallas_call | solution.py:20
  87.0 3.2 %collective-permute-start.24 = (bf16[8,32,128]{2,1,0:T(8,128)(2,1)S(1)}, bf16[8,32,128]{2,1,0:T(8,128)(2,1)S(1)}, u32[]{:S(2)}, u32[]{:S(2)}) collective-permute-start(bf16[8,32,128]{2,1,0:T(8,128)(2,1)S(1)} %get-tuple-element.77), channel_id=1, source_target_pairs={{0,8},{8,0},{16,24},{24,16},{32,40},{40,32},{48,56},{56,48},{64,72... | collective-permute-start | bytes 196616 | tf_op jit(solution)/shard_map/ppermute | solution.py:342
  90.3 4.4 %collective-permute-start.25 = (bf16[8,32,128]{2,1,0:T(8,128)(2,1)S(1)}, bf16[8,32,128]{2,1,0:T(8,128)(2,1)S(1)}, u32[]{:S(2)}, u32[]{:S(2)}) collective-permute-start(bf16[8,32,128]{2,1,0:T(8,128)(2,1)S(1)} %get-tuple-element.78), channel_id=1, source_target_pairs={{8,16},{24,32},{40,48},{56,64},{72,80},{88,96},{104,112},{120,128}... | collective-permute-start | bytes 196616 | tf_op jit(solution)/shard_map/ppermute | solution.py:341
  94.7 1.7 %shard_map.67 = (bf16[32,64,128]{2,1,0:T(8,128)(2,1)S(1)}, f32[16,32,128]{2,1,0:T(8,128)S(1)}) custom-call(s32[3]{0:T(128)S(1)} %copy-done, s32[3]{0:T(128)S(1)} %pad_add_fusion.place_ref, bf16[32,64,128]{2,1,0:T(8,128)(2,1)S(1)} %get-tuple-element.73.mean_ref, bf16[4,64,128]{2,1,0:T(8,128)(2,1)S(1)} %collective-permute-done.22.near_ref, ...), custom_call_target="tpu_custom_call" | custom-call | flops 335544320 | bytes 2097152 | tf_op jit(solution)/shard_map/pallas_call | solution.py:20
  96.4 7.9 %collective-permute-done.25.far_row = bf16[8,32,128]{2,1,0:T(8,128)(2,1)S(1)} collective-permute-done((bf16[8,32,128]{2,1,0:T(8,128)(2,1)S(1)}, bf16[8,32,128]{2,1,0:T(8,128)(2,1)S(1)}, u32[]{:S(2)}, u32[]{:S(2)}) %collective-permute-start.25) | collective-permute-done | bytes 65568 | tf_op jit(solution)/shard_map/ppermute | solution.py:341
  105.1 1.1 %copy.18 = bf16[64,32,128]{2,1,0:T(8,128)(2,1)} copy(bf16[64,32,128]{2,0,1:T(8,128)(2,1)S(1)} %bitcast.28) | data formatting | bytes 1048576 | tf_op jit(solution)/shard_map/transpose | solution.py:361
  (34 shorter events, 6.1 us)
Async XLA Ops:
  0.0 0.7 copy-start
  4.0 18.4 %collective-permute-start.10 = (bf16[12,64,128]{2,1,0:T(8,128)(2,1)S(1)}, bf16[12,64,128]{2,1,0:T(8,128)(2,1)S(1)}, u32[]{:S(2)}, u32[]{:S(2)}) collective-permute-start(bf16[12,64,128]{2,1,0:T(8,128)(2,1)S(1)} %get-tuple-element.90), channel_id=1, source_target_pairs={{8,16},{24,32},{40,48},{56,64},{72,80},{88,96},{104,112},{120,128}... | collective-permute-start | bytes 589832 | tf_op jit(solution)/shard_map/cond/branch_5_fun/ppermute | solution.py:265
  15.2 16.2 %collective-permute-start.11 = (bf16[12,64,128]{2,1,0:T(8,128)(2,1)S(1)}, bf16[12,64,128]{2,1,0:T(8,128)(2,1)S(1)}, u32[]{:S(2)}, u32[]{:S(2)}) collective-permute-start(bf16[12,64,128]{2,1,0:T(8,128)(2,1)S(1)} %get-tuple-element.89), channel_id=1, source_target_pairs={{0,8},{8,0},{16,24},{24,16},{32,40},{40,32},{48,56},{56,48},{64,72... | collective-permute-start | bytes 589832 | tf_op jit(solution)/shard_map/cond/branch_5_fun/ppermute | solution.py:266
  34.5 4.4 %copy-start.2 = (bf16[3,64,32]{1,2,0:T(8,128)(2,1)S(1)}, bf16[3,64,32]{1,2,0:T(8,128)(2,1)}, u32[]{:S(2)}) copy-start(bf16[3,64,32]{1,2,0:T(8,128)(2,1)} %param.19) | copy-start | bytes 36868
  34.5 4.5 %copy-start.1 = (bf16[3,9,32,64]{3,2,1,0:T(8,128)(2,1)S(1)}, bf16[3,9,32,64]{3,2,1,0:T(8,128)(2,1)}, u32[]{:S(2)}) copy-start(bf16[3,9,32,64]{3,2,1,0:T(8,128)(2,1)} %param.16) | copy-start | bytes 331780
  34.6 6.8 %collective-permute-start.17 = (bf16[8,64,128]{2,1,0:T(8,128)(2,1)S(1)}, bf16[8,64,128]{2,1,0:T(8,128)(2,1)S(1)}, u32[]{:S(2)}, u32[]{:S(2)}) collective-permute-start(bf16[8,64,128]{2,1,0:T(8,128)(2,1)S(1)} %get-tuple-element.99), channel_id=1, source_target_pairs={{1,2},{3,4},{5,6},{2,1},{4,3},{6,5},{9,10},{11,12},{13,14},{10,9},... | collective-permute-start | bytes 393224 | tf_op jit(solution)/shard_map/ppermute | solution.py:290
  38.8 2.6 %collective-permute-start.16 = (bf16[8,64,128]{2,1,0:T(8,128)(2,1)S(1)}, bf16[8,64,128]{2,1,0:T(8,128)(2,1)S(1)}, u32[]{:S(2)}, u32[]{:S(2)}) collective-permute-start(bf16[8,64,128]{2,1,0:T(8,128)(2,1)S(1)} %get-tuple-element.100), channel_id=1, source_target_pairs={{0,1},{1,0},{2,3},{3,2},{4,5},{5,4},{6,7},{7,6},{8,9},{9,8},{10,11... | collective-permute-start | bytes 393224 | tf_op jit(solution)/shard_map/ppermute | solution.py:291
  39.2 2.3 %copy-start.3 = (f32[3,32]{1,0:T(4,128)S(1)}, f32[3,32]{1,0:T(4,128)}, u32[]{:S(2)}) copy-start(f32[3,32]{1,0:T(4,128)} %param.17) | copy-start | bytes 1156
  39.4 2.1 %copy-start.4 = (f32[3,32]{1,0:T(4,128)S(1)}, f32[3,32]{1,0:T(4,128)}, u32[]{:S(2)}) copy-start(f32[3,32]{1,0:T(4,128)} %param.18) | copy-start | bytes 1156
  45.8 19.4 %collective-permute-start.21 = (bf16[512,128]{1,0:T(8,128)(2,1)S(1)}, bf16[512,128]{1,0:T(8,128)(2,1)S(1)}, u32[]{:S(2)}, u32[]{:S(2)}) collective-permute-start(bf16[512,128]{1,0:T(8,128)(2,1)S(1)} %get-tuple-element.95), channel_id=1, source_target_pairs={{0,24},{1,48},{2,72},{3,96},{4,152},{5,176},{6,200},{7,224},{8,16}... | collective-permute-start | bytes 393224 | tf_op jit(solution)/shard_map/ppermute | solution.py:318
  50.6 26.5 %collective-permute-start.20 = (bf16[512,128]{1,0:T(8,128)(2,1)S(1)}, bf16[512,128]{1,0:T(8,128)(2,1)S(1)}, u32[]{:S(2)}, u32[]{:S(2)}) collective-permute-start(bf16[512,128]{1,0:T(8,128)(2,1)S(1)} %get-tuple-element.96), channel_id=1, source_target_pairs={{0,16},{1,56},{2,64},{3,104},{4,144},{5,184},{6,192},{7,232},{8,24... | collective-permute-start | bytes 393224 | tf_op jit(solution)/shard_map/ppermute | solution.py:318
  59.0 18.1 %collective-permute-start.19 = (bf16[512,128]{1,0:T(8,128)(2,1)S(1)}, bf16[512,128]{1,0:T(8,128)(2,1)S(1)}, u32[]{:S(2)}, u32[]{:S(2)}) collective-permute-start(bf16[512,128]{1,0:T(8,128)(2,1)S(1)} %get-tuple-element.97), channel_id=1, source_target_pairs={{0,8},{1,32},{2,88},{3,112},{4,136},{5,160},{6,216},{7,240},{8,0},... | collective-permute-start | bytes 393224 | tf_op jit(solution)/shard_map/ppermute | solution.py:318
  60.7 17.7 %collective-permute-start.18 = (bf16[512,128]{1,0:T(8,128)(2,1)S(1)}, bf16[512,128]{1,0:T(8,128)(2,1)S(1)}, u32[]{:S(2)}, u32[]{:S(2)}) collective-permute-start(bf16[512,128]{1,0:T(8,128)(2,1)S(1)} %get-tuple-element.98), channel_id=1, source_target_pairs={{0,0},{1,40},{2,80},{3,120},{4,128},{5,168},{6,208},{7,248},{8,8},... | collective-permute-start | bytes 393224 | tf_op jit(solution)/shard_map/ppermute | solution.py:318
  80.0 5.6 %collective-permute-start.23 = (bf16[4,64,128]{2,1,0:T(8,128)(2,1)S(1)}, bf16[4,64,128]{2,1,0:T(8,128)(2,1)S(1)}, u32[]{:S(2)}, u32[]{:S(2)}) collective-permute-start(bf16[4,64,128]{2,1,0:T(8,128)(2,1)S(1)} %get-tuple-element.101), channel_id=1, source_target_pairs={{1,2},{3,4},{5,6},{2,1},{4,3},{6,5},{9,10},{11,12},{13,14},{10,9},... | collective-permute-start | bytes 196616 | tf_op jit(solution)/shard_map/ppermute | solution.py:328
  81.9 3.7 %collective-permute-start.22 = (bf16[4,64,128]{2,1,0:T(8,128)(2,1)S(1)}, bf16[4,64,128]{2,1,0:T(8,128)(2,1)S(1)}, u32[]{:S(2)}, u32[]{:S(2)}) collective-permute-start(bf16[4,64,128]{2,1,0:T(8,128)(2,1)S(1)} %get-tuple-element.102), channel_id=1, source_target_pairs={{0,1},{1,0},{2,3},{3,2},{4,5},{5,4},{6,7},{7,6},{8,9},{9,8},{10,11... | collective-permute-start | bytes 196616 | tf_op jit(solution)/shard_map/ppermute | solution.py:329
  87.0 9.4 %collective-permute-start.24 = (bf16[8,32,128]{2,1,0:T(8,128)(2,1)S(1)}, bf16[8,32,128]{2,1,0:T(8,128)(2,1)S(1)}, u32[]{:S(2)}, u32[]{:S(2)}) collective-permute-start(bf16[8,32,128]{2,1,0:T(8,128)(2,1)S(1)} %get-tuple-element.77), channel_id=1, source_target_pairs={{0,8},{8,0},{16,24},{24,16},{32,40},{40,32},{48,56},{56,48},{64,72... | collective-permute-start | bytes 196616 | tf_op jit(solution)/shard_map/ppermute | solution.py:342
  90.3 14.1 %collective-permute-start.25 = (bf16[8,32,128]{2,1,0:T(8,128)(2,1)S(1)}, bf16[8,32,128]{2,1,0:T(8,128)(2,1)S(1)}, u32[]{:S(2)}, u32[]{:S(2)}) collective-permute-start(bf16[8,32,128]{2,1,0:T(8,128)(2,1)S(1)} %get-tuple-element.78), channel_id=1, source_target_pairs={{8,16},{24,32},{40,48},{56,64},{72,80},{88,96},{104,112},{120,128}... | collective-permute-start | bytes 196616 | tf_op jit(solution)/shard_map/ppermute | solution.py:341

commit v9 on v8

--- a/solution.py
+++ b/solution.py
@@ -105,8 +105,7 @@
     )
 
 
-def pack_rows(rows, place_ref, sides_ref):
-    odd = lax.rem(place_ref[1], 2) == 1
+def pack_rows(rows, odd, sides_ref):
     for g in range(len(rows) // 8):
         pieces = rows[8 * g : 8 * g + 8]
         left, right = pack_strips(pieces, 0, 16), pack_strips(pieces, 112, 16)
@@ -114,52 +113,47 @@
         sides_ref[1, g] = jnp.where(odd, right, left).astype(BF)
 
 
-def pack_sides(place_ref, near_row, far_row, own_ref, up_ref, down_ref, sides_ref):
-    odd = lax.rem(place_ref[0], 2) == 1
-    up, down = [], []
-    for r in range(16):
-        near, far = near_row[r], far_row[r]
-        up.append(jnp.where(odd, near, far))
-        down.append(jnp.where(odd, far, near))
-        up_ref[r], down_ref[r] = up[r], down[r]
-    pack_rows(up + [own_ref[r] for r in range(32)] + down, place_ref, sides_ref)
-
-
-def fill_wide(wide, refs, place_ref, near_ref, far_ref, first=0):
-    odd = lax.rem(place_ref[1], 2) == 1
-    at = 0
-    for ref in refs:
-        for r in range(ref.shape[0]):
-            if at % 8 == 0:
-                near, far = near_ref[at // 8], far_ref[at // 8]
-                from_left, from_right = jnp.where(odd, near, far), jnp.where(odd, far, near)
-            wide[first + at, :, :128] = ref[r]
-            wide[first + at, :, 128:] = side_lanes(from_right, from_left, at % 8, 16)
-            at += 1
+def pack_sides(parity_ref, near_row, far_row, own_ref, sides_ref):
+    odd = jnp.broadcast_to(parity_ref[1], (64, 128)) == 1
+    rows = [ref[r] for ref in (near_row, own_ref, far_row) for r in range(ref.shape[0])]
+    pack_rows(rows, odd, sides_ref)
+
+
+def fill_wide(wide, parts, odd_col, near_ref, far_ref):
+    for ref, count, source, start, block in parts:
+        for r in range(count):
+            if r % 8 == 0:
+                near, far = near_ref[block + r // 8], far_ref[block + r // 8]
+                from_left = jnp.where(odd_col, near, far)
+                from_right = jnp.where(odd_col, far, near)
+            wide[start + r, :, :128] = ref[source + r]
+            wide[start + r, :, 128:] = side_lanes(from_right, from_left, r % 8, 16)
 
 
 def first_blocks(
-    spacing_ref, place_ref, up_ref, own_ref, down_ref, near_ref, far_ref,
+    scalar_ref, near_row, own_ref, far_row, near_ref, far_ref,
     kernel_ref, gain_ref, shift_ref, expand_ref,
     second_ref, message_ref, wide, middle, turned,
 ):
-    row, col = place_ref[0], place_ref[1]
-    members = place_ref[2]
-    weights = (spacing_ref, kernel_ref, gain_ref, shift_ref, expand_ref)
-    fill_wide(wide, (up_ref, own_ref, down_ref), place_ref, near_ref, far_ref)
+    row, col, members = scalar_ref[3], scalar_ref[4], scalar_ref[5]
+    weights = (scalar_ref, kernel_ref, gain_ref, shift_ref, expand_ref)
+    far_start = 48 * lax.rem(row, 2)
+    parts = (
+        (near_row, 16, 0, 48 - far_start, 0),
+        (own_ref, 32, 0, 16, 2),
+        (far_row, 16, 0, far_start, 6),
+    )
+    fill_wide(wide, parts, lax.rem(col, 2) == 1, near_ref, far_ref)
     lane = lax.broadcasted_iota(jnp.int32, (64, 256), 1)
     inside = (lane < 128) | ((lane < 192) & (col < 7)) | ((lane >= 192) & (col > 0))
 
-    def one(i, _):
-        start = i * 24
-        outs = block_rows(wide, [start + b + 8 for b in range(24)], *block_of(0, *weights))
-        for b, out in enumerate(outs):
-            number = 32 * row - 8 + start + b
+    outs = block_rows(wide, [r + 8 for r in range(48)], *block_of(0, *weights))
+    for r, out in enumerate(outs):
+        alive = inside
+        if not 8 <= r < 40:
+            number = 32 * row - 8 + r
             alive = inside & (number >= 0) & (number < 1024)
-            middle[start + b] = jnp.where(alive, out, 0.0).astype(BF)
-        return _
-
-    lax.fori_loop(0, 2, one, 0)
+        middle[r] = jnp.where(alive, out, 0.0).astype(BF)
     rows = [r for b in range(16) for r in (b, b + 16)]
     outs = block_rows(middle, [r + 8 for r in rows], *block_of(1, *weights), narrow=True)
     for r, out in zip(rows, outs):
@@ -171,8 +165,8 @@
         message_ref[lax.bitwise_xor(members, m)] = turned[512 * m : 512 * m + 512].astype(BF)
 
 
-def average(place_ref, second_ref, m0, m1, m2, m3, mean_ref, sides_ref, gathered):
-    members = place_ref[2]
+def average(scalar_ref, second_ref, m0, m1, m2, m3, mean_ref, sides_ref, gathered):
+    members = scalar_ref[5]
     for t, ref in enumerate((m0, m1, m2, m3)):
         gathered[lax.bitwise_xor(members, t)] = ref[...]
     mean = []
@@ -184,41 +178,40 @@
         mirrored = jnp.transpose(jnp.concatenate(blocks, axis=0))[:64]
         mean.append((0.5 * (second_ref[j].astype(F32) + mirrored)).astype(BF))
         mean_ref[j] = mean[j]
-    pack_rows(mean, place_ref, sides_ref)
-
-
-def fill_last(wide, place_ref, mean_ref, near_ref, far_ref):
+    pack_rows(mean, lax.rem(scalar_ref[4], 2) == 1, sides_ref)
+
+
+def last_edge(to_near, scalar_ref, mean_ref, near_ref, far_ref, kernel_ref, *rest):
+    edge_ref, wide = rest[-2:]
+    spacing = scalar_ref[2]
+    odd = lax.rem(scalar_ref[3], 2)
+    up = odd if to_near else 1 - odd
+    down = 1 - up
+    for r in range(8):
+        wide[8 * down + r] = jnp.zeros((64, 256), BF)
+    parts = ((mean_ref, 8, 24 * down, 8 * up, 3 * down),)
+    fill_wide(wide, parts, lax.rem(scalar_ref[4], 2) == 1, near_ref, far_ref)
+    kernel = kernel_ref[2]
+    kernel = jnp.where(up == 1, kernel[:, 128:], kernel[:, :64])
+    start = jnp.where(up == 1, spacing, 8 - spacing)
+    taps = [
+        jnp.dot(kernel, jnp.maximum(wide[start + i], 0), preferred_element_type=F32)
+        for i in range(8)
+    ]
+    for i, conv in enumerate(tap_sums(taps, spacing, True)):
+        edge_ref[i] = conv[0].astype(BF)
+
+
+def last_inner(
+    scalar_ref, mean_ref, near_ref, far_ref, kernel_ref, gain_ref, shift_ref, expand_ref,
+    out_ref, conv_ref, wide,
+):
     for at in range(8):
         wide[at] = jnp.zeros((64, 256), BF)
         wide[40 + at] = jnp.zeros((64, 256), BF)
-    fill_wide(wide, (mean_ref,), place_ref, near_ref, far_ref, 8)
-
-
-def last_edges(
-    spacing_ref, place_ref, mean_ref, near_ref, far_ref, kernel_ref, near_row, far_row, wide
-):
-    spacing, kernel = spacing_ref[2], kernel_ref[2]
-    odd = lax.rem(place_ref[0], 2) == 1
-    fill_last(wide, place_ref, mean_ref, near_ref, far_ref)
-    taps = []
-    for i in range(8):
-        up = jnp.maximum(wide[i + spacing], 0)
-        taps.append(jnp.dot(kernel[:, 128:], up, preferred_element_type=F32))
-        down = jnp.maximum(wide[40 + i - spacing], 0)
-        taps.append(jnp.dot(kernel[:, :64], down, preferred_element_type=F32))
-    sums = tap_sums(taps, spacing, True)
-    for i in range(8):
-        up, down = sums[2 * i][0], sums[2 * i + 1][0]
-        near_row[i] = jnp.where(odd, up, down).astype(BF)
-        far_row[i] = jnp.where(odd, down, up).astype(BF)
-
-
-def last_inner(
-    spacing_ref, place_ref, mean_ref, near_ref, far_ref, kernel_ref, gain_ref, shift_ref, expand_ref,
-    out_ref, conv_ref, wide,
-):
-    fill_last(wide, place_ref, mean_ref, near_ref, far_ref)
-    sums = conv_rows(wide, [r + 8 for r in range(32)], spacing_ref[2], kernel_ref[2], True)
+    parts = ((mean_ref, 32, 0, 8, 0),)
+    fill_wide(wide, parts, lax.rem(scalar_ref[4], 2) == 1, near_ref, far_ref)
+    sums = conv_rows(wide, [r + 8 for r in range(32)], scalar_ref[2], kernel_ref[2], True)
     sums = [row[0] for row in sums]
     for i in range(8):
         conv_ref[i] = sums[i]
@@ -229,10 +222,10 @@
 
 
 def last_outer(
-    place_ref, inner_ref, mean_ref, conv_ref, near_row, far_row, gain_ref, shift_ref, expand_ref,
+    parity_ref, inner_ref, mean_ref, conv_ref, near_row, far_row, gain_ref, shift_ref, expand_ref,
     out_ref,
 ):
-    odd = lax.rem(place_ref[0], 2) == 1
+    odd = jnp.broadcast_to(parity_ref[0], (32, 128)) == 1
     near = [near_row[i].astype(F32) for i in range(8)]
     far = [far_row[i].astype(F32) for i in range(8)]
     sums = [conv_ref[i] + jnp.where(odd, near[i], far[i]) for i in range(8)]
@@ -248,7 +241,10 @@
     rows, cols = lax.axis_size("row"), lax.axis_size("col")
     row, col = lax.axis_index("row"), lax.axis_index("col")
     mixed = lax.bitwise_xor(lax.rem(row, 4), lax.rem(lax.div(row, 4) + col, 4))
-    place = jnp.stack([row, col, mixed]).astype(jnp.int32)
+    scalars = jnp.concatenate([dilations, jnp.stack([row, col, mixed]).astype(jnp.int32)])
+    parity = jnp.broadcast_to(
+        jnp.stack([lax.rem(row, 2), lax.rem(col, 2)]).astype(jnp.int32)[:, None, None], (2, 1, 128)
+    )
     near_rows = [(r, r ^ 1) for r in range(rows)]
     far_rows = [(r, r + 1) for r in range(1, rows - 1, 2)]
     far_rows += [(d, r) for r, d in far_rows]
@@ -259,30 +255,16 @@
     own = jnp.transpose(contact_map, (1, 0, 2))
     odd_row = lax.rem(row, 2)
 
-    def row_rims(depth):
-        def exchange(own, odd):
-            first, last = (32 - depth) * odd, (32 - depth) * (1 - odd)
-            far = lax.ppermute(lax.dynamic_slice_in_dim(own, first, depth, 0), "row", far_rows)
-            near = lax.ppermute(lax.dynamic_slice_in_dim(own, last, depth, 0), "row", near_rows)
-            empty = jnp.zeros((16, 64, 128), BF)
-            spare = 16 - depth
-            return (
-                lax.dynamic_update_slice_in_dim(empty, far, spare * (1 - odd), 0),
-                lax.dynamic_update_slice_in_dim(empty, near, spare * odd, 0),
-            )
-
-        return exchange
-
-    reach = dilations[0] + dilations[1]
-    far_row, near_row = lax.switch(
-        lax.div(reach - 1, 2), [row_rims(depth) for depth in range(2, 17, 2)], own, odd_row
-    )
-    rim = jax.ShapeDtypeStruct((16, 64, 128), BF)
-    above, below, sides = call(
+    def rim(start):
+        return jnp.transpose(lax.dynamic_slice_in_dim(contact_map, start, 16, 1), (1, 0, 2))
+
+    far_row = lax.ppermute(rim(16 * odd_row), "row", far_rows)
+    near_row = lax.ppermute(rim(16 - 16 * odd_row), "row", near_rows)
+    sides = call(
         pack_sides,
-        (rim, rim, jax.ShapeDtypeStruct((2, 8, 64, 128), BF)),
-        (place, near_row, far_row, own),
-        1,
+        jax.ShapeDtypeStruct((2, 8, 64, 128), BF),
+        (parity, near_row, far_row, own),
+        0,
         [],
         0,
         1 << 20,
@@ -298,8 +280,8 @@
     second, messages = call(
         first_blocks,
         (tile, jax.ShapeDtypeStruct((4, 512, 128), BF)),
-        (dilations, place, above, own, below, near, far, *weights),
-        2,
+        (scalars, near_row, own, far_row, near, far, *weights),
+        1,
         [
             pltpu.VMEM((64, 64, 256), BF),
             pltpu.VMEM((48, 64, 256), BF),
@@ -319,7 +301,7 @@
     mean, sides = call(
         average,
         (tile, jax.ShapeDtypeStruct((2, 4, 64, 128), BF)),
-        (place, second, *received),
+        (scalars, second, *received),
         1,
         [pltpu.VMEM((4, 512, 128), BF)],
         0,
@@ -327,33 +309,33 @@
     )
     far = lax.ppermute(sides[1], "col", far_pairs)
     near = lax.ppermute(sides[0], "col", near_pairs)
-    wide = [pltpu.VMEM((48, 64, 256), BF)]
-    edge = jax.ShapeDtypeStruct((8, 32, 128), BF)
-    to_near, to_far = call(
-        last_edges,
-        (edge, edge),
-        (dilations, place, mean, near, far, kernel),
-        2,
-        wide,
-        16 * 256 * 64 * 96 * 2,
-        1 << 20,
-    )
+    edge = functools.partial(
+        call,
+        outs=jax.ShapeDtypeStruct((8, 32, 128), BF),
+        n_smem=1,
+        scratch=[pltpu.VMEM((16, 64, 256), BF)],
+        flops=8 * 256 * 64 * 96 * 2,
+        moved=1 << 19,
+    )
+    sources = (scalars, mean, near, far, kernel)
+    to_far = edge(functools.partial(last_edge, False), args=sources)
     far_row = lax.ppermute(to_far, "row", far_rows)
+    to_near = edge(functools.partial(last_edge, True), args=(*sources, to_far))
     near_row = lax.ppermute(to_near, "row", near_rows)
     inner, conv = call(
         last_inner,
         (tile, jax.ShapeDtypeStruct((16, 32, 128), F32)),
-        (dilations, place, mean, near, far, *weights),
-        2,
-        wide,
+        (scalars, mean, near, far, *weights),
+        1,
+        [pltpu.VMEM((48, 64, 256), BF)],
         32 * 256 * 64 * 32 * 20,
         2 << 20,
     )
     out = call(
         last_outer,
         tile,
-        (place, inner, mean, conv, near_row, far_row, gain, shift, out_weight),
-        1,
+        (parity, inner, mean, conv, near_row, far_row, gain, shift, out_weight),
+        0,
         [],
         16 * 256 * 64 * 32 * 2,
         2 << 20,

time: 108 us -> 107 us (level); the launches traced: 106 us -> 106 us
  waiting for transfers between devices: 41.3 us -> 48.3 us
  local copies, waits for them, and re-layouts: 7.32 us -> 3.62 us
  Pallas kernels: 11.3 us -> 10 us
  between operations: 1.54 us -> 0.26 us
    ppermute x2, waiting for transfers between devices: 14.7 us -> 21.6 us  [the longest x1 14.6 us: on_device(): near_row = lax.ppermute(rim(16 - 16 * odd_row), 'row', near_rows)]
    another operation x2 -> x0, local copies, waits for them, and re-layouts: 1.52 us -> none
    dynamic_update_slice x2 -> x0, local copies, waits for them, and re-layouts: 1.38 us -> none  [the longest x1 0.69 us: exchange(): lax.dynamic_update_slice_in_dim(empty, far, spare * (1 - odd), 0)]
    ppermute x1, starting transfers between devices: 4.45 us -> 3.14 us  [on_device(): far_row = lax.ppermute(to_far, 'row', far_rows)]
    pallas_call x6 -> x7, Pallas kernels: 11.3 us -> 10 us  [call(): pl.pallas_call(body, out_shape=outs, in_specs=[SMEM] * n_smem + [VMEM] *...]
  transfers between devices with their start and end apart: 12 -> 12, of which waited for: 7 -> 7; matrix products, arithmetic and copies ran while one was open for 2% -> 1% of each run, Pallas kernels for 2% -> 2%
where the time goes in v9:
time: 107 us; the launch traced here: 106 us
  waiting for transfers between devices  48.3 us (45%)
  starting transfers between devices  44 us (41%)
  Pallas kernels  10 us (9%)
  local copies, waits for them, and re-layouts  3.62 us (3%)
    ppermute x4, starting transfers between devices, on_device(): received.append(lax.ppermute(messages[t], BOTH, pairs))  19.2 us
    ppermute x1, waiting for transfers between devices, on_device(): near_row = lax.ppermute(rim(16 - 16 * odd_row), 'row', near_rows)  14.6 us
    ppermute x4, waiting for transfers between devices, on_device(): received.append(lax.ppermute(messages[t], BOTH, pairs))  13.9 us
    ppermute x1, starting transfers between devices, on_device(): far_row = lax.ppermute(rim(16 * odd_row), 'row', far_rows)  11.2 us
    pallas_call x7, Pallas kernels, call(): pl.pallas_call(body, out_shape=outs, in_specs=[SMEM] * n_smem + [VMEM] *...  10 us
    ppermute x1, waiting for transfers between devices, on_device(): far_row = lax.ppermute(to_far, 'row', far_rows)  7.77 us
    ppermute x1, waiting for transfers between devices, on_device(): far_row = lax.ppermute(rim(16 * odd_row), 'row', far_rows)  7 us
    ppermute x2, starting transfers between devices, on_device(): far = lax.ppermute(sides[1], 'col', far_pairs)  6.15 us
  transfers between devices with their start and end apart: 12, of which 7 were waited for; matrix products, arithmetic and copies ran while one was open for 1% of the time, Pallas kernels for 2%

profile of v9, /device:TPU:25, one launch (start us, length us, event | category | flops | bytes accessed | tf_op | source)
XLA Modules:
  0.0 106.4 jit_solution(9087502178996171186)
XLA Ops:
  0.0 1.2 %copy.27 = bf16[64,32,128]{2,0,1:T(8,128)(2,1)S(1)} copy(bf16[64,32,128]{2,1,0:T(8,128)(2,1)} %param.6) | data formatting | bytes 1048576 | tf_op args[0]
  1.3 11.2 %collective-permute-start.1 = (bf16[16,64,128]{2,1,0:T(8,128)(2,1)S(1)}, bf16[16,64,128]{2,1,0:T(8,128)(2,1)S(1)}, u32[]{:S(2)}, u32[]{:S(2)}) collective-permute-start(bf16[16,64,128]{2,1,0:T(8,128)(2,1)S(1)} %get-tuple-element.21), channel_id=1, source_target_pairs={{8,16},{24,32},{40,48},{56,64},{72,80},{88,96},{104,112},{120,128}... | collective-permute-start | bytes 786440 | tf_op jit(solution)/shard_map/ppermute | solution.py:261
  12.7 7.0 %collective-permute-done.1.far_row = bf16[16,64,128]{2,1,0:T(8,128)(2,1)S(1)} collective-permute-done((bf16[16,64,128]{2,1,0:T(8,128)(2,1)S(1)}, bf16[16,64,128]{2,1,0:T(8,128)(2,1)S(1)}, u32[]{:S(2)}, u32[]{:S(2)}) %collective-permute-start.1) | collective-permute-done | bytes 262176 | tf_op jit(solution)/shard_map/ppermute | solution.py:261
  19.7 14.6 %collective-permute-done.near_row = bf16[16,64,128]{2,1,0:T(8,128)(2,1)S(1)} collective-permute-done((bf16[16,64,128]{2,1,0:T(8,128)(2,1)S(1)}, bf16[16,64,128]{2,1,0:T(8,128)(2,1)S(1)}, u32[]{:S(2)}, u32[]{:S(2)}) %collective-permute-start) | collective-permute-done | bytes 262176 | tf_op jit(solution)/shard_map/ppermute | solution.py:262
  34.4 0.5 shard_map.64
  35.0 4.2 %collective-permute-start.3 = (bf16[8,64,128]{2,1,0:T(8,128)(2,1)S(1)}, bf16[8,64,128]{2,1,0:T(8,128)(2,1)S(1)}, u32[]{:S(2)}, u32[]{:S(2)}) collective-permute-start(bf16[8,64,128]{2,1,0:T(8,128)(2,1)S(1)} %get-tuple-element.25), channel_id=1, source_target_pairs={{1,2},{3,4},{5,6},{2,1},{4,3},{6,5},{9,10},{11,12},{13,14},{10,9},... | collective-permute-start | bytes 393224 | tf_op jit(solution)/shard_map/ppermute | solution.py:272
  39.8 0.4 copy-done.4
  40.3 1.5 %collective-permute-done.3.far_ref = bf16[8,64,128]{2,1,0:T(8,128)(2,1)S(1)} collective-permute-done((bf16[8,64,128]{2,1,0:T(8,128)(2,1)S(1)}, bf16[8,64,128]{2,1,0:T(8,128)(2,1)S(1)}, u32[]{:S(2)}, u32[]{:S(2)}) %collective-permute-start.3) | collective-permute-done | bytes 131104 | tf_op jit(solution)/shard_map/ppermute | solution.py:272
  42.0 3.9 %shard_map.65 = (bf16[32,64,128]{2,1,0:T(8,128)(2,1)S(1)}, bf16[4,512,128]{2,1,0:T(8,128)(2,1)S(1)}) custom-call(s32[6]{0:T(128)S(1)} %pad_add_fusion.1.scalar_ref, bf16[16,64,128]{2,1,0:T(8,128)(2,1)S(1)} %collective-permute-done.near_row, bf16[32,64,128]{2,1,0:T(8,128)(2,1)S(1)} %bitcast.34, bf16[16,64,128]{2,1,0:T(8,128)(2,1)S(1)} %collective-permute-done.1.far_row, ...), custom_call_target="tpu_custom_call" | custom-call | flops 838860800 | bytes 4194304 | tf_op jit(solution)/shard_map/pallas_call | solution.py:20
  46.0 4.9 %collective-permute-start.7 = (bf16[512,128]{1,0:T(8,128)(2,1)S(1)}, bf16[512,128]{1,0:T(8,128)(2,1)S(1)}, u32[]{:S(2)}, u32[]{:S(2)}) collective-permute-start(bf16[512,128]{1,0:T(8,128)(2,1)S(1)} %get-tuple-element.17), channel_id=1, source_target_pairs={{0,24},{1,48},{2,72},{3,96},{4,152},{5,176},{6,200},{7,224},{8,16}... | collective-permute-start | bytes 393224 | tf_op jit(solution)/shard_map/ppermute | solution.py:300
  50.9 8.3 %collective-permute-start.6 = (bf16[512,128]{1,0:T(8,128)(2,1)S(1)}, bf16[512,128]{1,0:T(8,128)(2,1)S(1)}, u32[]{:S(2)}, u32[]{:S(2)}) collective-permute-start(bf16[512,128]{1,0:T(8,128)(2,1)S(1)} %get-tuple-element.18), channel_id=1, source_target_pairs={{0,16},{1,56},{2,64},{3,104},{4,144},{5,184},{6,192},{7,232},{8,24... | collective-permute-start | bytes 393224 | tf_op jit(solution)/shard_map/ppermute | solution.py:300
  59.1 1.5 %collective-permute-start.5 = (bf16[512,128]{1,0:T(8,128)(2,1)S(1)}, bf16[512,128]{1,0:T(8,128)(2,1)S(1)}, u32[]{:S(2)}, u32[]{:S(2)}) collective-permute-start(bf16[512,128]{1,0:T(8,128)(2,1)S(1)} %get-tuple-element.19), channel_id=1, source_target_pairs={{0,8},{1,32},{2,88},{3,112},{4,136},{5,160},{6,216},{7,240},{8,0},... | collective-permute-start | bytes 393224 | tf_op jit(solution)/shard_map/ppermute | solution.py:300
  60.7 4.5 %collective-permute-start.4 = (bf16[512,128]{1,0:T(8,128)(2,1)S(1)}, bf16[512,128]{1,0:T(8,128)(2,1)S(1)}, u32[]{:S(2)}, u32[]{:S(2)}) collective-permute-start(bf16[512,128]{1,0:T(8,128)(2,1)S(1)} %get-tuple-element.20), channel_id=1, source_target_pairs={{0,0},{1,40},{2,80},{3,120},{4,128},{5,168},{6,208},{7,248},{8,8},... | collective-permute-start | bytes 393224 | tf_op jit(solution)/shard_map/ppermute | solution.py:300
  65.2 13.8 %collective-permute-done.6.m2 = bf16[512,128]{1,0:T(8,128)(2,1)S(1)} collective-permute-done((bf16[512,128]{1,0:T(8,128)(2,1)S(1)}, bf16[512,128]{1,0:T(8,128)(2,1)S(1)}, u32[]{:S(2)}, u32[]{:S(2)}) %collective-permute-start.6) | collective-permute-done | bytes 131104 | tf_op jit(solution)/shard_map/ppermute | solution.py:300
  79.1 1.6 %shard_map.66 = (bf16[32,64,128]{2,1,0:T(8,128)(2,1)S(1)}, bf16[2,4,64,128]{3,2,1,0:T(8,128)(2,1)S(1)}) custom-call(s32[6]{0:T(128)S(1)} %pad_add_fusion.1.scalar_ref, bf16[32,64,128]{2,1,0:T(8,128)(2,1)S(1)} %get-tuple-element.11.second_ref, bf16[512,128]{1,0:T(8,128)(2,1)S(1)} %collective-permute-done.4.m0, ...), custom_call_target="tpu_custom_call" | custom-call | bytes 2097152 | tf_op jit(solution)/shard_map/pallas_call | solution.py:20
  80.7 1.9 %collective-permute-start.9 = (bf16[4,64,128]{2,1,0:T(8,128)(2,1)S(1)}, bf16[4,64,128]{2,1,0:T(8,128)(2,1)S(1)}, u32[]{:S(2)}, u32[]{:S(2)}) collective-permute-start(bf16[4,64,128]{2,1,0:T(8,128)(2,1)S(1)} %get-tuple-element.27), channel_id=1, source_target_pairs={{1,2},{3,4},{5,6},{2,1},{4,3},{6,5},{9,10},{11,12},{13,14},{10,9},... | collective-permute-start | bytes 196616 | tf_op jit(solution)/shard_map/ppermute | solution.py:310
  82.8 3.6 %collective-permute-done.9.far_ref = bf16[4,64,128]{2,1,0:T(8,128)(2,1)S(1)} collective-permute-done((bf16[4,64,128]{2,1,0:T(8,128)(2,1)S(1)}, bf16[4,64,128]{2,1,0:T(8,128)(2,1)S(1)}, u32[]{:S(2)}, u32[]{:S(2)}) %collective-permute-start.9) | collective-permute-done | bytes 65568 | tf_op jit(solution)/shard_map/ppermute | solution.py:310
  86.3 1.0 shard_map.68.rest_0_
  87.3 1.0 shard_map.69
  88.4 4.1 %collective-permute-start.10 = (bf16[8,32,128]{2,1,0:T(8,128)(2,1)S(1)}, bf16[8,32,128]{2,1,0:T(8,128)(2,1)S(1)}, u32[]{:S(2)}, u32[]{:S(2)}) collective-permute-start(bf16[8,32,128]{2,1,0:T(8,128)(2,1)S(1)} %shard_map.69), channel_id=1, source_target_pairs={{0,8},{8,0},{16,24},{24,16},{32,40},{40,32},{48,56},{56,48},{64,72... | collective-permute-start | bytes 196616 | tf_op jit(solution)/shard_map/ppermute | solution.py:324
  92.4 3.1 %collective-permute-start.11 = (bf16[8,32,128]{2,1,0:T(8,128)(2,1)S(1)}, bf16[8,32,128]{2,1,0:T(8,128)(2,1)S(1)}, u32[]{:S(2)}, u32[]{:S(2)}) collective-permute-start(bf16[8,32,128]{2,1,0:T(8,128)(2,1)S(1)} %shard_map.68.rest_0_), channel_id=1, source_target_pairs={{8,16},{24,32},{40,48},{56,64},{72,80},{88,96},{104,112},{120,128}... | collective-permute-start | bytes 196616 | tf_op jit(solution)/shard_map/ppermute | solution.py:322
  95.6 1.7 %shard_map.67 = (bf16[32,64,128]{2,1,0:T(8,128)(2,1)S(1)}, f32[16,32,128]{2,1,0:T(8,128)S(1)}) custom-call(s32[6]{0:T(128)S(1)} %pad_add_fusion.1.scalar_ref, bf16[32,64,128]{2,1,0:T(8,128)(2,1)S(1)} %get-tuple-element.13.mean_ref, bf16[4,64,128]{2,1,0:T(8,128)(2,1)S(1)} %collective-permute-done.8.near_ref, ...), custom_call_target="tpu_custom_call" | custom-call | flops 335544320 | bytes 2097152 | tf_op jit(solution)/shard_map/pallas_call | solution.py:20
  97.3 7.8 %collective-permute-done.11.far_row = bf16[8,32,128]{2,1,0:T(8,128)(2,1)S(1)} collective-permute-done((bf16[8,32,128]{2,1,0:T(8,128)(2,1)S(1)}, bf16[8,32,128]{2,1,0:T(8,128)(2,1)S(1)}, u32[]{:S(2)}, u32[]{:S(2)}) %collective-permute-start.11) | collective-permute-done | bytes 65568 | tf_op jit(solution)/shard_map/ppermute | solution.py:322
  105.3 1.1 %copy.22 = bf16[64,32,128]{2,1,0:T(8,128)(2,1)} copy(bf16[64,32,128]{2,0,1:T(8,128)(2,1)S(1)} %bitcast.35) | data formatting | bytes 1048576 | tf_op jit(solution)/shard_map/transpose | solution.py:343
  (31 shorter events, 1.6 us)
Async XLA Ops:
  1.3 18.4 %collective-permute-start.1 = (bf16[16,64,128]{2,1,0:T(8,128)(2,1)S(1)}, bf16[16,64,128]{2,1,0:T(8,128)(2,1)S(1)}, u32[]{:S(2)}, u32[]{:S(2)}) collective-permute-start(bf16[16,64,128]{2,1,0:T(8,128)(2,1)S(1)} %get-tuple-element.21), channel_id=1, source_target_pairs={{8,16},{24,32},{40,48},{56,64},{72,80},{88,96},{104,112},{120,128}... | collective-permute-start | bytes 786440 | tf_op jit(solution)/shard_map/ppermute | solution.py:261
  12.5 21.8 %collective-permute-start = (bf16[16,64,128]{2,1,0:T(8,128)(2,1)S(1)}, bf16[16,64,128]{2,1,0:T(8,128)(2,1)S(1)}, u32[]{:S(2)}, u32[]{:S(2)}) collective-permute-start(bf16[16,64,128]{2,1,0:T(8,128)(2,1)S(1)} %get-tuple-element.22), channel_id=1, source_target_pairs={{0,8},{8,0},{16,24},{24,16},{32,40},{40,32},{48,56},{56,48},{64,72... | collective-permute-start | bytes 786440 | tf_op jit(solution)/shard_map/ppermute | solution.py:262
  34.9 4.5 %copy-start = (bf16[3,9,32,64]{3,2,1,0:T(8,128)(2,1)S(1)}, bf16[3,9,32,64]{3,2,1,0:T(8,128)(2,1)}, u32[]{:S(2)}) copy-start(bf16[3,9,32,64]{3,2,1,0:T(8,128)(2,1)} %param.8) | copy-start | bytes 331780
  34.9 4.4 %copy-start.1 = (bf16[3,64,32]{1,2,0:T(8,128)(2,1)S(1)}, bf16[3,64,32]{1,2,0:T(8,128)(2,1)}, u32[]{:S(2)}) copy-start(bf16[3,64,32]{1,2,0:T(8,128)(2,1)} %param.11) | copy-start | bytes 36868
  35.0 6.9 %collective-permute-start.3 = (bf16[8,64,128]{2,1,0:T(8,128)(2,1)S(1)}, bf16[8,64,128]{2,1,0:T(8,128)(2,1)S(1)}, u32[]{:S(2)}, u32[]{:S(2)}) collective-permute-start(bf16[8,64,128]{2,1,0:T(8,128)(2,1)S(1)} %get-tuple-element.25), channel_id=1, source_target_pairs={{1,2},{3,4},{5,6},{2,1},{4,3},{6,5},{9,10},{11,12},{13,14},{10,9},... | collective-permute-start | bytes 393224 | tf_op jit(solution)/shard_map/ppermute | solution.py:272
  39.2 2.6 %collective-permute-start.2 = (bf16[8,64,128]{2,1,0:T(8,128)(2,1)S(1)}, bf16[8,64,128]{2,1,0:T(8,128)(2,1)S(1)}, u32[]{:S(2)}, u32[]{:S(2)}) collective-permute-start(bf16[8,64,128]{2,1,0:T(8,128)(2,1)S(1)} %get-tuple-element.26), channel_id=1, source_target_pairs={{0,1},{1,0},{2,3},{3,2},{4,5},{5,4},{6,7},{7,6},{8,9},{9,8},{10,11... | collective-permute-start | bytes 393224 | tf_op jit(solution)/shard_map/ppermute | solution.py:273
  39.6 0.7 copy-start.4
  39.8 2.0 %copy-start.2 = (f32[3,32]{1,0:T(4,128)S(1)}, f32[3,32]{1,0:T(4,128)}, u32[]{:S(2)}) copy-start(f32[3,32]{1,0:T(4,128)} %param.9) | copy-start | bytes 1156
  40.3 1.6 %copy-start.3 = (f32[3,32]{1,0:T(4,128)S(1)}, f32[3,32]{1,0:T(4,128)}, u32[]{:S(2)}) copy-start(f32[3,32]{1,0:T(4,128)} %param.10) | copy-start | bytes 1156
  46.0 19.2 %collective-permute-start.7 = (bf16[512,128]{1,0:T(8,128)(2,1)S(1)}, bf16[512,128]{1,0:T(8,128)(2,1)S(1)}, u32[]{:S(2)}, u32[]{:S(2)}) collective-permute-start(bf16[512,128]{1,0:T(8,128)(2,1)S(1)} %get-tuple-element.17), channel_id=1, source_target_pairs={{0,24},{1,48},{2,72},{3,96},{4,152},{5,176},{6,200},{7,224},{8,16}... | collective-permute-start | bytes 393224 | tf_op jit(solution)/shard_map/ppermute | solution.py:300
  50.9 28.1 %collective-permute-start.6 = (bf16[512,128]{1,0:T(8,128)(2,1)S(1)}, bf16[512,128]{1,0:T(8,128)(2,1)S(1)}, u32[]{:S(2)}, u32[]{:S(2)}) collective-permute-start(bf16[512,128]{1,0:T(8,128)(2,1)S(1)} %get-tuple-element.18), channel_id=1, source_target_pairs={{0,16},{1,56},{2,64},{3,104},{4,144},{5,184},{6,192},{7,232},{8,24... | collective-permute-start | bytes 393224 | tf_op jit(solution)/shard_map/ppermute | solution.py:300
  59.1 19.8 %collective-permute-start.5 = (bf16[512,128]{1,0:T(8,128)(2,1)S(1)}, bf16[512,128]{1,0:T(8,128)(2,1)S(1)}, u32[]{:S(2)}, u32[]{:S(2)}) collective-permute-start(bf16[512,128]{1,0:T(8,128)(2,1)S(1)} %get-tuple-element.19), channel_id=1, source_target_pairs={{0,8},{1,32},{2,88},{3,112},{4,136},{5,160},{6,216},{7,240},{8,0},... | collective-permute-start | bytes 393224 | tf_op jit(solution)/shard_map/ppermute | solution.py:300
  60.7 18.4 %collective-permute-start.4 = (bf16[512,128]{1,0:T(8,128)(2,1)S(1)}, bf16[512,128]{1,0:T(8,128)(2,1)S(1)}, u32[]{:S(2)}, u32[]{:S(2)}) collective-permute-start(bf16[512,128]{1,0:T(8,128)(2,1)S(1)} %get-tuple-element.20), channel_id=1, source_target_pairs={{0,0},{1,40},{2,80},{3,120},{4,128},{5,168},{6,208},{7,248},{8,8},... | collective-permute-start | bytes 393224 | tf_op jit(solution)/shard_map/ppermute | solution.py:300
  80.7 5.6 %collective-permute-start.9 = (bf16[4,64,128]{2,1,0:T(8,128)(2,1)S(1)}, bf16[4,64,128]{2,1,0:T(8,128)(2,1)S(1)}, u32[]{:S(2)}, u32[]{:S(2)}) collective-permute-start(bf16[4,64,128]{2,1,0:T(8,128)(2,1)S(1)} %get-tuple-element.27), channel_id=1, source_target_pairs={{1,2},{3,4},{5,6},{2,1},{4,3},{6,5},{9,10},{11,12},{13,14},{10,9},... | collective-permute-start | bytes 196616 | tf_op jit(solution)/shard_map/ppermute | solution.py:310
  82.7 3.7 %collective-permute-start.8 = (bf16[4,64,128]{2,1,0:T(8,128)(2,1)S(1)}, bf16[4,64,128]{2,1,0:T(8,128)(2,1)S(1)}, u32[]{:S(2)}, u32[]{:S(2)}) collective-permute-start(bf16[4,64,128]{2,1,0:T(8,128)(2,1)S(1)} %get-tuple-element.28), channel_id=1, source_target_pairs={{0,1},{1,0},{2,3},{3,2},{4,5},{5,4},{6,7},{7,6},{8,9},{9,8},{10,11... | collective-permute-start | bytes 196616 | tf_op jit(solution)/shard_map/ppermute | solution.py:311
  88.4 8.9 %collective-permute-start.10 = (bf16[8,32,128]{2,1,0:T(8,128)(2,1)S(1)}, bf16[8,32,128]{2,1,0:T(8,128)(2,1)S(1)}, u32[]{:S(2)}, u32[]{:S(2)}) collective-permute-start(bf16[8,32,128]{2,1,0:T(8,128)(2,1)S(1)} %shard_map.69), channel_id=1, source_target_pairs={{0,8},{8,0},{16,24},{24,16},{32,40},{40,32},{48,56},{56,48},{64,72... | collective-permute-start | bytes 196616 | tf_op jit(solution)/shard_map/ppermute | solution.py:324
  92.4 12.6 %collective-permute-start.11 = (bf16[8,32,128]{2,1,0:T(8,128)(2,1)S(1)}, bf16[8,32,128]{2,1,0:T(8,128)(2,1)S(1)}, u32[]{:S(2)}, u32[]{:S(2)}) collective-permute-start(bf16[8,32,128]{2,1,0:T(8,128)(2,1)S(1)} %shard_map.68.rest_0_), channel_id=1, source_target_pairs={{8,16},{24,32},{40,48},{56,64},{72,80},{88,96},{104,112},{120,128}... | collective-permute-start | bytes 196616 | tf_op jit(solution)/shard_map/ppermute | solution.py:322

commit v10 on v9

--- a/solution.py
+++ b/solution.py
@@ -1,5 +1,3 @@
-import functools
-
 import jax
 import jax.numpy as jnp
 from jax import lax
@@ -165,7 +163,7 @@
         message_ref[lax.bitwise_xor(members, m)] = turned[512 * m : 512 * m + 512].astype(BF)
 
 
-def average(scalar_ref, second_ref, m0, m1, m2, m3, mean_ref, sides_ref, gathered):
+def average(scalar_ref, second_ref, m1, m3, m0, m2, mean_ref, sides_ref, gathered):
     members = scalar_ref[5]
     for t, ref in enumerate((m0, m1, m2, m3)):
         gathered[lax.bitwise_xor(members, t)] = ref[...]
@@ -181,39 +179,44 @@
     pack_rows(mean, lax.rem(scalar_ref[4], 2) == 1, sides_ref)
 
 
-def last_edge(to_near, scalar_ref, mean_ref, near_ref, far_ref, kernel_ref, *rest):
-    edge_ref, wide = rest[-2:]
+def edge_taps(up, spacing, wide, first, above, kernel):
+    kernel = jnp.where(up == 1, kernel[:, 128:], kernel[:, :64])
+    start = jnp.where(up == 1, first - 8 + spacing, above - spacing)
+    return [
+        jnp.dot(kernel, jnp.maximum(wide[start + i], 0), preferred_element_type=F32)
+        for i in range(8)
+    ]
+
+
+def last_far(scalar_ref, mean_ref, near_ref, far_ref, kernel_ref, edge_ref, wide):
     spacing = scalar_ref[2]
-    odd = lax.rem(scalar_ref[3], 2)
-    up = odd if to_near else 1 - odd
-    down = 1 - up
+    down = lax.rem(scalar_ref[3], 2)
+    up = 1 - down
     for r in range(8):
         wide[8 * down + r] = jnp.zeros((64, 256), BF)
     parts = ((mean_ref, 8, 24 * down, 8 * up, 3 * down),)
     fill_wide(wide, parts, lax.rem(scalar_ref[4], 2) == 1, near_ref, far_ref)
-    kernel = kernel_ref[2]
-    kernel = jnp.where(up == 1, kernel[:, 128:], kernel[:, :64])
-    start = jnp.where(up == 1, spacing, 8 - spacing)
-    taps = [
-        jnp.dot(kernel, jnp.maximum(wide[start + i], 0), preferred_element_type=F32)
-        for i in range(8)
-    ]
+    taps = edge_taps(up, spacing, wide, 8, 8, kernel_ref[2])
     for i, conv in enumerate(tap_sums(taps, spacing, True)):
         edge_ref[i] = conv[0].astype(BF)
 
 
 def last_inner(
     scalar_ref, mean_ref, near_ref, far_ref, kernel_ref, gain_ref, shift_ref, expand_ref,
-    out_ref, conv_ref, wide,
+    out_ref, conv_ref, edge_ref, wide,
 ):
     for at in range(8):
         wide[at] = jnp.zeros((64, 256), BF)
         wide[40 + at] = jnp.zeros((64, 256), BF)
     parts = ((mean_ref, 32, 0, 8, 0),)
     fill_wide(wide, parts, lax.rem(scalar_ref[4], 2) == 1, near_ref, far_ref)
-    sums = conv_rows(wide, [r + 8 for r in range(32)], scalar_ref[2], kernel_ref[2], True)
+    spacing = scalar_ref[2]
+    taps = edge_taps(lax.rem(scalar_ref[3], 2), spacing, wide, 8, 40, kernel_ref[2])
+    edge = tap_sums(taps, spacing, True)
+    sums = conv_rows(wide, [r + 8 for r in range(32)], spacing, kernel_ref[2], True)
     sums = [row[0] for row in sums]
     for i in range(8):
+        edge_ref[i] = edge[i][0].astype(BF)
         conv_ref[i] = sums[i]
         conv_ref[8 + i] = sums[24 + i]
     grown = grow(sums[8:24], gain_ref[2], shift_ref[2], expand_ref[2])
@@ -290,18 +293,18 @@
         80 * 256 * 64 * 32 * 20,
         4 << 20,
     )
-    received = []
-    for t in range(4):
+    received = {}
+    for t in (1, 3, 0, 2):
         pairs = []
         for a in range(rows // 4):
             for k in range(4):
                 for b in range(cols):
                     pairs.append(((4 * a + k) * cols + b, (4 * b + (k ^ t ^ (a + b) % 4)) * cols + a))
-        received.append(lax.ppermute(messages[t], BOTH, pairs))
+        received[t] = lax.ppermute(messages[t], BOTH, pairs)
     mean, sides = call(
         average,
         (tile, jax.ShapeDtypeStruct((2, 4, 64, 128), BF)),
-        (scalars, second, *received),
+        (scalars, second, *received.values()),
         1,
         [pltpu.VMEM((4, 512, 128), BF)],
         0,
@@ -309,28 +312,27 @@
     )
     far = lax.ppermute(sides[1], "col", far_pairs)
     near = lax.ppermute(sides[0], "col", near_pairs)
-    edge = functools.partial(
-        call,
-        outs=jax.ShapeDtypeStruct((8, 32, 128), BF),
-        n_smem=1,
-        scratch=[pltpu.VMEM((16, 64, 256), BF)],
-        flops=8 * 256 * 64 * 96 * 2,
-        moved=1 << 19,
-    )
-    sources = (scalars, mean, near, far, kernel)
-    to_far = edge(functools.partial(last_edge, False), args=sources)
+    edge = jax.ShapeDtypeStruct((8, 32, 128), BF)
+    to_far = call(
+        last_far,
+        edge,
+        (scalars, mean, near, far, kernel),
+        1,
+        [pltpu.VMEM((16, 64, 256), BF)],
+        8 * 256 * 64 * 96 * 2,
+        1 << 19,
+    )
     far_row = lax.ppermute(to_far, "row", far_rows)
-    to_near = edge(functools.partial(last_edge, True), args=(*sources, to_far))
-    near_row = lax.ppermute(to_near, "row", near_rows)
-    inner, conv = call(
+    inner, conv, to_near = call(
         last_inner,
-        (tile, jax.ShapeDtypeStruct((16, 32, 128), F32)),
+        (tile, jax.ShapeDtypeStruct((16, 32, 128), F32), edge),
         (scalars, mean, near, far, *weights),
         1,
         [pltpu.VMEM((48, 64, 256), BF)],
         32 * 256 * 64 * 32 * 20,
         2 << 20,
     )
+    near_row = lax.ppermute(to_near, "row", near_rows)
     out = call(
         last_outer,
         tile,

time: 107 us -> 111 us (1.037)
  starting transfers between devices: 44 us -> 46.9 us
  waiting for transfers between devices: 48.3 us -> 50.8 us
    ppermute x1, starting transfers between devices: 3.14 us -> 10.6 us  [on_device(): far_row = lax.ppermute(to_far, 'row', far_rows)]
    ppermute x1, waiting for transfers between devices: 7.77 us -> 1.41 us  [on_device(): far_row = lax.ppermute(to_far, 'row', far_rows)]
    ppermute x1, waiting for transfers between devices: 0.01 us -> 6.3 us  [on_device(): near_row = lax.ppermute(to_near, 'row', near_rows)]
    ppermute x1, starting transfers between devices: 4.07 us -> 0.09 us  [on_device(): near_row = lax.ppermute(to_near, 'row', near_rows)]
    ppermute x4, waiting for transfers between devices: 13.9 us -> 16.4 us  [on_device(): received[t] = lax.ppermute(messages[t], BOTH, pairs)]
    pallas_call x7 -> x6, Pallas kernels: 10 us -> 9.13 us  [call(): pl.pallas_call(body, out_shape=outs, in_specs=[SMEM] * n_smem + [VMEM] *...]
  transfers between devices with their start and end apart: 12 -> 12, of which waited for: 7 -> 8; matrix products, arithmetic and copies ran while one was open for 1% -> 1% of each run, Pallas kernels for 2% -> 2%
where the time goes in v10:
time: 111 us
  waiting for transfers between devices  50.8 us (46%)
  starting transfers between devices  46.9 us (42%)
  Pallas kernels  9.13 us (8%)
  local copies, waits for them, and re-layouts  3.62 us (3%)
    ppermute x4, starting transfers between devices, on_device(): received[t] = lax.ppermute(messages[t], BOTH, pairs)  18.5 us
    ppermute x4, waiting for transfers between devices, on_device(): received[t] = lax.ppermute(messages[t], BOTH, pairs)  16.4 us
    ppermute x1, waiting for transfers between devices, on_device(): near_row = lax.ppermute(rim(16 - 16 * odd_row), 'row', near_rows)  14.6 us
    ppermute x1, starting transfers between devices, on_device(): far_row = lax.ppermute(rim(16 * odd_row), 'row', far_rows)  11.2 us
    ppermute x1, starting transfers between devices, on_device(): far_row = lax.ppermute(to_far, 'row', far_rows)  10.6 us
    pallas_call x6, Pallas kernels, call(): pl.pallas_call(body, out_shape=outs, in_specs=[SMEM] * n_smem + [VMEM] *...  9.13 us
    ppermute x1, waiting for transfers between devices, on_device(): far_row = lax.ppermute(rim(16 * odd_row), 'row', far_rows)  7 us
    ppermute x1, waiting for transfers between devices, on_device(): near_row = lax.ppermute(to_near, 'row', near_rows)  6.3 us
  transfers between devices with their start and end apart: 12, of which 8 were waited for; matrix products, arithmetic and copies ran while one was open for 1% of the time, Pallas kernels for 2%

profile of v10, /device:TPU:25, one launch (start us, length us, event | category | flops | bytes accessed | tf_op | source)
XLA Modules:
  0.0 110.8 jit_solution(11603729513835110363)
XLA Ops:
  0.0 1.2 %copy.27 = bf16[64,32,128]{2,0,1:T(8,128)(2,1)S(1)} copy(bf16[64,32,128]{2,1,0:T(8,128)(2,1)} %param.6) | data formatting | bytes 1048576 | tf_op args[0]
  1.3 11.2 %collective-permute-start.1 = (bf16[16,64,128]{2,1,0:T(8,128)(2,1)S(1)}, bf16[16,64,128]{2,1,0:T(8,128)(2,1)S(1)}, u32[]{:S(2)}, u32[]{:S(2)}) collective-permute-start(bf16[16,64,128]{2,1,0:T(8,128)(2,1)S(1)} %get-tuple-element.23), channel_id=1, source_target_pairs={{8,16},{24,32},{40,48},{56,64},{72,80},{88,96},{104,112},{120,128}... | collective-permute-start | bytes 786440 | tf_op jit(solution)/shard_map/ppermute | solution.py:264
  12.7 7.0 %collective-permute-done.1.far_row = bf16[16,64,128]{2,1,0:T(8,128)(2,1)S(1)} collective-permute-done((bf16[16,64,128]{2,1,0:T(8,128)(2,1)S(1)}, bf16[16,64,128]{2,1,0:T(8,128)(2,1)S(1)}, u32[]{:S(2)}, u32[]{:S(2)}) %collective-permute-start.1) | collective-permute-done | bytes 262176 | tf_op jit(solution)/shard_map/ppermute | solution.py:264
  19.7 14.6 %collective-permute-done.near_row = bf16[16,64,128]{2,1,0:T(8,128)(2,1)S(1)} collective-permute-done((bf16[16,64,128]{2,1,0:T(8,128)(2,1)S(1)}, bf16[16,64,128]{2,1,0:T(8,128)(2,1)S(1)}, u32[]{:S(2)}, u32[]{:S(2)}) %collective-permute-start) | collective-permute-done | bytes 262176 | tf_op jit(solution)/shard_map/ppermute | solution.py:265
  34.4 0.5 shard_map.64
  35.0 4.2 %collective-permute-start.3 = (bf16[8,64,128]{2,1,0:T(8,128)(2,1)S(1)}, bf16[8,64,128]{2,1,0:T(8,128)(2,1)S(1)}, u32[]{:S(2)}, u32[]{:S(2)}) collective-permute-start(bf16[8,64,128]{2,1,0:T(8,128)(2,1)S(1)} %get-tuple-element.27), channel_id=1, source_target_pairs={{1,2},{3,4},{5,6},{2,1},{4,3},{6,5},{9,10},{11,12},{13,14},{10,9},... | collective-permute-start | bytes 393224 | tf_op jit(solution)/shard_map/ppermute | solution.py:275
  39.8 0.4 copy-done.4
  40.3 1.5 %collective-permute-done.3.far_ref = bf16[8,64,128]{2,1,0:T(8,128)(2,1)S(1)} collective-permute-done((bf16[8,64,128]{2,1,0:T(8,128)(2,1)S(1)}, bf16[8,64,128]{2,1,0:T(8,128)(2,1)S(1)}, u32[]{:S(2)}, u32[]{:S(2)}) %collective-permute-start.3) | collective-permute-done | bytes 131104 | tf_op jit(solution)/shard_map/ppermute | solution.py:275
  42.0 3.9 %shard_map.65 = (bf16[32,64,128]{2,1,0:T(8,128)(2,1)S(1)}, bf16[4,512,128]{2,1,0:T(8,128)(2,1)S(1)}) custom-call(s32[6]{0:T(128)S(1)} %pad_add_fusion.1.scalar_ref, bf16[16,64,128]{2,1,0:T(8,128)(2,1)S(1)} %collective-permute-done.near_row, bf16[32,64,128]{2,1,0:T(8,128)(2,1)S(1)} %bitcast.34, bf16[16,64,128]{2,1,0:T(8,128)(2,1)S(1)} %collective-permute-done.1.far_row, ...), custom_call_target="tpu_custom_call" | custom-call | flops 838860800 | bytes 4194304 | tf_op jit(solution)/shard_map/pallas_call | solution.py:18
  46.0 6.5 %collective-permute-start.7 = (bf16[512,128]{1,0:T(8,128)(2,1)S(1)}, bf16[512,128]{1,0:T(8,128)(2,1)S(1)}, u32[]{:S(2)}, u32[]{:S(2)}) collective-permute-start(bf16[512,128]{1,0:T(8,128)(2,1)S(1)} %get-tuple-element.19), channel_id=1, source_target_pairs={{0,16},{1,56},{2,64},{3,104},{4,144},{5,184},{6,192},{7,232},{8,24... | collective-permute-start | bytes 393224 | tf_op jit(solution)/shard_map/ppermute | solution.py:303
  52.4 1.9 %collective-permute-start.6 = (bf16[512,128]{1,0:T(8,128)(2,1)S(1)}, bf16[512,128]{1,0:T(8,128)(2,1)S(1)}, u32[]{:S(2)}, u32[]{:S(2)}) collective-permute-start(bf16[512,128]{1,0:T(8,128)(2,1)S(1)} %get-tuple-element.20), channel_id=1, source_target_pairs={{0,0},{1,40},{2,80},{3,120},{4,128},{5,168},{6,208},{7,248},{8,8},... | collective-permute-start | bytes 393224 | tf_op jit(solution)/shard_map/ppermute | solution.py:303
  54.4 7.2 %collective-permute-start.5 = (bf16[512,128]{1,0:T(8,128)(2,1)S(1)}, bf16[512,128]{1,0:T(8,128)(2,1)S(1)}, u32[]{:S(2)}, u32[]{:S(2)}) collective-permute-start(bf16[512,128]{1,0:T(8,128)(2,1)S(1)} %get-tuple-element.21), channel_id=1, source_target_pairs={{0,24},{1,48},{2,72},{3,96},{4,152},{5,176},{6,200},{7,224},{8,16}... | collective-permute-start | bytes 393224 | tf_op jit(solution)/shard_map/ppermute | solution.py:303
  61.6 2.9 %collective-permute-start.4 = (bf16[512,128]{1,0:T(8,128)(2,1)S(1)}, bf16[512,128]{1,0:T(8,128)(2,1)S(1)}, u32[]{:S(2)}, u32[]{:S(2)}) collective-permute-start(bf16[512,128]{1,0:T(8,128)(2,1)S(1)} %get-tuple-element.22), channel_id=1, source_target_pairs={{0,8},{1,32},{2,88},{3,112},{4,136},{5,160},{6,216},{7,240},{8,0},... | collective-permute-start | bytes 393224 | tf_op jit(solution)/shard_map/ppermute | solution.py:303
  64.5 15.4 %collective-permute-done.7.m2 = bf16[512,128]{1,0:T(8,128)(2,1)S(1)} collective-permute-done((bf16[512,128]{1,0:T(8,128)(2,1)S(1)}, bf16[512,128]{1,0:T(8,128)(2,1)S(1)}, u32[]{:S(2)}, u32[]{:S(2)}) %collective-permute-start.7) | collective-permute-done | bytes 131104 | tf_op jit(solution)/shard_map/ppermute | solution.py:303
  79.9 1.0 collective-permute-done.6.m0
  80.9 1.6 %shard_map.66 = (bf16[32,64,128]{2,1,0:T(8,128)(2,1)S(1)}, bf16[2,4,64,128]{3,2,1,0:T(8,128)(2,1)S(1)}) custom-call(s32[6]{0:T(128)S(1)} %pad_add_fusion.1.scalar_ref, bf16[32,64,128]{2,1,0:T(8,128)(2,1)S(1)} %get-tuple-element.12.second_ref, bf16[512,128]{1,0:T(8,128)(2,1)S(1)} %collective-permute-done.4.m1, ...), custom_call_target="tpu_custom_call" | custom-call | bytes 2097152 | tf_op jit(solution)/shard_map/pallas_call | solution.py:18
  82.6 1.9 %collective-permute-start.9 = (bf16[4,64,128]{2,1,0:T(8,128)(2,1)S(1)}, bf16[4,64,128]{2,1,0:T(8,128)(2,1)S(1)}, u32[]{:S(2)}, u32[]{:S(2)}) collective-permute-start(bf16[4,64,128]{2,1,0:T(8,128)(2,1)S(1)} %get-tuple-element.29), channel_id=1, source_target_pairs={{1,2},{3,4},{5,6},{2,1},{4,3},{6,5},{9,10},{11,12},{13,14},{10,9},... | collective-permute-start | bytes 196616 | tf_op jit(solution)/shard_map/ppermute | solution.py:313
  84.6 3.6 %collective-permute-done.9.far_ref = bf16[4,64,128]{2,1,0:T(8,128)(2,1)S(1)} collective-permute-done((bf16[4,64,128]{2,1,0:T(8,128)(2,1)S(1)}, bf16[4,64,128]{2,1,0:T(8,128)(2,1)S(1)}, u32[]{:S(2)}, u32[]{:S(2)}) %collective-permute-start.9) | collective-permute-done | bytes 65568 | tf_op jit(solution)/shard_map/ppermute | solution.py:313
  88.2 1.0 shard_map.68
  89.2 10.6 %collective-permute-start.11 = (bf16[8,32,128]{2,1,0:T(8,128)(2,1)S(1)}, bf16[8,32,128]{2,1,0:T(8,128)(2,1)S(1)}, u32[]{:S(2)}, u32[]{:S(2)}) collective-permute-start(bf16[8,32,128]{2,1,0:T(8,128)(2,1)S(1)} %shard_map.68), channel_id=1, source_target_pairs={{8,16},{24,32},{40,48},{56,64},{72,80},{88,96},{104,112},{120,128}... | collective-permute-start | bytes 196616 | tf_op jit(solution)/shard_map/ppermute | solution.py:325
  99.8 1.8 %shard_map.67 = (bf16[32,64,128]{2,1,0:T(8,128)(2,1)S(1)}, f32[16,32,128]{2,1,0:T(8,128)S(1)}, bf16[8,32,128]{2,1,0:T(8,128)(2,1)S(1)}) custom-call(s32[6]{0:T(128)S(1)} %pad_add_fusion.1.scalar_ref, bf16[32,64,128]{2,1,0:T(8,128)(2,1)S(1)} %get-tuple-element.14.mean_ref, bf16[4,64,128]{2,1,0:T(8,128)(2,1)S(1)} %collective-permute-done.8.near_ref, ...), custom_call_target="tpu_custom_call" | custom-call | flops 335544320 | bytes 2097152 | tf_op jit(solution)/shard_map/pallas_call | solution.py:18
  101.7 1.4 %collective-permute-done.11.far_row = bf16[8,32,128]{2,1,0:T(8,128)(2,1)S(1)} collective-permute-done((bf16[8,32,128]{2,1,0:T(8,128)(2,1)S(1)}, bf16[8,32,128]{2,1,0:T(8,128)(2,1)S(1)}, u32[]{:S(2)}, u32[]{:S(2)}) %collective-permute-start.11) | collective-permute-done | bytes 65568 | tf_op jit(solution)/shard_map/ppermute | solution.py:325
  103.1 6.3 %collective-permute-done.10.near_row = bf16[8,32,128]{2,1,0:T(8,128)(2,1)S(1)} collective-permute-done((bf16[8,32,128]{2,1,0:T(8,128)(2,1)S(1)}, bf16[8,32,128]{2,1,0:T(8,128)(2,1)S(1)}, u32[]{:S(2)}, u32[]{:S(2)}) %collective-permute-start.10) | collective-permute-done | bytes 65568 | tf_op jit(solution)/shard_map/ppermute | solution.py:335
  109.7 1.1 %copy.22 = bf16[64,32,128]{2,1,0:T(8,128)(2,1)} copy(bf16[64,32,128]{2,0,1:T(8,128)(2,1)S(1)} %bitcast.35) | data formatting | bytes 1048576 | tf_op jit(solution)/shard_map/transpose | solution.py:345
  (30 shorter events, 1.6 us)
Async XLA Ops:
  1.3 18.4 %collective-permute-start.1 = (bf16[16,64,128]{2,1,0:T(8,128)(2,1)S(1)}, bf16[16,64,128]{2,1,0:T(8,128)(2,1)S(1)}, u32[]{:S(2)}, u32[]{:S(2)}) collective-permute-start(bf16[16,64,128]{2,1,0:T(8,128)(2,1)S(1)} %get-tuple-element.23), channel_id=1, source_target_pairs={{8,16},{24,32},{40,48},{56,64},{72,80},{88,96},{104,112},{120,128}... | collective-permute-start | bytes 786440 | tf_op jit(solution)/shard_map/ppermute | solution.py:264
  12.5 21.8 %collective-permute-start = (bf16[16,64,128]{2,1,0:T(8,128)(2,1)S(1)}, bf16[16,64,128]{2,1,0:T(8,128)(2,1)S(1)}, u32[]{:S(2)}, u32[]{:S(2)}) collective-permute-start(bf16[16,64,128]{2,1,0:T(8,128)(2,1)S(1)} %get-tuple-element.24), channel_id=1, source_target_pairs={{0,8},{8,0},{16,24},{24,16},{32,40},{40,32},{48,56},{56,48},{64,72... | collective-permute-start | bytes 786440 | tf_op jit(solution)/shard_map/ppermute | solution.py:265
  34.9 4.5 %copy-start = (bf16[3,9,32,64]{3,2,1,0:T(8,128)(2,1)S(1)}, bf16[3,9,32,64]{3,2,1,0:T(8,128)(2,1)}, u32[]{:S(2)}) copy-start(bf16[3,9,32,64]{3,2,1,0:T(8,128)(2,1)} %param.8) | copy-start | bytes 331780
  34.9 4.4 %copy-start.1 = (bf16[3,64,32]{1,2,0:T(8,128)(2,1)S(1)}, bf16[3,64,32]{1,2,0:T(8,128)(2,1)}, u32[]{:S(2)}) copy-start(bf16[3,64,32]{1,2,0:T(8,128)(2,1)} %param.11) | copy-start | bytes 36868
  35.0 6.9 %collective-permute-start.3 = (bf16[8,64,128]{2,1,0:T(8,128)(2,1)S(1)}, bf16[8,64,128]{2,1,0:T(8,128)(2,1)S(1)}, u32[]{:S(2)}, u32[]{:S(2)}) collective-permute-start(bf16[8,64,128]{2,1,0:T(8,128)(2,1)S(1)} %get-tuple-element.27), channel_id=1, source_target_pairs={{1,2},{3,4},{5,6},{2,1},{4,3},{6,5},{9,10},{11,12},{13,14},{10,9},... | collective-permute-start | bytes 393224 | tf_op jit(solution)/shard_map/ppermute | solution.py:275
  39.2 2.6 %collective-permute-start.2 = (bf16[8,64,128]{2,1,0:T(8,128)(2,1)S(1)}, bf16[8,64,128]{2,1,0:T(8,128)(2,1)S(1)}, u32[]{:S(2)}, u32[]{:S(2)}) collective-permute-start(bf16[8,64,128]{2,1,0:T(8,128)(2,1)S(1)} %get-tuple-element.28), channel_id=1, source_target_pairs={{0,1},{1,0},{2,3},{3,2},{4,5},{5,4},{6,7},{7,6},{8,9},{9,8},{10,11... | collective-permute-start | bytes 393224 | tf_op jit(solution)/shard_map/ppermute | solution.py:276
  39.6 0.7 copy-start.4
  39.8 2.0 %copy-start.2 = (f32[3,32]{1,0:T(4,128)S(1)}, f32[3,32]{1,0:T(4,128)}, u32[]{:S(2)}) copy-start(f32[3,32]{1,0:T(4,128)} %param.9) | copy-start | bytes 1156
  40.3 1.6 %copy-start.3 = (f32[3,32]{1,0:T(4,128)S(1)}, f32[3,32]{1,0:T(4,128)}, u32[]{:S(2)}) copy-start(f32[3,32]{1,0:T(4,128)} %param.10) | copy-start | bytes 1156
  46.0 34.0 %collective-permute-start.7 = (bf16[512,128]{1,0:T(8,128)(2,1)S(1)}, bf16[512,128]{1,0:T(8,128)(2,1)S(1)}, u32[]{:S(2)}, u32[]{:S(2)}) collective-permute-start(bf16[512,128]{1,0:T(8,128)(2,1)S(1)} %get-tuple-element.19), channel_id=1, source_target_pairs={{0,16},{1,56},{2,64},{3,104},{4,144},{5,184},{6,192},{7,232},{8,24... | collective-permute-start | bytes 393224 | tf_op jit(solution)/shard_map/ppermute | solution.py:303
  52.4 28.5 %collective-permute-start.6 = (bf16[512,128]{1,0:T(8,128)(2,1)S(1)}, bf16[512,128]{1,0:T(8,128)(2,1)S(1)}, u32[]{:S(2)}, u32[]{:S(2)}) collective-permute-start(bf16[512,128]{1,0:T(8,128)(2,1)S(1)} %get-tuple-element.20), channel_id=1, source_target_pairs={{0,0},{1,40},{2,80},{3,120},{4,128},{5,168},{6,208},{7,248},{8,8},... | collective-permute-start | bytes 393224 | tf_op jit(solution)/shard_map/ppermute | solution.py:303
  54.4 26.5 %collective-permute-start.5 = (bf16[512,128]{1,0:T(8,128)(2,1)S(1)}, bf16[512,128]{1,0:T(8,128)(2,1)S(1)}, u32[]{:S(2)}, u32[]{:S(2)}) collective-permute-start(bf16[512,128]{1,0:T(8,128)(2,1)S(1)} %get-tuple-element.21), channel_id=1, source_target_pairs={{0,24},{1,48},{2,72},{3,96},{4,152},{5,176},{6,200},{7,224},{8,16}... | collective-permute-start | bytes 393224 | tf_op jit(solution)/shard_map/ppermute | solution.py:303
  61.6 19.3 %collective-permute-start.4 = (bf16[512,128]{1,0:T(8,128)(2,1)S(1)}, bf16[512,128]{1,0:T(8,128)(2,1)S(1)}, u32[]{:S(2)}, u32[]{:S(2)}) collective-permute-start(bf16[512,128]{1,0:T(8,128)(2,1)S(1)} %get-tuple-element.22), channel_id=1, source_target_pairs={{0,8},{1,32},{2,88},{3,112},{4,136},{5,160},{6,216},{7,240},{8,0},... | collective-permute-start | bytes 393224 | tf_op jit(solution)/shard_map/ppermute | solution.py:303
  82.6 5.6 %collective-permute-start.9 = (bf16[4,64,128]{2,1,0:T(8,128)(2,1)S(1)}, bf16[4,64,128]{2,1,0:T(8,128)(2,1)S(1)}, u32[]{:S(2)}, u32[]{:S(2)}) collective-permute-start(bf16[4,64,128]{2,1,0:T(8,128)(2,1)S(1)} %get-tuple-element.29), channel_id=1, source_target_pairs={{1,2},{3,4},{5,6},{2,1},{4,3},{6,5},{9,10},{11,12},{13,14},{10,9},... | collective-permute-start | bytes 196616 | tf_op jit(solution)/shard_map/ppermute | solution.py:313
  84.5 3.7 %collective-permute-start.8 = (bf16[4,64,128]{2,1,0:T(8,128)(2,1)S(1)}, bf16[4,64,128]{2,1,0:T(8,128)(2,1)S(1)}, u32[]{:S(2)}, u32[]{:S(2)}) collective-permute-start(bf16[4,64,128]{2,1,0:T(8,128)(2,1)S(1)} %get-tuple-element.30), channel_id=1, source_target_pairs={{0,1},{1,0},{2,3},{3,2},{4,5},{5,4},{6,7},{7,6},{8,9},{9,8},{10,11... | collective-permute-start | bytes 196616 | tf_op jit(solution)/shard_map/ppermute | solution.py:314
  89.2 14.0 %collective-permute-start.11 = (bf16[8,32,128]{2,1,0:T(8,128)(2,1)S(1)}, bf16[8,32,128]{2,1,0:T(8,128)(2,1)S(1)}, u32[]{:S(2)}, u32[]{:S(2)}) collective-permute-start(bf16[8,32,128]{2,1,0:T(8,128)(2,1)S(1)} %shard_map.68), channel_id=1, source_target_pairs={{8,16},{24,32},{40,48},{56,64},{72,80},{88,96},{104,112},{120,128}... | collective-permute-start | bytes 196616 | tf_op jit(solution)/shard_map/ppermute | solution.py:325
  101.6 7.8 %collective-permute-start.10 = (bf16[8,32,128]{2,1,0:T(8,128)(2,1)S(1)}, bf16[8,32,128]{2,1,0:T(8,128)(2,1)S(1)}, u32[]{:S(2)}, u32[]{:S(2)}) collective-permute-start(bf16[8,32,128]{2,1,0:T(8,128)(2,1)S(1)} %get-tuple-element.18), channel_id=1, source_target_pairs={{0,8},{8,0},{16,24},{24,16},{32,40},{40,32},{48,56},{56,48},{64,72... | collective-permute-start | bytes 196616 | tf_op jit(solution)/shard_map/ppermute | solution.py:335

commit v11 on v9

--- a/solution.py
+++ b/solution.py
@@ -1,5 +1,3 @@
-import functools
-
 import jax
 import jax.numpy as jnp
 from jax import lax
@@ -181,25 +179,31 @@
     pack_rows(mean, lax.rem(scalar_ref[4], 2) == 1, sides_ref)
 
 
-def last_edge(to_near, scalar_ref, mean_ref, near_ref, far_ref, kernel_ref, *rest):
-    edge_ref, wide = rest[-2:]
-    spacing = scalar_ref[2]
-    odd = lax.rem(scalar_ref[3], 2)
-    up = odd if to_near else 1 - odd
-    down = 1 - up
+def edge_rows(mean_ref, scalar_ref, near_ref, far_ref, wide):
     for r in range(8):
-        wide[8 * down + r] = jnp.zeros((64, 256), BF)
-    parts = ((mean_ref, 8, 24 * down, 8 * up, 3 * down),)
+        wide[r] = jnp.zeros((64, 256), BF)
+        wide[24 + r] = jnp.zeros((64, 256), BF)
+    parts = ((mean_ref, 8, 0, 8, 0), (mean_ref, 8, 24, 16, 3))
     fill_wide(wide, parts, lax.rem(scalar_ref[4], 2) == 1, near_ref, far_ref)
-    kernel = kernel_ref[2]
-    kernel = jnp.where(up == 1, kernel[:, 128:], kernel[:, :64])
-    start = jnp.where(up == 1, spacing, 8 - spacing)
-    taps = [
-        jnp.dot(kernel, jnp.maximum(wide[start + i], 0), preferred_element_type=F32)
-        for i in range(8)
-    ]
-    for i, conv in enumerate(tap_sums(taps, spacing, True)):
-        edge_ref[i] = conv[0].astype(BF)
+
+
+def last_edges(
+    scalar_ref, mean_ref, near_ref, far_ref, kernel_ref, to_far_ref, to_near_ref, wide
+):
+    spacing, kernel = scalar_ref[2], kernel_ref[2]
+    odd = lax.rem(scalar_ref[3], 2) == 1
+    edge_rows(mean_ref, scalar_ref, near_ref, far_ref, wide)
+    taps = []
+    for i in range(8):
+        up = jnp.maximum(wide[i + spacing], 0)
+        taps.append(jnp.dot(kernel[:, 128:], up, preferred_element_type=F32))
+        down = jnp.maximum(wide[24 + i - spacing], 0)
+        taps.append(jnp.dot(kernel[:, :64], down, preferred_element_type=F32))
+    sums = tap_sums(taps, spacing, True)
+    for i in range(8):
+        up, down = sums[2 * i][0], sums[2 * i + 1][0]
+        to_far_ref[i] = jnp.where(odd, down, up).astype(BF)
+        to_near_ref[i] = jnp.where(odd, up, down).astype(BF)
 
 
 def last_inner(
@@ -222,7 +226,7 @@
 
 
 def last_outer(
-    parity_ref, inner_ref, mean_ref, conv_ref, near_row, far_row, gain_ref, shift_ref, expand_ref,
+    parity_ref, inner_ref, mean_ref, conv_ref, far_row, near_row, gain_ref, shift_ref, expand_ref,
     out_ref,
 ):
     odd = jnp.broadcast_to(parity_ref[0], (32, 128)) == 1
@@ -309,18 +313,17 @@
     )
     far = lax.ppermute(sides[1], "col", far_pairs)
     near = lax.ppermute(sides[0], "col", near_pairs)
-    edge = functools.partial(
-        call,
-        outs=jax.ShapeDtypeStruct((8, 32, 128), BF),
-        n_smem=1,
-        scratch=[pltpu.VMEM((16, 64, 256), BF)],
-        flops=8 * 256 * 64 * 96 * 2,
-        moved=1 << 19,
-    )
-    sources = (scalars, mean, near, far, kernel)
-    to_far = edge(functools.partial(last_edge, False), args=sources)
+    edge = jax.ShapeDtypeStruct((8, 32, 128), BF)
+    to_far, to_near = call(
+        last_edges,
+        (edge, edge),
+        (scalars, mean, near, far, kernel),
+        1,
+        [pltpu.VMEM((32, 64, 256), BF)],
+        16 * 256 * 64 * 96 * 2,
+        1 << 19,
+    )
     far_row = lax.ppermute(to_far, "row", far_rows)
-    to_near = edge(functools.partial(last_edge, True), args=(*sources, to_far))
     near_row = lax.ppermute(to_near, "row", near_rows)
     inner, conv = call(
         last_inner,
@@ -334,7 +337,7 @@
     out = call(
         last_outer,
         tile,
-        (parity, inner, mean, conv, near_row, far_row, gain, shift, out_weight),
+        (parity, inner, mean, conv, far_row, near_row, gain, shift, out_weight),
         0,
         [],
         16 * 256 * 64 * 32 * 2,

time: 107 us -> 105 us (0.981)
  the two profiles are of different devices: /device:TPU:25 before, /device:TPU:9 now
where the time goes in v11:
time: 105 us
  starting transfers between devices  48.6 us (46%)
  waiting for transfers between devices  43 us (41%)
  Pallas kernels  9.25 us (9%)
  local copies, waits for them, and re-layouts  3.62 us (3%)
    ppermute x4, starting transfers between devices, on_device(): received.append(lax.ppermute(messages[t], BOTH, pairs))  16.8 us
    ppermute x1, waiting for transfers between devices, on_device(): near_row = lax.ppermute(rim(16 - 16 * odd_row), 'row', near_rows)  14.8 us
    ppermute x4, waiting for transfers between devices, on_device(): received.append(lax.ppermute(messages[t], BOTH, pairs))  12.7 us
    ppermute x1, starting transfers between devices, on_device(): far_row = lax.ppermute(rim(16 * odd_row), 'row', far_rows)  10.9 us
    ppermute x1, starting transfers between devices, on_device(): far_row = lax.ppermute(to_far, 'row', far_rows)  10.9 us
    ppermute x2, starting transfers between devices, on_device(): far = lax.ppermute(sides[1], 'col', far_pairs)  9.72 us
    pallas_call x6, Pallas kernels, call(): pl.pallas_call(body, out_shape=outs, in_specs=[SMEM] * n_smem + [VMEM] *...  9.25 us
    ppermute x1, waiting for transfers between devices, on_device(): far_row = lax.ppermute(rim(16 * odd_row), 'row', far_rows)  6.82 us
  transfers between devices with their start and end apart: 12, of which 9 were waited for; matrix products, arithmetic and copies ran while one was open for 1% of the time, Pallas kernels for 2%

profile of v11, /device:TPU:9, one launch (start us, length us, event | category | flops | bytes accessed | tf_op | source)
XLA Modules:
  0.0 104.9 jit_solution(13688131071219752976)
XLA Ops:
  0.0 1.2 %copy.27 = bf16[64,32,128]{2,0,1:T(8,128)(2,1)S(1)} copy(bf16[64,32,128]{2,1,0:T(8,128)(2,1)} %param.6) | data formatting | bytes 1048576 | tf_op args[0]
  1.3 10.9 %collective-permute-start.1 = (bf16[16,64,128]{2,1,0:T(8,128)(2,1)S(1)}, bf16[16,64,128]{2,1,0:T(8,128)(2,1)S(1)}, u32[]{:S(2)}, u32[]{:S(2)}) collective-permute-start(bf16[16,64,128]{2,1,0:T(8,128)(2,1)S(1)} %get-tuple-element.25), channel_id=1, source_target_pairs={{8,16},{24,32},{40,48},{56,64},{72,80},{88,96},{104,112},{120,128}... | collective-permute-start | bytes 786440 | tf_op jit(solution)/shard_map/ppermute | solution.py:265
  12.4 6.8 %collective-permute-done.1.far_row = bf16[16,64,128]{2,1,0:T(8,128)(2,1)S(1)} collective-permute-done((bf16[16,64,128]{2,1,0:T(8,128)(2,1)S(1)}, bf16[16,64,128]{2,1,0:T(8,128)(2,1)S(1)}, u32[]{:S(2)}, u32[]{:S(2)}) %collective-permute-start.1) | collective-permute-done | bytes 262176 | tf_op jit(solution)/shard_map/ppermute | solution.py:265
  19.2 14.8 %collective-permute-done.near_row = bf16[16,64,128]{2,1,0:T(8,128)(2,1)S(1)} collective-permute-done((bf16[16,64,128]{2,1,0:T(8,128)(2,1)S(1)}, bf16[16,64,128]{2,1,0:T(8,128)(2,1)S(1)}, u32[]{:S(2)}, u32[]{:S(2)}) %collective-permute-start) | collective-permute-done | bytes 262176 | tf_op jit(solution)/shard_map/ppermute | solution.py:266
  34.1 0.5 shard_map.64
  34.7 4.2 %collective-permute-start.3 = (bf16[8,64,128]{2,1,0:T(8,128)(2,1)S(1)}, bf16[8,64,128]{2,1,0:T(8,128)(2,1)S(1)}, u32[]{:S(2)}, u32[]{:S(2)}) collective-permute-start(bf16[8,64,128]{2,1,0:T(8,128)(2,1)S(1)} %get-tuple-element.29), channel_id=1, source_target_pairs={{1,2},{3,4},{5,6},{2,1},{4,3},{6,5},{9,10},{11,12},{13,14},{10,9},... | collective-permute-start | bytes 393224 | tf_op jit(solution)/shard_map/ppermute | solution.py:276
  39.5 0.4 copy-done.4
  40.0 1.5 %collective-permute-done.3.far_ref = bf16[8,64,128]{2,1,0:T(8,128)(2,1)S(1)} collective-permute-done((bf16[8,64,128]{2,1,0:T(8,128)(2,1)S(1)}, bf16[8,64,128]{2,1,0:T(8,128)(2,1)S(1)}, u32[]{:S(2)}, u32[]{:S(2)}) %collective-permute-start.3) | collective-permute-done | bytes 131104 | tf_op jit(solution)/shard_map/ppermute | solution.py:276
  41.7 3.9 %shard_map.65 = (bf16[32,64,128]{2,1,0:T(8,128)(2,1)S(1)}, bf16[4,512,128]{2,1,0:T(8,128)(2,1)S(1)}) custom-call(s32[6]{0:T(128)S(1)} %pad_add_fusion.1.scalar_ref, bf16[16,64,128]{2,1,0:T(8,128)(2,1)S(1)} %collective-permute-done.near_row, bf16[32,64,128]{2,1,0:T(8,128)(2,1)S(1)} %bitcast.34, bf16[16,64,128]{2,1,0:T(8,128)(2,1)S(1)} %collective-permute-done.1.far_row, ...), custom_call_target="tpu_custom_call" | custom-call | flops 838860800 | bytes 4194304 | tf_op jit(solution)/shard_map/pallas_call | solution.py:18
  45.7 2.3 %collective-permute-start.7 = (bf16[512,128]{1,0:T(8,128)(2,1)S(1)}, bf16[512,128]{1,0:T(8,128)(2,1)S(1)}, u32[]{:S(2)}, u32[]{:S(2)}) collective-permute-start(bf16[512,128]{1,0:T(8,128)(2,1)S(1)} %get-tuple-element.21), channel_id=1, source_target_pairs={{0,24},{1,48},{2,72},{3,96},{4,152},{5,176},{6,200},{7,224},{8,16}... | collective-permute-start | bytes 393224 | tf_op jit(solution)/shard_map/ppermute | solution.py:304
  48.0 9.6 %collective-permute-start.6 = (bf16[512,128]{1,0:T(8,128)(2,1)S(1)}, bf16[512,128]{1,0:T(8,128)(2,1)S(1)}, u32[]{:S(2)}, u32[]{:S(2)}) collective-permute-start(bf16[512,128]{1,0:T(8,128)(2,1)S(1)} %get-tuple-element.22), channel_id=1, source_target_pairs={{0,16},{1,56},{2,64},{3,104},{4,144},{5,184},{6,192},{7,232},{8,24... | collective-permute-start | bytes 393224 | tf_op jit(solution)/shard_map/ppermute | solution.py:304
  57.6 2.2 %collective-permute-start.5 = (bf16[512,128]{1,0:T(8,128)(2,1)S(1)}, bf16[512,128]{1,0:T(8,128)(2,1)S(1)}, u32[]{:S(2)}, u32[]{:S(2)}) collective-permute-start(bf16[512,128]{1,0:T(8,128)(2,1)S(1)} %get-tuple-element.23), channel_id=1, source_target_pairs={{0,8},{1,32},{2,88},{3,112},{4,136},{5,160},{6,216},{7,240},{8,0},... | collective-permute-start | bytes 393224 | tf_op jit(solution)/shard_map/ppermute | solution.py:304
  59.8 2.6 %collective-permute-start.4 = (bf16[512,128]{1,0:T(8,128)(2,1)S(1)}, bf16[512,128]{1,0:T(8,128)(2,1)S(1)}, u32[]{:S(2)}, u32[]{:S(2)}) collective-permute-start(bf16[512,128]{1,0:T(8,128)(2,1)S(1)} %get-tuple-element.24), channel_id=1, source_target_pairs={{0,0},{1,40},{2,80},{3,120},{4,128},{5,168},{6,208},{7,248},{8,8},... | collective-permute-start | bytes 393224 | tf_op jit(solution)/shard_map/ppermute | solution.py:304
  62.5 1.5 %collective-permute-done.6.m2 = bf16[512,128]{1,0:T(8,128)(2,1)S(1)} collective-permute-done((bf16[512,128]{1,0:T(8,128)(2,1)S(1)}, bf16[512,128]{1,0:T(8,128)(2,1)S(1)}, u32[]{:S(2)}, u32[]{:S(2)}) %collective-permute-start.6) | collective-permute-done | bytes 131104 | tf_op jit(solution)/shard_map/ppermute | solution.py:304
  64.0 8.1 %collective-permute-done.5.m1 = bf16[512,128]{1,0:T(8,128)(2,1)S(1)} collective-permute-done((bf16[512,128]{1,0:T(8,128)(2,1)S(1)}, bf16[512,128]{1,0:T(8,128)(2,1)S(1)}, u32[]{:S(2)}, u32[]{:S(2)}) %collective-permute-start.5) | collective-permute-done | bytes 131104 | tf_op jit(solution)/shard_map/ppermute | solution.py:304
  72.0 3.1 %collective-permute-done.4.m0 = bf16[512,128]{1,0:T(8,128)(2,1)S(1)} collective-permute-done((bf16[512,128]{1,0:T(8,128)(2,1)S(1)}, bf16[512,128]{1,0:T(8,128)(2,1)S(1)}, u32[]{:S(2)}, u32[]{:S(2)}) %collective-permute-start.4) | collective-permute-done | bytes 131104 | tf_op jit(solution)/shard_map/ppermute | solution.py:304
  75.2 1.6 %shard_map.66 = (bf16[32,64,128]{2,1,0:T(8,128)(2,1)S(1)}, bf16[2,4,64,128]{3,2,1,0:T(8,128)(2,1)S(1)}) custom-call(s32[6]{0:T(128)S(1)} %pad_add_fusion.1.scalar_ref, bf16[32,64,128]{2,1,0:T(8,128)(2,1)S(1)} %get-tuple-element.13.second_ref, bf16[512,128]{1,0:T(8,128)(2,1)S(1)} %collective-permute-done.4.m0, ...), custom_call_target="tpu_custom_call" | custom-call | bytes 2097152 | tf_op jit(solution)/shard_map/pallas_call | solution.py:18
  76.8 5.5 %collective-permute-start.9 = (bf16[4,64,128]{2,1,0:T(8,128)(2,1)S(1)}, bf16[4,64,128]{2,1,0:T(8,128)(2,1)S(1)}, u32[]{:S(2)}, u32[]{:S(2)}) collective-permute-start(bf16[4,64,128]{2,1,0:T(8,128)(2,1)S(1)} %get-tuple-element.31), channel_id=1, source_target_pairs={{1,2},{3,4},{5,6},{2,1},{4,3},{6,5},{9,10},{11,12},{13,14},{10,9},... | collective-permute-start | bytes 196616 | tf_op jit(solution)/shard_map/ppermute | solution.py:314
  82.4 1.8 %collective-permute-done.9.far_ref = bf16[4,64,128]{2,1,0:T(8,128)(2,1)S(1)} collective-permute-done((bf16[4,64,128]{2,1,0:T(8,128)(2,1)S(1)}, bf16[4,64,128]{2,1,0:T(8,128)(2,1)S(1)}, u32[]{:S(2)}, u32[]{:S(2)}) %collective-permute-start.9) | collective-permute-done | bytes 65568 | tf_op jit(solution)/shard_map/ppermute | solution.py:314
  84.2 1.3 %shard_map.68 = (bf16[8,32,128]{2,1,0:T(8,128)(2,1)S(1)}, bf16[8,32,128]{2,1,0:T(8,128)(2,1)S(1)}) custom-call(s32[6]{0:T(128)S(1)} %pad_add_fusion.1.scalar_ref, bf16[32,64,128]{2,1,0:T(8,128)(2,1)S(1)} %get-tuple-element.15.mean_ref, bf16[4,64,128]{2,1,0:T(8,128)(2,1)S(1)} %collective-permute-done.8.near_ref, ...), custom_call_target="tpu_custom_call" | custom-call | flops 50331648 | bytes 524288 | tf_op jit(solution)/shard_map/pallas_call | solution.py:18
  85.5 10.9 %collective-permute-start.10 = (bf16[8,32,128]{2,1,0:T(8,128)(2,1)S(1)}, bf16[8,32,128]{2,1,0:T(8,128)(2,1)S(1)}, u32[]{:S(2)}, u32[]{:S(2)}) collective-permute-start(bf16[8,32,128]{2,1,0:T(8,128)(2,1)S(1)} %get-tuple-element.19), channel_id=1, source_target_pairs={{8,16},{24,32},{40,48},{56,64},{72,80},{88,96},{104,112},{120,128}... | collective-permute-start | bytes 196616 | tf_op jit(solution)/shard_map/ppermute | solution.py:326
  96.5 1.7 %shard_map.67 = (bf16[32,64,128]{2,1,0:T(8,128)(2,1)S(1)}, f32[16,32,128]{2,1,0:T(8,128)S(1)}) custom-call(s32[6]{0:T(128)S(1)} %pad_add_fusion.1.scalar_ref, bf16[32,64,128]{2,1,0:T(8,128)(2,1)S(1)} %get-tuple-element.15.mean_ref, bf16[4,64,128]{2,1,0:T(8,128)(2,1)S(1)} %collective-permute-done.8.near_ref, ...), custom_call_target="tpu_custom_call" | custom-call | flops 335544320 | bytes 2097152 | tf_op jit(solution)/shard_map/pallas_call | solution.py:18
  98.3 5.3 %collective-permute-done.11.near_row = bf16[8,32,128]{2,1,0:T(8,128)(2,1)S(1)} collective-permute-done((bf16[8,32,128]{2,1,0:T(8,128)(2,1)S(1)}, bf16[8,32,128]{2,1,0:T(8,128)(2,1)S(1)}, u32[]{:S(2)}, u32[]{:S(2)}) %collective-permute-start.11) | collective-permute-done | bytes 65568 | tf_op jit(solution)/shard_map/ppermute | solution.py:327
  103.8 1.1 %copy.22 = bf16[64,32,128]{2,1,0:T(8,128)(2,1)} copy(bf16[64,32,128]{2,0,1:T(8,128)(2,1)S(1)} %bitcast.35) | data formatting | bytes 1048576 | tf_op jit(solution)/shard_map/transpose | solution.py:346
  (30 shorter events, 1.7 us)
Async XLA Ops:
  1.3 17.9 %collective-permute-start.1 = (bf16[16,64,128]{2,1,0:T(8,128)(2,1)S(1)}, bf16[16,64,128]{2,1,0:T(8,128)(2,1)S(1)}, u32[]{:S(2)}, u32[]{:S(2)}) collective-permute-start(bf16[16,64,128]{2,1,0:T(8,128)(2,1)S(1)} %get-tuple-element.25), channel_id=1, source_target_pairs={{8,16},{24,32},{40,48},{56,64},{72,80},{88,96},{104,112},{120,128}... | collective-permute-start | bytes 786440 | tf_op jit(solution)/shard_map/ppermute | solution.py:265
  12.2 21.8 %collective-permute-start = (bf16[16,64,128]{2,1,0:T(8,128)(2,1)S(1)}, bf16[16,64,128]{2,1,0:T(8,128)(2,1)S(1)}, u32[]{:S(2)}, u32[]{:S(2)}) collective-permute-start(bf16[16,64,128]{2,1,0:T(8,128)(2,1)S(1)} %get-tuple-element.26), channel_id=1, source_target_pairs={{0,8},{8,0},{16,24},{24,16},{32,40},{40,32},{48,56},{56,48},{64,72... | collective-permute-start | bytes 786440 | tf_op jit(solution)/shard_map/ppermute | solution.py:266
  34.6 4.5 %copy-start = (bf16[3,9,32,64]{3,2,1,0:T(8,128)(2,1)S(1)}, bf16[3,9,32,64]{3,2,1,0:T(8,128)(2,1)}, u32[]{:S(2)}) copy-start(bf16[3,9,32,64]{3,2,1,0:T(8,128)(2,1)} %param.8) | copy-start | bytes 331780
  34.7 4.4 %copy-start.1 = (bf16[3,64,32]{1,2,0:T(8,128)(2,1)S(1)}, bf16[3,64,32]{1,2,0:T(8,128)(2,1)}, u32[]{:S(2)}) copy-start(bf16[3,64,32]{1,2,0:T(8,128)(2,1)} %param.11) | copy-start | bytes 36868
  34.7 6.9 %collective-permute-start.3 = (bf16[8,64,128]{2,1,0:T(8,128)(2,1)S(1)}, bf16[8,64,128]{2,1,0:T(8,128)(2,1)S(1)}, u32[]{:S(2)}, u32[]{:S(2)}) collective-permute-start(bf16[8,64,128]{2,1,0:T(8,128)(2,1)S(1)} %get-tuple-element.29), channel_id=1, source_target_pairs={{1,2},{3,4},{5,6},{2,1},{4,3},{6,5},{9,10},{11,12},{13,14},{10,9},... | collective-permute-start | bytes 393224 | tf_op jit(solution)/shard_map/ppermute | solution.py:276
  38.9 2.6 %collective-permute-start.2 = (bf16[8,64,128]{2,1,0:T(8,128)(2,1)S(1)}, bf16[8,64,128]{2,1,0:T(8,128)(2,1)S(1)}, u32[]{:S(2)}, u32[]{:S(2)}) collective-permute-start(bf16[8,64,128]{2,1,0:T(8,128)(2,1)S(1)} %get-tuple-element.30), channel_id=1, source_target_pairs={{0,1},{1,0},{2,3},{3,2},{4,5},{5,4},{6,7},{7,6},{8,9},{9,8},{10,11... | collective-permute-start | bytes 393224 | tf_op jit(solution)/shard_map/ppermute | solution.py:277
  39.3 0.7 copy-start.4
  39.5 2.0 %copy-start.2 = (f32[3,32]{1,0:T(4,128)S(1)}, f32[3,32]{1,0:T(4,128)}, u32[]{:S(2)}) copy-start(f32[3,32]{1,0:T(4,128)} %param.9) | copy-start | bytes 1156
  40.0 1.6 %copy-start.3 = (f32[3,32]{1,0:T(4,128)S(1)}, f32[3,32]{1,0:T(4,128)}, u32[]{:S(2)}) copy-start(f32[3,32]{1,0:T(4,128)} %param.10) | copy-start | bytes 1156
  45.7 16.8 %collective-permute-start.7 = (bf16[512,128]{1,0:T(8,128)(2,1)S(1)}, bf16[512,128]{1,0:T(8,128)(2,1)S(1)}, u32[]{:S(2)}, u32[]{:S(2)}) collective-permute-start(bf16[512,128]{1,0:T(8,128)(2,1)S(1)} %get-tuple-element.21), channel_id=1, source_target_pairs={{0,24},{1,48},{2,72},{3,96},{4,152},{5,176},{6,200},{7,224},{8,16}... | collective-permute-start | bytes 393224 | tf_op jit(solution)/shard_map/ppermute | solution.py:304
  48.0 16.0 %collective-permute-start.6 = (bf16[512,128]{1,0:T(8,128)(2,1)S(1)}, bf16[512,128]{1,0:T(8,128)(2,1)S(1)}, u32[]{:S(2)}, u32[]{:S(2)}) collective-permute-start(bf16[512,128]{1,0:T(8,128)(2,1)S(1)} %get-tuple-element.22), channel_id=1, source_target_pairs={{0,16},{1,56},{2,64},{3,104},{4,144},{5,184},{6,192},{7,232},{8,24... | collective-permute-start | bytes 393224 | tf_op jit(solution)/shard_map/ppermute | solution.py:304
  57.6 14.4 %collective-permute-start.5 = (bf16[512,128]{1,0:T(8,128)(2,1)S(1)}, bf16[512,128]{1,0:T(8,128)(2,1)S(1)}, u32[]{:S(2)}, u32[]{:S(2)}) collective-permute-start(bf16[512,128]{1,0:T(8,128)(2,1)S(1)} %get-tuple-element.23), channel_id=1, source_target_pairs={{0,8},{1,32},{2,88},{3,112},{4,136},{5,160},{6,216},{7,240},{8,0},... | collective-permute-start | bytes 393224 | tf_op jit(solution)/shard_map/ppermute | solution.py:304
  59.8 15.3 %collective-permute-start.4 = (bf16[512,128]{1,0:T(8,128)(2,1)S(1)}, bf16[512,128]{1,0:T(8,128)(2,1)S(1)}, u32[]{:S(2)}, u32[]{:S(2)}) collective-permute-start(bf16[512,128]{1,0:T(8,128)(2,1)S(1)} %get-tuple-element.24), channel_id=1, source_target_pairs={{0,0},{1,40},{2,80},{3,120},{4,128},{5,168},{6,208},{7,248},{8,8},... | collective-permute-start | bytes 393224 | tf_op jit(solution)/shard_map/ppermute | solution.py:304
  76.8 7.4 %collective-permute-start.9 = (bf16[4,64,128]{2,1,0:T(8,128)(2,1)S(1)}, bf16[4,64,128]{2,1,0:T(8,128)(2,1)S(1)}, u32[]{:S(2)}, u32[]{:S(2)}) collective-permute-start(bf16[4,64,128]{2,1,0:T(8,128)(2,1)S(1)} %get-tuple-element.31), channel_id=1, source_target_pairs={{1,2},{3,4},{5,6},{2,1},{4,3},{6,5},{9,10},{11,12},{13,14},{10,9},... | collective-permute-start | bytes 196616 | tf_op jit(solution)/shard_map/ppermute | solution.py:314
  82.3 1.9 %collective-permute-start.8 = (bf16[4,64,128]{2,1,0:T(8,128)(2,1)S(1)}, bf16[4,64,128]{2,1,0:T(8,128)(2,1)S(1)}, u32[]{:S(2)}, u32[]{:S(2)}) collective-permute-start(bf16[4,64,128]{2,1,0:T(8,128)(2,1)S(1)} %get-tuple-element.32), channel_id=1, source_target_pairs={{0,1},{1,0},{2,3},{3,2},{4,5},{5,4},{6,7},{7,6},{8,9},{9,8},{10,11... | collective-permute-start | bytes 196616 | tf_op jit(solution)/shard_map/ppermute | solution.py:315
  85.5 12.8 %collective-permute-start.10 = (bf16[8,32,128]{2,1,0:T(8,128)(2,1)S(1)}, bf16[8,32,128]{2,1,0:T(8,128)(2,1)S(1)}, u32[]{:S(2)}, u32[]{:S(2)}) collective-permute-start(bf16[8,32,128]{2,1,0:T(8,128)(2,1)S(1)} %get-tuple-element.19), channel_id=1, source_target_pairs={{8,16},{24,32},{40,48},{56,64},{72,80},{88,96},{104,112},{120,128}... | collective-permute-start | bytes 196616 | tf_op jit(solution)/shard_map/ppermute | solution.py:326
  96.4 7.2 %collective-permute-start.11 = (bf16[8,32,128]{2,1,0:T(8,128)(2,1)S(1)}, bf16[8,32,128]{2,1,0:T(8,128)(2,1)S(1)}, u32[]{:S(2)}, u32[]{:S(2)}) collective-permute-start(bf16[8,32,128]{2,1,0:T(8,128)(2,1)S(1)} %get-tuple-element.20), channel_id=1, source_target_pairs={{0,8},{8,0},{16,24},{24,16},{32,40},{40,32},{48,56},{56,48},{64,72... | collective-permute-start | bytes 196616 | tf_op jit(solution)/shard_map/ppermute | solution.py:327

commit v12 on v11

--- a/solution.py
+++ b/solution.py
@@ -188,7 +188,7 @@
 
 
 def last_edges(
-    scalar_ref, mean_ref, near_ref, far_ref, kernel_ref, to_far_ref, to_near_ref, wide
+    scalar_ref, mean_ref, near_ref, far_ref, kernel_ref, edges_ref, wide
 ):
     spacing, kernel = scalar_ref[2], kernel_ref[2]
     odd = lax.rem(scalar_ref[3], 2) == 1
@@ -202,8 +202,8 @@
     sums = tap_sums(taps, spacing, True)
     for i in range(8):
         up, down = sums[2 * i][0], sums[2 * i + 1][0]
-        to_far_ref[i] = jnp.where(odd, down, up).astype(BF)
-        to_near_ref[i] = jnp.where(odd, up, down).astype(BF)
+        edges_ref[0, i] = jnp.where(odd, up, down).astype(BF)
+        edges_ref[1, i] = jnp.where(odd, down, up).astype(BF)
 
 
 def last_inner(
@@ -226,11 +226,11 @@
 
 
 def last_outer(
-    parity_ref, inner_ref, mean_ref, conv_ref, far_row, near_row, gain_ref, shift_ref, expand_ref,
+    parity_ref, inner_ref, mean_ref, conv_ref, near_rows, far_row, gain_ref, shift_ref, expand_ref,
     out_ref,
 ):
     odd = jnp.broadcast_to(parity_ref[0], (32, 128)) == 1
-    near = [near_row[i].astype(F32) for i in range(8)]
+    near = [near_rows[0, i].astype(F32) for i in range(8)]
     far = [far_row[i].astype(F32) for i in range(8)]
     sums = [conv_ref[i] + jnp.where(odd, near[i], far[i]) for i in range(8)]
     sums += [conv_ref[8 + i] + jnp.where(odd, far[i], near[i]) for i in range(8)]
@@ -252,6 +252,8 @@
     near_rows = [(r, r ^ 1) for r in range(rows)]
     far_rows = [(r, r + 1) for r in range(1, rows - 1, 2)]
     far_rows += [(d, r) for r, d in far_rows]
+    two_rows = [(r, r + 2) for r in range(0, rows - 2, 2)]
+    two_rows += [(r, r - 2) for r in range(3, rows, 2)]
     near_pairs = [(c, c ^ 1) for c in range(cols)]
     far_pairs = [(c, c + 1) for c in range(1, cols - 1, 2)]
     far_pairs += [(d, c) for c, d in far_pairs]
@@ -313,18 +315,17 @@
     )
     far = lax.ppermute(sides[1], "col", far_pairs)
     near = lax.ppermute(sides[0], "col", near_pairs)
-    edge = jax.ShapeDtypeStruct((8, 32, 128), BF)
-    to_far, to_near = call(
+    edges = call(
         last_edges,
-        (edge, edge),
+        jax.ShapeDtypeStruct((2, 8, 32, 128), BF),
         (scalars, mean, near, far, kernel),
         1,
         [pltpu.VMEM((32, 64, 256), BF)],
         16 * 256 * 64 * 96 * 2,
         1 << 19,
     )
-    far_row = lax.ppermute(to_far, "row", far_rows)
-    near_row = lax.ppermute(to_near, "row", near_rows)
+    swapped = lax.ppermute(edges, "row", near_rows)
+    far_row = lax.ppermute(swapped[1], "row", two_rows)
     inner, conv = call(
         last_inner,
         (tile, jax.ShapeDtypeStruct((16, 32, 128), F32)),
@@ -337,7 +338,7 @@
     out = call(
         last_outer,
         tile,
-        (parity, inner, mean, conv, far_row, near_row, gain, shift, out_weight),
+        (parity, inner, mean, conv, swapped, far_row, gain, shift, out_weight),
         0,
         [],
         16 * 256 * 64 * 32 * 2,

time: 105 us -> 107 us (1.019)
  the two profiles are of different devices: /device:TPU:9 before, /device:TPU:48 now
where the time goes in v12:
time: 107 us
  waiting for transfers between devices  58.8 us (55%)
  starting transfers between devices  34.6 us (32%)
  Pallas kernels  9.26 us (9%)
  local copies, waits for them, and re-layouts  3.63 us (3%)
    ppermute x4, waiting for transfers between devices, on_device(): received.append(lax.ppermute(messages[t], BOTH, pairs))  18.2 us
    ppermute x1, waiting for transfers between devices, on_device(): far_row = lax.ppermute(rim(16 * odd_row), 'row', far_rows)  17.5 us
    ppermute x4, starting transfers between devices, on_device(): received.append(lax.ppermute(messages[t], BOTH, pairs))  13.7 us
    ppermute x1, starting transfers between devices, on_device(): far_row = lax.ppermute(rim(16 * odd_row), 'row', far_rows)  10.3 us
    pallas_call x6, Pallas kernels, call(): pl.pallas_call(body, out_shape=outs, in_specs=[SMEM] * n_smem + [VMEM] *...  9.26 us
    ppermute x1, waiting for transfers between devices, on_device(): swapped = lax.ppermute(edges, 'row', near_rows)  7.76 us
    ppermute x2, waiting for transfers between devices, on_device(): far = lax.ppermute(sides[1], 'col', far_pairs)  5.98 us
    ppermute x1, waiting for transfers between devices, on_device(): near_row = lax.ppermute(rim(16 - 16 * odd_row), 'row', near_rows)  4.74 us
  transfers between devices with their start and end apart: 12, of which 9 were waited for; matrix products, arithmetic and copies ran while one was open for 1% of the time, Pallas kernels for 2%

profile of v12, /device:TPU:48, one launch (start us, length us, event | category | flops | bytes accessed | tf_op | source)
XLA Modules:
  0.0 106.7 jit_solution(9533201489916802250)
XLA Ops:
  0.0 1.2 %copy.27 = bf16[64,32,128]{2,0,1:T(8,128)(2,1)S(1)} copy(bf16[64,32,128]{2,1,0:T(8,128)(2,1)} %param.6) | data formatting | bytes 1048576 | tf_op args[0]
  1.3 10.3 %collective-permute-start.1 = (bf16[16,64,128]{2,1,0:T(8,128)(2,1)S(1)}, bf16[16,64,128]{2,1,0:T(8,128)(2,1)S(1)}, u32[]{:S(2)}, u32[]{:S(2)}) collective-permute-start(bf16[16,64,128]{2,1,0:T(8,128)(2,1)S(1)} %get-tuple-element.21), channel_id=1, source_target_pairs={{8,16},{24,32},{40,48},{56,64},{72,80},{88,96},{104,112},{120,128}... | collective-permute-start | bytes 786440 | tf_op jit(solution)/shard_map/ppermute | solution.py:267
  11.8 17.5 %collective-permute-done.1.far_row = bf16[16,64,128]{2,1,0:T(8,128)(2,1)S(1)} collective-permute-done((bf16[16,64,128]{2,1,0:T(8,128)(2,1)S(1)}, bf16[16,64,128]{2,1,0:T(8,128)(2,1)S(1)}, u32[]{:S(2)}, u32[]{:S(2)}) %collective-permute-start.1) | collective-permute-done | bytes 262176 | tf_op jit(solution)/shard_map/ppermute | solution.py:267
  29.2 4.7 %collective-permute-done.near_row = bf16[16,64,128]{2,1,0:T(8,128)(2,1)S(1)} collective-permute-done((bf16[16,64,128]{2,1,0:T(8,128)(2,1)S(1)}, bf16[16,64,128]{2,1,0:T(8,128)(2,1)S(1)}, u32[]{:S(2)}, u32[]{:S(2)}) %collective-permute-start) | collective-permute-done | bytes 262176 | tf_op jit(solution)/shard_map/ppermute | solution.py:268
  34.7 2.1 %collective-permute-start.3 = (bf16[8,64,128]{2,1,0:T(8,128)(2,1)S(1)}, bf16[8,64,128]{2,1,0:T(8,128)(2,1)S(1)}, u32[]{:S(2)}, u32[]{:S(2)}) collective-permute-start(bf16[8,64,128]{2,1,0:T(8,128)(2,1)S(1)} %get-tuple-element.25), channel_id=1, source_target_pairs={{1,2},{3,4},{5,6},{2,1},{4,3},{6,5},{9,10},{11,12},{13,14},{10,9},... | collective-permute-start | bytes 393224 | tf_op jit(solution)/shard_map/ppermute | solution.py:278
  36.7 0.9 collective-permute-start.2
  38.7 2.4 %collective-permute-done.3.far_ref = bf16[8,64,128]{2,1,0:T(8,128)(2,1)S(1)} collective-permute-done((bf16[8,64,128]{2,1,0:T(8,128)(2,1)S(1)}, bf16[8,64,128]{2,1,0:T(8,128)(2,1)S(1)}, u32[]{:S(2)}, u32[]{:S(2)}) %collective-permute-start.3) | collective-permute-done | bytes 131104 | tf_op jit(solution)/shard_map/ppermute | solution.py:278
  41.2 3.9 %shard_map.65 = (bf16[32,64,128]{2,1,0:T(8,128)(2,1)S(1)}, bf16[4,512,128]{2,1,0:T(8,128)(2,1)S(1)}) custom-call(s32[6]{0:T(128)S(1)} %pad_add_fusion.1.scalar_ref, bf16[16,64,128]{2,1,0:T(8,128)(2,1)S(1)} %collective-permute-done.near_row, bf16[32,64,128]{2,1,0:T(8,128)(2,1)S(1)} %bitcast.36, bf16[16,64,128]{2,1,0:T(8,128)(2,1)S(1)} %collective-permute-done.1.far_row, ...), custom_call_target="tpu_custom_call" | custom-call | flops 838860800 | bytes 4194304 | tf_op jit(solution)/shard_map/pallas_call | solution.py:18
  45.2 3.9 %collective-permute-start.7 = (bf16[512,128]{1,0:T(8,128)(2,1)S(1)}, bf16[512,128]{1,0:T(8,128)(2,1)S(1)}, u32[]{:S(2)}, u32[]{:S(2)}) collective-permute-start(bf16[512,128]{1,0:T(8,128)(2,1)S(1)} %get-tuple-element.17), channel_id=1, source_target_pairs={{0,24},{1,48},{2,72},{3,96},{4,152},{5,176},{6,200},{7,224},{8,16}... | collective-permute-start | bytes 393224 | tf_op jit(solution)/shard_map/ppermute | solution.py:306
  49.1 6.0 %collective-permute-start.6 = (bf16[512,128]{1,0:T(8,128)(2,1)S(1)}, bf16[512,128]{1,0:T(8,128)(2,1)S(1)}, u32[]{:S(2)}, u32[]{:S(2)}) collective-permute-start(bf16[512,128]{1,0:T(8,128)(2,1)S(1)} %get-tuple-element.18), channel_id=1, source_target_pairs={{0,16},{1,56},{2,64},{3,104},{4,144},{5,184},{6,192},{7,232},{8,24... | collective-permute-start | bytes 393224 | tf_op jit(solution)/shard_map/ppermute | solution.py:306
  55.1 3.8 %collective-permute-start.4 = (bf16[512,128]{1,0:T(8,128)(2,1)S(1)}, bf16[512,128]{1,0:T(8,128)(2,1)S(1)}, u32[]{:S(2)}, u32[]{:S(2)}) collective-permute-start(bf16[512,128]{1,0:T(8,128)(2,1)S(1)} %get-tuple-element.20), channel_id=1, source_target_pairs={{0,0},{1,40},{2,80},{3,120},{4,128},{5,168},{6,208},{7,248},{8,8},... | collective-permute-start | bytes 393224 | tf_op jit(solution)/shard_map/ppermute | solution.py:306
  59.0 4.8 %collective-permute-done.6.m2 = bf16[512,128]{1,0:T(8,128)(2,1)S(1)} collective-permute-done((bf16[512,128]{1,0:T(8,128)(2,1)S(1)}, bf16[512,128]{1,0:T(8,128)(2,1)S(1)}, u32[]{:S(2)}, u32[]{:S(2)}) %collective-permute-start.6) | collective-permute-done | bytes 131104 | tf_op jit(solution)/shard_map/ppermute | solution.py:306
  63.8 4.5 %collective-permute-done.5.m1 = bf16[512,128]{1,0:T(8,128)(2,1)S(1)} collective-permute-done((bf16[512,128]{1,0:T(8,128)(2,1)S(1)}, bf16[512,128]{1,0:T(8,128)(2,1)S(1)}, u32[]{:S(2)}, u32[]{:S(2)}) %collective-permute-start.5) | collective-permute-done | bytes 131104 | tf_op jit(solution)/shard_map/ppermute | solution.py:306
  68.3 8.9 %collective-permute-done.4.m0 = bf16[512,128]{1,0:T(8,128)(2,1)S(1)} collective-permute-done((bf16[512,128]{1,0:T(8,128)(2,1)S(1)}, bf16[512,128]{1,0:T(8,128)(2,1)S(1)}, u32[]{:S(2)}, u32[]{:S(2)}) %collective-permute-start.4) | collective-permute-done | bytes 131104 | tf_op jit(solution)/shard_map/ppermute | solution.py:306
  77.2 1.6 %shard_map.66 = (bf16[32,64,128]{2,1,0:T(8,128)(2,1)S(1)}, bf16[2,4,64,128]{3,2,1,0:T(8,128)(2,1)S(1)}) custom-call(s32[6]{0:T(128)S(1)} %pad_add_fusion.1.scalar_ref, bf16[32,64,128]{2,1,0:T(8,128)(2,1)S(1)} %get-tuple-element.11.second_ref, bf16[512,128]{1,0:T(8,128)(2,1)S(1)} %collective-permute-done.4.m0, ...), custom_call_target="tpu_custom_call" | custom-call | bytes 2097152 | tf_op jit(solution)/shard_map/pallas_call | solution.py:18
  78.8 1.9 %collective-permute-start.9 = (bf16[4,64,128]{2,1,0:T(8,128)(2,1)S(1)}, bf16[4,64,128]{2,1,0:T(8,128)(2,1)S(1)}, u32[]{:S(2)}, u32[]{:S(2)}) collective-permute-start(bf16[4,64,128]{2,1,0:T(8,128)(2,1)S(1)} %get-tuple-element.27), channel_id=1, source_target_pairs={{1,2},{3,4},{5,6},{2,1},{4,3},{6,5},{9,10},{11,12},{13,14},{10,9},... | collective-permute-start | bytes 196616 | tf_op jit(solution)/shard_map/ppermute | solution.py:316
  80.8 3.6 %collective-permute-done.9.far_ref = bf16[4,64,128]{2,1,0:T(8,128)(2,1)S(1)} collective-permute-done((bf16[4,64,128]{2,1,0:T(8,128)(2,1)S(1)}, bf16[4,64,128]{2,1,0:T(8,128)(2,1)S(1)}, u32[]{:S(2)}, u32[]{:S(2)}) %collective-permute-start.9) | collective-permute-done | bytes 65568 | tf_op jit(solution)/shard_map/ppermute | solution.py:316
  84.4 1.3 %shard_map.68 = bf16[2,8,32,128]{3,2,1,0:T(8,128)(2,1)S(1)} custom-call(s32[6]{0:T(128)S(1)} %pad_add_fusion.1.scalar_ref, bf16[32,64,128]{2,1,0:T(8,128)(2,1)S(1)} %get-tuple-element.13.mean_ref, bf16[4,64,128]{2,1,0:T(8,128)(2,1)S(1)} %collective-permute-done.8.near_ref, bf16[4,64,128]{2,1,0:T(8,128)(2,1)S(1)} %collective-permute-done.9.far_ref, ...), custom_call_target="tpu_custom_call" | custom-call | flops 50331648 | bytes 524288 | tf_op jit(solution)/shard_map/pallas_call | solution.py:18
  85.6 3.7 %collective-permute-start.10 = (bf16[2,8,32,128]{3,2,1,0:T(8,128)(2,1)S(1)}, bf16[2,8,32,128]{3,2,1,0:T(8,128)(2,1)S(1)}, u32[]{:S(2)}, u32[]{:S(2)}) collective-permute-start(bf16[2,8,32,128]{3,2,1,0:T(8,128)(2,1)S(1)} %shard_map.68), channel_id=1, source_target_pairs={{0,8},{8,0},{16,24},{24,16},{32,40},{40,32},{48,56},{56,48},{64,72... | collective-permute-start | bytes 393224 | tf_op jit(solution)/shard_map/ppermute | solution.py:327
  89.3 7.8 %collective-permute-done.10.near_rows = bf16[2,8,32,128]{3,2,1,0:T(8,128)(2,1)S(1)} collective-permute-done((bf16[2,8,32,128]{3,2,1,0:T(8,128)(2,1)S(1)}, bf16[2,8,32,128]{3,2,1,0:T(8,128)(2,1)S(1)}, u32[]{:S(2)}, u32[]{:S(2)}) %collective-permute-start.10) | collective-permute-done | bytes 131104 | tf_op jit(solution)/shard_map/ppermute | solution.py:327
  97.1 1.9 %collective-permute-start.11 = (bf16[8,32,128]{2,1,0:T(8,128)(2,1)S(1)}, bf16[8,32,128]{2,1,0:T(8,128)(2,1)S(1)}, u32[]{:S(2)}, u32[]{:S(2)}) collective-permute-start(bf16[8,32,128]{2,1,0:T(8,128)(2,1)S(1)} %slice_bitcast_fusion.6), channel_id=1, source_target_pairs={{0,16},{16,32},{32,48},{48,64},{64,80},{80,96},{96,112},{112,128},... | collective-permute-start | bytes 196616 | tf_op jit(solution)/shard_map/ppermute | solution.py:328
  99.0 1.7 %shard_map.67 = (bf16[32,64,128]{2,1,0:T(8,128)(2,1)S(1)}, f32[16,32,128]{2,1,0:T(8,128)S(1)}) custom-call(s32[6]{0:T(128)S(1)} %pad_add_fusion.1.scalar_ref, bf16[32,64,128]{2,1,0:T(8,128)(2,1)S(1)} %get-tuple-element.13.mean_ref, bf16[4,64,128]{2,1,0:T(8,128)(2,1)S(1)} %collective-permute-done.8.near_ref, ...), custom_call_target="tpu_custom_call" | custom-call | flops 335544320 | bytes 2097152 | tf_op jit(solution)/shard_map/pallas_call | solution.py:18
  100.7 4.6 %collective-permute-done.11.far_row = bf16[8,32,128]{2,1,0:T(8,128)(2,1)S(1)} collective-permute-done((bf16[8,32,128]{2,1,0:T(8,128)(2,1)S(1)}, bf16[8,32,128]{2,1,0:T(8,128)(2,1)S(1)}, u32[]{:S(2)}, u32[]{:S(2)}) %collective-permute-start.11) | collective-permute-done | bytes 65568 | tf_op jit(solution)/shard_map/ppermute | solution.py:328
  105.6 1.1 %copy.22 = bf16[64,32,128]{2,1,0:T(8,128)(2,1)} copy(bf16[64,32,128]{2,0,1:T(8,128)(2,1)S(1)} %bitcast.37) | data formatting | bytes 1048576 | tf_op jit(solution)/shard_map/transpose | solution.py:347
  (31 shorter events, 2.5 us)
Async XLA Ops:
  1.3 27.9 %collective-permute-start.1 = (bf16[16,64,128]{2,1,0:T(8,128)(2,1)S(1)}, bf16[16,64,128]{2,1,0:T(8,128)(2,1)S(1)}, u32[]{:S(2)}, u32[]{:S(2)}) collective-permute-start(bf16[16,64,128]{2,1,0:T(8,128)(2,1)S(1)} %get-tuple-element.21), channel_id=1, source_target_pairs={{8,16},{24,32},{40,48},{56,64},{72,80},{88,96},{104,112},{120,128}... | collective-permute-start | bytes 786440 | tf_op jit(solution)/shard_map/ppermute | solution.py:267
  11.6 22.4 %collective-permute-start = (bf16[16,64,128]{2,1,0:T(8,128)(2,1)S(1)}, bf16[16,64,128]{2,1,0:T(8,128)(2,1)S(1)}, u32[]{:S(2)}, u32[]{:S(2)}) collective-permute-start(bf16[16,64,128]{2,1,0:T(8,128)(2,1)S(1)} %get-tuple-element.22), channel_id=1, source_target_pairs={{0,8},{8,0},{16,24},{24,16},{32,40},{40,32},{48,56},{56,48},{64,72... | collective-permute-start | bytes 786440 | tf_op jit(solution)/shard_map/ppermute | solution.py:268
  34.6 3.1 %copy-start = (bf16[3,9,32,64]{3,2,1,0:T(8,128)(2,1)S(1)}, bf16[3,9,32,64]{3,2,1,0:T(8,128)(2,1)}, u32[]{:S(2)}) copy-start(bf16[3,9,32,64]{3,2,1,0:T(8,128)(2,1)} %param.8) | copy-start | bytes 331780
  34.6 3.0 %copy-start.1 = (bf16[3,64,32]{1,2,0:T(8,128)(2,1)S(1)}, bf16[3,64,32]{1,2,0:T(8,128)(2,1)}, u32[]{:S(2)}) copy-start(bf16[3,64,32]{1,2,0:T(8,128)(2,1)} %param.11) | copy-start | bytes 36868
  34.7 6.4 %collective-permute-start.3 = (bf16[8,64,128]{2,1,0:T(8,128)(2,1)S(1)}, bf16[8,64,128]{2,1,0:T(8,128)(2,1)S(1)}, u32[]{:S(2)}, u32[]{:S(2)}) collective-permute-start(bf16[8,64,128]{2,1,0:T(8,128)(2,1)S(1)} %get-tuple-element.25), channel_id=1, source_target_pairs={{1,2},{3,4},{5,6},{2,1},{4,3},{6,5},{9,10},{11,12},{13,14},{10,9},... | collective-permute-start | bytes 393224 | tf_op jit(solution)/shard_map/ppermute | solution.py:278
  36.7 4.4 %collective-permute-start.2 = (bf16[8,64,128]{2,1,0:T(8,128)(2,1)S(1)}, bf16[8,64,128]{2,1,0:T(8,128)(2,1)S(1)}, u32[]{:S(2)}, u32[]{:S(2)}) collective-permute-start(bf16[8,64,128]{2,1,0:T(8,128)(2,1)S(1)} %get-tuple-element.26), channel_id=1, source_target_pairs={{0,1},{1,0},{2,3},{3,2},{4,5},{5,4},{6,7},{7,6},{8,9},{9,8},{10,11... | collective-permute-start | bytes 393224 | tf_op jit(solution)/shard_map/ppermute | solution.py:279
  37.9 0.7 copy-start.4
  38.1 2.9 %copy-start.2 = (f32[3,32]{1,0:T(4,128)S(1)}, f32[3,32]{1,0:T(4,128)}, u32[]{:S(2)}) copy-start(f32[3,32]{1,0:T(4,128)} %param.9) | copy-start | bytes 1156
  38.7 2.5 %copy-start.3 = (f32[3,32]{1,0:T(4,128)S(1)}, f32[3,32]{1,0:T(4,128)}, u32[]{:S(2)}) copy-start(f32[3,32]{1,0:T(4,128)} %param.10) | copy-start | bytes 1156
  45.2 13.7 %collective-permute-start.7 = (bf16[512,128]{1,0:T(8,128)(2,1)S(1)}, bf16[512,128]{1,0:T(8,128)(2,1)S(1)}, u32[]{:S(2)}, u32[]{:S(2)}) collective-permute-start(bf16[512,128]{1,0:T(8,128)(2,1)S(1)} %get-tuple-element.17), channel_id=1, source_target_pairs={{0,24},{1,48},{2,72},{3,96},{4,152},{5,176},{6,200},{7,224},{8,16}... | collective-permute-start | bytes 393224 | tf_op jit(solution)/shard_map/ppermute | solution.py:306
  49.1 14.7 %collective-permute-start.6 = (bf16[512,128]{1,0:T(8,128)(2,1)S(1)}, bf16[512,128]{1,0:T(8,128)(2,1)S(1)}, u32[]{:S(2)}, u32[]{:S(2)}) collective-permute-start(bf16[512,128]{1,0:T(8,128)(2,1)S(1)} %get-tuple-element.18), channel_id=1, source_target_pairs={{0,16},{1,56},{2,64},{3,104},{4,144},{5,184},{6,192},{7,232},{8,24... | collective-permute-start | bytes 393224 | tf_op jit(solution)/shard_map/ppermute | solution.py:306
  55.0 13.3 %collective-permute-start.5 = (bf16[512,128]{1,0:T(8,128)(2,1)S(1)}, bf16[512,128]{1,0:T(8,128)(2,1)S(1)}, u32[]{:S(2)}, u32[]{:S(2)}) collective-permute-start(bf16[512,128]{1,0:T(8,128)(2,1)S(1)} %get-tuple-element.19), channel_id=1, source_target_pairs={{0,8},{1,32},{2,88},{3,112},{4,136},{5,160},{6,216},{7,240},{8,0},... | collective-permute-start | bytes 393224 | tf_op jit(solution)/shard_map/ppermute | solution.py:306
  55.1 22.0 %collective-permute-start.4 = (bf16[512,128]{1,0:T(8,128)(2,1)S(1)}, bf16[512,128]{1,0:T(8,128)(2,1)S(1)}, u32[]{:S(2)}, u32[]{:S(2)}) collective-permute-start(bf16[512,128]{1,0:T(8,128)(2,1)S(1)} %get-tuple-element.20), channel_id=1, source_target_pairs={{0,0},{1,40},{2,80},{3,120},{4,128},{5,168},{6,208},{7,248},{8,8},... | collective-permute-start | bytes 393224 | tf_op jit(solution)/shard_map/ppermute | solution.py:306
  78.8 5.6 %collective-permute-start.9 = (bf16[4,64,128]{2,1,0:T(8,128)(2,1)S(1)}, bf16[4,64,128]{2,1,0:T(8,128)(2,1)S(1)}, u32[]{:S(2)}, u32[]{:S(2)}) collective-permute-start(bf16[4,64,128]{2,1,0:T(8,128)(2,1)S(1)} %get-tuple-element.27), channel_id=1, source_target_pairs={{1,2},{3,4},{5,6},{2,1},{4,3},{6,5},{9,10},{11,12},{13,14},{10,9},... | collective-permute-start | bytes 196616 | tf_op jit(solution)/shard_map/ppermute | solution.py:316
  80.7 3.7 %collective-permute-start.8 = (bf16[4,64,128]{2,1,0:T(8,128)(2,1)S(1)}, bf16[4,64,128]{2,1,0:T(8,128)(2,1)S(1)}, u32[]{:S(2)}, u32[]{:S(2)}) collective-permute-start(bf16[4,64,128]{2,1,0:T(8,128)(2,1)S(1)} %get-tuple-element.28), channel_id=1, source_target_pairs={{0,1},{1,0},{2,3},{3,2},{4,5},{5,4},{6,7},{7,6},{8,9},{9,8},{10,11... | collective-permute-start | bytes 196616 | tf_op jit(solution)/shard_map/ppermute | solution.py:317
  85.6 11.4 %collective-permute-start.10 = (bf16[2,8,32,128]{3,2,1,0:T(8,128)(2,1)S(1)}, bf16[2,8,32,128]{3,2,1,0:T(8,128)(2,1)S(1)}, u32[]{:S(2)}, u32[]{:S(2)}) collective-permute-start(bf16[2,8,32,128]{3,2,1,0:T(8,128)(2,1)S(1)} %shard_map.68), channel_id=1, source_target_pairs={{0,8},{8,0},{16,24},{24,16},{32,40},{40,32},{48,56},{56,48},{64,72... | collective-permute-start | bytes 393224 | tf_op jit(solution)/shard_map/ppermute | solution.py:327
  97.1 8.3 %collective-permute-start.11 = (bf16[8,32,128]{2,1,0:T(8,128)(2,1)S(1)}, bf16[8,32,128]{2,1,0:T(8,128)(2,1)S(1)}, u32[]{:S(2)}, u32[]{:S(2)}) collective-permute-start(bf16[8,32,128]{2,1,0:T(8,128)(2,1)S(1)} %slice_bitcast_fusion.6), channel_id=1, source_target_pairs={{0,16},{16,32},{32,48},{48,64},{64,80},{80,96},{96,112},{112,128},... | collective-permute-start | bytes 196616 | tf_op jit(solution)/shard_map/ppermute | solution.py:328

commit v13 on v11

--- a/solution.py
+++ b/solution.py
@@ -163,7 +163,7 @@
         message_ref[lax.bitwise_xor(members, m)] = turned[512 * m : 512 * m + 512].astype(BF)
 
 
-def average(scalar_ref, second_ref, m0, m1, m2, m3, mean_ref, sides_ref, gathered):
+def average(scalar_ref, second_ref, m0, m2, m1, m3, mean_ref, sides_ref, gathered):
     members = scalar_ref[5]
     for t, ref in enumerate((m0, m1, m2, m3)):
         gathered[lax.bitwise_xor(members, t)] = ref[...]
@@ -305,7 +305,7 @@
     mean, sides = call(
         average,
         (tile, jax.ShapeDtypeStruct((2, 4, 64, 128), BF)),
-        (scalars, second, *received),
+        (scalars, second, received[0], received[2], received[1], received[3]),
         1,
         [pltpu.VMEM((4, 512, 128), BF)],
         0,

time: 105 us -> 106 us (level)
  the two profiles are of different devices: /device:TPU:9 before, /device:TPU:25 now
where the time goes in v13:
time: 106 us
  starting transfers between devices  46.4 us (44%)
  waiting for transfers between devices  46 us (43%)
  Pallas kernels  9.26 us (9%)
  local copies, waits for them, and re-layouts  3.62 us (3%)
    ppermute x4, starting transfers between devices, on_device(): received.append(lax.ppermute(messages[t], BOTH, pairs))  18.5 us
    ppermute x1, waiting for transfers between devices, on_device(): near_row = lax.ppermute(rim(16 - 16 * odd_row), 'row', near_rows)  14.6 us
    ppermute x4, waiting for transfers between devices, on_device(): received.append(lax.ppermute(messages[t], BOTH, pairs))  13.4 us
    ppermute x1, starting transfers between devices, on_device(): far_row = lax.ppermute(rim(16 * odd_row), 'row', far_rows)  11.2 us
    ppermute x1, starting transfers between devices, on_device(): far_row = lax.ppermute(to_far, 'row', far_rows)  10.1 us
    pallas_call x6, Pallas kernels, call(): pl.pallas_call(body, out_shape=outs, in_specs=[SMEM] * n_smem + [VMEM] *...  9.26 us
    ppermute x1, waiting for transfers between devices, on_device(): far_row = lax.ppermute(rim(16 * odd_row), 'row', far_rows)  7 us
    ppermute x2, starting transfers between devices, on_device(): far = lax.ppermute(sides[1], 'col', far_pairs)  6.15 us
  transfers between devices with their start and end apart: 12, of which 8 were waited for; matrix products, arithmetic and copies ran while one was open for 1% of the time, Pallas kernels for 2%

profile of v13, /device:TPU:25, one launch (start us, length us, event | category | flops | bytes accessed | tf_op | source)
XLA Modules:
  0.0 105.7 jit_solution(14301641684173543019)
XLA Ops:
  0.0 1.2 %copy.27 = bf16[64,32,128]{2,0,1:T(8,128)(2,1)S(1)} copy(bf16[64,32,128]{2,1,0:T(8,128)(2,1)} %param.6) | data formatting | bytes 1048576 | tf_op args[0]
  1.3 11.2 %collective-permute-start.1 = (bf16[16,64,128]{2,1,0:T(8,128)(2,1)S(1)}, bf16[16,64,128]{2,1,0:T(8,128)(2,1)S(1)}, u32[]{:S(2)}, u32[]{:S(2)}) collective-permute-start(bf16[16,64,128]{2,1,0:T(8,128)(2,1)S(1)} %get-tuple-element.25), channel_id=1, source_target_pairs={{8,16},{24,32},{40,48},{56,64},{72,80},{88,96},{104,112},{120,128}... | collective-permute-start | bytes 786440 | tf_op jit(solution)/shard_map/ppermute | solution.py:265
  12.7 7.0 %collective-permute-done.1.far_row = bf16[16,64,128]{2,1,0:T(8,128)(2,1)S(1)} collective-permute-done((bf16[16,64,128]{2,1,0:T(8,128)(2,1)S(1)}, bf16[16,64,128]{2,1,0:T(8,128)(2,1)S(1)}, u32[]{:S(2)}, u32[]{:S(2)}) %collective-permute-start.1) | collective-permute-done | bytes 262176 | tf_op jit(solution)/shard_map/ppermute | solution.py:265
  19.7 14.6 %collective-permute-done.near_row = bf16[16,64,128]{2,1,0:T(8,128)(2,1)S(1)} collective-permute-done((bf16[16,64,128]{2,1,0:T(8,128)(2,1)S(1)}, bf16[16,64,128]{2,1,0:T(8,128)(2,1)S(1)}, u32[]{:S(2)}, u32[]{:S(2)}) %collective-permute-start) | collective-permute-done | bytes 262176 | tf_op jit(solution)/shard_map/ppermute | solution.py:266
  34.4 0.5 shard_map.64
  35.0 4.2 %collective-permute-start.3 = (bf16[8,64,128]{2,1,0:T(8,128)(2,1)S(1)}, bf16[8,64,128]{2,1,0:T(8,128)(2,1)S(1)}, u32[]{:S(2)}, u32[]{:S(2)}) collective-permute-start(bf16[8,64,128]{2,1,0:T(8,128)(2,1)S(1)} %get-tuple-element.29), channel_id=1, source_target_pairs={{1,2},{3,4},{5,6},{2,1},{4,3},{6,5},{9,10},{11,12},{13,14},{10,9},... | collective-permute-start | bytes 393224 | tf_op jit(solution)/shard_map/ppermute | solution.py:276
  39.8 0.4 copy-done.4
  40.3 1.5 %collective-permute-done.3.far_ref = bf16[8,64,128]{2,1,0:T(8,128)(2,1)S(1)} collective-permute-done((bf16[8,64,128]{2,1,0:T(8,128)(2,1)S(1)}, bf16[8,64,128]{2,1,0:T(8,128)(2,1)S(1)}, u32[]{:S(2)}, u32[]{:S(2)}) %collective-permute-start.3) | collective-permute-done | bytes 131104 | tf_op jit(solution)/shard_map/ppermute | solution.py:276
  42.0 3.9 %shard_map.65 = (bf16[32,64,128]{2,1,0:T(8,128)(2,1)S(1)}, bf16[4,512,128]{2,1,0:T(8,128)(2,1)S(1)}) custom-call(s32[6]{0:T(128)S(1)} %pad_add_fusion.1.scalar_ref, bf16[16,64,128]{2,1,0:T(8,128)(2,1)S(1)} %collective-permute-done.near_row, bf16[32,64,128]{2,1,0:T(8,128)(2,1)S(1)} %bitcast.34, bf16[16,64,128]{2,1,0:T(8,128)(2,1)S(1)} %collective-permute-done.1.far_row, ...), custom_call_target="tpu_custom_call" | custom-call | flops 838860800 | bytes 4194304 | tf_op jit(solution)/shard_map/pallas_call | solution.py:18
  46.0 4.9 %collective-permute-start.7 = (bf16[512,128]{1,0:T(8,128)(2,1)S(1)}, bf16[512,128]{1,0:T(8,128)(2,1)S(1)}, u32[]{:S(2)}, u32[]{:S(2)}) collective-permute-start(bf16[512,128]{1,0:T(8,128)(2,1)S(1)} %get-tuple-element.21), channel_id=1, source_target_pairs={{0,24},{1,48},{2,72},{3,96},{4,152},{5,176},{6,200},{7,224},{8,16}... | collective-permute-start | bytes 393224 | tf_op jit(solution)/shard_map/ppermute | solution.py:304
  51.0 9.0 %collective-permute-start.5 = (bf16[512,128]{1,0:T(8,128)(2,1)S(1)}, bf16[512,128]{1,0:T(8,128)(2,1)S(1)}, u32[]{:S(2)}, u32[]{:S(2)}) collective-permute-start(bf16[512,128]{1,0:T(8,128)(2,1)S(1)} %get-tuple-element.23), channel_id=1, source_target_pairs={{0,16},{1,56},{2,64},{3,104},{4,144},{5,184},{6,192},{7,232},{8,24... | collective-permute-start | bytes 393224 | tf_op jit(solution)/shard_map/ppermute | solution.py:304
  60.0 4.5 %collective-permute-start.4 = (bf16[512,128]{1,0:T(8,128)(2,1)S(1)}, bf16[512,128]{1,0:T(8,128)(2,1)S(1)}, u32[]{:S(2)}, u32[]{:S(2)}) collective-permute-start(bf16[512,128]{1,0:T(8,128)(2,1)S(1)} %get-tuple-element.24), channel_id=1, source_target_pairs={{0,0},{1,40},{2,80},{3,120},{4,128},{5,168},{6,208},{7,248},{8,8},... | collective-permute-start | bytes 393224 | tf_op jit(solution)/shard_map/ppermute | solution.py:304
  64.5 11.9 %collective-permute-done.5.m2 = bf16[512,128]{1,0:T(8,128)(2,1)S(1)} collective-permute-done((bf16[512,128]{1,0:T(8,128)(2,1)S(1)}, bf16[512,128]{1,0:T(8,128)(2,1)S(1)}, u32[]{:S(2)}, u32[]{:S(2)}) %collective-permute-start.5) | collective-permute-done | bytes 131104 | tf_op jit(solution)/shard_map/ppermute | solution.py:304
  76.4 1.4 %collective-permute-done.4.m0 = bf16[512,128]{1,0:T(8,128)(2,1)S(1)} collective-permute-done((bf16[512,128]{1,0:T(8,128)(2,1)S(1)}, bf16[512,128]{1,0:T(8,128)(2,1)S(1)}, u32[]{:S(2)}, u32[]{:S(2)}) %collective-permute-start.4) | collective-permute-done | bytes 131104 | tf_op jit(solution)/shard_map/ppermute | solution.py:304
  77.9 1.6 %shard_map.66 = (bf16[32,64,128]{2,1,0:T(8,128)(2,1)S(1)}, bf16[2,4,64,128]{3,2,1,0:T(8,128)(2,1)S(1)}) custom-call(s32[6]{0:T(128)S(1)} %pad_add_fusion.1.scalar_ref, bf16[32,64,128]{2,1,0:T(8,128)(2,1)S(1)} %get-tuple-element.13.second_ref, bf16[512,128]{1,0:T(8,128)(2,1)S(1)} %collective-permute-done.4.m0, ...), custom_call_target="tpu_custom_call" | custom-call | bytes 2097152 | tf_op jit(solution)/shard_map/pallas_call | solution.py:18
  79.5 1.9 %collective-permute-start.9 = (bf16[4,64,128]{2,1,0:T(8,128)(2,1)S(1)}, bf16[4,64,128]{2,1,0:T(8,128)(2,1)S(1)}, u32[]{:S(2)}, u32[]{:S(2)}) collective-permute-start(bf16[4,64,128]{2,1,0:T(8,128)(2,1)S(1)} %get-tuple-element.31), channel_id=1, source_target_pairs={{1,2},{3,4},{5,6},{2,1},{4,3},{6,5},{9,10},{11,12},{13,14},{10,9},... | collective-permute-start | bytes 196616 | tf_op jit(solution)/shard_map/ppermute | solution.py:314
  81.5 3.6 %collective-permute-done.9.far_ref = bf16[4,64,128]{2,1,0:T(8,128)(2,1)S(1)} collective-permute-done((bf16[4,64,128]{2,1,0:T(8,128)(2,1)S(1)}, bf16[4,64,128]{2,1,0:T(8,128)(2,1)S(1)}, u32[]{:S(2)}, u32[]{:S(2)}) %collective-permute-start.9) | collective-permute-done | bytes 65568 | tf_op jit(solution)/shard_map/ppermute | solution.py:314
  85.1 1.3 %shard_map.68 = (bf16[8,32,128]{2,1,0:T(8,128)(2,1)S(1)}, bf16[8,32,128]{2,1,0:T(8,128)(2,1)S(1)}) custom-call(s32[6]{0:T(128)S(1)} %pad_add_fusion.1.scalar_ref, bf16[32,64,128]{2,1,0:T(8,128)(2,1)S(1)} %get-tuple-element.15.mean_ref, bf16[4,64,128]{2,1,0:T(8,128)(2,1)S(1)} %collective-permute-done.8.near_ref, ...), custom_call_target="tpu_custom_call" | custom-call | flops 50331648 | bytes 524288 | tf_op jit(solution)/shard_map/pallas_call | solution.py:18
  86.4 10.1 %collective-permute-start.10 = (bf16[8,32,128]{2,1,0:T(8,128)(2,1)S(1)}, bf16[8,32,128]{2,1,0:T(8,128)(2,1)S(1)}, u32[]{:S(2)}, u32[]{:S(2)}) collective-permute-start(bf16[8,32,128]{2,1,0:T(8,128)(2,1)S(1)} %get-tuple-element.19), channel_id=1, source_target_pairs={{8,16},{24,32},{40,48},{56,64},{72,80},{88,96},{104,112},{120,128}... | collective-permute-start | bytes 196616 | tf_op jit(solution)/shard_map/ppermute | solution.py:326
  96.6 1.7 %shard_map.67 = (bf16[32,64,128]{2,1,0:T(8,128)(2,1)S(1)}, f32[16,32,128]{2,1,0:T(8,128)S(1)}) custom-call(s32[6]{0:T(128)S(1)} %pad_add_fusion.1.scalar_ref, bf16[32,64,128]{2,1,0:T(8,128)(2,1)S(1)} %get-tuple-element.15.mean_ref, bf16[4,64,128]{2,1,0:T(8,128)(2,1)S(1)} %collective-permute-done.8.near_ref, ...), custom_call_target="tpu_custom_call" | custom-call | flops 335544320 | bytes 2097152 | tf_op jit(solution)/shard_map/pallas_call | solution.py:18
  98.3 0.3 collective-permute-done.10.far_row
  98.6 5.7 %collective-permute-done.11.near_row = bf16[8,32,128]{2,1,0:T(8,128)(2,1)S(1)} collective-permute-done((bf16[8,32,128]{2,1,0:T(8,128)(2,1)S(1)}, bf16[8,32,128]{2,1,0:T(8,128)(2,1)S(1)}, u32[]{:S(2)}, u32[]{:S(2)}) %collective-permute-start.11) | collective-permute-done | bytes 65568 | tf_op jit(solution)/shard_map/ppermute | solution.py:327
  104.3 0.2 shard_map.69
  104.6 1.1 %copy.22 = bf16[64,32,128]{2,1,0:T(8,128)(2,1)} copy(bf16[64,32,128]{2,0,1:T(8,128)(2,1)S(1)} %bitcast.35) | data formatting | bytes 1048576 | tf_op jit(solution)/shard_map/transpose | solution.py:346
  (30 shorter events, 1.5 us)
Async XLA Ops:
  1.3 18.4 %collective-permute-start.1 = (bf16[16,64,128]{2,1,0:T(8,128)(2,1)S(1)}, bf16[16,64,128]{2,1,0:T(8,128)(2,1)S(1)}, u32[]{:S(2)}, u32[]{:S(2)}) collective-permute-start(bf16[16,64,128]{2,1,0:T(8,128)(2,1)S(1)} %get-tuple-element.25), channel_id=1, source_target_pairs={{8,16},{24,32},{40,48},{56,64},{72,80},{88,96},{104,112},{120,128}... | collective-permute-start | bytes 786440 | tf_op jit(solution)/shard_map/ppermute | solution.py:265
  12.5 21.8 %collective-permute-start = (bf16[16,64,128]{2,1,0:T(8,128)(2,1)S(1)}, bf16[16,64,128]{2,1,0:T(8,128)(2,1)S(1)}, u32[]{:S(2)}, u32[]{:S(2)}) collective-permute-start(bf16[16,64,128]{2,1,0:T(8,128)(2,1)S(1)} %get-tuple-element.26), channel_id=1, source_target_pairs={{0,8},{8,0},{16,24},{24,16},{32,40},{40,32},{48,56},{56,48},{64,72... | collective-permute-start | bytes 786440 | tf_op jit(solution)/shard_map/ppermute | solution.py:266
  34.9 4.5 %copy-start = (bf16[3,9,32,64]{3,2,1,0:T(8,128)(2,1)S(1)}, bf16[3,9,32,64]{3,2,1,0:T(8,128)(2,1)}, u32[]{:S(2)}) copy-start(bf16[3,9,32,64]{3,2,1,0:T(8,128)(2,1)} %param.8) | copy-start | bytes 331780
  34.9 4.4 %copy-start.1 = (bf16[3,64,32]{1,2,0:T(8,128)(2,1)S(1)}, bf16[3,64,32]{1,2,0:T(8,128)(2,1)}, u32[]{:S(2)}) copy-start(bf16[3,64,32]{1,2,0:T(8,128)(2,1)} %param.11) | copy-start | bytes 36868
  35.0 6.9 %collective-permute-start.3 = (bf16[8,64,128]{2,1,0:T(8,128)(2,1)S(1)}, bf16[8,64,128]{2,1,0:T(8,128)(2,1)S(1)}, u32[]{:S(2)}, u32[]{:S(2)}) collective-permute-start(bf16[8,64,128]{2,1,0:T(8,128)(2,1)S(1)} %get-tuple-element.29), channel_id=1, source_target_pairs={{1,2},{3,4},{5,6},{2,1},{4,3},{6,5},{9,10},{11,12},{13,14},{10,9},... | collective-permute-start | bytes 393224 | tf_op jit(solution)/shard_map/ppermute | solution.py:276
  39.2 2.6 %collective-permute-start.2 = (bf16[8,64,128]{2,1,0:T(8,128)(2,1)S(1)}, bf16[8,64,128]{2,1,0:T(8,128)(2,1)S(1)}, u32[]{:S(2)}, u32[]{:S(2)}) collective-permute-start(bf16[8,64,128]{2,1,0:T(8,128)(2,1)S(1)} %get-tuple-element.30), channel_id=1, source_target_pairs={{0,1},{1,0},{2,3},{3,2},{4,5},{5,4},{6,7},{7,6},{8,9},{9,8},{10,11... | collective-permute-start | bytes 393224 | tf_op jit(solution)/shard_map/ppermute | solution.py:277
  39.6 0.7 copy-start.4
  39.8 2.0 %copy-start.2 = (f32[3,32]{1,0:T(4,128)S(1)}, f32[3,32]{1,0:T(4,128)}, u32[]{:S(2)}) copy-start(f32[3,32]{1,0:T(4,128)} %param.9) | copy-start | bytes 1156
  40.3 1.6 %copy-start.3 = (f32[3,32]{1,0:T(4,128)S(1)}, f32[3,32]{1,0:T(4,128)}, u32[]{:S(2)}) copy-start(f32[3,32]{1,0:T(4,128)} %param.10) | copy-start | bytes 1156
  46.0 18.5 %collective-permute-start.7 = (bf16[512,128]{1,0:T(8,128)(2,1)S(1)}, bf16[512,128]{1,0:T(8,128)(2,1)S(1)}, u32[]{:S(2)}, u32[]{:S(2)}) collective-permute-start(bf16[512,128]{1,0:T(8,128)(2,1)S(1)} %get-tuple-element.21), channel_id=1, source_target_pairs={{0,24},{1,48},{2,72},{3,96},{4,152},{5,176},{6,200},{7,224},{8,16}... | collective-permute-start | bytes 393224 | tf_op jit(solution)/shard_map/ppermute | solution.py:304
  50.9 13.7 %collective-permute-start.6 = (bf16[512,128]{1,0:T(8,128)(2,1)S(1)}, bf16[512,128]{1,0:T(8,128)(2,1)S(1)}, u32[]{:S(2)}, u32[]{:S(2)}) collective-permute-start(bf16[512,128]{1,0:T(8,128)(2,1)S(1)} %get-tuple-element.22), channel_id=1, source_target_pairs={{0,8},{1,32},{2,88},{3,112},{4,136},{5,160},{6,216},{7,240},{8,0},... | collective-permute-start | bytes 393224 | tf_op jit(solution)/shard_map/ppermute | solution.py:304
  51.0 25.5 %collective-permute-start.5 = (bf16[512,128]{1,0:T(8,128)(2,1)S(1)}, bf16[512,128]{1,0:T(8,128)(2,1)S(1)}, u32[]{:S(2)}, u32[]{:S(2)}) collective-permute-start(bf16[512,128]{1,0:T(8,128)(2,1)S(1)} %get-tuple-element.23), channel_id=1, source_target_pairs={{0,16},{1,56},{2,64},{3,104},{4,144},{5,184},{6,192},{7,232},{8,24... | collective-permute-start | bytes 393224 | tf_op jit(solution)/shard_map/ppermute | solution.py:304
  60.0 17.9 %collective-permute-start.4 = (bf16[512,128]{1,0:T(8,128)(2,1)S(1)}, bf16[512,128]{1,0:T(8,128)(2,1)S(1)}, u32[]{:S(2)}, u32[]{:S(2)}) collective-permute-start(bf16[512,128]{1,0:T(8,128)(2,1)S(1)} %get-tuple-element.24), channel_id=1, source_target_pairs={{0,0},{1,40},{2,80},{3,120},{4,128},{5,168},{6,208},{7,248},{8,8},... | collective-permute-start | bytes 393224 | tf_op jit(solution)/shard_map/ppermute | solution.py:304
  79.5 5.6 %collective-permute-start.9 = (bf16[4,64,128]{2,1,0:T(8,128)(2,1)S(1)}, bf16[4,64,128]{2,1,0:T(8,128)(2,1)S(1)}, u32[]{:S(2)}, u32[]{:S(2)}) collective-permute-start(bf16[4,64,128]{2,1,0:T(8,128)(2,1)S(1)} %get-tuple-element.31), channel_id=1, source_target_pairs={{1,2},{3,4},{5,6},{2,1},{4,3},{6,5},{9,10},{11,12},{13,14},{10,9},... | collective-permute-start | bytes 196616 | tf_op jit(solution)/shard_map/ppermute | solution.py:314
  81.4 3.7 %collective-permute-start.8 = (bf16[4,64,128]{2,1,0:T(8,128)(2,1)S(1)}, bf16[4,64,128]{2,1,0:T(8,128)(2,1)S(1)}, u32[]{:S(2)}, u32[]{:S(2)}) collective-permute-start(bf16[4,64,128]{2,1,0:T(8,128)(2,1)S(1)} %get-tuple-element.32), channel_id=1, source_target_pairs={{0,1},{1,0},{2,3},{3,2},{4,5},{5,4},{6,7},{7,6},{8,9},{9,8},{10,11... | collective-permute-start | bytes 196616 | tf_op jit(solution)/shard_map/ppermute | solution.py:315
  86.4 12.2 %collective-permute-start.10 = (bf16[8,32,128]{2,1,0:T(8,128)(2,1)S(1)}, bf16[8,32,128]{2,1,0:T(8,128)(2,1)S(1)}, u32[]{:S(2)}, u32[]{:S(2)}) collective-permute-start(bf16[8,32,128]{2,1,0:T(8,128)(2,1)S(1)} %get-tuple-element.19), channel_id=1, source_target_pairs={{8,16},{24,32},{40,48},{56,64},{72,80},{88,96},{104,112},{120,128}... | collective-permute-start | bytes 196616 | tf_op jit(solution)/shard_map/ppermute | solution.py:326
  96.5 7.8 %collective-permute-start.11 = (bf16[8,32,128]{2,1,0:T(8,128)(2,1)S(1)}, bf16[8,32,128]{2,1,0:T(8,128)(2,1)S(1)}, u32[]{:S(2)}, u32[]{:S(2)}) collective-permute-start(bf16[8,32,128]{2,1,0:T(8,128)(2,1)S(1)} %get-tuple-element.20), channel_id=1, source_target_pairs={{0,8},{8,0},{16,24},{24,16},{32,40},{40,32},{48,56},{56,48},{64,72... | collective-permute-start | bytes 196616 | tf_op jit(solution)/shard_map/ppermute | solution.py:327

commit v14 on v11

--- a/solution.py
+++ b/solution.py
@@ -256,11 +256,12 @@
     far_pairs = [(c, c + 1) for c in range(1, cols - 1, 2)]
     far_pairs += [(d, c) for c, d in far_pairs]
 
-    own = jnp.transpose(contact_map, (1, 0, 2))
+    own = jnp.transpose(lax.optimization_barrier(contact_map), (1, 0, 2))
     odd_row = lax.rem(row, 2)
 
     def rim(start):
-        return jnp.transpose(lax.dynamic_slice_in_dim(contact_map, start, 16, 1), (1, 0, 2))
+        part = lax.dynamic_slice_in_dim(contact_map, start, 16, 1)
+        return jnp.transpose(lax.optimization_barrier(part), (1, 0, 2))
 
     far_row = lax.ppermute(rim(16 * odd_row), "row", far_rows)
     near_row = lax.ppermute(rim(16 - 16 * odd_row), "row", near_rows)

time: 105 us -> 103 us (0.981)
  the two profiles are of different devices: /device:TPU:9 before, /device:TPU:25 now
where the time goes in v14:
time: 103 us
  starting transfers between devices  52.4 us (51%)
  waiting for transfers between devices  36.7 us (36%)
  Pallas kernels  9.26 us (9%)
  local copies, waits for them, and re-layouts  3.75 us (4%)
    ppermute x4, starting transfers between devices, on_device(): received.append(lax.ppermute(messages[t], BOTH, pairs))  19.2 us
    ppermute x2, starting transfers between devices, on_device(): far = lax.ppermute(sides[1], 'col', far_pairs)  13 us
    ppermute x4, waiting for transfers between devices, on_device(): received.append(lax.ppermute(messages[t], BOTH, pairs))  12.1 us
    ppermute x1, waiting for transfers between devices, on_device(): far_row = lax.ppermute(rim(16 * odd_row), 'row', far_rows)  11.2 us
    pallas_call x6, Pallas kernels, call(): pl.pallas_call(body, out_shape=outs, in_specs=[SMEM] * n_smem + [VMEM] *...  9.26 us
    ppermute x1, starting transfers between devices, on_device(): far_row = lax.ppermute(to_far, 'row', far_rows)  8.66 us
    ppermute x1, starting transfers between devices, on_device(): near_row = lax.ppermute(rim(16 - 16 * odd_row), 'row', near_rows)  7 us
    ppermute x2, waiting for transfers between devices, on_device(): far = lax.ppermute(sides[1], 'col', far_pairs)  5.05 us
  transfers between devices with their start and end apart: 12, of which 8 were waited for; matrix products, arithmetic and copies ran while one was open for 1% of the time, Pallas kernels for 2%

profile of v14, /device:TPU:25, one launch (start us, length us, event | category | flops | bytes accessed | tf_op | source)
XLA Modules:
  0.0 102.6 jit_solution(15389205581393384040)
XLA Ops:
  0.0 1.1 %constant_dynamic-slice_fusion = (bf16[64,16,128]{2,1,0:T(8,128)(2,1)S(1)}, bf16[64,16,128]{2,1,0:T(8,128)(2,1)S(1)}) fusion(bf16[64,32,128]{2,1,0:T(8,128)(2,1)} %param.6, s32[]{:T(128)S(6)} %select_n.7, s32[]{:T(128)S(6)} %select_n.6), kind=kLoop, calls=%fused_computation.12 | loop fusion | bytes 1048584 | tf_op jit(solution)/shard_map/dynamic_slice | solution.py:263
  1.2 7.0 %collective-permute-start = (bf16[16,64,128]{2,1,0:T(8,128)(2,1)S(1)}, bf16[16,64,128]{2,1,0:T(8,128)(2,1)S(1)}, u32[]{:S(2)}, u32[]{:S(2)}) collective-permute-start(bf16[16,64,128]{2,1,0:T(8,128)(2,1)S(1)} %bitcast.35), channel_id=1, source_target_pairs={{0,8},{8,0},{16,24},{24,16},{32,40},{40,32},{48,56},{56,48},{64,72... | collective-permute-start | bytes 786440 | tf_op jit(solution)/shard_map/ppermute | solution.py:267
  8.2 4.3 %collective-permute-start.1 = (bf16[16,64,128]{2,1,0:T(8,128)(2,1)S(1)}, bf16[16,64,128]{2,1,0:T(8,128)(2,1)S(1)}, u32[]{:S(2)}, u32[]{:S(2)}) collective-permute-start(bf16[16,64,128]{2,1,0:T(8,128)(2,1)S(1)} %bitcast.36), channel_id=1, source_target_pairs={{8,16},{24,32},{40,48},{56,64},{72,80},{88,96},{104,112},{120,128}... | collective-permute-start | bytes 786440 | tf_op jit(solution)/shard_map/ppermute | solution.py:266
  12.8 2.3 %collective-permute-done.near_row = bf16[16,64,128]{2,1,0:T(8,128)(2,1)S(1)} collective-permute-done((bf16[16,64,128]{2,1,0:T(8,128)(2,1)S(1)}, bf16[16,64,128]{2,1,0:T(8,128)(2,1)S(1)}, u32[]{:S(2)}, u32[]{:S(2)}) %collective-permute-start) | collective-permute-done | bytes 262176 | tf_op jit(solution)/shard_map/ppermute | solution.py:267
  15.2 11.2 %collective-permute-done.1.far_row = bf16[16,64,128]{2,1,0:T(8,128)(2,1)S(1)} collective-permute-done((bf16[16,64,128]{2,1,0:T(8,128)(2,1)S(1)}, bf16[16,64,128]{2,1,0:T(8,128)(2,1)S(1)}, u32[]{:S(2)}, u32[]{:S(2)}) %collective-permute-start.1) | collective-permute-done | bytes 262176 | tf_op jit(solution)/shard_map/ppermute | solution.py:266
  26.4 0.5 shard_map.64
  27.0 11.1 %collective-permute-start.3 = (bf16[8,64,128]{2,1,0:T(8,128)(2,1)S(1)}, bf16[8,64,128]{2,1,0:T(8,128)(2,1)S(1)}, u32[]{:S(2)}, u32[]{:S(2)}) collective-permute-start(bf16[8,64,128]{2,1,0:T(8,128)(2,1)S(1)} %get-tuple-element.27), channel_id=1, source_target_pairs={{1,2},{3,4},{5,6},{2,1},{4,3},{6,5},{9,10},{11,12},{13,14},{10,9},... | collective-permute-start | bytes 393224 | tf_op jit(solution)/shard_map/ppermute | solution.py:277
  38.8 0.4 copy-done.5
  39.3 1.5 %collective-permute-done.3.far_ref = bf16[8,64,128]{2,1,0:T(8,128)(2,1)S(1)} collective-permute-done((bf16[8,64,128]{2,1,0:T(8,128)(2,1)S(1)}, bf16[8,64,128]{2,1,0:T(8,128)(2,1)S(1)}, u32[]{:S(2)}, u32[]{:S(2)}) %collective-permute-start.3) | collective-permute-done | bytes 131104 | tf_op jit(solution)/shard_map/ppermute | solution.py:277
  40.9 3.9 %shard_map.65 = (bf16[32,64,128]{2,1,0:T(8,128)(2,1)S(1)}, bf16[4,512,128]{2,1,0:T(8,128)(2,1)S(1)}) custom-call(s32[6]{0:T(128)S(1)} %pad_add_fusion.1.scalar_ref, bf16[16,64,128]{2,1,0:T(8,128)(2,1)S(1)} %collective-permute-done.near_row, bf16[32,64,128]{2,1,0:T(8,128)(2,1)S(1)} %bitcast.32, bf16[16,64,128]{2,1,0:T(8,128)(2,1)S(1)} %collective-permute-done.1.far_row, ...), custom_call_target="tpu_custom_call" | custom-call | flops 838860800 | bytes 4194304 | tf_op jit(solution)/shard_map/pallas_call | solution.py:18
  44.9 0.8 collective-permute-start.7
  45.7 10.0 %collective-permute-start.6 = (bf16[512,128]{1,0:T(8,128)(2,1)S(1)}, bf16[512,128]{1,0:T(8,128)(2,1)S(1)}, u32[]{:S(2)}, u32[]{:S(2)}) collective-permute-start(bf16[512,128]{1,0:T(8,128)(2,1)S(1)} %get-tuple-element.22), channel_id=1, source_target_pairs={{0,16},{1,56},{2,64},{3,104},{4,144},{5,184},{6,192},{7,232},{8,24... | collective-permute-start | bytes 393224 | tf_op jit(solution)/shard_map/ppermute | solution.py:305
  55.7 2.3 %collective-permute-start.5 = (bf16[512,128]{1,0:T(8,128)(2,1)S(1)}, bf16[512,128]{1,0:T(8,128)(2,1)S(1)}, u32[]{:S(2)}, u32[]{:S(2)}) collective-permute-start(bf16[512,128]{1,0:T(8,128)(2,1)S(1)} %get-tuple-element.23), channel_id=1, source_target_pairs={{0,8},{1,32},{2,88},{3,112},{4,136},{5,160},{6,216},{7,240},{8,0},... | collective-permute-start | bytes 393224 | tf_op jit(solution)/shard_map/ppermute | solution.py:305
  58.0 6.1 %collective-permute-start.4 = (bf16[512,128]{1,0:T(8,128)(2,1)S(1)}, bf16[512,128]{1,0:T(8,128)(2,1)S(1)}, u32[]{:S(2)}, u32[]{:S(2)}) collective-permute-start(bf16[512,128]{1,0:T(8,128)(2,1)S(1)} %get-tuple-element.24), channel_id=1, source_target_pairs={{0,0},{1,40},{2,80},{3,120},{4,128},{5,168},{6,208},{7,248},{8,8},... | collective-permute-start | bytes 393224 | tf_op jit(solution)/shard_map/ppermute | solution.py:305
  64.1 11.9 %collective-permute-done.6.m2 = bf16[512,128]{1,0:T(8,128)(2,1)S(1)} collective-permute-done((bf16[512,128]{1,0:T(8,128)(2,1)S(1)}, bf16[512,128]{1,0:T(8,128)(2,1)S(1)}, u32[]{:S(2)}, u32[]{:S(2)}) %collective-permute-start.6) | collective-permute-done | bytes 131104 | tf_op jit(solution)/shard_map/ppermute | solution.py:305
  76.2 1.6 %shard_map.66 = (bf16[32,64,128]{2,1,0:T(8,128)(2,1)S(1)}, bf16[2,4,64,128]{3,2,1,0:T(8,128)(2,1)S(1)}) custom-call(s32[6]{0:T(128)S(1)} %pad_add_fusion.1.scalar_ref, bf16[32,64,128]{2,1,0:T(8,128)(2,1)S(1)} %get-tuple-element.13.second_ref, bf16[512,128]{1,0:T(8,128)(2,1)S(1)} %collective-permute-done.4.m0, ...), custom_call_target="tpu_custom_call" | custom-call | bytes 2097152 | tf_op jit(solution)/shard_map/pallas_call | solution.py:18
  77.9 1.9 %collective-permute-start.9 = (bf16[4,64,128]{2,1,0:T(8,128)(2,1)S(1)}, bf16[4,64,128]{2,1,0:T(8,128)(2,1)S(1)}, u32[]{:S(2)}, u32[]{:S(2)}) collective-permute-start(bf16[4,64,128]{2,1,0:T(8,128)(2,1)S(1)} %get-tuple-element.29), channel_id=1, source_target_pairs={{1,2},{3,4},{5,6},{2,1},{4,3},{6,5},{9,10},{11,12},{13,14},{10,9},... | collective-permute-start | bytes 196616 | tf_op jit(solution)/shard_map/ppermute | solution.py:315
  79.9 3.6 %collective-permute-done.9.far_ref = bf16[4,64,128]{2,1,0:T(8,128)(2,1)S(1)} collective-permute-done((bf16[4,64,128]{2,1,0:T(8,128)(2,1)S(1)}, bf16[4,64,128]{2,1,0:T(8,128)(2,1)S(1)}, u32[]{:S(2)}, u32[]{:S(2)}) %collective-permute-start.9) | collective-permute-done | bytes 65568 | tf_op jit(solution)/shard_map/ppermute | solution.py:315
  83.5 1.3 %shard_map.68 = (bf16[8,32,128]{2,1,0:T(8,128)(2,1)S(1)}, bf16[8,32,128]{2,1,0:T(8,128)(2,1)S(1)}) custom-call(s32[6]{0:T(128)S(1)} %pad_add_fusion.1.scalar_ref, bf16[32,64,128]{2,1,0:T(8,128)(2,1)S(1)} %get-tuple-element.15.mean_ref, bf16[4,64,128]{2,1,0:T(8,128)(2,1)S(1)} %collective-permute-done.8.near_ref, ...), custom_call_target="tpu_custom_call" | custom-call | flops 50331648 | bytes 524288 | tf_op jit(solution)/shard_map/pallas_call | solution.py:18
  84.7 8.7 %collective-permute-start.10 = (bf16[8,32,128]{2,1,0:T(8,128)(2,1)S(1)}, bf16[8,32,128]{2,1,0:T(8,128)(2,1)S(1)}, u32[]{:S(2)}, u32[]{:S(2)}) collective-permute-start(bf16[8,32,128]{2,1,0:T(8,128)(2,1)S(1)} %get-tuple-element.19), channel_id=1, source_target_pairs={{8,16},{24,32},{40,48},{56,64},{72,80},{88,96},{104,112},{120,128}... | collective-permute-start | bytes 196616 | tf_op jit(solution)/shard_map/ppermute | solution.py:327
  93.5 1.7 %shard_map.67 = (bf16[32,64,128]{2,1,0:T(8,128)(2,1)S(1)}, f32[16,32,128]{2,1,0:T(8,128)S(1)}) custom-call(s32[6]{0:T(128)S(1)} %pad_add_fusion.1.scalar_ref, bf16[32,64,128]{2,1,0:T(8,128)(2,1)S(1)} %get-tuple-element.15.mean_ref, bf16[4,64,128]{2,1,0:T(8,128)(2,1)S(1)} %collective-permute-done.8.near_ref, ...), custom_call_target="tpu_custom_call" | custom-call | flops 335544320 | bytes 2097152 | tf_op jit(solution)/shard_map/pallas_call | solution.py:18
  95.2 1.5 %collective-permute-done.10.far_row = bf16[8,32,128]{2,1,0:T(8,128)(2,1)S(1)} collective-permute-done((bf16[8,32,128]{2,1,0:T(8,128)(2,1)S(1)}, bf16[8,32,128]{2,1,0:T(8,128)(2,1)S(1)}, u32[]{:S(2)}, u32[]{:S(2)}) %collective-permute-start.10) | collective-permute-done | bytes 65568 | tf_op jit(solution)/shard_map/ppermute | solution.py:327
  96.7 4.5 %collective-permute-done.11.near_row = bf16[8,32,128]{2,1,0:T(8,128)(2,1)S(1)} collective-permute-done((bf16[8,32,128]{2,1,0:T(8,128)(2,1)S(1)}, bf16[8,32,128]{2,1,0:T(8,128)(2,1)S(1)}, u32[]{:S(2)}, u32[]{:S(2)}) %collective-permute-start.11) | collective-permute-done | bytes 65568 | tf_op jit(solution)/shard_map/ppermute | solution.py:328
  101.4 1.1 %copy.22 = bf16[64,32,128]{2,1,0:T(8,128)(2,1)} copy(bf16[64,32,128]{2,0,1:T(8,128)(2,1)S(1)} %bitcast.33) | data formatting | bytes 1048576 | tf_op jit(solution)/shard_map/transpose | solution.py:347
  (34 shorter events, 2.0 us)
Async XLA Ops:
  1.1 11.5 %copy-start = (bf16[64,32,128]{2,1,0:T(8,128)(2,1)S(1)}, bf16[64,32,128]{2,1,0:T(8,128)(2,1)}, u32[]{:S(2)}) copy-start(bf16[64,32,128]{2,1,0:T(8,128)(2,1)} %param.6) | copy-start | bytes 1572868
  1.2 14.0 %collective-permute-start = (bf16[16,64,128]{2,1,0:T(8,128)(2,1)S(1)}, bf16[16,64,128]{2,1,0:T(8,128)(2,1)S(1)}, u32[]{:S(2)}, u32[]{:S(2)}) collective-permute-start(bf16[16,64,128]{2,1,0:T(8,128)(2,1)S(1)} %bitcast.35), channel_id=1, source_target_pairs={{0,8},{8,0},{16,24},{24,16},{32,40},{40,32},{48,56},{56,48},{64,72... | collective-permute-start | bytes 786440 | tf_op jit(solution)/shard_map/ppermute | solution.py:267
  8.2 18.1 %collective-permute-start.1 = (bf16[16,64,128]{2,1,0:T(8,128)(2,1)S(1)}, bf16[16,64,128]{2,1,0:T(8,128)(2,1)S(1)}, u32[]{:S(2)}, u32[]{:S(2)}) collective-permute-start(bf16[16,64,128]{2,1,0:T(8,128)(2,1)S(1)} %bitcast.36), channel_id=1, source_target_pairs={{8,16},{24,32},{40,48},{56,64},{72,80},{88,96},{104,112},{120,128}... | collective-permute-start | bytes 786440 | tf_op jit(solution)/shard_map/ppermute | solution.py:266
  27.0 11.4 %copy-start.1 = (bf16[3,9,32,64]{3,2,1,0:T(8,128)(2,1)S(1)}, bf16[3,9,32,64]{3,2,1,0:T(8,128)(2,1)}, u32[]{:S(2)}) copy-start(bf16[3,9,32,64]{3,2,1,0:T(8,128)(2,1)} %param.8) | copy-start | bytes 331780
  27.0 11.2 %copy-start.2 = (bf16[3,64,32]{1,2,0:T(8,128)(2,1)S(1)}, bf16[3,64,32]{1,2,0:T(8,128)(2,1)}, u32[]{:S(2)}) copy-start(bf16[3,64,32]{1,2,0:T(8,128)(2,1)} %param.11) | copy-start | bytes 36868
  27.0 13.7 %collective-permute-start.3 = (bf16[8,64,128]{2,1,0:T(8,128)(2,1)S(1)}, bf16[8,64,128]{2,1,0:T(8,128)(2,1)S(1)}, u32[]{:S(2)}, u32[]{:S(2)}) collective-permute-start(bf16[8,64,128]{2,1,0:T(8,128)(2,1)S(1)} %get-tuple-element.27), channel_id=1, source_target_pairs={{1,2},{3,4},{5,6},{2,1},{4,3},{6,5},{9,10},{11,12},{13,14},{10,9},... | collective-permute-start | bytes 393224 | tf_op jit(solution)/shard_map/ppermute | solution.py:277
  38.1 2.6 %collective-permute-start.2 = (bf16[8,64,128]{2,1,0:T(8,128)(2,1)S(1)}, bf16[8,64,128]{2,1,0:T(8,128)(2,1)S(1)}, u32[]{:S(2)}, u32[]{:S(2)}) collective-permute-start(bf16[8,64,128]{2,1,0:T(8,128)(2,1)S(1)} %get-tuple-element.28), channel_id=1, source_target_pairs={{0,1},{1,0},{2,3},{3,2},{4,5},{5,4},{6,7},{7,6},{8,9},{9,8},{10,11... | collective-permute-start | bytes 393224 | tf_op jit(solution)/shard_map/ppermute | solution.py:278
  38.5 0.7 copy-start.5
  38.7 2.0 %copy-start.3 = (f32[3,32]{1,0:T(4,128)S(1)}, f32[3,32]{1,0:T(4,128)}, u32[]{:S(2)}) copy-start(f32[3,32]{1,0:T(4,128)} %param.9) | copy-start | bytes 1156
  39.3 1.6 %copy-start.4 = (f32[3,32]{1,0:T(4,128)S(1)}, f32[3,32]{1,0:T(4,128)}, u32[]{:S(2)}) copy-start(f32[3,32]{1,0:T(4,128)} %param.10) | copy-start | bytes 1156
  44.9 19.2 %collective-permute-start.7 = (bf16[512,128]{1,0:T(8,128)(2,1)S(1)}, bf16[512,128]{1,0:T(8,128)(2,1)S(1)}, u32[]{:S(2)}, u32[]{:S(2)}) collective-permute-start(bf16[512,128]{1,0:T(8,128)(2,1)S(1)} %get-tuple-element.21), channel_id=1, source_target_pairs={{0,24},{1,48},{2,72},{3,96},{4,152},{5,176},{6,200},{7,224},{8,16}... | collective-permute-start | bytes 393224 | tf_op jit(solution)/shard_map/ppermute | solution.py:305
  45.7 30.3 %collective-permute-start.6 = (bf16[512,128]{1,0:T(8,128)(2,1)S(1)}, bf16[512,128]{1,0:T(8,128)(2,1)S(1)}, u32[]{:S(2)}, u32[]{:S(2)}) collective-permute-start(bf16[512,128]{1,0:T(8,128)(2,1)S(1)} %get-tuple-element.22), channel_id=1, source_target_pairs={{0,16},{1,56},{2,64},{3,104},{4,144},{5,184},{6,192},{7,232},{8,24... | collective-permute-start | bytes 393224 | tf_op jit(solution)/shard_map/ppermute | solution.py:305
  55.7 20.3 %collective-permute-start.5 = (bf16[512,128]{1,0:T(8,128)(2,1)S(1)}, bf16[512,128]{1,0:T(8,128)(2,1)S(1)}, u32[]{:S(2)}, u32[]{:S(2)}) collective-permute-start(bf16[512,128]{1,0:T(8,128)(2,1)S(1)} %get-tuple-element.23), channel_id=1, source_target_pairs={{0,8},{1,32},{2,88},{3,112},{4,136},{5,160},{6,216},{7,240},{8,0},... | collective-permute-start | bytes 393224 | tf_op jit(solution)/shard_map/ppermute | solution.py:305
  58.0 18.2 %collective-permute-start.4 = (bf16[512,128]{1,0:T(8,128)(2,1)S(1)}, bf16[512,128]{1,0:T(8,128)(2,1)S(1)}, u32[]{:S(2)}, u32[]{:S(2)}) collective-permute-start(bf16[512,128]{1,0:T(8,128)(2,1)S(1)} %get-tuple-element.24), channel_id=1, source_target_pairs={{0,0},{1,40},{2,80},{3,120},{4,128},{5,168},{6,208},{7,248},{8,8},... | collective-permute-start | bytes 393224 | tf_op jit(solution)/shard_map/ppermute | solution.py:305
  77.9 5.6 %collective-permute-start.9 = (bf16[4,64,128]{2,1,0:T(8,128)(2,1)S(1)}, bf16[4,64,128]{2,1,0:T(8,128)(2,1)S(1)}, u32[]{:S(2)}, u32[]{:S(2)}) collective-permute-start(bf16[4,64,128]{2,1,0:T(8,128)(2,1)S(1)} %get-tuple-element.29), channel_id=1, source_target_pairs={{1,2},{3,4},{5,6},{2,1},{4,3},{6,5},{9,10},{11,12},{13,14},{10,9},... | collective-permute-start | bytes 196616 | tf_op jit(solution)/shard_map/ppermute | solution.py:315
  79.8 3.7 %collective-permute-start.8 = (bf16[4,64,128]{2,1,0:T(8,128)(2,1)S(1)}, bf16[4,64,128]{2,1,0:T(8,128)(2,1)S(1)}, u32[]{:S(2)}, u32[]{:S(2)}) collective-permute-start(bf16[4,64,128]{2,1,0:T(8,128)(2,1)S(1)} %get-tuple-element.30), channel_id=1, source_target_pairs={{0,1},{1,0},{2,3},{3,2},{4,5},{5,4},{6,7},{7,6},{8,9},{9,8},{10,11... | collective-permute-start | bytes 196616 | tf_op jit(solution)/shard_map/ppermute | solution.py:316
  84.7 12.0 %collective-permute-start.10 = (bf16[8,32,128]{2,1,0:T(8,128)(2,1)S(1)}, bf16[8,32,128]{2,1,0:T(8,128)(2,1)S(1)}, u32[]{:S(2)}, u32[]{:S(2)}) collective-permute-start(bf16[8,32,128]{2,1,0:T(8,128)(2,1)S(1)} %get-tuple-element.19), channel_id=1, source_target_pairs={{8,16},{24,32},{40,48},{56,64},{72,80},{88,96},{104,112},{120,128}... | collective-permute-start | bytes 196616 | tf_op jit(solution)/shard_map/ppermute | solution.py:327
  93.4 7.8 %collective-permute-start.11 = (bf16[8,32,128]{2,1,0:T(8,128)(2,1)S(1)}, bf16[8,32,128]{2,1,0:T(8,128)(2,1)S(1)}, u32[]{:S(2)}, u32[]{:S(2)}) collective-permute-start(bf16[8,32,128]{2,1,0:T(8,128)(2,1)S(1)} %get-tuple-element.20), channel_id=1, source_target_pairs={{0,8},{8,0},{16,24},{24,16},{32,40},{40,32},{48,56},{56,48},{64,72... | collective-permute-start | bytes 196616 | tf_op jit(solution)/shard_map/ppermute | solution.py:328
